TPU v7x, 32 devices: a whole 2x2x4 slice. The times are simulated.
32 devices in a mesh: grp: 2 (over x), prompt: 4 (over y, core), resp: 4 (over z).
Axes of the slice: x: 2, y: 2, z: 4, core: 2. Of those that a mesh axis runs over, the one named last changes fastest.
Arguments:
- prompt_states: bfloat16 [2, 256, 4096], P('grp', 'prompt'), may hold values from -6 to 6
- response_states: bfloat16 [2, 16, 512, 4096], P('grp', ('prompt', 'resp')), may hold values from -6 to 6
- queries: bfloat16 [2, 16, 512, 2048], P('grp', ('prompt', 'resp'))
- grad_output: bfloat16 [2, 16, 512, 2048], P('grp', ('prompt', 'resp')), may hold values from -24 to 24
- key_weight: bfloat16 [4096, 512], replicated, may hold values from -0.09375 to 0.09375
- value_weight: bfloat16 [4096, 512], replicated, may hold values from -0.09375 to 0.09375
- rewards: float32 [2, 16], P('grp', ('prompt', 'resp'))
- lengths: int32 [2, 16], P('grp', ('prompt', 'resp')), may hold values from 1 to 512, 4915 in all within a row
- group_ids: int32 [2, 16], P('grp', ('prompt', 'resp')), may hold values from 0 to 7
Outputs:
- query_grad: bfloat16 [2, 16, 512, 2048], P('grp', ('prompt', 'resp'))
- key_weight_grad: float32 [4096, 512], P(('prompt', 'resp'))
- value_weight_grad: float32 [4096, 512], P(('prompt', 'resp'))
Inputs may be any that keep to these rules, and one draw needn't show every extreme that they name: `lengths`: token slots at and above a response's length are padding; in every rollout group some response has all 512.
All inputs are finite; a program needn't handle non-finite values.
Results may differ from a plain program's by a relative error of at most 0.009.
The roundings to bfloat16 on the way count: a program that leaves them out, or rounds other values in their place, can miss the bound.
Values may be sent and summed in bfloat16 or wider, within the bound.
No kernel may reach another device: no remote copies, remote signals or barrier semaphores. Data moves between devices by JAX's collectives and lax.ppermute only.
A program may use at most 128 MiB of HBM per device.

v0:
```python
import jax
import jax.numpy as jnp
from jax import lax
from jax.sharding import PartitionSpec as P

HEAD_DIM = 128
RLEN = 512
QBLOCK = 128
NADV = 8


THETA = 1000000.0
EPS = 1e-06


def rotary_tables(positions, half):
    steps = jnp.arange(half, dtype=jnp.float32)
    freq = THETA ** (-2.0 * steps / (2.0 * half))
    angle = positions.astype(jnp.float32)[:, None] * freq[None, :]
    return (jnp.cos(angle)[:, None, :], jnp.sin(angle)[:, None, :])


def finish_keys(raw, positions):
    count = raw.shape[0]
    heads = raw.reshape(count, -1, HEAD_DIM)
    factor = lax.rsqrt(jnp.mean(heads * heads, axis=-1, keepdims=True) + EPS)
    normed = heads * factor
    half = HEAD_DIM // 2
    cosine, sine = rotary_tables(positions, half)
    first = normed[..., :half]
    second = normed[..., half:]
    turned = jnp.concatenate(
        [first * cosine - second * sine, second * cosine + first * sine], axis=-1
    )
    return turned.reshape(count, -1)


def keys_backward(grad, raw, positions):
    count = raw.shape[0]
    heads = raw.reshape(count, -1, HEAD_DIM)
    factor = lax.rsqrt(jnp.mean(heads * heads, axis=-1, keepdims=True) + EPS)
    normed = heads * factor
    half = HEAD_DIM // 2
    cosine, sine = rotary_tables(positions, half)
    upper = grad.reshape(count, -1, HEAD_DIM)
    grad_a = upper[..., :half]
    grad_b = upper[..., half:]
    unturned = jnp.concatenate(
        [grad_a * cosine + grad_b * sine, grad_b * cosine - grad_a * sine], axis=-1
    )
    inner = jnp.mean(unturned * normed, axis=-1, keepdims=True)
    return (factor * (unturned - normed * inner)).reshape(count, -1)


def attend(query, dout, keys, values, row_start, prompt_len):
    rows = query.shape[0]
    total = keys.shape[0]
    kv_heads = keys.shape[1] // HEAD_DIM
    fold = query.shape[1] // keys.shape[1]
    scale = HEAD_DIM ** (-0.5)
    q_all = query.reshape(rows, kv_heads, fold, HEAD_DIM)
    k_all = keys.reshape(total, kv_heads, HEAD_DIM)
    v_all = values.reshape(total, kv_heads, HEAD_DIM)
    d_all = dout.reshape(rows, kv_heads, fold, HEAD_DIM)
    scores = jnp.einsum("rhgd,nhd->hgrn", q_all, k_all, preferred_element_type=jnp.float32) * scale
    key_pos = jnp.arange(total, dtype=jnp.int32)
    row_pos = row_start + jnp.arange(rows, dtype=jnp.int32)
    visible = (key_pos[None, :] < prompt_len) | (key_pos[None, :] - prompt_len <= row_pos[:, None])
    scores = jnp.where(visible, scores, -jnp.inf)
    peak = jnp.max(scores, axis=-1, keepdims=True)
    expo = jnp.exp(scores - peak)
    probs = expo / jnp.sum(expo, axis=-1, keepdims=True)
    probs_b = probs.astype(jnp.bfloat16)
    attn = jnp.einsum("hgrn,nhd->rhgd", probs_b, v_all, preferred_element_type=jnp.float32)
    delta = jnp.sum(d_all.astype(jnp.float32) * attn, axis=-1)
    dprobs = jnp.einsum("rhgd,nhd->hgrn", d_all, v_all, preferred_element_type=jnp.float32)
    dscores = (probs * (dprobs - jnp.transpose(delta, (1, 2, 0))[..., None])).astype(jnp.bfloat16)
    grad_q = (
        jnp.einsum("hgrn,nhd->rhgd", dscores, k_all, preferred_element_type=jnp.float32) * scale
    )
    grad_k = (
        jnp.einsum("hgrn,rhgd->nhd", dscores, q_all, preferred_element_type=jnp.float32) * scale
    )
    grad_v = jnp.einsum("hgrn,rhgd->nhd", probs_b, d_all, preferred_element_type=jnp.float32)
    return (
        grad_q.reshape(rows, -1).astype(jnp.bfloat16),
        grad_k.reshape(total, -1),
        grad_v.reshape(total, -1),
    )


def from_sums(rewards, onehot, count, total, square):
    members = jnp.maximum(count, 1.0)
    mean = total / members
    spread = jnp.sqrt(jnp.maximum(square / members - mean * mean, 0.0))
    own_mean = jnp.sum(onehot * mean[None, :], axis=1)
    own_spread = jnp.sum(onehot * spread[None, :], axis=1)
    return (rewards - own_mean) / jnp.maximum(own_spread, 0.5)


def body(
    prompt_states,
    response_states,
    queries,
    grad_output,
    key_weight,
    value_weight,
    rewards,
    lengths,
    group_ids,
):
    width = key_weight.shape[1]
    shard_rows = prompt_states.shape[1]
    local_rewards = rewards[0]
    local_lengths = lengths[0]
    onehot = (group_ids[0][:, None] == jnp.arange(NADV, dtype=jnp.int32)[None, :]).astype(
        jnp.float32
    )
    count = jnp.sum(onehot, axis=0)
    total = jnp.sum(onehot * local_rewards[:, None], axis=0)
    square = jnp.sum(onehot * (local_rewards * local_rewards)[:, None], axis=0)
    sums = lax.psum((count, total, square), ("prompt", "resp"))
    advantage = from_sums(local_rewards, onehot, sums[0], sums[1], sums[2])
    sub_rows = shard_rows // lax.axis_size("resp")
    sub_offset = lax.axis_index("resp") * sub_rows
    slice_positions = (
        lax.axis_index("prompt") * shard_rows + sub_offset + jnp.arange(sub_rows, dtype=jnp.int32)
    )
    slice_rows = lax.dynamic_slice_in_dim(prompt_states[0], sub_offset, sub_rows, 0)
    slice_raw = jnp.dot(slice_rows, key_weight, preferred_element_type=jnp.float32)
    slice_keys = finish_keys(slice_raw, slice_positions).astype(jnp.bfloat16)
    slice_values = jnp.dot(slice_rows, value_weight, preferred_element_type=jnp.float32).astype(
        jnp.bfloat16
    )
    prompt_keys, prompt_values = (
        lax.all_gather(slice_keys, ("prompt", "resp"), axis=0, tiled=True),
        lax.all_gather(slice_values, ("prompt", "resp"), axis=0, tiled=True),
    )
    prompt_len = prompt_keys.shape[0]
    key_count = prompt_len + RLEN
    states = response_states[0, 0]
    positions = prompt_len + jnp.arange(RLEN, dtype=jnp.int32)
    own_raw = jnp.dot(states, key_weight, preferred_element_type=jnp.float32)
    own_keys = finish_keys(own_raw, positions).astype(jnp.bfloat16)
    own_values = jnp.dot(states, value_weight, preferred_element_type=jnp.float32).astype(
        jnp.bfloat16
    )
    keys = jnp.concatenate([prompt_keys, own_keys], axis=0)
    values = jnp.concatenate([prompt_values, own_values], axis=0)
    length = local_lengths[0]
    live = jnp.arange(RLEN, dtype=jnp.int32) < length
    coef = jnp.where(live, advantage[0] / length.astype(jnp.float32), jnp.float32(0.0))
    dout = (grad_output[0, 0].astype(jnp.float32) * coef[:, None]).astype(jnp.bfloat16)
    query = queries[0, 0]
    query_width = query.shape[1]

    def per_block(carry, block, query=query, dout=dout, keys=keys, values=values, length=length):
        acc_k, acc_v = carry
        row_start = block * QBLOCK
        query_rows = lax.dynamic_slice_in_dim(query, row_start, QBLOCK, 0)
        dout_rows = lax.dynamic_slice_in_dim(dout, row_start, QBLOCK, 0)

        def active():
            return attend(query_rows, dout_rows, keys, values, row_start, prompt_len)

        def skipped():
            return (
                jnp.zeros((QBLOCK, query_width), jnp.bfloat16),
                jnp.zeros((key_count, width), jnp.float32),
                jnp.zeros((key_count, width), jnp.float32),
            )

        grad_q, grad_k, grad_v = lax.cond(row_start < length, active, skipped)
        return ((acc_k + grad_k, acc_v + grad_v), grad_q)

    start = (jnp.zeros((key_count, width), jnp.float32), jnp.zeros((key_count, width), jnp.float32))
    (block_k, block_v), grad_blocks = lax.scan(
        per_block, start, jnp.arange(RLEN // QBLOCK, dtype=jnp.int32)
    )
    query_grads = [grad_blocks.reshape(RLEN, query_width)]
    sum_keys = block_k[:prompt_len]
    sum_values = block_v[:prompt_len]
    own_dk = keys_backward(block_k[prompt_len:], own_raw, positions).astype(jnp.bfloat16)
    own_dv = block_v[prompt_len:].astype(jnp.bfloat16)
    grad_wk = jnp.einsum("rd,rk->dk", states, own_dk, preferred_element_type=jnp.float32)
    grad_wv = jnp.einsum("rd,rk->dk", states, own_dv, preferred_element_type=jnp.float32)
    slice_dk, slice_dv = (
        lax.psum_scatter(sum_keys, ("prompt", "resp"), scatter_dimension=0, tiled=True),
        lax.psum_scatter(sum_values, ("prompt", "resp"), scatter_dimension=0, tiled=True),
    )
    slice_raw_grad = keys_backward(slice_dk, slice_raw, slice_positions).astype(jnp.bfloat16)
    grad_wk = grad_wk + jnp.einsum(
        "rd,rk->dk", slice_rows, slice_raw_grad, preferred_element_type=jnp.float32
    )
    grad_wv = grad_wv + jnp.einsum(
        "rd,rk->dk", slice_rows, slice_dv.astype(jnp.bfloat16), preferred_element_type=jnp.float32
    )
    shares = (
        lax.psum_scatter(grad_wk, ("prompt", "resp"), scatter_dimension=0, tiled=True),
        lax.psum_scatter(grad_wv, ("prompt", "resp"), scatter_dimension=0, tiled=True),
    )
    summed = lax.psum((shares[0], shares[1]), "grp")
    return (jnp.stack(query_grads, axis=0)[None], summed[0], summed[1])


def solution(mesh):
    placed = (
        P("grp", "prompt", None),
        P("grp", ("prompt", "resp"), None, None),
        P("grp", ("prompt", "resp"), None, None),
        P("grp", ("prompt", "resp"), None, None),
        P(),
        P(),
        P("grp", ("prompt", "resp")),
        P("grp", ("prompt", "resp")),
        P("grp", ("prompt", "resp")),
    )
    return jax.shard_map(
        body,
        mesh=mesh,
        in_specs=placed,
        out_specs=(
            P("grp", ("prompt", "resp"), None, None),
            P(("prompt", "resp"), None),
            P(("prompt", "resp"), None),
        ),
        check_vma=False,
    )
```

profile of v0, /device:TPU:0, one launch (start us, length us, event | category | flops | bytes accessed | tf_op | source)
XLA Modules:
  0.0 644.3 jit_solution(14823082033014504189)
XLA Ops:
  7.3 6.4 copy.86
  13.7 5.9 fusion.25
  20.3 1.5 copy-done.3
  21.9 1.3 multiply_reduce_fusion.3
  23.3 2.4 multiply_reduce_fusion.1
  27.7 36.0 %all_gather.7 = bf16[256,512]{1,0:T(8,128)(2,1)S(1)} all-gather(bf16[16,512]{1,0:T(8,128)(2,1)S(1)} %convolution_convert_fusion), channel_id=1, replica_groups=mesh['grp'=2,'prompt'=4,'resp'=4] {'prompt','resp'}, dimensions={0}, use_global_device_ids=true | all-gather | bytes 278528 | tf_op jit(solution)/shard_map/all_gather | solution.py:137
  64.4 1.2 copy.55
  65.6 4.0 copy.49
  69.6 3.9 copy.54
  73.7 30.8 %all_gather.6 = bf16[256,512]{1,0:T(8,128)(2,1)S(1)} all-gather(bf16[16,512]{1,0:T(8,128)(2,1)S(1)} %copy_bitcast_fusion), channel_id=1, replica_groups=mesh['grp'=2,'prompt'=4,'resp'=4] {'prompt','resp'}, dimensions={0}, use_global_device_ids=true | all-gather | bytes 278528 | tf_op jit(solution)/shard_map/all_gather | solution.py:136
  104.7 31.7 %all-reduce = (f32[8]{0:T(128)S(1)}, f32[8]{0:T(128)S(1)}, f32[8]{0:T(128)S(1)}) all-reduce(f32[8]{0:T(128)S(1)} %get-tuple-element.264, f32[8]{0:T(128)S(1)} %fusion.45, f32[8]{0:T(128)S(1)} %get-tuple-element.263), channel_id=1, replica_groups=mesh['grp'=2,'prompt'=4,'resp'=4] {'prompt','resp'}, use_global_device_ids=true, to_apply=%region_0.0 | all-reduce | flops 24 | bytes 192 | tf_op jit(solution)/shard_map/psum | solution.py:122
  136.4 0.7 select_reduce_fusion
  138.4 3.4 fusion.18
  142.2 0.9 pad_maximum_fusion.1
  143.1 60.5 %while.15 = (s32[]{:T(128)}, f32[768,512]{0,1:T(8,128)}, f32[768,512]{0,1:T(8,128)}, bf16[4,128,2048]{2,1,0:T(8,128)(2,1)}, s32[4]{0:T(128)S(1)}, /*index=5*/s32...) while((s32[]{:T(128)}, f32[768,512]{0,1:T(8,128)}, ...), condition=%wide.region_13.14_spmd.clone, body=%wide.region_7.13_spmd.clone.sunk | while | flops 2435121664 | bytes 83084128 | solution.py:177
  145.0 21.2 %conditional.3 = (f32[768,512]{0,1:T(8,128)}, f32[768,512]{0,1:T(8,128)S(1)}, bf16[1,128,2048]{1,2,0:T(8,128)(2,1)}) conditional(s32[]{:T(128)} %convert_element_type.153, () %tuple.69, (s32[]{:T(128)}, bf16[512,2048]{0,1:T(8,128)(2,1)}, bf16[768,512]{0,1:T(8,128)(2,1)}, bf16[512,2048]{0,1:T(8,128)(2,1)}, bf16[768,512]{0,1:T(8,128)(2,1)}) %tuple.70), branch_computations={%region_8.8_spmd, %region_9.12_spmd} | conditional | flops 2433548800 | bytes 71549576 | solution.py:173
  145.0 1.9 constant_dynamic-slice_fusion
  147.1 6.1 fusion.51
  153.2 3.4 fusion.10
  156.6 2.4 fusion.13
  159.7 2.7 fusion.2
  162.4 1.9 fusion.12
  164.4 1.8 bitcast_multiply_fusion
  166.1 3.5 select_add_fusion.3
  169.6 1.2 copy.99
  170.9 0.8 constant_dynamic-update-slice_fusion.2
  173.6 2.2 conditional.3
  173.6 0.9 broadcast_in_dim.22
  174.6 1.3 broadcast.230
  175.8 4.4 select_add_fusion.3
  180.3 1.2 copy.99
  181.5 0.8 constant_dynamic-update-slice_fusion.2
  184.2 2.2 conditional.3
  184.3 0.9 broadcast_in_dim.22
  185.2 1.3 broadcast.230
  186.5 4.4 select_add_fusion.3
  190.9 1.2 copy.99
  192.2 0.8 constant_dynamic-update-slice_fusion.2
  194.9 2.2 conditional.3
  194.9 0.9 broadcast_in_dim.22
  195.9 1.3 broadcast.230
  197.1 4.4 select_add_fusion.3
  201.6 1.2 copy.99
  202.8 0.8 constant_dynamic-update-slice_fusion.2
  203.7 1.1 slice.48
  204.7 1.0 copy.84
  205.8 1.1 slice.44
  206.9 1.0 copy.82
  207.9 107.7 %reduce-scatter.15.cloned.1.call-done = f32[16,512]{1,0:T(8,128)} async-done(((f32[256,512]{1,0:T(8,128)}), f32[16,512]{1,0:T(8,128)}) %reduce-scatter.15.cloned.1.call-update) | async-done | bytes 32784
  315.6 0.9 copy.85
  316.5 1.2 fusion.33
  317.9 1.3 copy-done.5
  319.2 5.6 bitcast_add_fusion
  325.1 1.1 copy-done.1
  327.1 47.9 %reduce-scatter.13.cloned.1.call-done = f32[16,512]{1,0:T(8,128)} async-done(((f32[256,512]{1,0:T(8,128)}), f32[16,512]{1,0:T(8,128)}) %reduce-scatter.13.cloned.1.call-update) | async-done | bytes 32784
  375.0 0.9 copy.83
  376.3 1.4 fusion.30
  377.7 0.8 copy-done.6
  378.5 5.6 bitcast_add_fusion.1
  384.1 98.9 %reduce-scatter.11.cloned.1.call-done = f32[256,512]{0,1:T(8,128)} async-done(((f32[4096,512]{0,1:T(8,128)}), f32[256,512]{0,1:T(8,128)}) %reduce-scatter.11.cloned.1.call-update) | async-done | bytes 524304 | tf_op jit(solution)/shard_map/reduce_scatter | solution.py:200
  483.0 108.6 %reduce-scatter.9.cloned.1.call-done = f32[256,512]{0,1:T(8,128)} async-done(((f32[4096,512]{0,1:T(8,128)}), f32[256,512]{0,1:T(8,128)}) %reduce-scatter.9.cloned.1.call-update) | async-done | bytes 524304 | tf_op jit(solution)/shard_map/reduce_scatter | solution.py:199
  591.6 42.2 %all-reduce.4.cloned.1.call-done = (f32[256,512]{0,1:T(8,128)}, f32[256,512]{0,1:T(8,128)}) async-done(((f32[256,512]{0,1:T(8,128)}, f32[256,512]{0,1:T(8,128)}), (f32[256,512]{0,1:T(8,128)}, f32[256,512]{0,1:T(8,128)})) %all-reduce.4.cloned.1.call-update) | async-done | bytes 1048592 | tf_op jit(solution)/shard_map/psum | solution.py:202
  633.7 2.0 copy.63
  635.8 2.0 copy.64
  (79 shorter events, 7.6 us)
Async XLA Ops:
  7.2 12.5 %copy-start = (bf16[1,64,4096]{2,1,0:T(8,128)(2,1)S(1)}, bf16[1,64,4096]{2,1,0:T(8,128)(2,1)}, u32[]{:S(2)}) copy-start(bf16[1,64,4096]{2,1,0:T(8,128)(2,1)} %param.13) | copy-start | bytes 1572868
  7.2 308.5 %reduce-scatter.15.cloned.1.call-start = ((), (), s32[]{:S(2)}) async-start(), calls=%async_computation.7 | async-start | bytes 557056
  13.7 5.9 copy-start.9
  19.7 2.2 copy-start.3
  20.3 3.0 copy-start.4
  25.7 116.1 %copy-start.7 = (f32[512,4,128]{0,2,1:T(8,128)}, f32[512,4,128]{0,2,1:T(8,128)S(1)}, u32[]{:S(2)}) copy-start(f32[512,4,128]{0,2,1:T(8,128)S(1)} %get-tuple-element.260) | copy-start | bytes 3145732
  153.2 6.5 %slice-start = ((s8[6291456]{0:T(1024)(128)(4,1)}), s8[4194304]{0:T(1024)(128)(4,1)S(1)}, s32[]{:S(2)}) async-start(s8[6291456]{0:T(1024)(128)(4,1)} %bitcast.154), calls=%async_computation.9 | async-start | bytes 8388608 | tf_op jit(solution)/shard_map/while/body/eval_jaxpr/cond
  156.6 3.1 slice-start.1
  159.7 2.7 copy-start.10
  205.7 169.2 %reduce-scatter.13.cloned.1.call-start = ((), (), s32[]{:S(2)}) async-start(), calls=%async_computation.6 | async-start | bytes 557056
  207.9 275.1 %reduce-scatter.11.cloned.1.call-start = ((), (), s32[]{:S(2)}) async-start(), calls=%async_computation.5 | async-start | bytes 8912896 | tf_op jit(solution)/shard_map/reduce_scatter | solution.py:200
  316.5 1.4 copy-start.2
  316.5 2.7 copy-start.5
  324.8 1.4 copy-start.1
  324.8 1.7 copy-start.8
  324.8 266.7 %reduce-scatter.9.cloned.1.call-start = ((), (), s32[]{:S(2)}) async-start(), calls=%async_computation.4 | async-start | bytes 8912896 | tf_op jit(solution)/shard_map/reduce_scatter | solution.py:199
  376.3 2.2 copy-start.6
  384.1 249.7 %all-reduce.4.cloned.1.call-start = ((), (), s32[]{:S(2)}) async-start(), calls=%async_computation.8 | async-start | bytes 2097152 | tf_op jit(solution)/shard_map/psum | solution.py:202
Sparse Core Ops, SparseCore 0:
  205.9 109.7 reduce-scatter.14
  320.2 54.7 reduce-scatter.12
  379.1 103.8 reduce-scatter.10
  486.9 104.5 reduce-scatter.8
  593.7 39.9 all-reduce.3
where the time goes:
time: 646 us; the launch traced here: 644 us
  waiting for transfers between devices  405 us (63%)
  blocking collectives  98.5 us (15%)
  local copies, waits for them, and re-layouts  50.2 us (8%)
  matrix products  39.5 us (6%)
  other arithmetic  27.6 us (4%)
  between operations  17.4 us (3%)
    unnamed x7, waiting for transfers between devices  156 us
    reduce_scatter x1, waiting for transfers between devices, body(): lax.psum_scatter(grad_wk, ('prompt', 'resp'), scatter_dimension=0, tiled=...  109 us
    reduce_scatter x1, waiting for transfers between devices, body(): lax.psum_scatter(grad_wv, ('prompt', 'resp'), scatter_dimension=0, tiled=...  98.9 us
    psum x1, waiting for transfers between devices, body(): summed = lax.psum((shares[0], shares[1]), 'grp')  42.2 us
    all_gather x1, blocking collectives, body(): lax.all_gather(slice_values, ('prompt', 'resp'), axis=0, tiled=True)  36 us
    psum x1, blocking collectives, body(): sums = lax.psum((count, total, square), ('prompt', 'resp'))  31.7 us
    all_gather x1, blocking collectives, body(): lax.all_gather(slice_keys, ('prompt', 'resp'), axis=0, tiled=True)  30.8 us
    unnamed x31, local copies, waits for them, and re-layouts  22.1 us
  transfers between devices with their start and end apart: 5, of which 5 were waited for; matrix products, arithmetic and copies ran while one was open for 3% of the time, Pallas kernels for 0%

commit v1 on v0

v1 whole, which is shorter than its diff:
```python
import functools
import math

import jax
import jax.numpy as jnp
from jax import lax
from jax.experimental import pallas as pl
from jax.experimental.pallas import tpu as pltpu
from jax.sharding import PartitionSpec as P

HEAD_DIM = 128
NADV = 8
THETA = 1000000.0
EPS = 1e-06
STATE_BOUND = 6.0
QROWS = 128
CALLS = (2, 2)
VMEM = 58 * 1024 * 1024
MARK = 16
PROJECT_BLOCK = 1024

BF16 = jnp.bfloat16
FREE = pl.CostEstimate(flops=1, bytes_accessed=1, transcendentals=0)
F32 = jnp.float32
BY_ROWS = (((0,), (0,)), ((), ()))
BY_COLS = (((1,), (1,)), ((), ()))


def exchange(value, steps):
    names = tuple(name for name, step in steps if step)
    sizes = [lax.axis_size(name) for name in names]
    mask = 0
    for (name, step), size in zip([s for s in steps if s[1]], sizes):
        mask = mask * size + step
    total = math.prod(sizes)
    return lax.ppermute(value, names, [(j, j ^ mask) for j in range(total)])


def rotary_tables(positions):
    lane = jnp.arange(HEAD_DIM, dtype=jnp.int32)
    half = HEAD_DIM // 2
    steps = (lane % half).astype(F32)
    freq = THETA ** (-2.0 * steps / HEAD_DIM)
    angle = positions.astype(F32)[:, None] * freq[None, :]
    sign = jnp.where(lane < half, -1.0, 1.0).astype(F32)
    return jnp.cos(angle), jnp.sin(angle) * sign[None, :]


def project_kernel(groups, counts, place_ref, p_hbm, r_hbm, wk_hbm, wv_hbm, cos_ref, sin_ref, *refs):
    n_grp, n_chip, n_core, n_resp, block = counts
    p_raw, p_both, r_raw, r_both = refs[:4]
    selected = refs[4:-7]
    x_ref, wk_ref, wv_ref, acc_k, acc_v, sems, out_sems = refs[-7:]
    depth, width = wk_ref.shape
    shard = p_raw.shape[0]
    rows = r_raw.shape[0]
    steps = depth // PROJECT_BLOCK
    copies = []
    for k in range(steps):
        part = slice(k * PROJECT_BLOCK, (k + 1) * PROJECT_BLOCK)
        pairs = (
            (wk_hbm.at[part, :], wk_ref.at[part, :]),
            (p_hbm.at[:, part], x_ref.at[:shard, part]),
            (r_hbm.at[:, part], x_ref.at[shard:, part]),
            (wv_hbm.at[part, :], wv_ref.at[part, :]),
        )
        copies.append([pltpu.make_async_copy(src, dst, sems.at[k, i]) for i, (src, dst) in enumerate(pairs)])
        for copy in copies[-1]:
            copy.start()
    leaving = []
    for k in range(steps):
        part = slice(k * PROJECT_BLOCK, (k + 1) * PROJECT_BLOCK)
        for copy in copies[k]:
            copy.wait()
        if k == steps - 1:
            sub = shard // n_resp
            own = pl.ds(pl.multiple_of(place_ref[3] * sub, sub), sub)
            for i, (e, c) in enumerate(groups if selected else ()):
                for d in range(n_chip):
                    for r in range(n_resp):
                        chip = place_ref[1] ^ d
                        core = place_ref[2] ^ c
                        index = ((chip * n_core + core) * n_resp + r) * n_grp + (place_ref[0] ^ e)
                        source = pl.ds(pl.multiple_of(index * block, block), block)
                        j = d * n_resp + r
                        target = slice(j * block, (j + 1) * block)
                        pairs = (
                            (x_ref.at[shard:, source], selected[i].at[:rows, target]),
                            (x_ref.at[own, source], selected[i].at[rows:, target]),
                        )
                        for m, (src, dst) in enumerate(pairs):
                            leaving.append(pltpu.make_async_copy(src, dst, out_sems.at[i, j, m]))
                            leaving[-1].start()
        for acc, w_ref in ((acc_k, wk_ref), (acc_v, wv_ref)):
            share = jnp.dot(x_ref[:, part], w_ref[part, :], preferred_element_type=F32)
            if k:
                acc[...] += share
            else:
                acc[...] = share
    for place, raw_ref, both_ref in (
        (slice(0, shard), p_raw, p_both),
        (slice(shard, shard + rows), r_raw, r_both),
    ):
        both_ref[:, width:] = acc_v[place, :].astype(BF16)
        raw_ref[...] = acc_k[place, :]
        cosine = cos_ref[place, :]
        sine = sin_ref[place, :]
        for head in range(width // HEAD_DIM):
            cols = slice(head * HEAD_DIM, (head + 1) * HEAD_DIM)
            x = acc_k[place, cols]
            factor = lax.rsqrt(jnp.mean(x * x, axis=-1, keepdims=True) + EPS)
            normed = x * factor
            turned = normed * cosine + pltpu.roll(normed, HEAD_DIM // 2, 1) * sine
            both_ref[:, cols] = turned.astype(BF16)
    for copy in leaving:
        copy.wait()


def project(prompt, response, key_weight, value_weight, cosine, sine, place, groups, counts):
    depth, width = key_weight.shape
    shard, rows = prompt.shape[0], response.shape[0]
    n_grp, n_chip, n_core, n_resp, block = counts
    direct = block % HEAD_DIM == 0
    blocks = n_chip * n_resp
    part = jax.ShapeDtypeStruct((rows + shard // n_resp, blocks * block), BF16)
    any_spec = pl.BlockSpec(memory_space=pl.ANY)
    vmem = pl.BlockSpec(memory_space=pltpu.VMEM)
    out = pl.pallas_call(
        functools.partial(project_kernel, groups, counts),
        in_specs=[pl.BlockSpec(memory_space=pltpu.SMEM)] + [any_spec] * 4 + [vmem] * 2,
        out_specs=[vmem] * 4 + ([any_spec] * len(groups) if direct else []),
        out_shape=[
            jax.ShapeDtypeStruct((count, scale * width), kind)
            for count in (shard, rows)
            for scale, kind in ((1, F32), (2, BF16))
        ]
        + ([part] * len(groups) if direct else []),
        scratch_shapes=[pltpu.VMEM((shard + rows, depth), BF16)]
        + [pltpu.VMEM((depth, width), BF16)] * 2
        + [pltpu.VMEM((shard + rows, width), F32)] * 2
        + [
            pltpu.SemaphoreType.DMA((depth // PROJECT_BLOCK, 4)),
            pltpu.SemaphoreType.DMA((len(groups), blocks, 2)),
        ],
        compiler_params=pltpu.CompilerParams(vmem_limit_bytes=VMEM),
        cost_estimate=FREE,
        name="project",
    )(place, prompt, response, key_weight, value_weight, cosine, sine)
    if direct:
        return out[:4], out[4:]
    own = lax.dynamic_slice_in_dim(prompt, place[3] * (shard // n_resp), shard // n_resp, 0)
    split = jnp.concatenate([response, own]).reshape(-1, n_chip, n_core, n_resp, n_grp, block)
    parts = []
    for e, c in groups:
        piece = lax.dynamic_index_in_dim(split, place[0] ^ e, 4, keepdims=False)
        piece = lax.dynamic_index_in_dim(piece, place[2] ^ c, 2, keepdims=False)
        pieces = [lax.dynamic_index_in_dim(piece, place[1] ^ d, 1, keepdims=False) for d in range(n_chip)]
        parts.append(jnp.stack(pieces, axis=1).reshape(part.shape))
    return out, parts


def tied(value, *others):
    return pl.pallas_call(
        lambda *refs: None,
        in_specs=[pl.BlockSpec(memory_space=pl.ANY)] * (1 + len(others)),
        out_specs=pl.BlockSpec(memory_space=pl.ANY),
        out_shape=jax.ShapeDtypeStruct(value.shape, value.dtype),
        input_output_aliases={0: 0},
        cost_estimate=FREE,
        name="tied",
    )(value, *others)


def attend_kernel(parts, fold, coef_ref, ints_ref, q_ref, go_ref, *refs):
    prompt_k = refs[:parts]
    prompt_v = refs[parts : 2 * parts]
    own_k, own_v, raw_ref, cos_ref, sin_ref = refs[2 * parts : 2 * parts + 5]
    gq_ref, sum_ref, g_ref, k_all, v_all, k_turned, acc_k, acc_v = refs[-8:]
    rows = q_ref.shape[0]
    shard = prompt_k[0].shape[0]
    prompt_len = parts * shard
    scale = HEAD_DIM ** (-0.5)
    length = ints_ref[0]
    coef = coef_ref[0]
    prompt = ints_ref[1]
    for d in range(parts):
        place = pl.ds(pl.multiple_of((prompt ^ d) * shard, shard), shard)
        k_all[place, :] = prompt_k[d][...]
        v_all[place, :] = prompt_v[d][...]
    k_all[prompt_len:, :] = own_k[...]
    v_all[prompt_len:, :] = own_v[...]
    k_turned[...] = k_all[...].T
    acc_k[...] = jnp.zeros_like(acc_k)
    acc_v[...] = jnp.zeros_like(acc_v)
    def one_block(first):
        seen = prompt_len + first + QROWS
        width = fold * QROWS
        position = first + lax.broadcasted_iota(jnp.int32, (QROWS, HEAD_DIM), 0)
        factor = jnp.where(position < length, coef, 0.0)
        parts_q = []
        parts_d = []
        for f in range(fold):
            cols = slice(f * HEAD_DIM, (f + 1) * HEAD_DIM)
            parts_q.append(q_ref[first : first + QROWS, cols])
            parts_d.append((go_ref[first : first + QROWS, cols].astype(F32) * factor).astype(BF16))
        query = jnp.concatenate(parts_q, axis=0)
        dout = jnp.concatenate(parts_d, axis=0)
        scores = lax.dot_general(k_all[:seen, :], query, BY_COLS, preferred_element_type=F32)
        key = lax.broadcasted_iota(jnp.int32, (QROWS, width), 0)
        row = lax.broadcasted_iota(jnp.int32, (QROWS, width), 1) % QROWS
        tail = jnp.where(key <= row, scores[seen - QROWS :, :], -jnp.inf)
        scores = jnp.concatenate([scores[: seen - QROWS, :], tail], axis=0)
        peak = jnp.max(scores, axis=0, keepdims=True)
        expo = jnp.exp2((scores - peak) * (scale * math.log2(math.e)))
        probs = expo * (1.0 / jnp.sum(expo, axis=0, keepdims=True))
        probs_b = probs.astype(BF16)
        dprobs = lax.dot_general(v_all[:seen, :], dout, BY_COLS, preferred_element_type=F32)
        delta = jnp.sum(probs_b.astype(F32) * dprobs, axis=0, keepdims=True)
        dscores = (probs * (dprobs - delta)).astype(BF16)
        grad_q = jnp.dot(k_turned[:, :seen], dscores, preferred_element_type=F32) * scale
        for f in range(fold):
            gq_ref[first : first + QROWS, f * HEAD_DIM : (f + 1) * HEAD_DIM] = (
                grad_q[:, f * QROWS : (f + 1) * QROWS].T.astype(BF16)
            )
        acc_k[:seen, :] += jnp.dot(dscores, query, preferred_element_type=F32)
        acc_v[:seen, :] += jnp.dot(probs_b, dout, preferred_element_type=F32)

    for start in range(0, rows, 2 * QROWS):

        @pl.when(start < length)
        def _(start=start):
            one_block(start)
            one_block(start + QROWS)

        @pl.when(start >= length)
        def _(start=start):
            gq_ref[start : start + 2 * QROWS, :] = jnp.zeros((2 * QROWS, gq_ref.shape[1]), BF16)

    sum_ref[:, :HEAD_DIM] = acc_k[:prompt_len, :] * scale
    sum_ref[:, HEAD_DIM:] = acc_v[:prompt_len, :]
    x = raw_ref[...]
    factor = lax.rsqrt(jnp.mean(x * x, axis=-1, keepdims=True) + EPS)
    normed = x * factor
    grad = acc_k[prompt_len:, :] * scale
    unturned = grad * cos_ref[...] - pltpu.roll(grad, HEAD_DIM // 2, 1) * sin_ref[...]
    inner = jnp.mean(unturned * normed, axis=-1, keepdims=True)
    g_ref[0, 0] = (factor * (unturned - normed * inner)).T.astype(BF16)
    g_ref[0, 1] = acc_v[prompt_len:, :].T.astype(BF16)


def attend(first, per, offset, chunk_heads, coef, ints, query, grad_output, prompt_both, own_both, raw, cosine, sine, before, after):
    rows, query_width = query.shape
    width = raw.shape[1]
    heads = width // HEAD_DIM
    fold = query_width // width
    parts = len(prompt_both)
    shard = prompt_both[0].shape[0]
    prompt_len = parts * shard
    total = prompt_len + rows
    here = lambda h: (0, first + h)
    there = lambda h: (0, heads + first + h)
    scalar = pl.BlockSpec(memory_space=pltpu.SMEM)
    table = pl.BlockSpec((rows, HEAD_DIM), lambda h: (0, 0))
    wide = pl.BlockSpec((rows, fold * HEAD_DIM), here)
    in_specs = [scalar, scalar, wide, wide]
    in_specs += [pl.BlockSpec((shard, HEAD_DIM), here)] * parts + [pl.BlockSpec((shard, HEAD_DIM), there)] * parts
    in_specs += [pl.BlockSpec((rows, HEAD_DIM), here), pl.BlockSpec((rows, HEAD_DIM), there)]
    in_specs += [pl.BlockSpec((rows, HEAD_DIM), here), table, table]
    operands = [coef, ints, query, grad_output, *prompt_both, *prompt_both, own_both, own_both, raw, cosine, sine]
    aliases = {}
    for i, value in enumerate(before):
        if value is not None:
            aliases[len(operands)] = i
            in_specs.append(pl.BlockSpec(memory_space=pl.ANY))
            operands.append(value)
    in_specs += [pl.BlockSpec(memory_space=pl.ANY)] * len(after)
    operands += after
    return pl.pallas_call(
        functools.partial(attend_kernel, parts, fold),
        grid=(per,),
        in_specs=in_specs,
        out_specs=[
            wide,
            pl.BlockSpec((prompt_len, 2 * HEAD_DIM), lambda h: (0, offset + h)),
            pl.BlockSpec((1, 2, HEAD_DIM, rows), lambda h: (h, 0, 0, 0)),
        ],
        out_shape=[
            jax.ShapeDtypeStruct((rows, query_width), BF16),
            jax.ShapeDtypeStruct((prompt_len, 2 * chunk_heads * HEAD_DIM), F32),
            jax.ShapeDtypeStruct((per, 2, HEAD_DIM, rows), BF16),
        ],
        scratch_shapes=[
            pltpu.VMEM((total, HEAD_DIM), BF16),
            pltpu.VMEM((total, HEAD_DIM), BF16),
            pltpu.VMEM((HEAD_DIM, total), BF16),
            pltpu.VMEM((total, HEAD_DIM), F32),
            pltpu.VMEM((total, HEAD_DIM), F32),
        ],
        input_output_aliases=aliases,
        compiler_params=pltpu.CompilerParams(vmem_limit_bytes=VMEM),
        cost_estimate=FREE,
        name="attend",
    )(*operands)


def everyone(value, names):
    return lax.all_to_all(value, names, split_axis=0, concat_axis=0, tiled=True)


def weight_kernel(parts, count, *refs):
    states = refs[:parts]
    grads = refs[parts : parts + count]
    tokens_ref = refs[parts + count]
    out_ref, scale_ref = refs[-2:]
    rows = grads[0].shape[1]
    total_rows = parts * states[0].shape[0]

    @pl.when(pl.program_id(0) == 0)
    def _():
        peak = jnp.max(jnp.abs(tokens_ref[...].astype(F32)), axis=0, keepdims=True)
        peak = jnp.max(peak, axis=1, keepdims=True)
        highest = jnp.zeros((1, rows), F32)
        for grad in grads:
            highest = jnp.maximum(highest, jnp.max(jnp.abs(grad[...]), axis=0, keepdims=True).astype(F32))
        peak = jnp.maximum(peak, jnp.max(highest, axis=1, keepdims=True))
        reach = jnp.maximum(peak * (STATE_BOUND * total_rows), 1e-30)
        exponent = jnp.clip(jnp.ceil(jnp.log2(reach)), -90.0, 120.0)
        scale_ref[...] = jnp.broadcast_to(exponent, scale_ref.shape)

    exponent = scale_ref[:1, :1]
    scale = jnp.exp2(14.0 - exponent)
    prompt = jnp.concatenate([part[rows:, :] for part in states], axis=0)
    first = 0
    for call in range(count // parts):
        rest = first + grads[call * parts].shape[0]
        total = lax.dot_general(tokens_ref[:, first:rest], prompt, BY_ROWS, preferred_element_type=F32)
        for d in range(parts):
            total = total + jnp.dot(grads[call * parts + d][...], states[d][:rows, :], preferred_element_type=F32)
        out_ref[first:rest, :] = total * scale
        first = rest
    out_ref[first:, :] = jnp.broadcast_to(exponent, (MARK, out_ref.shape[1]))


def weight_shares(states, grads, tokens):
    parts = len(states)
    rows, depth = states[0].shape
    columns = tokens.shape[1]
    step = 2 * HEAD_DIM
    return pl.pallas_call(
        functools.partial(weight_kernel, parts, len(grads)),
        grid=(depth // step,),
        in_specs=[pl.BlockSpec((rows, step), lambda j: (0, j))] * parts
        + [pl.BlockSpec(x.shape, lambda j: (0, 0)) for x in (*grads, tokens)],
        out_specs=pl.BlockSpec((columns + MARK, step), lambda j: (0, j)),
        out_shape=jax.ShapeDtypeStruct((columns + MARK, depth), F32),
        scratch_shapes=[pltpu.VMEM((8, HEAD_DIM), F32)],
        compiler_params=pltpu.CompilerParams(vmem_limit_bytes=VMEM),
        cost_estimate=FREE,
        name="weight_shares",
    )(*states, *grads, tokens)


def rows_kernel(sums_ref, raw_ref, cos_ref, sin_ref, *refs):
    out_ref = refs[-1]
    cosine = cos_ref[...]
    sine = sin_ref[...]
    for head in range(raw_ref.shape[1] // HEAD_DIM):
        cols = slice(head * HEAD_DIM, (head + 1) * HEAD_DIM)
        both = jnp.sum(sums_ref[:, :, 2 * head * HEAD_DIM : 2 * (head + 1) * HEAD_DIM], axis=0)
        grad = both[:, :HEAD_DIM]
        raw = raw_ref[:, cols]
        factor = lax.rsqrt(jnp.mean(raw * raw, axis=-1, keepdims=True) + EPS)
        normed = raw * factor
        unturned = grad * cosine - pltpu.roll(grad, HEAD_DIM // 2, 1) * sine
        inner = jnp.mean(unturned * normed, axis=-1, keepdims=True)
        start = 2 * head * HEAD_DIM
        out_ref[:, start : start + HEAD_DIM] = (factor * (unturned - normed * inner)).astype(BF16)
        out_ref[:, start + HEAD_DIM : start + 2 * HEAD_DIM] = both[:, HEAD_DIM:].astype(BF16)


def row_grads(sums, raw, cosine, sine, after):
    return pl.pallas_call(
        rows_kernel,
        in_specs=[pl.BlockSpec(memory_space=pltpu.VMEM)] * 4 + [pl.BlockSpec(memory_space=pl.ANY)] * len(after),
        out_shape=jax.ShapeDtypeStruct((raw.shape[0], 2 * raw.shape[1]), BF16),
        compiler_params=pltpu.CompilerParams(vmem_limit_bytes=VMEM),
        cost_estimate=FREE,
        name="row_grads",
    )(sums, raw, cosine, sine, *after)


def advantage_of(rewards, group_ids):
    onehot = (group_ids[:, None] == jnp.arange(NADV, dtype=jnp.int32)[None, :]).astype(F32)
    sums = jnp.stack(
        [
            jnp.sum(onehot, axis=0),
            jnp.sum(onehot * rewards[:, None], axis=0),
            jnp.sum(onehot * (rewards * rewards)[:, None], axis=0),
        ]
    )
    names = ("chip", "core", "resp")
    peers = lax.axis_size(names)
    sums = jnp.sum(everyone(jnp.broadcast_to(sums[None], (peers,) + sums.shape), names), axis=0)
    members = jnp.maximum(sums[0], 1.0)
    mean = sums[1] / members
    spread = jnp.sqrt(jnp.maximum(sums[2] / members - mean * mean, 0.0))
    own_mean = jnp.sum(onehot * mean[None, :], axis=1)
    own_spread = jnp.sum(onehot * spread[None, :], axis=1)
    return (rewards - own_mean) / jnp.maximum(own_spread, 0.5)


def exponent_of(payload):
    return payload[-MARK : 1 - MARK, :1].astype(F32)


def values_of(payload, exponent):
    return payload[:-MARK].astype(F32) * jnp.exp2(exponent)


def body(prompt_states, response_states, queries, grad_output, key_weight, value_weight, rewards, lengths, group_ids):
    depth, width = key_weight.shape
    shard = prompt_states.shape[1]
    rows = response_states.shape[2]
    n_grp = lax.axis_size("grp")
    n_chip = lax.axis_size("chip")
    n_core = lax.axis_size("core")
    n_resp = lax.axis_size("resp")
    n_prompt = n_chip * n_core
    grp = lax.axis_index("grp")
    chip = lax.axis_index("chip")
    core = lax.axis_index("core")
    resp = lax.axis_index("resp")
    prompt = chip * n_core + core
    prompt_len = shard * n_prompt
    block = depth // (n_prompt * n_resp * n_grp)
    sub = shard // n_resp
    states = response_states[0, 0]
    own_prompt = prompt_states[0]

    advantage = advantage_of(rewards[0], group_ids[0])
    length = lengths[0]
    coef = advantage / length.astype(F32)
    ints = jnp.stack([length[0], prompt.astype(jnp.int32)])

    prompt_cos, prompt_sin = rotary_tables(prompt * shard + jnp.arange(shard, dtype=jnp.int32))
    own_cos, own_sin = rotary_tables(prompt_len + jnp.arange(rows, dtype=jnp.int32))
    groups = [(e, c) for e in range(n_grp) for c in range(n_core)]
    place = jnp.stack([grp, chip, core, resp]).astype(jnp.int32)
    (prompt_raw, mine, own_raw, own_both), parts = project(
        own_prompt,
        states,
        key_weight,
        value_weight,
        jnp.concatenate([prompt_cos, own_cos]),
        jnp.concatenate([prompt_sin, own_sin]),
        place,
        groups,
        (n_grp, n_chip, n_core, n_resp, block),
    )
    prompt_both = [mine]
    for d in range(1, n_prompt):
        prompt_both.append(exchange(mine, [("chip", d // n_core), ("core", d % n_core)]))
    parts = [exchange(x, [("grp", e), ("core", c)]) if e or c else x for x, (e, c) in zip(parts, groups)]

    sub_raw = lax.dynamic_slice_in_dim(prompt_raw, resp * sub, sub, 0)
    sub_cos = lax.dynamic_slice_in_dim(prompt_cos, resp * sub, sub, 0)
    sub_sin = lax.dynamic_slice_in_dim(prompt_sin, resp * sub, sub, 0)

    def gather_rows(row_g):
        held = jnp.concatenate([row_g] + [exchange(row_g, [("core", c)]) for c in range(1, n_core)])
        return jnp.concatenate([held] + [exchange(held, [("grp", e)]) for e in range(1, n_grp)])

    def run(first, per, chunk_first, chunk_heads, grads, sums, after):
        grads, sums, own_g = attend(
            first, per, first - chunk_first, chunk_heads, coef, ints, queries[0, 0], grad_output[0, 0],
            prompt_both, own_both, own_raw, own_cos, own_sin, [grads, sums], after,
        )
        return grads, sums, own_g.reshape(-1, rows)

    def across(own_g):
        return [exchange(own_g, [("grp", e)]) for e in range(1, n_grp)]

    def everywhere(own_g, hops):
        held = [own_g] + hops
        return [exchange(held[e], [("core", c)]) if c else held[e] for e, c in groups]

    def row_tokens(sums, chunk_first, after):
        sums = everyone(sums.reshape(n_prompt * n_resp, sub, -1), ("chip", "core", "resp"))
        raw = lax.slice_in_dim(sub_raw, chunk_first * HEAD_DIM, chunk_first * HEAD_DIM + sums.shape[2] // 2, axis=1)
        own = row_grads(sums, raw, sub_cos, sub_sin, after)
        held = jnp.concatenate([own] + [exchange(own, [("core", c)]) for c in range(1, n_core)])
        return jnp.concatenate([held] + [exchange(held, [("grp", e)]) for e in range(1, n_grp)])

    def summed(shares):
        wide = n_resp * block
        kept = shares[:, :wide]
        sent = [
            exchange(shares[:, d * wide : (d + 1) * wide].astype(jnp.float16), [("chip", d)]) for d in range(1, n_chip)
        ]
        exponents = [exponent_of(x) for x in [kept] + sent]
        top = functools.reduce(jnp.maximum, exponents) + math.ceil(math.log2(n_chip))
        total = values_of(kept, exponents[0] - top)
        for payload, exponent in zip(sent, exponents[1:]):
            total = total + values_of(payload, exponent - top)
        tail = jnp.broadcast_to(top, (MARK, wide))
        payload = jnp.concatenate([total, tail], axis=0).astype(jnp.float16)
        half = lax.dynamic_slice_in_dim(total, resp * block, block, 1) * jnp.exp2(top - 14.0)
        for d in range(1, n_resp):
            part = lax.dynamic_slice_in_dim(payload, (resp ^ d) * block, block, 1)
            part = exchange(part, [("resp", d)])
            half = half + values_of(part, exponent_of(part) - 14.0)
        return half, exchange(half, [("grp", 1)])

    early, late = CALLS
    grads, sums_early, g_early = run(0, early, 0, early, None, None, [])
    hops_early = across(g_early)
    grads, sums_late, g_late = run(early, late, early, late, grads, None, parts[1:])
    hops_early = [tied(x, g_late) for x in hops_early]
    hops_late = across(g_late)
    tokens = row_tokens(sums_early, 0, [g_late])
    shares_early = weight_shares(parts, everywhere(g_early, hops_early), tokens)
    tokens = row_tokens(sums_late, early, [])
    shares_late = weight_shares(parts, everywhere(g_late, hops_late), tokens)
    finished = [summed(shares_early), summed(shares_late)]

    mine = jnp.concatenate([pair[0] for pair in finished], axis=0)
    theirs = jnp.concatenate([pair[1] for pair in finished], axis=0)
    low = jnp.where(grp == 0, mine, theirs)
    high = jnp.where(grp == 0, theirs, mine)
    both = jnp.concatenate([low, high], axis=1).reshape(width // HEAD_DIM, 2, HEAD_DIM, n_grp * block)
    sides = [both[:, side].reshape(width, n_grp * block).T for side in range(2)]
    return (grads[None, None], sides[0], sides[1])


def solution(mesh):
    devices = mesh.devices
    n_grp, n_prompt, n_resp = devices.shape
    split = jax.sharding.Mesh(
        devices.reshape(n_grp, n_prompt // 2, 2, n_resp), ("grp", "chip", "core", "resp")
    )
    prompt = ("chip", "core")
    owner = ("chip", "core", "resp")
    placed = (
        P("grp", prompt, None),
        P("grp", owner, None, None),
        P("grp", owner, None, None),
        P("grp", owner, None, None),
        P(),
        P(),
        P("grp", owner),
        P("grp", owner),
        P("grp", owner),
    )
    return jax.shard_map(
        body,
        mesh=split,
        in_specs=placed,
        out_specs=(
            P("grp", owner, None, None),
            P(owner, None),
            P(owner, None),
        ),
        check_vma=False,
    )
```

time: 646 us -> 197 us (0.30)
  waiting for transfers between devices: 405 us -> 51.6 us
  blocking collectives: 98.5 us -> 0 us
  Pallas kernels: 0 us -> 59.6 us
  matrix products: 39.5 us -> 0 us
  starting transfers between devices: 0.43 us -> 39.7 us
  local copies, waits for them, and re-layouts: 50.2 us -> 17.6 us
  other arithmetic: 27.6 us -> 14.2 us
    reduce_scatter x2 -> x0, waiting for transfers between devices: 207 us -> none  [the longest x1 109 us: body(): lax.psum_scatter(grad_wk, ('prompt', 'resp'), scatter_dimension=0, tiled=...]
    unnamed x7 -> x0, waiting for transfers between devices: 156 us -> none
    all_gather x2 -> x0, blocking collectives: 66.8 us -> none  [the longest x1 36 us: body(): lax.all_gather(slice_values, ('prompt', 'resp'), axis=0, tiled=True)]
    pallas_call x0 -> x8, Pallas kernels: none -> 59.6 us  [the longest x2 28.3 us: attend(): pl.pallas_call(functools.partial(attend_kernel, parts, fold), grid=(per,)...]
    ppermute x0 -> x26, waiting for transfers between devices: none -> 48.3 us  [exchange(): return lax.ppermute(value, names, [(j, j ^ mask) for j in range(total)])]
    psum x1 -> x0, waiting for transfers between devices: 42.2 us -> none  [body(): summed = lax.psum((shares[0], shares[1]), 'grp')]
    dot_general x13 -> x0, matrix products: 33.5 us -> none  [the longest x1 5.92 us: body(): jnp.dot(states, value_weight, preferred_element_type=jnp.float32)]
    psum x1 -> x0, blocking collectives: 31.7 us -> none  [body(): sums = lax.psum((count, total, square), ('prompt', 'resp'))]
  transfers between devices with their start and end apart: 5 -> 29, of which waited for: 5 -> 10; matrix products, arithmetic and copies ran while one was open for 3% -> 10% of each run, Pallas kernels for 0% -> 24%
where the time goes in v1:
time: 197 us; the launch traced here: 195 us
  Pallas kernels  59.6 us (30%)
  waiting for transfers between devices  51.6 us (26%)
  starting transfers between devices  39.7 us (20%)
  local copies, waits for them, and re-layouts  17.6 us (9%)
  other arithmetic  14.2 us (7%)
  between operations  12.7 us (6%)
    ppermute x26, waiting for transfers between devices, exchange(): return lax.ppermute(value, names, [(j, j ^ mask) for j in range(total)])  48.3 us
    pallas_call x2, Pallas kernels, attend(): pl.pallas_call(functools.partial(attend_kernel, parts, fold), grid=(per,)...  28.3 us
    ppermute x26, starting transfers between devices, exchange(): return lax.ppermute(value, names, [(j, j ^ mask) for j in range(total)])  22.9 us
    all_to_all x3, starting transfers between devices, everyone(): return lax.all_to_all(value, names, split_axis=0, concat_axis=0, tiled=True)  16.8 us
    pallas_call x2, Pallas kernels, weight_shares(): pl.pallas_call(functools.partial(weight_kernel, parts, len(grads)), grid=...  14.6 us
    pallas_call x1, Pallas kernels, project(): pl.pallas_call(functools.partial(project_kernel, groups, counts), in_spec...  13 us
    slice x10, local copies, waits for them, and re-layouts, exponent_of(): return payload[-MARK:1 - MARK, :1].astype(F32)  7.33 us
    another operation x4, other arithmetic  5.7 us
  transfers between devices with their start and end apart: 29, of which 10 were waited for; matrix products, arithmetic and copies ran while one was open for 10% of the time, Pallas kernels for 24%

profile of v1, /device:TPU:0, one launch (start us, length us, event | category | flops | bytes accessed | tf_op | source)
XLA Modules:
  0.0 195.4 jit_solution(192048395029677286)
XLA Ops:
  0.9 1.0 fusion.5
  1.9 0.7 pad_add_fusion.1.place_ref
  2.6 0.8 pad_maximum_fusion.2
  3.5 13.0 %project.1 = (f32[64,512]{1,0:T(8,128)}, bf16[64,1024]{1,0:T(8,128)(2,1)}, f32[512,512]{1,0:T(8,128)}, bf16[512,1024]{1,0:T(8,128)(2,1)}, bf16[528,1024]{1,0:T(8...) custom-call(s32[4]{0:T(128)} %pad_add_fusion.1.place_ref, ...), custom_call_target="tpu_custom_call" | custom-call | flops 1 | bytes 1 | tf_op jit(solution)/shard_map/project/pallas_call | solution.py:128
  16.5 2.5 %collective-permute-start.2 = (bf16[64,1024]{1,0:T(8,128)(2,1)}, bf16[64,1024]{1,0:T(8,128)(2,1)S(1)}, u32[]{:S(2)}, u32[]{:S(2)}) collective-permute-start(bf16[64,1024]{1,0:T(8,128)(2,1)} %get-tuple-element.17.refs_0_.refs_4_), channel_id=1, source_target_pairs={{0,12},{4,8},{8,4},{12,0},{1,13},{5,9},{9,5},{13,1},{2,14},{6,10},... | collective-permute-start | bytes 393224 | tf_op jit(solution)/shard_map/ppermute | solution.py:36
  18.9 0.6 collective-permute-start.1
  21.0 0.6 broadcast_in_dim.20
  21.6 6.2 %all-to-all-start = ((f32[16,3,8]{2,1,0:T(4,128)}), f32[16,3,8]{2,1,0:T(4,128)S(1)}, u32[]{:S(2)}, u32[]{:S(2)}) async-start(f32[16,3,8]{2,1,0:T(4,128)} %broadcast_in_dim.20), calls=%async_computation | async-start | bytes 65536 | tf_op jit(solution)/shard_map/all_to_all | solution.py:307
  28.1 1.5 collective-permute-start.4
  30.3 0.6 pad_add_fusion.ints_ref
  30.9 3.3 %all-to-all-done = f32[16,3,8]{2,1,0:T(4,128)S(1)} async-done(((f32[16,3,8]{2,1,0:T(4,128)}), f32[16,3,8]{2,1,0:T(4,128)S(1)}, u32[]{:S(2)}, u32[]{:S(2)}) %all-to-all-start) | async-done | bytes 1568 | tf_op jit(solution)/shard_map/all_to_all | solution.py:307
  34.3 1.3 collective-permute-start.5
  35.6 0.7 select_reduce_fusion
  37.7 0.6 copy-done.7
  38.3 14.1 %attend.2 = (bf16[512,2048]{1,0:T(8,128)(2,1)}, f32[256,512]{1,0:T(8,128)}, bf16[2,2,128,512]{3,2,1,0:T(8,128)(2,1)}) custom-call(f32[1]{0:T(128)S(6)} %div.33.coef_ref, s32[2]{0:T(128)} %pad_add_fusion.ints_ref, bf16[512,2048]{1,0:T(8,128)(2,1)} %bitcast.50, bf16[512,2048]{1,0:T(8,128)(2,1)} %bitcast.52, ...), custom_call_target="tpu_custom_call" | custom-call | flops 1 | bytes 1 | tf_op jit(solution)/shard_map/attend/pallas_call | solution.py:278
  52.5 4.4 %all-to-all-start.1 = ((f32[16,16,512]{2,1,0:T(8,128)}), f32[16,16,512]{2,1,0:T(8,128)}, u32[]{:S(2)}, u32[]{:S(2)}) async-start(f32[16,16,512]{2,1,0:T(8,128)} %bitcast.69), calls=%async_computation.1 | async-start | bytes 1048576 | tf_op jit(solution)/shard_map/all_to_all | solution.py:307
  57.0 20.3 %collective-permute-done.5.refs_16_.refs_3_ = bf16[528,1024]{1,0:T(8,128)(2,1)S(1)} collective-permute-done((bf16[528,1024]{1,0:T(8,128)(2,1)}, bf16[528,1024]{1,0:T(8,128)(2,1)S(1)}, u32[]{:S(2)}, u32[]{:S(2)}) %collective-permute-start.5) | collective-permute-done | bytes 1081376 | tf_op jit(solution)/shard_map/ppermute | solution.py:36
  77.4 1.0 copy-done.2
  78.3 14.2 %attend.3 = (bf16[512,2048]{1,0:T(8,128)(2,1)}, f32[256,512]{1,0:T(8,128)}, bf16[2,2,128,512]{3,2,1,0:T(8,128)(2,1)}) custom-call(f32[1]{0:T(128)S(6)} %div.33.coef_ref, s32[2]{0:T(128)} %pad_add_fusion.ints_ref, bf16[512,2048]{1,0:T(8,128)(2,1)} %bitcast.51, bf16[512,2048]{1,0:T(8,128)(2,1)} %bitcast.53, ...), custom_call_target="tpu_custom_call", output_to_operand_aliasing={{0}: (17, {})} | custom-call | flops 1 | bytes 1 | tf_op jit(solution)/shard_map/attend/pallas_call | solution.py:278
  92.5 6.2 %all-to-all-start.2 = ((f32[16,16,512]{2,1,0:T(8,128)}), f32[16,16,512]{2,1,0:T(8,128)S(1)}, u32[]{:S(2)}, u32[]{:S(2)}) async-start(f32[16,16,512]{2,1,0:T(8,128)} %bitcast.68), calls=%async_computation.2 | async-start | bytes 1048576 | tf_op jit(solution)/shard_map/all_to_all | solution.py:307
  99.1 0.6 collective-permute-start.16
  99.8 1.3 constant_dynamic-slice_fusion.1
  101.1 1.3 fusion.17
  102.4 1.8 row_grads.2
  104.8 1.0 collective-permute-done.9
  105.8 0.7 pad_maximum_fusion.6
  106.5 1.4 collective-permute-start.10
  108.0 6.0 %collective-permute-done.10 = bf16[32,512]{1,0:T(8,128)(2,1)S(1)} collective-permute-done((bf16[32,512]{1,0:T(8,128)(2,1)S(1)}, bf16[32,512]{1,0:T(8,128)(2,1)S(1)}, u32[]{:S(2)}, u32[]{:S(2)}) %collective-permute-start.10) | collective-permute-done | bytes 32800 | tf_op jit(solution)/shard_map/ppermute | solution.py:36
  114.0 1.3 pad_maximum_fusion.4.refs_8_
  115.4 0.8 copy-done.12
  116.2 7.3 %weight_shares.2 = f32[528,1024]{1,0:T(8,128)} custom-call(bf16[528,1024]{1,0:T(8,128)(2,1)} %get-tuple-element.25.refs_0_, bf16[528,1024]{1,0:T(8,128)(2,1)} %copy-done, bf16[528,1024]{1,0:T(8,128)(2,1)} %copy-done.1, bf16[528,1024]{1,0:T(8,128)(2,1)} %copy-done.2, bf16[512,512]{1,0:T(8,128)(2,1)} %bitcast.67, bf16[512,512]{1,0:T(8,128)(2,1)} %copy-done.12, ...), custom_call_target="tpu_custom_call" | custom-call | flops 1 | bytes 1 | tf_op jit(solution)/shard_map/weight_shares/pallas_call | solution.py:349
  123.5 0.8 copy-done.8
  124.3 1.8 row_grads.3
  126.6 1.3 slice_convert_fusion.1
  128.0 1.9 collective-permute-start.11
  129.9 0.7 pad_maximum_fusion.7
  130.6 0.6 collective-permute-start.19
  131.2 1.2 slice.125
  132.5 2.1 %collective-permute-done.19 = bf16[32,512]{1,0:T(8,128)(2,1)S(1)} collective-permute-done((bf16[32,512]{1,0:T(8,128)(2,1)S(1)}, bf16[32,512]{1,0:T(8,128)(2,1)S(1)}, u32[]{:S(2)}, u32[]{:S(2)}) %collective-permute-start.19) | collective-permute-done | bytes 32800 | tf_op jit(solution)/shard_map/ppermute | solution.py:36
  134.5 1.3 pad_maximum_fusion.5.refs_8_
  135.9 0.8 copy-done.10
  136.7 0.8 copy-done.11
  137.5 7.3 %weight_shares.3 = f32[528,1024]{1,0:T(8,128)} custom-call(bf16[528,1024]{1,0:T(8,128)(2,1)} %get-tuple-element.25.refs_0_, bf16[528,1024]{1,0:T(8,128)(2,1)} %copy-done, bf16[528,1024]{1,0:T(8,128)(2,1)} %copy-done.1, bf16[528,1024]{1,0:T(8,128)(2,1)} %copy-done.2, bf16[512,512]{1,0:T(8,128)(2,1)} %bitcast.57, bf16[512,512]{1,0:T(8,128)(2,1)} %copy-done.10, ...), custom_call_target="tpu_custom_call" | custom-call | flops 1 | bytes 1 | tf_op jit(solution)/shard_map/weight_shares/pallas_call | solution.py:349
  144.8 1.3 slice_convert_fusion
  146.3 1.2 slice.127
  149.5 1.6 fusion.15
  151.2 1.9 collective-permute-start.12
  153.1 2.4 %collective-permute-start.13 = (f16[528,128]{1,0:T(8,128)(2,1)S(1)}, f16[528,128]{1,0:T(8,128)(2,1)S(1)}, u32[]{:S(2)}, u32[]{:S(2)}) collective-permute-start(f16[528,128]{1,0:T(8,128)(2,1)S(1)} %get-tuple-element.45), channel_id=1, source_target_pairs={{0,2},{1,3},{2,0},{3,1},{4,6},{5,7},{6,4},{7,5},{8,10},{9,11},{10,... | collective-permute-start | bytes 405512 | tf_op jit(solution)/shard_map/ppermute | solution.py:36
  155.7 1.2 slice.136
  157.0 0.8 collective-permute-done.12
  158.9 6.3 %collective-permute-done.13 = f16[528,128]{1,0:T(8,128)(2,1)S(1)} collective-permute-done((f16[528,128]{1,0:T(8,128)(2,1)S(1)}, f16[528,128]{1,0:T(8,128)(2,1)S(1)}, u32[]{:S(2)}, u32[]{:S(2)}) %collective-permute-start.13) | collective-permute-done | bytes 135200 | tf_op jit(solution)/shard_map/ppermute | solution.py:36
  166.5 0.5 slice.134
  167.7 0.6 slice.138
  170.3 1.4 fusion.13
  171.8 0.9 collective-permute-start.21
  172.7 2.1 %collective-permute-start.22 = (f16[528,128]{1,0:T(8,128)(2,1)S(1)}, f16[528,128]{1,0:T(8,128)(2,1)S(1)}, u32[]{:S(2)}, u32[]{:S(2)}) collective-permute-start(f16[528,128]{1,0:T(8,128)(2,1)S(1)} %get-tuple-element.42), channel_id=1, source_target_pairs={{0,2},{1,3},{2,0},{3,1},{4,6},{5,7},{6,4},{7,5},{8,10},{9,11},{10,... | collective-permute-start | bytes 405512 | tf_op jit(solution)/shard_map/ppermute | solution.py:36
  174.8 1.5 collective-permute-start.23
  176.4 0.7 collective-permute-start.24
  177.1 2.6 %collective-permute-done.21 = f16[528,128]{1,0:T(8,128)(2,1)S(1)} collective-permute-done((f16[528,128]{1,0:T(8,128)(2,1)S(1)}, f16[528,128]{1,0:T(8,128)(2,1)S(1)}, u32[]{:S(2)}, u32[]{:S(2)}) %collective-permute-start.21) | collective-permute-done | bytes 135200 | tf_op jit(solution)/shard_map/ppermute | solution.py:36
  180.9 3.4 %collective-permute-done.22 = f16[528,128]{1,0:T(8,128)(2,1)S(1)} collective-permute-done((f16[528,128]{1,0:T(8,128)(2,1)S(1)}, f16[528,128]{1,0:T(8,128)(2,1)S(1)}, u32[]{:S(2)}, u32[]{:S(2)}) %collective-permute-start.22) | collective-permute-done | bytes 135200 | tf_op jit(solution)/shard_map/ppermute | solution.py:36
  186.8 0.7 collective-permute-start.25
  187.5 5.7 %collective-permute-done.25 = f32[512,128]{1,0:T(8,128)S(1)} collective-permute-done((f32[512,128]{1,0:T(8,128)S(1)}, f32[512,128]{1,0:T(8,128)S(1)}, u32[]{:S(2)}, u32[]{:S(2)}) %collective-permute-start.25) | collective-permute-done | bytes 262176 | tf_op jit(solution)/shard_map/ppermute | solution.py:36
  193.4 1.0 copy.22
  194.4 1.0 copy.21
  (75 shorter events, 5.9 us)
Async XLA Ops:
  0.9 15.5 %copy-start.13 = (f32[64,128]{1,0:T(8,128)}, f32[64,128]{1,0:T(8,128)S(1)}, u32[]{:S(2)}) copy-start(f32[64,128]{1,0:T(8,128)S(1)} %get-tuple-element.52) | copy-start | bytes 98308
  1.9 0.7 copy-start.5
  1.9 14.5 %copy-start.4 = (f32[512,128]{1,0:T(8,128)}, f32[512,128]{1,0:T(8,128)S(1)}, u32[]{:S(2)}) copy-start(f32[512,128]{1,0:T(8,128)S(1)} %get-tuple-element.49.refs_12_) | copy-start | bytes 786436
  16.5 17.8 %collective-permute-start.2 = (bf16[64,1024]{1,0:T(8,128)(2,1)}, bf16[64,1024]{1,0:T(8,128)(2,1)S(1)}, u32[]{:S(2)}, u32[]{:S(2)}) collective-permute-start(bf16[64,1024]{1,0:T(8,128)(2,1)} %get-tuple-element.17.refs_0_.refs_4_), channel_id=1, source_target_pairs={{0,12},{4,8},{8,4},{12,0},{1,13},{5,9},{9,5},{13,1},{2,14},{6,10},... | collective-permute-start | bytes 393224 | tf_op jit(solution)/shard_map/ppermute | solution.py:36
  18.9 18.7 %collective-permute-start.1 = (bf16[64,1024]{1,0:T(8,128)(2,1)}, bf16[64,1024]{1,0:T(8,128)(2,1)S(1)}, u32[]{:S(2)}, u32[]{:S(2)}) collective-permute-start(bf16[64,1024]{1,0:T(8,128)(2,1)} %get-tuple-element.17.refs_0_.refs_4_), channel_id=1, source_target_pairs={{0,8},{8,0},{1,9},{9,1},{2,10},{10,2},{3,11},{11,3},{4,12},{12,4},... | collective-permute-start | bytes 393224 | tf_op jit(solution)/shard_map/ppermute | solution.py:36
  19.6 18.1 %collective-permute-start = (bf16[64,1024]{1,0:T(8,128)(2,1)}, bf16[64,1024]{1,0:T(8,128)(2,1)}, u32[]{:S(2)}, u32[]{:S(2)}) collective-permute-start(bf16[64,1024]{1,0:T(8,128)(2,1)} %get-tuple-element.17.refs_0_.refs_4_), channel_id=1, source_target_pairs={{0,4},{4,0},{1,5},{5,1},{2,6},{6,2},{3,7},{7,3},{8,12},{12,8},{9,1... | collective-permute-start | bytes 393224 | tf_op jit(solution)/shard_map/ppermute | solution.py:36
  21.6 12.7 %all-to-all-start = ((f32[16,3,8]{2,1,0:T(4,128)}), f32[16,3,8]{2,1,0:T(4,128)S(1)}, u32[]{:S(2)}, u32[]{:S(2)}) async-start(f32[16,3,8]{2,1,0:T(4,128)} %broadcast_in_dim.20), calls=%async_computation | async-start | bytes 65536 | tf_op jit(solution)/shard_map/all_to_all | solution.py:307
  27.7 29.3 %collective-permute-start.3 = (bf16[528,1024]{1,0:T(8,128)(2,1)}, bf16[528,1024]{1,0:T(8,128)(2,1)S(1)}, u32[]{:S(2)}, u32[]{:S(2)}) collective-permute-start(bf16[528,1024]{1,0:T(8,128)(2,1)} %get-tuple-element.21), channel_id=1, source_target_pairs={{0,4},{4,0},{1,5},{5,1},{2,6},{6,2},{3,7},{7,3},{8,12},{12,8},{9,1... | collective-permute-start | bytes 3244040 | tf_op jit(solution)/shard_map/ppermute | solution.py:36
  28.1 28.9 %collective-permute-start.4 = (bf16[528,1024]{1,0:T(8,128)(2,1)}, bf16[528,1024]{1,0:T(8,128)(2,1)S(1)}, u32[]{:S(2)}, u32[]{:S(2)}) collective-permute-start(bf16[528,1024]{1,0:T(8,128)(2,1)} %get-tuple-element.22), channel_id=1, source_target_pairs={{0,16},{16,0},{1,17},{17,1},{2,18},{18,2},{3,19},{19,3},{4,20},{20... | collective-permute-start | bytes 3244040 | tf_op jit(solution)/shard_map/ppermute | solution.py:36
  34.3 3.4 %copy-start.6 = (bf16[64,1024]{1,0:T(8,128)(2,1)}, bf16[64,1024]{1,0:T(8,128)(2,1)S(1)}, u32[]{:S(2)}) copy-start(bf16[64,1024]{1,0:T(8,128)(2,1)S(1)} %collective-permute-done.2.refs_3_.refs_7_) | copy-start | bytes 393220
  34.3 43.1 %collective-permute-start.5 = (bf16[528,1024]{1,0:T(8,128)(2,1)}, bf16[528,1024]{1,0:T(8,128)(2,1)S(1)}, u32[]{:S(2)}, u32[]{:S(2)}) collective-permute-start(bf16[528,1024]{1,0:T(8,128)(2,1)} %get-tuple-element.23), channel_id=1, source_target_pairs={{0,20},{4,16},{16,4},{20,0},{1,21},{5,17},{17,5},{21,1},{2,22},{6,... | collective-permute-start | bytes 3244040 | tf_op jit(solution)/shard_map/ppermute | solution.py:36
  37.7 0.7 copy-start.7
  52.5 40.1 %all-to-all-start.1 = ((f32[16,16,512]{2,1,0:T(8,128)}), f32[16,16,512]{2,1,0:T(8,128)}, u32[]{:S(2)}, u32[]{:S(2)}) async-start(f32[16,16,512]{2,1,0:T(8,128)} %bitcast.69), calls=%async_computation.1 | async-start | bytes 1048576 | tf_op jit(solution)/shard_map/all_to_all | solution.py:307
  56.9 42.8 %collective-permute-start.7 = (bf16[512,512]{1,0:T(8,128)(2,1)}, bf16[512,512]{1,0:T(8,128)(2,1)}, u32[]{:S(2)}, u32[]{:S(2)}) collective-permute-start(bf16[512,512]{1,0:T(8,128)(2,1)} %bitcast.65), channel_id=1, source_target_pairs={{0,16},{16,0},{1,17},{17,1},{2,18},{18,2},{3,19},{19,3},{4,20},{20... | collective-permute-start | bytes 1572872 | tf_op jit(solution)/shard_map/ppermute | solution.py:36
  57.0 20.4 %copy-start = (bf16[528,1024]{1,0:T(8,128)(2,1)}, bf16[528,1024]{1,0:T(8,128)(2,1)S(1)}, u32[]{:S(2)}) copy-start(bf16[528,1024]{1,0:T(8,128)(2,1)S(1)} %collective-permute-done.3.refs_14_.refs_1_) | copy-start | bytes 3244036
  57.0 20.3 %copy-start.1 = (bf16[528,1024]{1,0:T(8,128)(2,1)}, bf16[528,1024]{1,0:T(8,128)(2,1)S(1)}, u32[]{:S(2)}) copy-start(bf16[528,1024]{1,0:T(8,128)(2,1)S(1)} %collective-permute-done.4.refs_15_.refs_2_) | copy-start | bytes 3244036
  77.4 1.0 copy-start.2
  92.5 15.4 %copy-start.3 = (bf16[2,2,128,512]{3,2,1,0:T(8,128)(2,1)S(1)}, bf16[2,2,128,512]{3,2,1,0:T(8,128)(2,1)}, u32[]{:S(2)}) copy-start(bf16[2,2,128,512]{3,2,1,0:T(8,128)(2,1)} %get-tuple-element.27) | copy-start | bytes 1572868
  92.5 31.0 %all-to-all-start.2 = ((f32[16,16,512]{2,1,0:T(8,128)}), f32[16,16,512]{2,1,0:T(8,128)S(1)}, u32[]{:S(2)}, u32[]{:S(2)}) async-start(f32[16,16,512]{2,1,0:T(8,128)} %bitcast.68), calls=%async_computation.2 | async-start | bytes 1048576 | tf_op jit(solution)/shard_map/all_to_all | solution.py:307
  98.7 16.7 %collective-permute-start.6 = (bf16[512,512]{1,0:T(8,128)(2,1)}, bf16[512,512]{1,0:T(8,128)(2,1)S(1)}, u32[]{:S(2)}, u32[]{:S(2)}) collective-permute-start(bf16[512,512]{1,0:T(8,128)(2,1)} %bitcast.66), channel_id=1, source_target_pairs={{0,4},{4,0},{1,5},{5,1},{2,6},{6,2},{3,7},{7,3},{8,12},{12,8},{9,1... | collective-permute-start | bytes 1572872 | tf_op jit(solution)/shard_map/ppermute | solution.py:36
  99.1 16.2 %collective-permute-start.16 = (bf16[512,512]{1,0:T(8,128)(2,1)}, bf16[512,512]{1,0:T(8,128)(2,1)S(1)}, u32[]{:S(2)}, u32[]{:S(2)}) collective-permute-start(bf16[512,512]{1,0:T(8,128)(2,1)} %bitcast.54), channel_id=1, source_target_pairs={{0,16},{16,0},{1,17},{17,1},{2,18},{18,2},{3,19},{19,3},{4,20},{20... | collective-permute-start | bytes 1572872 | tf_op jit(solution)/shard_map/ppermute | solution.py:36
  99.8 15.7 %collective-permute-start.8 = (bf16[512,512]{1,0:T(8,128)(2,1)}, bf16[512,512]{1,0:T(8,128)(2,1)}, u32[]{:S(2)}, u32[]{:S(2)}) collective-permute-start(bf16[512,512]{1,0:T(8,128)(2,1)} %tied.1.refs_6_), channel_id=1, source_target_pairs={{0,4},{4,0},{1,5},{5,1},{2,6},{6,2},{3,7},{7,3},{8,12},{12,8},{9,1... | collective-permute-start | bytes 1572872 | tf_op jit(solution)/shard_map/ppermute | solution.py:36
  104.2 1.6 collective-permute-start.9
  106.5 7.5 %collective-permute-start.10 = (bf16[32,512]{1,0:T(8,128)(2,1)S(1)}, bf16[32,512]{1,0:T(8,128)(2,1)S(1)}, u32[]{:S(2)}, u32[]{:S(2)}) collective-permute-start(bf16[32,512]{1,0:T(8,128)(2,1)S(1)} %pad_maximum_fusion.6), channel_id=1, source_target_pairs={{0,16},{16,0},{1,17},{17,1},{2,18},{18,2},{3,19},{19,3},{4,20},{20... | collective-permute-start | bytes 98312 | tf_op jit(solution)/shard_map/ppermute | solution.py:36
  107.9 27.9 %collective-permute-start.15 = (bf16[512,512]{1,0:T(8,128)(2,1)S(1)}, bf16[512,512]{1,0:T(8,128)(2,1)S(1)}, u32[]{:S(2)}, u32[]{:S(2)}) collective-permute-start(bf16[512,512]{1,0:T(8,128)(2,1)S(1)} %bitcast.58), channel_id=1, source_target_pairs={{0,4},{4,0},{1,5},{5,1},{2,6},{6,2},{3,7},{7,3},{8,12},{12,8},{9,1... | collective-permute-start | bytes 1572872 | tf_op jit(solution)/shard_map/ppermute | solution.py:36
  115.4 8.1 %copy-start.9 = (bf16[512,512]{1,0:T(8,128)(2,1)}, bf16[512,512]{1,0:T(8,128)(2,1)S(1)}, u32[]{:S(2)}) copy-start(bf16[512,512]{1,0:T(8,128)(2,1)S(1)} %collective-permute-done.16.refs_6_) | copy-start | bytes 1572868
  115.4 20.5 %collective-permute-start.17 = (bf16[512,512]{1,0:T(8,128)(2,1)S(1)}, bf16[512,512]{1,0:T(8,128)(2,1)S(1)}, u32[]{:S(2)}, u32[]{:S(2)}) collective-permute-start(bf16[512,512]{1,0:T(8,128)(2,1)S(1)} %collective-permute-done.16.refs_6_), channel_id=1, source_target_pairs={{0,4},{4,0},{1,5},{5,1},{2,6},{6,2},{3,7},{7,3},{8,12},{12,8},{9,1... | collective-permute-start | bytes 1572872 | tf_op jit(solution)/shard_map/ppermute | solution.py:36
  115.4 0.8 copy-start.12
  123.5 0.8 copy-start.8
  126.2 3.7 %collective-permute-start.18 = (bf16[16,512]{1,0:T(8,128)(2,1)}, bf16[16,512]{1,0:T(8,128)(2,1)S(1)}, u32[]{:S(2)}, u32[]{:S(2)}) collective-permute-start(bf16[16,512]{1,0:T(8,128)(2,1)} %row_grads.3), channel_id=1, source_target_pairs={{0,4},{4,0},{1,5},{5,1},{2,6},{6,2},{3,7},{7,3},{8,12},{12,8},{9,1... | collective-permute-start | bytes 49160 | tf_op jit(solution)/shard_map/ppermute | solution.py:36
  128.0 18.4 %collective-permute-start.11 = (f16[528,512]{1,0:T(8,128)(2,1)S(1)}, f16[528,512]{1,0:T(8,128)(2,1)}, u32[]{:S(2)}, u32[]{:S(2)}) collective-permute-start(f16[528,512]{1,0:T(8,128)(2,1)S(1)} %slice_convert_fusion.1), channel_id=1, source_target_pairs={{0,8},{8,0},{1,9},{9,1},{2,10},{10,2},{3,11},{11,3},{4,12},{12,4},... | collective-permute-start | bytes 1622024 | tf_op jit(solution)/shard_map/ppermute | solution.py:36
  130.6 3.9 %collective-permute-start.19 = (bf16[32,512]{1,0:T(8,128)(2,1)S(1)}, bf16[32,512]{1,0:T(8,128)(2,1)S(1)}, u32[]{:S(2)}, u32[]{:S(2)}) collective-permute-start(bf16[32,512]{1,0:T(8,128)(2,1)S(1)} %pad_maximum_fusion.7), channel_id=1, source_target_pairs={{0,16},{16,0},{1,17},{17,1},{2,18},{18,2},{3,19},{19,3},{4,20},{20... | collective-permute-start | bytes 98312 | tf_op jit(solution)/shard_map/ppermute | solution.py:36
  135.9 0.8 copy-start.10
  136.7 0.8 copy-start.11
  146.1 21.6 %collective-permute-start.20 = (f16[528,512]{1,0:T(8,128)(2,1)S(1)}, f16[528,512]{1,0:T(8,128)(2,1)S(1)}, u32[]{:S(2)}, u32[]{:S(2)}) collective-permute-start(f16[528,512]{1,0:T(8,128)(2,1)S(1)} %slice_convert_fusion), channel_id=1, source_target_pairs={{0,8},{8,0},{1,9},{9,1},{2,10},{10,2},{3,11},{11,3},{4,12},{12,4},... | collective-permute-start | bytes 1622024 | tf_op jit(solution)/shard_map/ppermute | solution.py:36
  151.2 6.5 %collective-permute-start.12 = (f16[528,128]{1,0:T(8,128)(2,1)S(1)}, f16[528,128]{1,0:T(8,128)(2,1)S(1)}, u32[]{:S(2)}, u32[]{:S(2)}) collective-permute-start(f16[528,128]{1,0:T(8,128)(2,1)S(1)} %get-tuple-element.44), channel_id=1, source_target_pairs={{0,1},{1,0},{2,3},{3,2},{4,5},{5,4},{6,7},{7,6},{8,9},{9,8},{10,11... | collective-permute-start | bytes 405512 | tf_op jit(solution)/shard_map/ppermute | solution.py:36
  153.1 12.1 %collective-permute-start.13 = (f16[528,128]{1,0:T(8,128)(2,1)S(1)}, f16[528,128]{1,0:T(8,128)(2,1)S(1)}, u32[]{:S(2)}, u32[]{:S(2)}) collective-permute-start(f16[528,128]{1,0:T(8,128)(2,1)S(1)} %get-tuple-element.45), channel_id=1, source_target_pairs={{0,2},{1,3},{2,0},{3,1},{4,6},{5,7},{6,4},{7,5},{8,10},{9,11},{10,... | collective-permute-start | bytes 405512 | tf_op jit(solution)/shard_map/ppermute | solution.py:36
  155.5 11.0 %collective-permute-start.14 = (f16[528,128]{1,0:T(8,128)(2,1)S(1)}, f16[528,128]{1,0:T(8,128)(2,1)S(1)}, u32[]{:S(2)}, u32[]{:S(2)}) collective-permute-start(f16[528,128]{1,0:T(8,128)(2,1)S(1)} %get-tuple-element.46), channel_id=1, source_target_pairs={{0,3},{1,2},{2,1},{3,0},{4,7},{5,6},{6,5},{7,4},{8,11},{9,10},{10,... | collective-permute-start | bytes 405512 | tf_op jit(solution)/shard_map/ppermute | solution.py:36
  171.8 7.8 %collective-permute-start.21 = (f16[528,128]{1,0:T(8,128)(2,1)S(1)}, f16[528,128]{1,0:T(8,128)(2,1)S(1)}, u32[]{:S(2)}, u32[]{:S(2)}) collective-permute-start(f16[528,128]{1,0:T(8,128)(2,1)S(1)} %get-tuple-element.41), channel_id=1, source_target_pairs={{0,1},{1,0},{2,3},{3,2},{4,5},{5,4},{6,7},{7,6},{8,9},{9,8},{10,11... | collective-permute-start | bytes 405512 | tf_op jit(solution)/shard_map/ppermute | solution.py:36
  172.7 11.6 %collective-permute-start.22 = (f16[528,128]{1,0:T(8,128)(2,1)S(1)}, f16[528,128]{1,0:T(8,128)(2,1)S(1)}, u32[]{:S(2)}, u32[]{:S(2)}) collective-permute-start(f16[528,128]{1,0:T(8,128)(2,1)S(1)} %get-tuple-element.42), channel_id=1, source_target_pairs={{0,2},{1,3},{2,0},{3,1},{4,6},{5,7},{6,4},{7,5},{8,10},{9,11},{10,... | collective-permute-start | bytes 405512 | tf_op jit(solution)/shard_map/ppermute | solution.py:36
  174.8 10.7 %collective-permute-start.23 = (f16[528,128]{1,0:T(8,128)(2,1)S(1)}, f16[528,128]{1,0:T(8,128)(2,1)S(1)}, u32[]{:S(2)}, u32[]{:S(2)}) collective-permute-start(f16[528,128]{1,0:T(8,128)(2,1)S(1)} %get-tuple-element.43), channel_id=1, source_target_pairs={{0,3},{1,2},{2,1},{3,0},{4,7},{5,6},{6,5},{7,4},{8,11},{9,10},{10,... | collective-permute-start | bytes 405512 | tf_op jit(solution)/shard_map/ppermute | solution.py:36
  176.4 11.1 %collective-permute-start.24 = (f32[512,128]{1,0:T(8,128)S(1)}, f32[512,128]{1,0:T(8,128)S(1)}, u32[]{:S(2)}, u32[]{:S(2)}) collective-permute-start(f32[512,128]{1,0:T(8,128)S(1)} %multiply_add_fusion.1), channel_id=1, source_target_pairs={{0,16},{16,0},{1,17},{17,1},{2,18},{18,2},{3,19},{19,3},{4,20},{20... | collective-permute-start | bytes 786440 | tf_op jit(solution)/shard_map/ppermute | solution.py:36
  186.8 6.4 %collective-permute-start.25 = (f32[512,128]{1,0:T(8,128)S(1)}, f32[512,128]{1,0:T(8,128)S(1)}, u32[]{:S(2)}, u32[]{:S(2)}) collective-permute-start(f32[512,128]{1,0:T(8,128)S(1)} %multiply_add_fusion), channel_id=1, source_target_pairs={{0,16},{16,0},{1,17},{17,1},{2,18},{18,2},{3,19},{19,3},{4,20},{20... | collective-permute-start | bytes 786440 | tf_op jit(solution)/shard_map/ppermute | solution.py:36

commit v2 on v1

--- a/solution.py
+++ b/solution.py
@@ -46,8 +46,82 @@
     return jnp.cos(angle), jnp.sin(angle) * sign[None, :]
 
 
-def project_kernel(groups, counts, place_ref, p_hbm, r_hbm, wk_hbm, wv_hbm, cos_ref, sin_ref, *refs):
+def column_copies(groups, counts, place_ref, source_ref, first, sub_ref, targets, sems):
     n_grp, n_chip, n_core, n_resp, block = counts
+    rows = source_ref.shape[0] - first
+    sub = targets[0].shape[0] - rows
+    own = pl.ds(pl.multiple_of(place_ref[3] * sub, sub), sub)
+    copies = []
+    for i, (e, c) in enumerate(groups):
+        copies.append([])
+        for d in range(n_chip):
+            for r in range(n_resp):
+                chip = place_ref[1] ^ d
+                core = place_ref[2] ^ c
+                index = ((chip * n_core + core) * n_resp + r) * n_grp + (place_ref[0] ^ e)
+                source = pl.ds(pl.multiple_of(index * block, block), block)
+                j = d * n_resp + r
+                target = slice(j * block, (j + 1) * block)
+                pairs = (
+                    (source_ref.at[first:, source], targets[i].at[:rows, target]),
+                    (sub_ref.at[own, source], targets[i].at[rows:, target]),
+                )
+                for m, (src, dst) in enumerate(pairs):
+                    copies[-1].append(pltpu.make_async_copy(src, dst, sems.at[i, j, m]))
+                    copies[-1][-1].start()
+    return copies
+
+
+def select_kernel(groups, counts, place_ref, states_ref, prompt_ref, *refs):
+    beside, across, held, sems, out_sems = refs
+    outs = [beside, across.at[0], across.at[1]]
+    targets = [held.at[i] for i in range(len(groups))]
+    copies = column_copies(groups, counts, place_ref, states_ref, 0, prompt_ref, targets, sems)
+    leaving = []
+    for i, arriving in enumerate(copies):
+        for copy in arriving:
+            copy.wait()
+        leaving.append(pltpu.make_async_copy(held.at[i], outs[i], out_sems.at[i]))
+        leaving[-1].start()
+    for copy in leaving:
+        copy.wait()
+
+
+def select_columns(states, prompt, place, groups, counts):
+    n_grp, n_chip, n_core, n_resp, block = counts
+    sub = prompt.shape[0] // n_resp
+    rows = states.shape[0] + sub
+    width = n_chip * n_resp * block
+    if block % HEAD_DIM:
+        own = lax.dynamic_slice_in_dim(prompt, place[3] * sub, sub, 0)
+        split = jnp.concatenate([states, own]).reshape(rows, n_chip, n_core, n_resp, n_grp, block)
+        out = []
+        for e, c in groups:
+            part = lax.dynamic_index_in_dim(split, place[0] ^ e, 4, keepdims=False)
+            part = lax.dynamic_index_in_dim(part, place[2] ^ c, 2, keepdims=False)
+            parts = [lax.dynamic_index_in_dim(part, place[1] ^ d, 1, keepdims=False) for d in range(n_chip)]
+            out.append(jnp.stack(parts, axis=1).reshape(rows, width))
+        return out if len(out) == 1 else (out[0], jnp.stack(out[1:]))
+    return pl.pallas_call(
+        functools.partial(select_kernel, groups, counts),
+        in_specs=[pl.BlockSpec(memory_space=pltpu.SMEM)] + [pl.BlockSpec(memory_space=pl.ANY)] * 2,
+        out_specs=[pl.BlockSpec(memory_space=pl.ANY)] * 2,
+        out_shape=[
+            jax.ShapeDtypeStruct((rows, width), states.dtype),
+            jax.ShapeDtypeStruct((2, rows, width), states.dtype),
+        ],
+        scratch_shapes=[
+            pltpu.VMEM((len(groups), rows, width), states.dtype),
+            pltpu.SemaphoreType.DMA((len(groups), n_chip * n_resp, 2)),
+            pltpu.SemaphoreType.DMA((len(groups),)),
+        ],
+        compiler_params=pltpu.CompilerParams(vmem_limit_bytes=VMEM),
+        cost_estimate=FREE,
+        name="select_columns",
+    )(place, states, prompt)
+
+
+def project_kernel(groups, counts, place_ref, p_hbm, r_hbm, wk_hbm, wv_hbm, cos_ref, sin_ref, after_ref, *refs):
     p_raw, p_both, r_raw, r_both = refs[:4]
     selected = refs[4:-7]
     x_ref, wk_ref, wv_ref, acc_k, acc_v, sems, out_sems = refs[-7:]
@@ -72,25 +146,8 @@
         part = slice(k * PROJECT_BLOCK, (k + 1) * PROJECT_BLOCK)
         for copy in copies[k]:
             copy.wait()
-        if k == steps - 1:
-            sub = shard // n_resp
-            own = pl.ds(pl.multiple_of(place_ref[3] * sub, sub), sub)
-            for i, (e, c) in enumerate(groups if selected else ()):
-                for d in range(n_chip):
-                    for r in range(n_resp):
-                        chip = place_ref[1] ^ d
-                        core = place_ref[2] ^ c
-                        index = ((chip * n_core + core) * n_resp + r) * n_grp + (place_ref[0] ^ e)
-                        source = pl.ds(pl.multiple_of(index * block, block), block)
-                        j = d * n_resp + r
-                        target = slice(j * block, (j + 1) * block)
-                        pairs = (
-                            (x_ref.at[shard:, source], selected[i].at[:rows, target]),
-                            (x_ref.at[own, source], selected[i].at[rows:, target]),
-                        )
-                        for m, (src, dst) in enumerate(pairs):
-                            leaving.append(pltpu.make_async_copy(src, dst, out_sems.at[i, j, m]))
-                            leaving[-1].start()
+        if k == steps - 1 and selected:
+            leaving = column_copies(groups, counts, place_ref, x_ref, shard, x_ref, selected, out_sems)
         for acc, w_ref in ((acc_k, wk_ref), (acc_v, wv_ref)):
             share = jnp.dot(x_ref[:, part], w_ref[part, :], preferred_element_type=F32)
             if k:
@@ -112,11 +169,11 @@
             normed = x * factor
             turned = normed * cosine + pltpu.roll(normed, HEAD_DIM // 2, 1) * sine
             both_ref[:, cols] = turned.astype(BF16)
-    for copy in leaving:
+    for copy in sum(leaving, []):
         copy.wait()
 
 
-def project(prompt, response, key_weight, value_weight, cosine, sine, place, groups, counts):
+def project(prompt, response, key_weight, value_weight, cosine, sine, place, groups, counts, after):
     depth, width = key_weight.shape
     shard, rows = prompt.shape[0], response.shape[0]
     n_grp, n_chip, n_core, n_resp, block = counts
@@ -127,7 +184,7 @@
     vmem = pl.BlockSpec(memory_space=pltpu.VMEM)
     out = pl.pallas_call(
         functools.partial(project_kernel, groups, counts),
-        in_specs=[pl.BlockSpec(memory_space=pltpu.SMEM)] + [any_spec] * 4 + [vmem] * 2,
+        in_specs=[pl.BlockSpec(memory_space=pltpu.SMEM)] + [any_spec] * 4 + [vmem] * 2 + [any_spec],
         out_specs=[vmem] * 4 + ([any_spec] * len(groups) if direct else []),
         out_shape=[
             jax.ShapeDtypeStruct((count, scale * width), kind)
@@ -145,18 +202,10 @@
         compiler_params=pltpu.CompilerParams(vmem_limit_bytes=VMEM),
         cost_estimate=FREE,
         name="project",
-    )(place, prompt, response, key_weight, value_weight, cosine, sine)
+    )(place, prompt, response, key_weight, value_weight, cosine, sine, after)
     if direct:
         return out[:4], out[4:]
-    own = lax.dynamic_slice_in_dim(prompt, place[3] * (shard // n_resp), shard // n_resp, 0)
-    split = jnp.concatenate([response, own]).reshape(-1, n_chip, n_core, n_resp, n_grp, block)
-    parts = []
-    for e, c in groups:
-        piece = lax.dynamic_index_in_dim(split, place[0] ^ e, 4, keepdims=False)
-        piece = lax.dynamic_index_in_dim(piece, place[2] ^ c, 2, keepdims=False)
-        pieces = [lax.dynamic_index_in_dim(piece, place[1] ^ d, 1, keepdims=False) for d in range(n_chip)]
-        parts.append(jnp.stack(pieces, axis=1).reshape(part.shape))
-    return out, parts
+    return out, select_columns(response, prompt, place, groups, counts)
 
 
 def tied(value, *others):
@@ -307,86 +356,93 @@
     return lax.all_to_all(value, names, split_axis=0, concat_axis=0, tiled=True)
 
 
-def weight_kernel(parts, count, *refs):
+def weight_kernel(parts, tokens_count, *refs):
     states = refs[:parts]
-    grads = refs[parts : parts + count]
-    tokens_ref = refs[parts + count]
-    out_ref, scale_ref = refs[-2:]
-    rows = grads[0].shape[1]
-    total_rows = parts * states[0].shape[0]
+    grads = refs[parts : 2 * parts]
+    tokens = refs[2 * parts : 2 * parts + tokens_count]
+    out_ref, scale_ref, side_ref = refs[-3:]
+    columns, rows = grads[0].shape
+    total_rows = parts * states[0].shape[-2]
 
     @pl.when(pl.program_id(0) == 0)
     def _():
-        peak = jnp.max(jnp.abs(tokens_ref[...].astype(F32)), axis=0, keepdims=True)
-        peak = jnp.max(peak, axis=1, keepdims=True)
         highest = jnp.zeros((1, rows), F32)
-        for grad in grads:
-            highest = jnp.maximum(highest, jnp.max(jnp.abs(grad[...]), axis=0, keepdims=True).astype(F32))
-        peak = jnp.maximum(peak, jnp.max(highest, axis=1, keepdims=True))
+        for d, grad in enumerate(grads):
+            value = grad[...]
+            side_ref[:, d * rows : (d + 1) * rows] = value
+            highest = jnp.maximum(highest, jnp.max(jnp.abs(value), axis=0, keepdims=True).astype(F32))
+        peak = jnp.max(highest, axis=1, keepdims=True)
+        for token in tokens:
+            highest = jnp.max(jnp.abs(token[...].astype(F32)), axis=0, keepdims=True)
+            peak = jnp.maximum(peak, jnp.max(highest, axis=1, keepdims=True))
         reach = jnp.maximum(peak * (STATE_BOUND * total_rows), 1e-30)
         exponent = jnp.clip(jnp.ceil(jnp.log2(reach)), -90.0, 120.0)
         scale_ref[...] = jnp.broadcast_to(exponent, scale_ref.shape)
 
     exponent = scale_ref[:1, :1]
-    scale = jnp.exp2(14.0 - exponent)
+    response = jnp.concatenate([part[:rows, :] for part in states], axis=0)
     prompt = jnp.concatenate([part[rows:, :] for part in states], axis=0)
-    first = 0
-    for call in range(count // parts):
-        rest = first + grads[call * parts].shape[0]
-        total = lax.dot_general(tokens_ref[:, first:rest], prompt, BY_ROWS, preferred_element_type=F32)
-        for d in range(parts):
-            total = total + jnp.dot(grads[call * parts + d][...], states[d][:rows, :], preferred_element_type=F32)
-        out_ref[first:rest, :] = total * scale
-        first = rest
-    out_ref[first:, :] = jnp.broadcast_to(exponent, (MARK, out_ref.shape[1]))
+    token = jnp.concatenate([token[...] for token in tokens], axis=0)
+    total = jnp.dot(side_ref[...], response, preferred_element_type=F32)
+    total = total + lax.dot_general(token, prompt, BY_ROWS, preferred_element_type=F32)
+    out_ref[:columns, :] = total * jnp.exp2(14.0 - exponent)
+    out_ref[columns:, :] = jnp.broadcast_to(exponent, (MARK, out_ref.shape[1]))
 
 
 def weight_shares(states, grads, tokens):
     parts = len(states)
-    rows, depth = states[0].shape
-    columns = tokens.shape[1]
+    rows, depth = states[0][0].shape
+    columns = grads[0].shape[0]
     step = 2 * HEAD_DIM
     return pl.pallas_call(
-        functools.partial(weight_kernel, parts, len(grads)),
+        functools.partial(weight_kernel, parts, len(tokens)),
         grid=(depth // step,),
-        in_specs=[pl.BlockSpec((rows, step), lambda j: (0, j))] * parts
-        + [pl.BlockSpec(x.shape, lambda j: (0, 0)) for x in (*grads, tokens)],
+        in_specs=[
+            pl.BlockSpec((rows, step), lambda j: (0, j))
+            if index is None
+            else pl.BlockSpec((None, rows, step), lambda j, index=index: (index, 0, j))
+            for _, index in states
+        ]
+        + [pl.BlockSpec(x.shape, lambda j: (0, 0)) for x in (*grads, *tokens)],
         out_specs=pl.BlockSpec((columns + MARK, step), lambda j: (0, j)),
         out_shape=jax.ShapeDtypeStruct((columns + MARK, depth), F32),
-        scratch_shapes=[pltpu.VMEM((8, HEAD_DIM), F32)],
+        scratch_shapes=[pltpu.VMEM((8, HEAD_DIM), F32), pltpu.VMEM((columns, parts * grads[0].shape[1]), BF16)],
         compiler_params=pltpu.CompilerParams(vmem_limit_bytes=VMEM),
         cost_estimate=FREE,
         name="weight_shares",
-    )(*states, *grads, tokens)
-
-
-def rows_kernel(sums_ref, raw_ref, cos_ref, sin_ref, *refs):
+    )(*[array for array, _ in states], *grads, *tokens)
+
+
+def rows_kernel(first, place_ref, sums_ref, raw_ref, cos_ref, sin_ref, *refs):
     out_ref = refs[-1]
-    cosine = cos_ref[...]
-    sine = sin_ref[...]
-    for head in range(raw_ref.shape[1] // HEAD_DIM):
-        cols = slice(head * HEAD_DIM, (head + 1) * HEAD_DIM)
-        both = jnp.sum(sums_ref[:, :, 2 * head * HEAD_DIM : 2 * (head + 1) * HEAD_DIM], axis=0)
+    sub = sums_ref.shape[1]
+    own = pl.ds(pl.multiple_of(place_ref[3] * sub, sub), sub)
+    cosine = cos_ref[own, :]
+    sine = sin_ref[own, :]
+    for head in range(out_ref.shape[1] // (2 * HEAD_DIM)):
+        start = 2 * head * HEAD_DIM
+        both = jnp.sum(sums_ref[:, :, start : start + 2 * HEAD_DIM], axis=0)
         grad = both[:, :HEAD_DIM]
-        raw = raw_ref[:, cols]
+        raw = raw_ref[own, (first + head) * HEAD_DIM : (first + head + 1) * HEAD_DIM]
         factor = lax.rsqrt(jnp.mean(raw * raw, axis=-1, keepdims=True) + EPS)
         normed = raw * factor
         unturned = grad * cosine - pltpu.roll(grad, HEAD_DIM // 2, 1) * sine
         inner = jnp.mean(unturned * normed, axis=-1, keepdims=True)
-        start = 2 * head * HEAD_DIM
         out_ref[:, start : start + HEAD_DIM] = (factor * (unturned - normed * inner)).astype(BF16)
         out_ref[:, start + HEAD_DIM : start + 2 * HEAD_DIM] = both[:, HEAD_DIM:].astype(BF16)
 
 
-def row_grads(sums, raw, cosine, sine, after):
+def row_grads(first, place, sums, raw, cosine, sine, after):
     return pl.pallas_call(
-        rows_kernel,
-        in_specs=[pl.BlockSpec(memory_space=pltpu.VMEM)] * 4 + [pl.BlockSpec(memory_space=pl.ANY)] * len(after),
-        out_shape=jax.ShapeDtypeStruct((raw.shape[0], 2 * raw.shape[1]), BF16),
+        functools.partial(rows_kernel, first),
+        in_specs=[pl.BlockSpec(memory_space=pltpu.SMEM)]
+        + [pl.BlockSpec(memory_space=pltpu.VMEM)] * 4
+        + [pl.BlockSpec(memory_space=pl.ANY)] * len(after),
+        out_shape=jax.ShapeDtypeStruct(sums.shape[1:], BF16),
         compiler_params=pltpu.CompilerParams(vmem_limit_bytes=VMEM),
         cost_estimate=FREE,
         name="row_grads",
-    )(sums, raw, cosine, sine, *after)
+    )(place, sums, raw, cosine, sine, *after)
 
 
 def advantage_of(rewards, group_ids):
@@ -410,7 +466,7 @@
 
 
 def exponent_of(payload):
-    return payload[-MARK : 1 - MARK, :1].astype(F32)
+    return payload[-MARK : 1 - MARK].astype(F32)
 
 
 def values_of(payload, exponent):
@@ -437,6 +493,14 @@
     states = response_states[0, 0]
     own_prompt = prompt_states[0]
 
+    groups = [(e, c) for e in range(n_grp) for c in range(n_core)]
+    counts = (n_grp, n_chip, n_core, n_resp, block)
+    place = jnp.stack([grp, chip, core, resp]).astype(jnp.int32)
+    beside, across_grp = select_columns(states, own_prompt, place, groups[1:], counts)
+    chosen = across_grp
+    beside = exchange(beside, [("core", 1)])
+    across_grp = exchange(across_grp, [("grp", 1)])
+
     advantage = advantage_of(rewards[0], group_ids[0])
     length = lengths[0]
     coef = advantage / length.astype(F32)
@@ -444,8 +508,6 @@
 
     prompt_cos, prompt_sin = rotary_tables(prompt * shard + jnp.arange(shard, dtype=jnp.int32))
     own_cos, own_sin = rotary_tables(prompt_len + jnp.arange(rows, dtype=jnp.int32))
-    groups = [(e, c) for e in range(n_grp) for c in range(n_core)]
-    place = jnp.stack([grp, chip, core, resp]).astype(jnp.int32)
     (prompt_raw, mine, own_raw, own_both), parts = project(
         own_prompt,
         states,
@@ -454,21 +516,13 @@
         jnp.concatenate([prompt_cos, own_cos]),
         jnp.concatenate([prompt_sin, own_sin]),
         place,
-        groups,
-        (n_grp, n_chip, n_core, n_resp, block),
+        groups[:1],
+        counts,
+        chosen,
     )
     prompt_both = [mine]
     for d in range(1, n_prompt):
         prompt_both.append(exchange(mine, [("chip", d // n_core), ("core", d % n_core)]))
-    parts = [exchange(x, [("grp", e), ("core", c)]) if e or c else x for x, (e, c) in zip(parts, groups)]
-
-    sub_raw = lax.dynamic_slice_in_dim(prompt_raw, resp * sub, sub, 0)
-    sub_cos = lax.dynamic_slice_in_dim(prompt_cos, resp * sub, sub, 0)
-    sub_sin = lax.dynamic_slice_in_dim(prompt_sin, resp * sub, sub, 0)
-
-    def gather_rows(row_g):
-        held = jnp.concatenate([row_g] + [exchange(row_g, [("core", c)]) for c in range(1, n_core)])
-        return jnp.concatenate([held] + [exchange(held, [("grp", e)]) for e in range(1, n_grp)])
 
     def run(first, per, chunk_first, chunk_heads, grads, sums, after):
         grads, sums, own_g = attend(
@@ -486,42 +540,55 @@
 
     def row_tokens(sums, chunk_first, after):
         sums = everyone(sums.reshape(n_prompt * n_resp, sub, -1), ("chip", "core", "resp"))
-        raw = lax.slice_in_dim(sub_raw, chunk_first * HEAD_DIM, chunk_first * HEAD_DIM + sums.shape[2] // 2, axis=1)
-        own = row_grads(sums, raw, sub_cos, sub_sin, after)
+        own = row_grads(chunk_first, place, sums, prompt_raw, prompt_cos, prompt_sin, after)
         held = jnp.concatenate([own] + [exchange(own, [("core", c)]) for c in range(1, n_core)])
-        return jnp.concatenate([held] + [exchange(held, [("grp", e)]) for e in range(1, n_grp)])
-
-    def summed(shares):
-        wide = n_resp * block
-        kept = shares[:, :wide]
-        sent = [
-            exchange(shares[:, d * wide : (d + 1) * wide].astype(jnp.float16), [("chip", d)]) for d in range(1, n_chip)
-        ]
+        return [held] + [exchange(held, [("grp", e)]) for e in range(1, n_grp)]
+
+    wide = n_resp * block
+
+    def chip_terms(shares):
+        return [exchange(shares[:, d * wide : (d + 1) * wide].astype(jnp.float16), [("chip", d)]) for d in range(1, n_chip)]
+
+    def resp_terms(kept, sent):
         exponents = [exponent_of(x) for x in [kept] + sent]
         top = functools.reduce(jnp.maximum, exponents) + math.ceil(math.log2(n_chip))
         total = values_of(kept, exponents[0] - top)
         for payload, exponent in zip(sent, exponents[1:]):
             total = total + values_of(payload, exponent - top)
-        tail = jnp.broadcast_to(top, (MARK, wide))
-        payload = jnp.concatenate([total, tail], axis=0).astype(jnp.float16)
-        half = lax.dynamic_slice_in_dim(total, resp * block, block, 1) * jnp.exp2(top - 14.0)
+        payload = jnp.concatenate([total, jnp.broadcast_to(top, (MARK, wide))], axis=0).astype(jnp.float16)
+        half = lax.dynamic_slice_in_dim(total * jnp.exp2(top - 14.0), resp * block, block, 1)
+        pieces = []
         for d in range(1, n_resp):
             part = lax.dynamic_slice_in_dim(payload, (resp ^ d) * block, block, 1)
-            part = exchange(part, [("resp", d)])
+            pieces.append(exchange(part, [("resp", d)]))
+        return half, pieces
+
+    def finish(half, pieces):
+        for part in pieces:
             half = half + values_of(part, exponent_of(part) - 14.0)
         return half, exchange(half, [("grp", 1)])
 
     early, late = CALLS
     grads, sums_early, g_early = run(0, early, 0, early, None, None, [])
     hops_early = across(g_early)
-    grads, sums_late, g_late = run(early, late, early, late, grads, None, parts[1:])
+    across_grp = tied(across_grp, g_early)
+    grads, sums_late, g_late = run(early, late, early, late, grads, None, [beside, across_grp])
+    parts = [(parts[0], None), (beside, None), (across_grp, 0), (exchange(across_grp, [("core", 1)]), 1)]
     hops_early = [tied(x, g_late) for x in hops_early]
+    g_late = tied(g_late, *hops_early)
+    sums_late = tied(sums_late, *hops_early)
     hops_late = across(g_late)
     tokens = row_tokens(sums_early, 0, [g_late])
     shares_early = weight_shares(parts, everywhere(g_early, hops_early), tokens)
     tokens = row_tokens(sums_late, early, [])
     shares_late = weight_shares(parts, everywhere(g_late, hops_late), tokens)
-    finished = [summed(shares_early), summed(shares_late)]
+    sent_early = chip_terms(shares_early)
+    sent_late = chip_terms(shares_late)
+    half_early, pieces_early = resp_terms(shares_early[:, :wide], sent_early)
+    done_early = finish(half_early, pieces_early)
+    sent_late = [lax.optimization_barrier((x, done_early[0]))[0] for x in sent_late]
+    half_late, pieces_late = resp_terms(shares_late[:, :wide], sent_late)
+    finished = [done_early, finish(half_late, pieces_late)]
 
     mine = jnp.concatenate([pair[0] for pair in finished], axis=0)
     theirs = jnp.concatenate([pair[1] for pair in finished], axis=0)

time: 197 us -> 175 us (0.89)
  between operations: 12.7 us -> 4.36 us
  local copies, waits for them, and re-layouts: 17.6 us -> 10.3 us
  waiting for transfers between devices: 51.6 us -> 44.7 us
  other arithmetic: 14.2 us -> 11 us
  Pallas kernels: 59.6 us -> 62.7 us
    ppermute x26, waiting for transfers between devices: 48.3 us -> 39.5 us  [exchange(): return lax.ppermute(value, names, [(j, j ^ mask) for j in range(total)])]
    slice x11 -> x0, local copies, waits for them, and re-layouts: 8.68 us -> none  [the longest x10 7.33 us: exponent_of(): return payload[-MARK:1 - MARK, :1].astype(F32)]
    pallas_call x4 -> x5, Pallas kernels: 18.3 us -> 22.8 us  [the longest x2 14.7 us: weight_shares(): pl.pallas_call(functools.partial(weight_kernel, parts, len(tokens)), grid...]
    unnamed x29 -> x41, local copies, waits for them, and re-layouts: 4.85 us -> 7.53 us
    another operation x4 -> x6, other arithmetic: 5.7 us -> 3.14 us
    concatenate x2, other arithmetic: 2.68 us -> 0.24 us  [resp_terms(): jnp.concatenate([total, jnp.broadcast_to(top, (MARK, wide))], axis=0)]
  transfers between devices with their start and end apart: 29 -> 29, of which waited for: 10 -> 12; matrix products, arithmetic and copies ran while one was open for 10% -> 4% of each run, Pallas kernels for 24% -> 33%
where the time goes in v2:
time: 175 us; the launch traced here: 174 us
  Pallas kernels  62.7 us (36%)
  waiting for transfers between devices  44.7 us (26%)
  starting transfers between devices  41.2 us (24%)
  other arithmetic  11 us (6%)
  local copies, waits for them, and re-layouts  10.3 us (6%)
  between operations  4.36 us (2%)
    ppermute x26, waiting for transfers between devices, exchange(): return lax.ppermute(value, names, [(j, j ^ mask) for j in range(total)])  39.5 us
    pallas_call x2, Pallas kernels, attend(): pl.pallas_call(functools.partial(attend_kernel, parts, fold), grid=(per,)...  28.3 us
    ppermute x26, starting transfers between devices, exchange(): return lax.ppermute(value, names, [(j, j ^ mask) for j in range(total)])  22.7 us
    all_to_all x3, starting transfers between devices, everyone(): return lax.all_to_all(value, names, split_axis=0, concat_axis=0, tiled=True)  18.6 us
    pallas_call x2, Pallas kernels, weight_shares(): pl.pallas_call(functools.partial(weight_kernel, parts, len(tokens)), grid...  14.7 us
    pallas_call x1, Pallas kernels, project(): pl.pallas_call(functools.partial(project_kernel, groups, counts), in_spec...  11.6 us
    unnamed x41, local copies, waits for them, and re-layouts  7.53 us
    all_to_all x3, waiting for transfers between devices, everyone(): return lax.all_to_all(value, names, split_axis=0, concat_axis=0, tiled=True)  5.21 us
  transfers between devices with their start and end apart: 29, of which 12 were waited for; matrix products, arithmetic and copies ran while one was open for 4% of the time, Pallas kernels for 33%

profile of v2, /device:TPU:0, one launch (start us, length us, event | category | flops | bytes accessed | tf_op | source)
XLA Modules:
  0.0 174.4 jit_solution(16531830006472156963)
XLA Ops:
  0.6 0.7 pad_add_fusion.1.place_ref
  1.3 4.3 %select_columns.1 = (bf16[528,1024]{1,0:T(8,128)(2,1)}, bf16[2,528,1024]{2,1,0:T(8,128)(2,1)}) custom-call(s32[4]{0:T(128)} %pad_add_fusion.1.place_ref, bf16[512,4096]{1,0:T(8,128)(2,1)} %bitcast.54, bf16[64,4096]{1,0:T(8,128)(2,1)} %bitcast.63), custom_call_target="tpu_custom_call" | custom-call | flops 1 | bytes 1 | tf_op jit(solution)/shard_map/select_columns/pallas_call | solution.py:105
  5.6 3.0 %collective-permute-start.4 = (bf16[2,528,1024]{2,1,0:T(8,128)(2,1)}, bf16[2,528,1024]{2,1,0:T(8,128)(2,1)S(1)}, u32[]{:S(2)}, u32[]{:S(2)}) collective-permute-start(bf16[2,528,1024]{2,1,0:T(8,128)(2,1)} %get-tuple-element.17.after_ref), channel_id=1, source_target_pairs={{0,16},{16,0},{1,17},{17,1},{2,18},{18,2},{3,19},{19,3},{4,20},{20... | collective-permute-start | bytes 6488072 | tf_op jit(solution)/shard_map/ppermute | solution.py:36
  8.8 1.0 fusion.5
  9.9 0.9 pad_maximum_fusion.2
  10.8 11.6 %project.1 = (f32[64,512]{1,0:T(8,128)}, bf16[64,1024]{1,0:T(8,128)(2,1)}, f32[512,512]{1,0:T(8,128)}, bf16[512,1024]{1,0:T(8,128)(2,1)}, bf16[528,1024]{1,0:T(8,128)(2,1)}) custom-call(s32[4]{0:T(128)} %pad_add_fusion.1.place_ref, bf16[64,4096]{1,0:T(8,128)(2,1)} %bitcast.64, bf16[512,4096]{1,0:T(8,128)(2,1)} %bitcast.55, bf16[4096,512]{1,0:T(8,128)(2,1)} %wk_hbm.1, ...), custom_call_target="tpu_custom_call" | custom-call | flops 1 | bytes 1 | tf_op jit(solution)/shard_map/project/pallas_call | solution.py:185
  22.5 1.6 collective-permute-start.1
  24.1 0.3 collective-permute-start.2
  25.7 0.6 broadcast_in_dim.22
  26.4 5.9 %all-to-all-start = ((f32[16,3,8]{2,1,0:T(4,128)}), f32[16,3,8]{2,1,0:T(4,128)S(1)}, u32[]{:S(2)}, u32[]{:S(2)}) async-start(f32[16,3,8]{2,1,0:T(4,128)} %broadcast_in_dim.22), calls=%async_computation | async-start | bytes 65536 | tf_op jit(solution)/shard_map/all_to_all | solution.py:356
  33.0 0.7 pad_add_fusion.ints_ref
  33.6 5.2 %all-to-all-done = f32[16,3,8]{2,1,0:T(4,128)S(1)} async-done(((f32[16,3,8]{2,1,0:T(4,128)}), f32[16,3,8]{2,1,0:T(4,128)S(1)}, u32[]{:S(2)}, u32[]{:S(2)}) %all-to-all-start) | async-done | bytes 1568 | tf_op jit(solution)/shard_map/all_to_all | solution.py:356
  38.8 0.6 select_reduce_fusion
  40.9 0.6 copy-done.7
  41.6 14.1 %attend.2 = (bf16[512,2048]{1,0:T(8,128)(2,1)}, f32[256,512]{1,0:T(8,128)}, bf16[2,2,128,512]{3,2,1,0:T(8,128)(2,1)}) custom-call(f32[1]{0:T(128)S(6)} %div.33.coef_ref, s32[2]{0:T(128)} %pad_add_fusion.ints_ref, bf16[512,2048]{1,0:T(8,128)(2,1)} %bitcast.56, bf16[512,2048]{1,0:T(8,128)(2,1)} %bitcast.58, ...), custom_call_target="tpu_custom_call" | custom-call | flops 1 | bytes 1 | tf_op jit(solution)/shard_map/attend/pallas_call | solution.py:327
  55.8 1.4 copy-done
  57.3 0.5 collective-permute-start.3
  57.8 6.3 %all-to-all-start.1 = ((f32[16,16,512]{2,1,0:T(8,128)}), f32[16,16,512]{2,1,0:T(8,128)}, u32[]{:S(2)}, u32[]{:S(2)}) async-start(f32[16,16,512]{2,1,0:T(8,128)} %bitcast.74), calls=%async_computation.1 | async-start | bytes 1048576 | tf_op jit(solution)/shard_map/all_to_all | solution.py:356
  64.0 1.6 collective-permute-start.7
  65.6 1.0 copy-done.1
  66.6 14.2 %attend.3 = (bf16[512,2048]{1,0:T(8,128)(2,1)}, f32[256,512]{1,0:T(8,128)}, bf16[2,2,128,512]{3,2,1,0:T(8,128)(2,1)}) custom-call(f32[1]{0:T(128)S(6)} %div.33.coef_ref, s32[2]{0:T(128)} %pad_add_fusion.ints_ref, bf16[512,2048]{1,0:T(8,128)(2,1)} %bitcast.57, bf16[512,2048]{1,0:T(8,128)(2,1)} %bitcast.59, ...), custom_call_target="tpu_custom_call", output_to_operand_aliasing={{0}: (17, {})} | custom-call | flops 1 | bytes 1 | tf_op jit(solution)/shard_map/attend/pallas_call | solution.py:327
  80.9 6.4 %all-to-all-start.2 = ((f32[16,16,512]{2,1,0:T(8,128)}), f32[16,16,512]{2,1,0:T(8,128)S(1)}, u32[]{:S(2)}, u32[]{:S(2)}) async-start(f32[16,16,512]{2,1,0:T(8,128)} %bitcast.65), calls=%async_computation.2 | async-start | bytes 1048576 | tf_op jit(solution)/shard_map/all_to_all | solution.py:356
  87.3 0.2 collective-permute-start.16
  87.5 1.9 %row_grads.2 = bf16[16,512]{1,0:T(8,128)(2,1)} custom-call(s32[4]{0:T(128)} %pad_add_fusion.1.place_ref, f32[16,16,512]{2,1,0:T(8,128)} %all-to-all-done.1.sums_ref, f32[64,512]{1,0:T(8,128)} %get-tuple-element.28.raw_ref, f32[64,128]{1,0:T(8,128)} %copy-done.12, f32[64,128]{1,0:T(8,128)} %copy-done.11, bf16[512,512]{1,0:T(8,128)(2,1)} %tied.6.refs_0_.refs_4_), custom_call_target="tpu_custom_call" | custom-call | flops 1 | bytes 1 | tf_op jit(solution)/shard_map/row_grads/pallas_call | solution.py:436
  89.4 0.3 collective-permute-start.9
  89.7 1.1 collective-permute-done.9
  90.8 0.7 pad_maximum_fusion.4.refs_8_
  91.6 1.9 %collective-permute-start.10 = (bf16[32,512]{1,0:T(8,128)(2,1)S(1)}, bf16[32,512]{1,0:T(8,128)(2,1)S(1)}, u32[]{:S(2)}, u32[]{:S(2)}) collective-permute-start(bf16[32,512]{1,0:T(8,128)(2,1)S(1)} %pad_maximum_fusion.4.refs_8_), channel_id=1, source_target_pairs={{0,16},{16,0},{1,17},{17,1},{2,18},{18,2},{3,19},{19,3},{4,20},{20... | collective-permute-start | bytes 98312 | tf_op jit(solution)/shard_map/ppermute | solution.py:36
  93.4 9.1 %collective-permute-done.10.refs_9_ = bf16[32,512]{1,0:T(8,128)(2,1)S(1)} collective-permute-done((bf16[32,512]{1,0:T(8,128)(2,1)S(1)}, bf16[32,512]{1,0:T(8,128)(2,1)S(1)}, u32[]{:S(2)}, u32[]{:S(2)}) %collective-permute-start.10) | collective-permute-done | bytes 32800 | tf_op jit(solution)/shard_map/ppermute | solution.py:36
  102.6 0.8 copy-done.15
  103.4 1.4 copy-done.2
  104.8 7.4 %weight_shares.2 = f32[528,1024]{1,0:T(8,128)} custom-call(bf16[528,1024]{1,0:T(8,128)(2,1)} %get-tuple-element.25.refs_0_, bf16[528,1024]{1,0:T(8,128)(2,1)} %copy-done.1, bf16[2,528,1024]{2,1,0:T(8,128)(2,1)} %tied.4.refs_15_.refs_2_, bf16[2,528,1024]{2,1,0:T(8,128)(2,1)} %copy-done.2, bf16[512,512]{1,0:T(8,128)(2,1)} %bitcast.73, ...), custom_call_target="tpu_custom_call" | custom-call | flops 1 | bytes 1 | tf_op jit(solution)/shard_map/weight_shares/pallas_call | solution.py:397
  112.1 1.3 slice_convert_fusion.1
  113.5 1.7 collective-permute-start.11
  115.2 0.5 collective-permute-start.17
  115.7 0.8 copy-done.10
  116.5 1.9 %row_grads.3 = bf16[16,512]{1,0:T(8,128)(2,1)} custom-call(s32[4]{0:T(128)} %pad_add_fusion.1.place_ref, f32[16,16,512]{2,1,0:T(8,128)} %copy-done.10, f32[64,512]{1,0:T(8,128)} %get-tuple-element.28.raw_ref, f32[64,128]{1,0:T(8,128)} %copy-done.12, f32[64,128]{1,0:T(8,128)} %copy-done.11), custom_call_target="tpu_custom_call" | custom-call | flops 1 | bytes 1 | tf_op jit(solution)/shard_map/row_grads/pallas_call | solution.py:436
  118.5 1.3 collective-permute-done.18
  119.8 0.7 pad_maximum_fusion.5.refs_8_
  120.5 0.3 collective-permute-start.19
  120.8 3.6 %collective-permute-done.19.refs_9_ = bf16[32,512]{1,0:T(8,128)(2,1)S(1)} collective-permute-done((bf16[32,512]{1,0:T(8,128)(2,1)S(1)}, bf16[32,512]{1,0:T(8,128)(2,1)S(1)}, u32[]{:S(2)}, u32[]{:S(2)}) %collective-permute-start.19) | collective-permute-done | bytes 32800 | tf_op jit(solution)/shard_map/ppermute | solution.py:36
  124.4 0.6 copy-done.18
  125.0 0.8 copy-done.14
  125.8 7.3 %weight_shares.3 = f32[528,1024]{1,0:T(8,128)} custom-call(bf16[528,1024]{1,0:T(8,128)(2,1)} %get-tuple-element.25.refs_0_, bf16[528,1024]{1,0:T(8,128)(2,1)} %copy-done.1, bf16[2,528,1024]{2,1,0:T(8,128)(2,1)} %tied.4.refs_15_.refs_2_, bf16[2,528,1024]{2,1,0:T(8,128)(2,1)} %copy-done.2, bf16[512,512]{1,0:T(8,128)(2,1)} %tied.6.refs_0_.refs_4_, ...), custom_call_target="tpu_custom_call" | custom-call | flops 1 | bytes 1 | tf_op jit(solution)/shard_map/weight_shares/pallas_call | solution.py:397
  133.1 0.9 multiply_exponential_fusion.3
  134.1 0.7 multiply_exponential_fusion.5
  134.8 1.4 fusion.53
  136.4 3.3 %collective-permute-start.14 = (f16[528,128]{1,0:T(8,128)(2,1)S(1)}, f16[528,128]{1,0:T(8,128)(2,1)S(1)}, u32[]{:S(2)}, u32[]{:S(2)}) collective-permute-start(f16[528,128]{1,0:T(8,128)(2,1)S(1)} %get-tuple-element.50), channel_id=1, source_target_pairs={{0,3},{1,2},{2,1},{3,0},{4,7},{5,6},{6,5},{7,4},{8,11},{9,10},{10,... | collective-permute-start | bytes 405512 | tf_op jit(solution)/shard_map/ppermute | solution.py:36
  139.8 0.6 collective-permute-start.20
  140.4 0.9 collective-permute-start.12
  141.5 3.4 %collective-permute-done.14 = f16[528,128]{1,0:T(8,128)(2,1)S(1)} collective-permute-done((f16[528,128]{1,0:T(8,128)(2,1)S(1)}, f16[528,128]{1,0:T(8,128)(2,1)S(1)}, u32[]{:S(2)}, u32[]{:S(2)}) %collective-permute-start.14) | collective-permute-done | bytes 135200 | tf_op jit(solution)/shard_map/ppermute | solution.py:36
  144.8 6.0 %collective-permute-done.13 = f16[528,128]{1,0:T(8,128)(2,1)S(1)} collective-permute-done((f16[528,128]{1,0:T(8,128)(2,1)S(1)}, f16[528,128]{1,0:T(8,128)(2,1)S(1)}, u32[]{:S(2)}, u32[]{:S(2)}) %collective-permute-start.13) | collective-permute-done | bytes 135200 | tf_op jit(solution)/shard_map/ppermute | solution.py:36
  151.0 2.1 %collective-permute-done.20 = f16[528,512]{1,0:T(8,128)(2,1)S(1)} collective-permute-done((f16[528,512]{1,0:T(8,128)(2,1)S(1)}, f16[528,512]{1,0:T(8,128)(2,1)S(1)}, u32[]{:S(2)}, u32[]{:S(2)}) %collective-permute-start.20) | collective-permute-done | bytes 540704 | tf_op jit(solution)/shard_map/ppermute | solution.py:36
  153.1 0.2 fusion.50
  153.5 0.6 collective-permute-start.23
  154.1 0.3 collective-permute-start.24
  154.4 0.6 collective-permute-start.22
  155.0 3.3 %collective-permute-start.21 = (f16[528,128]{1,0:T(8,128)(2,1)S(1)}, f16[528,128]{1,0:T(8,128)(2,1)S(1)}, u32[]{:S(2)}, u32[]{:S(2)}) collective-permute-start(f16[528,128]{1,0:T(8,128)(2,1)S(1)} %get-tuple-element.45), channel_id=1, source_target_pairs={{0,1},{1,0},{2,3},{3,2},{4,5},{5,4},{6,7},{7,6},{8,9},{9,8},{10,11... | collective-permute-start | bytes 405512 | tf_op jit(solution)/shard_map/ppermute | solution.py:36
  158.3 3.6 %collective-permute-done.23 = f16[528,128]{1,0:T(8,128)(2,1)S(1)} collective-permute-done((f16[528,128]{1,0:T(8,128)(2,1)S(1)}, f16[528,128]{1,0:T(8,128)(2,1)S(1)}, u32[]{:S(2)}, u32[]{:S(2)}) %collective-permute-start.23) | collective-permute-done | bytes 135200 | tf_op jit(solution)/shard_map/ppermute | solution.py:36
  161.9 3.7 %collective-permute-done.22 = f16[528,128]{1,0:T(8,128)(2,1)S(1)} collective-permute-done((f16[528,128]{1,0:T(8,128)(2,1)S(1)}, f16[528,128]{1,0:T(8,128)(2,1)S(1)}, u32[]{:S(2)}, u32[]{:S(2)}) %collective-permute-start.22) | collective-permute-done | bytes 135200 | tf_op jit(solution)/shard_map/ppermute | solution.py:36
  165.7 1.0 collective-permute-start.25
  166.7 5.4 %collective-permute-done.25 = f32[512,128]{1,0:T(8,128)S(1)} collective-permute-done((f32[512,128]{1,0:T(8,128)S(1)}, f32[512,128]{1,0:T(8,128)S(1)}, u32[]{:S(2)}, u32[]{:S(2)}) %collective-permute-start.25) | collective-permute-done | bytes 262176 | tf_op jit(solution)/shard_map/ppermute | solution.py:36
  172.4 1.0 copy.24
  173.4 1.0 copy.25
  (93 shorter events, 1.9 us)
Async XLA Ops:
  5.6 50.2 %collective-permute-start.4 = (bf16[2,528,1024]{2,1,0:T(8,128)(2,1)}, bf16[2,528,1024]{2,1,0:T(8,128)(2,1)S(1)}, u32[]{:S(2)}, u32[]{:S(2)}) collective-permute-start(bf16[2,528,1024]{2,1,0:T(8,128)(2,1)} %get-tuple-element.17.after_ref), channel_id=1, source_target_pairs={{0,16},{16,0},{1,17},{17,1},{2,18},{18,2},{3,19},{19,3},{4,20},{20... | collective-permute-start | bytes 6488072 | tf_op jit(solution)/shard_map/ppermute | solution.py:36
  8.8 13.6 %copy-start.11 = (f32[64,128]{1,0:T(8,128)}, f32[64,128]{1,0:T(8,128)S(1)}, u32[]{:S(2)}) copy-start(f32[64,128]{1,0:T(8,128)S(1)} %get-tuple-element.57.sin_ref) | copy-start | bytes 98308
  8.8 13.6 %copy-start.12 = (f32[64,128]{1,0:T(8,128)}, f32[64,128]{1,0:T(8,128)S(1)}, u32[]{:S(2)}) copy-start(f32[64,128]{1,0:T(8,128)S(1)} %get-tuple-element.58.cos_ref) | copy-start | bytes 98308
  9.8 12.6 %copy-start.5 = (f32[512,128]{1,0:T(8,128)}, f32[512,128]{1,0:T(8,128)S(1)}, u32[]{:S(2)}) copy-start(f32[512,128]{1,0:T(8,128)S(1)} %get-tuple-element.51.refs_12_) | copy-start | bytes 786436
  9.9 12.6 %copy-start.6 = (f32[512,128]{1,0:T(8,128)}, f32[512,128]{1,0:T(8,128)S(1)}, u32[]{:S(2)}) copy-start(f32[512,128]{1,0:T(8,128)S(1)} %get-tuple-element.52.refs_11_) | copy-start | bytes 786436
  22.5 18.4 %collective-permute-start = (bf16[64,1024]{1,0:T(8,128)(2,1)}, bf16[64,1024]{1,0:T(8,128)(2,1)S(1)}, u32[]{:S(2)}, u32[]{:S(2)}) collective-permute-start(bf16[64,1024]{1,0:T(8,128)(2,1)} %get-tuple-element.18.refs_0_.refs_4_), channel_id=1, source_target_pairs={{0,4},{4,0},{1,5},{5,1},{2,6},{6,2},{3,7},{7,3},{8,12},{12,8},{9,1... | collective-permute-start | bytes 393224 | tf_op jit(solution)/shard_map/ppermute | solution.py:36
  22.5 18.3 %collective-permute-start.1 = (bf16[64,1024]{1,0:T(8,128)(2,1)}, bf16[64,1024]{1,0:T(8,128)(2,1)S(1)}, u32[]{:S(2)}, u32[]{:S(2)}) collective-permute-start(bf16[64,1024]{1,0:T(8,128)(2,1)} %get-tuple-element.18.refs_0_.refs_4_), channel_id=1, source_target_pairs={{0,8},{8,0},{1,9},{9,1},{2,10},{10,2},{3,11},{11,3},{4,12},{12,4},... | collective-permute-start | bytes 393224 | tf_op jit(solution)/shard_map/ppermute | solution.py:36
  24.1 16.7 %collective-permute-start.2 = (bf16[64,1024]{1,0:T(8,128)(2,1)}, bf16[64,1024]{1,0:T(8,128)(2,1)S(1)}, u32[]{:S(2)}, u32[]{:S(2)}) collective-permute-start(bf16[64,1024]{1,0:T(8,128)(2,1)} %get-tuple-element.18.refs_0_.refs_4_), channel_id=1, source_target_pairs={{0,12},{4,8},{8,4},{12,0},{1,13},{5,9},{9,5},{13,1},{2,14},{6,10},... | collective-permute-start | bytes 393224 | tf_op jit(solution)/shard_map/ppermute | solution.py:36
  26.4 12.4 %all-to-all-start = ((f32[16,3,8]{2,1,0:T(4,128)}), f32[16,3,8]{2,1,0:T(4,128)S(1)}, u32[]{:S(2)}, u32[]{:S(2)}) async-start(f32[16,3,8]{2,1,0:T(4,128)} %broadcast_in_dim.22), calls=%async_computation | async-start | bytes 65536 | tf_op jit(solution)/shard_map/all_to_all | solution.py:356
  40.8 0.7 copy-start.7
  40.8 0.7 copy-start.8
  40.9 0.7 copy-start.9
  55.8 1.4 copy-start
  57.2 45.3 %collective-permute-start.5 = (bf16[2,528,1024]{2,1,0:T(8,128)(2,1)}, bf16[2,528,1024]{2,1,0:T(8,128)(2,1)S(1)}, u32[]{:S(2)}, u32[]{:S(2)}) collective-permute-start(bf16[2,528,1024]{2,1,0:T(8,128)(2,1)} %tied.4.refs_15_.refs_2_), channel_id=1, source_target_pairs={{0,4},{4,0},{1,5},{5,1},{2,6},{6,2},{3,7},{7,3},{8,12},{12,8},{9,1... | collective-permute-start | bytes 6488072 | tf_op jit(solution)/shard_map/ppermute | solution.py:36
  57.3 8.4 %collective-permute-start.3 = (bf16[528,1024]{1,0:T(8,128)(2,1)}, bf16[528,1024]{1,0:T(8,128)(2,1)S(1)}, u32[]{:S(2)}, u32[]{:S(2)}) collective-permute-start(bf16[528,1024]{1,0:T(8,128)(2,1)} %get-tuple-element.22), channel_id=1, source_target_pairs={{0,4},{4,0},{1,5},{5,1},{2,6},{6,2},{3,7},{7,3},{8,12},{12,8},{9,1... | collective-permute-start | bytes 3244040 | tf_op jit(solution)/shard_map/ppermute | solution.py:36
  57.8 23.2 %all-to-all-start.1 = ((f32[16,16,512]{2,1,0:T(8,128)}), f32[16,16,512]{2,1,0:T(8,128)}, u32[]{:S(2)}, u32[]{:S(2)}) async-start(f32[16,16,512]{2,1,0:T(8,128)} %bitcast.74), calls=%async_computation.1 | async-start | bytes 1048576 | tf_op jit(solution)/shard_map/all_to_all | solution.py:356
  64.0 16.8 %collective-permute-start.7 = (bf16[512,512]{1,0:T(8,128)(2,1)}, bf16[512,512]{1,0:T(8,128)(2,1)}, u32[]{:S(2)}, u32[]{:S(2)}) collective-permute-start(bf16[512,512]{1,0:T(8,128)(2,1)} %bitcast.71), channel_id=1, source_target_pairs={{0,16},{16,0},{1,17},{17,1},{2,18},{18,2},{3,19},{19,3},{4,20},{20... | collective-permute-start | bytes 1572872 | tf_op jit(solution)/shard_map/ppermute | solution.py:36
  65.6 27.9 %collective-permute-start.6 = (bf16[512,512]{1,0:T(8,128)(2,1)}, bf16[512,512]{1,0:T(8,128)(2,1)}, u32[]{:S(2)}, u32[]{:S(2)}) collective-permute-start(bf16[512,512]{1,0:T(8,128)(2,1)} %bitcast.72), channel_id=1, source_target_pairs={{0,4},{4,0},{1,5},{5,1},{2,6},{6,2},{3,7},{7,3},{8,12},{12,8},{9,1... | collective-permute-start | bytes 1572872 | tf_op jit(solution)/shard_map/ppermute | solution.py:36
  65.6 1.0 copy-start.1
  80.8 21.7 %collective-permute-start.8 = (bf16[512,512]{1,0:T(8,128)(2,1)}, bf16[512,512]{1,0:T(8,128)(2,1)S(1)}, u32[]{:S(2)}, u32[]{:S(2)}) collective-permute-start(bf16[512,512]{1,0:T(8,128)(2,1)} %tied.5.refs_1_.refs_6_), channel_id=1, source_target_pairs={{0,4},{4,0},{1,5},{5,1},{2,6},{6,2},{3,7},{7,3},{8,12},{12,8},{9,1... | collective-permute-start | bytes 1572872 | tf_op jit(solution)/shard_map/ppermute | solution.py:36
  80.9 34.8 %all-to-all-start.2 = ((f32[16,16,512]{2,1,0:T(8,128)}), f32[16,16,512]{2,1,0:T(8,128)S(1)}, u32[]{:S(2)}, u32[]{:S(2)}) async-start(f32[16,16,512]{2,1,0:T(8,128)} %bitcast.65), calls=%async_computation.2 | async-start | bytes 1048576 | tf_op jit(solution)/shard_map/all_to_all | solution.py:356
  87.3 27.9 %collective-permute-start.16 = (bf16[512,512]{1,0:T(8,128)(2,1)}, bf16[512,512]{1,0:T(8,128)(2,1)}, u32[]{:S(2)}, u32[]{:S(2)}) collective-permute-start(bf16[512,512]{1,0:T(8,128)(2,1)} %tied.6.refs_0_.refs_4_), channel_id=1, source_target_pairs={{0,16},{16,0},{1,17},{17,1},{2,18},{18,2},{3,19},{19,3},{4,20},{20... | collective-permute-start | bytes 1572872 | tf_op jit(solution)/shard_map/ppermute | solution.py:36
  89.4 1.4 collective-permute-start.9
  91.6 11.8 %copy-start.17 = (bf16[32,512]{1,0:T(8,128)(2,1)}, bf16[32,512]{1,0:T(8,128)(2,1)S(1)}, u32[]{:S(2)}) copy-start(bf16[32,512]{1,0:T(8,128)(2,1)S(1)} %pad_maximum_fusion.4.refs_8_) | copy-start | bytes 98308
  91.6 11.0 %collective-permute-start.10 = (bf16[32,512]{1,0:T(8,128)(2,1)S(1)}, bf16[32,512]{1,0:T(8,128)(2,1)S(1)}, u32[]{:S(2)}, u32[]{:S(2)}) collective-permute-start(bf16[32,512]{1,0:T(8,128)(2,1)S(1)} %pad_maximum_fusion.4.refs_8_), channel_id=1, source_target_pairs={{0,16},{16,0},{1,17},{17,1},{2,18},{18,2},{3,19},{19,3},{4,20},{20... | collective-permute-start | bytes 98312 | tf_op jit(solution)/shard_map/ppermute | solution.py:36
  102.6 0.8 copy-start.19
  102.6 0.8 copy-start.15
  103.4 1.4 copy-start.2
  104.8 10.4 %copy-start.4 = (bf16[512,512]{1,0:T(8,128)(2,1)S(1)}, bf16[512,512]{1,0:T(8,128)(2,1)}, u32[]{:S(2)}) copy-start(bf16[512,512]{1,0:T(8,128)(2,1)} %tied.6.refs_0_.refs_4_) | copy-start | bytes 1572868
  113.5 19.7 %collective-permute-start.11 = (f16[528,512]{1,0:T(8,128)(2,1)S(1)}, f16[528,512]{1,0:T(8,128)(2,1)S(1)}, u32[]{:S(2)}, u32[]{:S(2)}) collective-permute-start(f16[528,512]{1,0:T(8,128)(2,1)S(1)} %slice_convert_fusion.1), channel_id=1, source_target_pairs={{0,8},{8,0},{1,9},{9,1},{2,10},{10,2},{3,11},{11,3},{4,12},{12,4},... | collective-permute-start | bytes 1622024 | tf_op jit(solution)/shard_map/ppermute | solution.py:36
  115.2 5.6 %collective-permute-start.15 = (bf16[512,512]{1,0:T(8,128)(2,1)S(1)}, bf16[512,512]{1,0:T(8,128)(2,1)S(1)}, u32[]{:S(2)}, u32[]{:S(2)}) collective-permute-start(bf16[512,512]{1,0:T(8,128)(2,1)S(1)} %copy-done.4), channel_id=1, source_target_pairs={{0,4},{4,0},{1,5},{5,1},{2,6},{6,2},{3,7},{7,3},{8,12},{12,8},{9,1... | collective-permute-start | bytes 1572872 | tf_op jit(solution)/shard_map/ppermute | solution.py:36
  115.2 9.2 %collective-permute-start.17 = (bf16[512,512]{1,0:T(8,128)(2,1)}, bf16[512,512]{1,0:T(8,128)(2,1)S(1)}, u32[]{:S(2)}, u32[]{:S(2)}) collective-permute-start(bf16[512,512]{1,0:T(8,128)(2,1)} %collective-permute-done.16.refs_6_), channel_id=1, source_target_pairs={{0,4},{4,0},{1,5},{5,1},{2,6},{6,2},{3,7},{7,3},{8,12},{12,8},{9,1... | collective-permute-start | bytes 1572872 | tf_op jit(solution)/shard_map/ppermute | solution.py:36
  115.7 0.8 copy-start.10
  118.4 1.4 collective-permute-start.18
  120.5 3.9 %copy-start.16 = (bf16[32,512]{1,0:T(8,128)(2,1)}, bf16[32,512]{1,0:T(8,128)(2,1)S(1)}, u32[]{:S(2)}) copy-start(bf16[32,512]{1,0:T(8,128)(2,1)S(1)} %pad_maximum_fusion.5.refs_8_) | copy-start | bytes 98308
  120.5 3.9 %collective-permute-start.19 = (bf16[32,512]{1,0:T(8,128)(2,1)S(1)}, bf16[32,512]{1,0:T(8,128)(2,1)S(1)}, u32[]{:S(2)}, u32[]{:S(2)}) collective-permute-start(bf16[32,512]{1,0:T(8,128)(2,1)S(1)} %pad_maximum_fusion.5.refs_8_), channel_id=1, source_target_pairs={{0,16},{16,0},{1,17},{17,1},{2,18},{18,2},{3,19},{19,3},{4,20},{20... | collective-permute-start | bytes 98312 | tf_op jit(solution)/shard_map/ppermute | solution.py:36
  120.8 3.6 %copy-start.13 = (bf16[512,512]{1,0:T(8,128)(2,1)}, bf16[512,512]{1,0:T(8,128)(2,1)S(1)}, u32[]{:S(2)}) copy-start(bf16[512,512]{1,0:T(8,128)(2,1)S(1)} %collective-permute-done.15.refs_5_) | copy-start | bytes 1572868
  124.4 0.6 copy-start.18
  125.0 0.8 copy-start.14
  133.1 6.6 %copy-start.3 = (f32[528,1024]{1,0:T(8,128)S(1)}, f32[528,1024]{1,0:T(8,128)}, u32[]{:S(2)}) copy-start(f32[528,1024]{1,0:T(8,128)} %weight_shares.3) | copy-start | bytes 6488068
  136.4 8.5 %collective-permute-start.14 = (f16[528,128]{1,0:T(8,128)(2,1)S(1)}, f16[528,128]{1,0:T(8,128)(2,1)S(1)}, u32[]{:S(2)}, u32[]{:S(2)}) collective-permute-start(f16[528,128]{1,0:T(8,128)(2,1)S(1)} %get-tuple-element.50), channel_id=1, source_target_pairs={{0,3},{1,2},{2,1},{3,0},{4,7},{5,6},{6,5},{7,4},{8,11},{9,10},{10,... | collective-permute-start | bytes 405512 | tf_op jit(solution)/shard_map/ppermute | solution.py:36
  139.8 13.3 %collective-permute-start.20 = (f16[528,512]{1,0:T(8,128)(2,1)S(1)}, f16[528,512]{1,0:T(8,128)(2,1)S(1)}, u32[]{:S(2)}, u32[]{:S(2)}) collective-permute-start(f16[528,512]{1,0:T(8,128)(2,1)S(1)} %slice_convert_fusion), channel_id=1, source_target_pairs={{0,8},{8,0},{1,9},{9,1},{2,10},{10,2},{3,11},{11,3},{4,12},{12,4},... | collective-permute-start | bytes 1622024 | tf_op jit(solution)/shard_map/ppermute | solution.py:36
  140.4 10.4 %collective-permute-start.13 = (f16[528,128]{1,0:T(8,128)(2,1)S(1)}, f16[528,128]{1,0:T(8,128)(2,1)S(1)}, u32[]{:S(2)}, u32[]{:S(2)}) collective-permute-start(f16[528,128]{1,0:T(8,128)(2,1)S(1)} %get-tuple-element.49), channel_id=1, source_target_pairs={{0,2},{1,3},{2,0},{3,1},{4,6},{5,7},{6,4},{7,5},{8,10},{9,11},{10,... | collective-permute-start | bytes 405512 | tf_op jit(solution)/shard_map/ppermute | solution.py:36
  140.4 10.4 %collective-permute-start.12 = (f16[528,128]{1,0:T(8,128)(2,1)S(1)}, f16[528,128]{1,0:T(8,128)(2,1)S(1)}, u32[]{:S(2)}, u32[]{:S(2)}) collective-permute-start(f16[528,128]{1,0:T(8,128)(2,1)S(1)} %get-tuple-element.48), channel_id=1, source_target_pairs={{0,1},{1,0},{2,3},{3,2},{4,5},{5,4},{6,7},{7,6},{8,9},{9,8},{10,11... | collective-permute-start | bytes 405512 | tf_op jit(solution)/shard_map/ppermute | solution.py:36
  153.5 8.4 %collective-permute-start.23 = (f16[528,128]{1,0:T(8,128)(2,1)S(1)}, f16[528,128]{1,0:T(8,128)(2,1)S(1)}, u32[]{:S(2)}, u32[]{:S(2)}) collective-permute-start(f16[528,128]{1,0:T(8,128)(2,1)S(1)} %get-tuple-element.47), channel_id=1, source_target_pairs={{0,3},{1,2},{2,1},{3,0},{4,7},{5,6},{6,5},{7,4},{8,11},{9,10},{10,... | collective-permute-start | bytes 405512 | tf_op jit(solution)/shard_map/ppermute | solution.py:36
  154.1 12.6 %collective-permute-start.24 = (f32[512,128]{1,0:T(8,128)S(1)}, f32[512,128]{1,0:T(8,128)S(1)}, u32[]{:S(2)}, u32[]{:S(2)}) collective-permute-start(f32[512,128]{1,0:T(8,128)S(1)} %fusion.11), channel_id=1, source_target_pairs={{0,16},{16,0},{1,17},{17,1},{2,18},{18,2},{3,19},{19,3},{4,20},{20... | collective-permute-start | bytes 786440 | tf_op jit(solution)/shard_map/ppermute | solution.py:36
  154.4 11.2 %collective-permute-start.22 = (f16[528,128]{1,0:T(8,128)(2,1)S(1)}, f16[528,128]{1,0:T(8,128)(2,1)S(1)}, u32[]{:S(2)}, u32[]{:S(2)}) collective-permute-start(f16[528,128]{1,0:T(8,128)(2,1)S(1)} %get-tuple-element.46), channel_id=1, source_target_pairs={{0,2},{1,3},{2,0},{3,1},{4,6},{5,7},{6,4},{7,5},{8,10},{9,11},{10,... | collective-permute-start | bytes 405512 | tf_op jit(solution)/shard_map/ppermute | solution.py:36
  155.0 10.6 %collective-permute-start.21 = (f16[528,128]{1,0:T(8,128)(2,1)S(1)}, f16[528,128]{1,0:T(8,128)(2,1)S(1)}, u32[]{:S(2)}, u32[]{:S(2)}) collective-permute-start(f16[528,128]{1,0:T(8,128)(2,1)S(1)} %get-tuple-element.45), channel_id=1, source_target_pairs={{0,1},{1,0},{2,3},{3,2},{4,5},{5,4},{6,7},{7,6},{8,9},{9,8},{10,11... | collective-permute-start | bytes 405512 | tf_op jit(solution)/shard_map/ppermute | solution.py:36
  165.7 6.4 %collective-permute-start.25 = (f32[512,128]{1,0:T(8,128)S(1)}, f32[512,128]{1,0:T(8,128)S(1)}, u32[]{:S(2)}, u32[]{:S(2)}) collective-permute-start(f32[512,128]{1,0:T(8,128)S(1)} %fusion.8), channel_id=1, source_target_pairs={{0,16},{16,0},{1,17},{17,1},{2,18},{18,2},{3,19},{19,3},{4,20},{20... | collective-permute-start | bytes 786440 | tf_op jit(solution)/shard_map/ppermute | solution.py:36

commit v3 on v2

--- a/solution.py
+++ b/solution.py
@@ -18,6 +18,7 @@
 VMEM = 58 * 1024 * 1024
 MARK = 16
 PROJECT_BLOCK = 1024
+WEIGHT_BLOCK = 256
 
 BF16 = jnp.bfloat16
 FREE = pl.CostEstimate(flops=1, bytes_accessed=1, transcendentals=0)
@@ -46,11 +47,10 @@
     return jnp.cos(angle), jnp.sin(angle) * sign[None, :]
 
 
-def column_copies(groups, counts, place_ref, source_ref, first, sub_ref, targets, sems):
+def column_copies(groups, counts, place_ref, source_ref, rows, sub_ref, first, targets, sems):
     n_grp, n_chip, n_core, n_resp, block = counts
-    rows = source_ref.shape[0] - first
     sub = targets[0].shape[0] - rows
-    own = pl.ds(pl.multiple_of(place_ref[3] * sub, sub), sub)
+    own = pl.ds(pl.multiple_of(first + place_ref[3] * sub, sub), sub)
     copies = []
     for i, (e, c) in enumerate(groups):
         copies.append([])
@@ -63,7 +63,7 @@
                 j = d * n_resp + r
                 target = slice(j * block, (j + 1) * block)
                 pairs = (
-                    (source_ref.at[first:, source], targets[i].at[:rows, target]),
+                    (source_ref.at[:rows, source], targets[i].at[:rows, target]),
                     (sub_ref.at[own, source], targets[i].at[rows:, target]),
                 )
                 for m, (src, dst) in enumerate(pairs):
@@ -76,7 +76,7 @@
     beside, across, held, sems, out_sems = refs
     outs = [beside, across.at[0], across.at[1]]
     targets = [held.at[i] for i in range(len(groups))]
-    copies = column_copies(groups, counts, place_ref, states_ref, 0, prompt_ref, targets, sems)
+    copies = column_copies(groups, counts, place_ref, states_ref, states_ref.shape[0], prompt_ref, 0, targets, sems)
     leaving = []
     for i, arriving in enumerate(copies):
         for copy in arriving:
@@ -134,8 +134,8 @@
         part = slice(k * PROJECT_BLOCK, (k + 1) * PROJECT_BLOCK)
         pairs = (
             (wk_hbm.at[part, :], wk_ref.at[part, :]),
-            (p_hbm.at[:, part], x_ref.at[:shard, part]),
-            (r_hbm.at[:, part], x_ref.at[shard:, part]),
+            (p_hbm.at[:, part], x_ref.at[rows:, part]),
+            (r_hbm.at[:, part], x_ref.at[:rows, part]),
             (wv_hbm.at[part, :], wv_ref.at[part, :]),
         )
         copies.append([pltpu.make_async_copy(src, dst, sems.at[k, i]) for i, (src, dst) in enumerate(pairs)])
@@ -147,7 +147,7 @@
         for copy in copies[k]:
             copy.wait()
         if k == steps - 1 and selected:
-            leaving = column_copies(groups, counts, place_ref, x_ref, shard, x_ref, selected, out_sems)
+            leaving = column_copies(groups, counts, place_ref, x_ref, rows, x_ref, rows, selected, out_sems)
         for acc, w_ref in ((acc_k, wk_ref), (acc_v, wv_ref)):
             share = jnp.dot(x_ref[:, part], w_ref[part, :], preferred_element_type=F32)
             if k:
@@ -155,8 +155,8 @@
             else:
                 acc[...] = share
     for place, raw_ref, both_ref in (
-        (slice(0, shard), p_raw, p_both),
-        (slice(shard, shard + rows), r_raw, r_both),
+        (slice(rows, rows + shard), p_raw, p_both),
+        (slice(0, rows), r_raw, r_both),
     ):
         both_ref[:, width:] = acc_v[place, :].astype(BF16)
         raw_ref[...] = acc_k[place, :]
@@ -356,57 +356,74 @@
     return lax.all_to_all(value, names, split_axis=0, concat_axis=0, tiled=True)
 
 
-def weight_kernel(parts, tokens_count, *refs):
-    states = refs[:parts]
+def weight_kernel(places, tokens_count, *refs):
+    parts = len(places)
+    states = [ref if index is None else ref.at[index] for ref, index in zip(refs, places)]
     grads = refs[parts : 2 * parts]
     tokens = refs[2 * parts : 2 * parts + tokens_count]
-    out_ref, scale_ref, side_ref = refs[-3:]
+    out_ref, held, side, result, sems, side_sems, out_sems = refs[2 * parts + tokens_count :]
     columns, rows = grads[0].shape
-    total_rows = parts * states[0].shape[-2]
-
-    @pl.when(pl.program_id(0) == 0)
-    def _():
-        highest = jnp.zeros((1, rows), F32)
-        for d, grad in enumerate(grads):
-            value = grad[...]
-            side_ref[:, d * rows : (d + 1) * rows] = value
-            highest = jnp.maximum(highest, jnp.max(jnp.abs(value), axis=0, keepdims=True).astype(F32))
-        peak = jnp.max(highest, axis=1, keepdims=True)
-        for token in tokens:
-            highest = jnp.max(jnp.abs(token[...].astype(F32)), axis=0, keepdims=True)
-            peak = jnp.maximum(peak, jnp.max(highest, axis=1, keepdims=True))
-        reach = jnp.maximum(peak * (STATE_BOUND * total_rows), 1e-30)
-        exponent = jnp.clip(jnp.ceil(jnp.log2(reach)), -90.0, 120.0)
-        scale_ref[...] = jnp.broadcast_to(exponent, scale_ref.shape)
-
-    exponent = scale_ref[:1, :1]
-    response = jnp.concatenate([part[:rows, :] for part in states], axis=0)
-    prompt = jnp.concatenate([part[rows:, :] for part in states], axis=0)
+    depth = out_ref.shape[1]
+    total_rows = parts * held.shape[1]
+    steps = depth // WEIGHT_BLOCK
+    arriving = []
+    for d in range(parts):
+        arriving.append(pltpu.make_async_copy(grads[d], side.at[:, d * rows : (d + 1) * rows], side_sems.at[d]))
+        arriving[-1].start()
+    pieces = []
+    for j in range(steps):
+        lanes = slice(j * WEIGHT_BLOCK, (j + 1) * WEIGHT_BLOCK)
+        pieces.append([])
+        for d in range(parts):
+            pieces[-1].append(pltpu.make_async_copy(states[d].at[:, lanes], held.at[d, :, lanes], sems.at[j, d]))
+            pieces[-1][-1].start()
+    for copy in arriving:
+        copy.wait()
     token = jnp.concatenate([token[...] for token in tokens], axis=0)
-    total = jnp.dot(side_ref[...], response, preferred_element_type=F32)
-    total = total + lax.dot_general(token, prompt, BY_ROWS, preferred_element_type=F32)
-    out_ref[:columns, :] = total * jnp.exp2(14.0 - exponent)
-    out_ref[columns:, :] = jnp.broadcast_to(exponent, (MARK, out_ref.shape[1]))
+    highest = jnp.max(jnp.abs(token.astype(F32)), axis=0, keepdims=True)
+    peak = jnp.max(highest, axis=1, keepdims=True)
+    highest = jnp.max(jnp.abs(side[...]), axis=0, keepdims=True).astype(F32)
+    peak = jnp.maximum(peak, jnp.max(highest, axis=1, keepdims=True))
+    reach = jnp.maximum(peak * (STATE_BOUND * total_rows), 1e-30)
+    exponent = jnp.clip(jnp.ceil(jnp.log2(reach)), -90.0, 120.0)
+    scale = jnp.exp2(14.0 - exponent)
+    leaving = []
+    for j in range(steps):
+        lanes = slice(j * WEIGHT_BLOCK, (j + 1) * WEIGHT_BLOCK)
+        for copy in pieces[j]:
+            copy.wait()
+        response = jnp.concatenate([held[d, :rows, lanes] for d in range(parts)], axis=0)
+        prompt = jnp.concatenate([held[d, rows:, lanes] for d in range(parts)], axis=0)
+        total = jnp.dot(side[...], response, preferred_element_type=F32)
+        total = total + lax.dot_general(token, prompt, BY_ROWS, preferred_element_type=F32)
+        result[:columns, lanes] = total * scale
+        result[columns:, lanes] = jnp.broadcast_to(exponent, (MARK, WEIGHT_BLOCK))
+        leaving.append(pltpu.make_async_copy(result.at[:, lanes], out_ref.at[:, lanes], out_sems.at[j]))
+        leaving[-1].start()
+    for copy in leaving:
+        copy.wait()
 
 
 def weight_shares(states, grads, tokens):
     parts = len(states)
     rows, depth = states[0][0].shape
     columns = grads[0].shape[0]
-    step = 2 * HEAD_DIM
+    steps = depth // WEIGHT_BLOCK
+    out = jax.ShapeDtypeStruct((columns + MARK, depth), F32)
     return pl.pallas_call(
-        functools.partial(weight_kernel, parts, len(tokens)),
-        grid=(depth // step,),
-        in_specs=[
-            pl.BlockSpec((rows, step), lambda j: (0, j))
-            if index is None
-            else pl.BlockSpec((None, rows, step), lambda j, index=index: (index, 0, j))
-            for _, index in states
-        ]
-        + [pl.BlockSpec(x.shape, lambda j: (0, 0)) for x in (*grads, *tokens)],
-        out_specs=pl.BlockSpec((columns + MARK, step), lambda j: (0, j)),
-        out_shape=jax.ShapeDtypeStruct((columns + MARK, depth), F32),
-        scratch_shapes=[pltpu.VMEM((8, HEAD_DIM), F32), pltpu.VMEM((columns, parts * grads[0].shape[1]), BF16)],
+        functools.partial(weight_kernel, [index for _, index in states], len(tokens)),
+        in_specs=[pl.BlockSpec(memory_space=pl.ANY)] * (2 * parts)
+        + [pl.BlockSpec(memory_space=pltpu.VMEM)] * len(tokens),
+        out_specs=pl.BlockSpec(memory_space=pl.ANY),
+        out_shape=out,
+        scratch_shapes=[
+            pltpu.VMEM((parts, rows, depth), BF16),
+            pltpu.VMEM((columns, parts * grads[0].shape[1]), BF16),
+            pltpu.VMEM(out.shape, F32),
+            pltpu.SemaphoreType.DMA((steps, parts)),
+            pltpu.SemaphoreType.DMA((parts,)),
+            pltpu.SemaphoreType.DMA((steps,)),
+        ],
         compiler_params=pltpu.CompilerParams(vmem_limit_bytes=VMEM),
         cost_estimate=FREE,
         name="weight_shares",
@@ -417,8 +434,9 @@
     out_ref = refs[-1]
     sub = sums_ref.shape[1]
     own = pl.ds(pl.multiple_of(place_ref[3] * sub, sub), sub)
-    cosine = cos_ref[own, :]
-    sine = sin_ref[own, :]
+    turn = pl.ds(pl.multiple_of(cos_ref.shape[0] - raw_ref.shape[0] + place_ref[3] * sub, sub), sub)
+    cosine = cos_ref[turn, :]
+    sine = sin_ref[turn, :]
     for head in range(out_ref.shape[1] // (2 * HEAD_DIM)):
         start = 2 * head * HEAD_DIM
         both = jnp.sum(sums_ref[:, :, start : start + 2 * HEAD_DIM], axis=0)
@@ -506,15 +524,15 @@
     coef = advantage / length.astype(F32)
     ints = jnp.stack([length[0], prompt.astype(jnp.int32)])
 
-    prompt_cos, prompt_sin = rotary_tables(prompt * shard + jnp.arange(shard, dtype=jnp.int32))
-    own_cos, own_sin = rotary_tables(prompt_len + jnp.arange(rows, dtype=jnp.int32))
+    line = jnp.arange(rows + shard, dtype=jnp.int32)
+    cosine, sine = rotary_tables(jnp.where(line < rows, prompt_len + line, prompt * shard + line - rows))
     (prompt_raw, mine, own_raw, own_both), parts = project(
         own_prompt,
         states,
         key_weight,
         value_weight,
-        jnp.concatenate([prompt_cos, own_cos]),
-        jnp.concatenate([prompt_sin, own_sin]),
+        cosine,
+        sine,
         place,
         groups[:1],
         counts,
@@ -527,7 +545,7 @@
     def run(first, per, chunk_first, chunk_heads, grads, sums, after):
         grads, sums, own_g = attend(
             first, per, first - chunk_first, chunk_heads, coef, ints, queries[0, 0], grad_output[0, 0],
-            prompt_both, own_both, own_raw, own_cos, own_sin, [grads, sums], after,
+            prompt_both, own_both, own_raw, cosine, sine, [grads, sums], after,
         )
         return grads, sums, own_g.reshape(-1, rows)
 
@@ -540,9 +558,9 @@
 
     def row_tokens(sums, chunk_first, after):
         sums = everyone(sums.reshape(n_prompt * n_resp, sub, -1), ("chip", "core", "resp"))
-        own = row_grads(chunk_first, place, sums, prompt_raw, prompt_cos, prompt_sin, after)
+        own = row_grads(chunk_first, place, sums, prompt_raw, cosine, sine, after)
         held = jnp.concatenate([own] + [exchange(own, [("core", c)]) for c in range(1, n_core)])
-        return [held] + [exchange(held, [("grp", e)]) for e in range(1, n_grp)]
+        return [held] + across(held)
 
     wide = n_resp * block
 
@@ -577,8 +595,9 @@
     hops_early = [tied(x, g_late) for x in hops_early]
     g_late = tied(g_late, *hops_early)
     sums_late = tied(sums_late, *hops_early)
+    tokens = row_tokens(sums_early, 0, [g_late])
+    g_late = tied(g_late, *tokens[1:])
     hops_late = across(g_late)
-    tokens = row_tokens(sums_early, 0, [g_late])
     shares_early = weight_shares(parts, everywhere(g_early, hops_early), tokens)
     tokens = row_tokens(sums_late, early, [])
     shares_late = weight_shares(parts, everywhere(g_late, hops_late), tokens)

time: 175 us -> 176 us (level)
  waiting for transfers between devices: 44.7 us -> 36.7 us
  Pallas kernels: 62.7 us -> 69.6 us
    ppermute x26, waiting for transfers between devices: 39.5 us -> 31.5 us  [exchange(): return lax.ppermute(value, names, [(j, j ^ mask) for j in range(total)])]
    pallas_call x2, Pallas kernels: 14.7 us -> 21.1 us  [weight_shares(): pl.pallas_call(functools.partial(weight_kernel, [index for _, index in st...]
    ppermute x26, starting transfers between devices: 22.7 us -> 24.5 us  [exchange(): return lax.ppermute(value, names, [(j, j ^ mask) for j in range(total)])]
    unnamed x41 -> x43, local copies, waits for them, and re-layouts: 7.53 us -> 8.51 us
  transfers between devices with their start and end apart: 29 -> 29, of which waited for: 12 -> 10; matrix products, arithmetic and copies ran while one was open for 4% -> 4% of each run, Pallas kernels for 33% -> 37%
where the time goes in v3:
time: 176 us; the launch traced here: 175 us
  Pallas kernels  69.6 us (40%)
  starting transfers between devices  42.5 us (24%)
  waiting for transfers between devices  36.7 us (21%)
  local copies, waits for them, and re-layouts  11.3 us (6%)
  other arithmetic  10.3 us (6%)
  between operations  4.27 us (2%)
    ppermute x26, waiting for transfers between devices, exchange(): return lax.ppermute(value, names, [(j, j ^ mask) for j in range(total)])  31.5 us
    pallas_call x2, Pallas kernels, attend(): pl.pallas_call(functools.partial(attend_kernel, parts, fold), grid=(per,)...  28.3 us
    ppermute x26, starting transfers between devices, exchange(): return lax.ppermute(value, names, [(j, j ^ mask) for j in range(total)])  24.5 us
    pallas_call x2, Pallas kernels, weight_shares(): pl.pallas_call(functools.partial(weight_kernel, [index for _, index in st...  21.1 us
    all_to_all x3, starting transfers between devices, everyone(): return lax.all_to_all(value, names, split_axis=0, concat_axis=0, tiled=True)  18 us
    pallas_call x1, Pallas kernels, project(): pl.pallas_call(functools.partial(project_kernel, groups, counts), in_spec...  11.9 us
    unnamed x43, local copies, waits for them, and re-layouts  8.51 us
    all_to_all x3, waiting for transfers between devices, everyone(): return lax.all_to_all(value, names, split_axis=0, concat_axis=0, tiled=True)  5.22 us
  transfers between devices with their start and end apart: 29, of which 10 were waited for; matrix products, arithmetic and copies ran while one was open for 4% of the time, Pallas kernels for 37%

profile of v3, /device:TPU:0, one launch (start us, length us, event | category | flops | bytes accessed | tf_op | source)
XLA Modules:
  0.0 174.7 jit_solution(10915837835063646441)
XLA Ops:
  0.6 0.7 pad_add_fusion.1.place_ref
  1.3 4.3 %select_columns.1 = (bf16[528,1024]{1,0:T(8,128)(2,1)}, bf16[2,528,1024]{2,1,0:T(8,128)(2,1)}) custom-call(s32[4]{0:T(128)} %pad_add_fusion.1.place_ref, bf16[512,4096]{1,0:T(8,128)(2,1)} %bitcast.54, bf16[64,4096]{1,0:T(8,128)(2,1)} %bitcast.63), custom_call_target="tpu_custom_call" | custom-call | flops 1 | bytes 1 | tf_op jit(solution)/shard_map/select_columns/pallas_call | solution.py:105
  5.6 3.0 %collective-permute-start.4 = (bf16[2,528,1024]{2,1,0:T(8,128)(2,1)}, bf16[2,528,1024]{2,1,0:T(8,128)(2,1)S(1)}, u32[]{:S(2)}, u32[]{:S(2)}) collective-permute-start(bf16[2,528,1024]{2,1,0:T(8,128)(2,1)} %get-tuple-element.17.after_ref), channel_id=1, source_target_pairs={{0,16},{16,0},{1,17},{17,1},{2,18},{18,2},{3,19},{19,3},{4,20},{20... | collective-permute-start | bytes 6488072 | tf_op jit(solution)/shard_map/ppermute | solution.py:37
  8.6 2.0 %fusion.5 = (f32[576,128]{1,0:T(8,128)}, f32[576,128]{1,0:T(8,128)}) fusion(f32[128]{0:T(128)S(1)} %get-tuple-element.59, f32[128]{0:T(128)S(1)} %get-tuple-element.60, f32[576]{0:T(1024)S(1)} %select_convert_fusion), kind=kLoop, calls=%fused_computation.27 | loop fusion | flops 147456 | bytes 593152 | tf_op jit(solution)/shard_map/mul | solution.py:47
  10.6 11.9 %project.1 = (f32[64,512]{1,0:T(8,128)}, bf16[64,1024]{1,0:T(8,128)(2,1)}, f32[512,512]{1,0:T(8,128)}, bf16[512,1024]{1,0:T(8,128)(2,1)}, bf16[528,1024]{1,0:T(8,128)(2,1)}) custom-call(s32[4]{0:T(128)} %pad_add_fusion.1.place_ref, bf16[64,4096]{1,0:T(8,128)(2,1)} %bitcast.64, bf16[512,4096]{1,0:T(8,128)(2,1)} %bitcast.55, bf16[4096,512]{1,0:T(8,128)(2,1)} %wk_hbm.1, ...), custom_call_target="tpu_custom_call" | custom-call | flops 1 | bytes 1 | tf_op jit(solution)/shard_map/project/pallas_call | solution.py:185
  22.4 0.7 collective-permute-start.2
  23.2 0.9 collective-permute-start.1
  24.1 0.3 collective-permute-start
  25.7 0.6 broadcast_in_dim.20
  26.3 5.9 %all-to-all-start = ((f32[16,3,8]{2,1,0:T(4,128)}), f32[16,3,8]{2,1,0:T(4,128)S(1)}, u32[]{:S(2)}, u32[]{:S(2)}) async-start(f32[16,3,8]{2,1,0:T(4,128)} %broadcast_in_dim.20), calls=%async_computation | async-start | bytes 65536 | tf_op jit(solution)/shard_map/all_to_all | solution.py:356
  32.9 0.6 pad_add_fusion.ints_ref
  33.5 5.2 %all-to-all-done = f32[16,3,8]{2,1,0:T(4,128)S(1)} async-done(((f32[16,3,8]{2,1,0:T(4,128)}), f32[16,3,8]{2,1,0:T(4,128)S(1)}, u32[]{:S(2)}, u32[]{:S(2)}) %all-to-all-start) | async-done | bytes 1568 | tf_op jit(solution)/shard_map/all_to_all | solution.py:356
  38.8 0.6 select_reduce_fusion
  40.7 0.6 copy-done.5
  41.4 14.1 %attend.2 = (bf16[512,2048]{1,0:T(8,128)(2,1)}, f32[256,512]{1,0:T(8,128)}, bf16[2,2,128,512]{3,2,1,0:T(8,128)(2,1)}) custom-call(f32[1]{0:T(128)S(6)} %div.21.coef_ref, s32[2]{0:T(128)} %pad_add_fusion.ints_ref, bf16[512,2048]{1,0:T(8,128)(2,1)} %bitcast.58, bf16[512,2048]{1,0:T(8,128)(2,1)} %bitcast.60, ...), custom_call_target="tpu_custom_call" | custom-call | flops 1 | bytes 1 | tf_op jit(solution)/shard_map/attend/pallas_call | solution.py:327
  55.6 0.2 collective-permute-done.4.refs_0_
  55.8 1.4 copy-done
  57.2 0.5 collective-permute-start.3
  57.8 6.2 %all-to-all-start.1 = ((f32[16,16,512]{2,1,0:T(8,128)}), f32[16,16,512]{2,1,0:T(8,128)S(1)}, u32[]{:S(2)}, u32[]{:S(2)}) async-start(f32[16,16,512]{2,1,0:T(8,128)} %bitcast.19), calls=%async_computation.1 | async-start | bytes 1048576 | tf_op jit(solution)/shard_map/all_to_all | solution.py:356
  64.0 1.6 collective-permute-start.7
  65.7 1.0 copy-done.2
  66.7 14.2 %attend.3 = (bf16[512,2048]{1,0:T(8,128)(2,1)}, f32[256,512]{1,0:T(8,128)}, bf16[2,2,128,512]{3,2,1,0:T(8,128)(2,1)}) custom-call(f32[1]{0:T(128)S(6)} %div.21.coef_ref, s32[2]{0:T(128)} %pad_add_fusion.ints_ref, bf16[512,2048]{1,0:T(8,128)(2,1)} %bitcast.59, bf16[512,2048]{1,0:T(8,128)(2,1)} %bitcast.61, ...), custom_call_target="tpu_custom_call", output_to_operand_aliasing={{0}: (17, {})} | custom-call | flops 1 | bytes 1 | tf_op jit(solution)/shard_map/attend/pallas_call | solution.py:327
  80.9 0.8 copy-done.4
  81.7 0.3 collective-permute-start.8
  82.0 0.8 copy-done.9
  82.8 2.1 %row_grads.2 = bf16[16,512]{1,0:T(8,128)(2,1)} custom-call(s32[4]{0:T(128)} %pad_add_fusion.1.place_ref, f32[16,16,512]{2,1,0:T(8,128)} %copy-done.9, f32[64,512]{1,0:T(8,128)} %get-tuple-element.28.raw_ref, f32[576,128]{1,0:T(8,128)} %get-tuple-element.52.cos_ref.refs_11_, f32[576,128]{1,0:T(8,128)} %get-tuple-element.51.sin_ref.refs_12_, ...), custom_call_target="tpu_custom_call" | custom-call | flops 1 | bytes 1 | tf_op jit(solution)/shard_map/row_grads/pallas_call | solution.py:454
  85.1 5.8 %all-to-all-start.2 = ((f32[16,16,512]{2,1,0:T(8,128)}), f32[16,16,512]{2,1,0:T(8,128)S(1)}, u32[]{:S(2)}, u32[]{:S(2)}) async-start(f32[16,16,512]{2,1,0:T(8,128)} %bitcast.65), calls=%async_computation.2 | async-start | bytes 1048576 | tf_op jit(solution)/shard_map/all_to_all | solution.py:356
  91.0 0.6 collective-permute-start.10
  91.6 3.4 %collective-permute-done.10.refs_9_.refs_1_ = bf16[32,512]{1,0:T(8,128)(2,1)S(1)} collective-permute-done((bf16[32,512]{1,0:T(8,128)(2,1)S(1)}, bf16[32,512]{1,0:T(8,128)(2,1)S(1)}, u32[]{:S(2)}, u32[]{:S(2)}) %collective-permute-start.10) | collective-permute-done | bytes 32800 | tf_op jit(solution)/shard_map/ppermute | solution.py:37
  94.9 0.6 copy-done.16
  95.5 0.5 collective-permute-start.16
  96.1 0.8 copy-done.14
  97.1 10.6 %weight_shares.2 = f32[528,1024]{1,0:T(8,128)} custom-call(bf16[528,1024]{1,0:T(8,128)(2,1)} %get-tuple-element.25.refs_0_, bf16[528,1024]{1,0:T(8,128)(2,1)} %copy-done.2, bf16[2,528,1024]{2,1,0:T(8,128)(2,1)} %tied.5.refs_15_.refs_2_, bf16[2,528,1024]{2,1,0:T(8,128)(2,1)} %collective-permute-done.5.refs_3_, bf16[512,512]{1,0:T(8,128)(2,1)} %bitcast.71, ...), custom_call_target="tpu_custom_call" | custom-call | flops 1 | bytes 1 | tf_op jit(solution)/shard_map/weight_shares/pallas_call | solution.py:413
  107.6 1.3 slice_convert_fusion.1
  109.0 2.0 %collective-permute-start.11 = (f16[528,512]{1,0:T(8,128)(2,1)S(1)}, f16[528,512]{1,0:T(8,128)(2,1)}, u32[]{:S(2)}, u32[]{:S(2)}) collective-permute-start(f16[528,512]{1,0:T(8,128)(2,1)S(1)} %slice_convert_fusion.1), channel_id=1, source_target_pairs={{0,8},{8,0},{1,9},{9,1},{2,10},{10,2},{3,11},{11,3},{4,12},{12,4},... | collective-permute-start | bytes 1622024 | tf_op jit(solution)/shard_map/ppermute | solution.py:37
  111.0 0.5 collective-permute-start.17
  111.5 0.8 copy-done.8
  112.3 2.1 %row_grads.3 = bf16[16,512]{1,0:T(8,128)(2,1)} custom-call(s32[4]{0:T(128)} %pad_add_fusion.1.place_ref, f32[16,16,512]{2,1,0:T(8,128)} %copy-done.8, f32[64,512]{1,0:T(8,128)} %get-tuple-element.28.raw_ref, f32[576,128]{1,0:T(8,128)} %get-tuple-element.52.cos_ref.refs_11_, f32[576,128]{1,0:T(8,128)} %get-tuple-element.51.sin_ref.refs_12_), custom_call_target="tpu_custom_call" | custom-call | flops 1 | bytes 1 | tf_op jit(solution)/shard_map/row_grads/pallas_call | solution.py:454
  114.5 1.2 collective-permute-done.18
  115.8 0.7 pad_maximum_fusion.3.refs_8_
  116.5 1.5 collective-permute-start.19
  118.0 2.4 %collective-permute-done.19.refs_9_ = bf16[32,512]{1,0:T(8,128)(2,1)S(1)} collective-permute-done((bf16[32,512]{1,0:T(8,128)(2,1)S(1)}, bf16[32,512]{1,0:T(8,128)(2,1)S(1)}, u32[]{:S(2)}, u32[]{:S(2)}) %collective-permute-start.19) | collective-permute-done | bytes 32800 | tf_op jit(solution)/shard_map/ppermute | solution.py:37
  120.4 0.6 copy-done.20
  121.0 0.8 copy-done.13
  121.8 10.5 %weight_shares.3 = f32[528,1024]{1,0:T(8,128)} custom-call(bf16[528,1024]{1,0:T(8,128)(2,1)} %get-tuple-element.25.refs_0_, bf16[528,1024]{1,0:T(8,128)(2,1)} %copy-done.2, bf16[2,528,1024]{2,1,0:T(8,128)(2,1)} %tied.5.refs_15_.refs_2_, bf16[2,528,1024]{2,1,0:T(8,128)(2,1)} %collective-permute-done.5.refs_3_, bf16[512,512]{1,0:T(8,128)(2,1)} %tied.8.refs_4_, ...), custom_call_target="tpu_custom_call" | custom-call | flops 1 | bytes 1 | tf_op jit(solution)/shard_map/weight_shares/pallas_call | solution.py:413
  132.3 0.9 multiply_exponential_fusion.3
  133.3 0.7 multiply_exponential_fusion.5
  134.0 1.6 fusion.52
  135.7 1.5 collective-permute-start.12
  137.4 0.6 collective-permute-start.20
  138.0 2.4 %collective-permute-start.13 = (f16[528,128]{1,0:T(8,128)(2,1)S(1)}, f16[528,128]{1,0:T(8,128)(2,1)S(1)}, u32[]{:S(2)}, u32[]{:S(2)}) collective-permute-start(f16[528,128]{1,0:T(8,128)(2,1)S(1)} %get-tuple-element.49), channel_id=1, source_target_pairs={{0,2},{1,3},{2,0},{3,1},{4,6},{5,7},{6,4},{7,5},{8,10},{9,11},{10,... | collective-permute-start | bytes 405512 | tf_op jit(solution)/shard_map/ppermute | solution.py:37
  140.5 1.3 collective-permute-done.12
  141.8 8.6 %collective-permute-done.13 = f16[528,128]{1,0:T(8,128)(2,1)S(1)} collective-permute-done((f16[528,128]{1,0:T(8,128)(2,1)S(1)}, f16[528,128]{1,0:T(8,128)(2,1)S(1)}, u32[]{:S(2)}, u32[]{:S(2)}) %collective-permute-start.13) | collective-permute-done | bytes 135200 | tf_op jit(solution)/shard_map/ppermute | solution.py:37
  150.6 0.2 collective-permute-done.20
  150.8 0.2 fusion.49
  151.2 1.9 %collective-permute-start.21 = (f16[528,128]{1,0:T(8,128)(2,1)S(1)}, f16[528,128]{1,0:T(8,128)(2,1)S(1)}, u32[]{:S(2)}, u32[]{:S(2)}) collective-permute-start(f16[528,128]{1,0:T(8,128)(2,1)S(1)} %get-tuple-element.45), channel_id=1, source_target_pairs={{0,1},{1,0},{2,3},{3,2},{4,5},{5,4},{6,7},{7,6},{8,9},{9,8},{10,11... | collective-permute-start | bytes 405512 | tf_op jit(solution)/shard_map/ppermute | solution.py:37
  153.2 1.5 collective-permute-start.24
  154.7 1.0 collective-permute-start.22
  155.8 1.5 collective-permute-start.23
  157.2 8.7 %collective-permute-done.22 = f16[528,128]{1,0:T(8,128)(2,1)S(1)} collective-permute-done((f16[528,128]{1,0:T(8,128)(2,1)S(1)}, f16[528,128]{1,0:T(8,128)(2,1)S(1)}, u32[]{:S(2)}, u32[]{:S(2)}) %collective-permute-start.22) | collective-permute-done | bytes 135200 | tf_op jit(solution)/shard_map/ppermute | solution.py:37
  166.1 1.0 collective-permute-start.25
  167.2 5.4 %collective-permute-done.25 = f32[512,128]{1,0:T(8,128)S(1)} collective-permute-done((f32[512,128]{1,0:T(8,128)S(1)}, f32[512,128]{1,0:T(8,128)S(1)}, u32[]{:S(2)}, u32[]{:S(2)}) %collective-permute-start.25) | collective-permute-done | bytes 262176 | tf_op jit(solution)/shard_map/ppermute | solution.py:37
  172.8 1.0 copy.26
  173.7 1.0 copy.25
  (92 shorter events, 2.1 us)
Async XLA Ops:
  5.6 50.2 %collective-permute-start.4 = (bf16[2,528,1024]{2,1,0:T(8,128)(2,1)}, bf16[2,528,1024]{2,1,0:T(8,128)(2,1)S(1)}, u32[]{:S(2)}, u32[]{:S(2)}) collective-permute-start(bf16[2,528,1024]{2,1,0:T(8,128)(2,1)} %get-tuple-element.17.after_ref), channel_id=1, source_target_pairs={{0,16},{16,0},{1,17},{17,1},{2,18},{18,2},{3,19},{19,3},{4,20},{20... | collective-permute-start | bytes 6488072 | tf_op jit(solution)/shard_map/ppermute | solution.py:37
  22.4 18.3 %collective-permute-start.2 = (bf16[64,1024]{1,0:T(8,128)(2,1)}, bf16[64,1024]{1,0:T(8,128)(2,1)S(1)}, u32[]{:S(2)}, u32[]{:S(2)}) collective-permute-start(bf16[64,1024]{1,0:T(8,128)(2,1)} %get-tuple-element.18.refs_0_.refs_4_), channel_id=1, source_target_pairs={{0,12},{4,8},{8,4},{12,0},{1,13},{5,9},{9,5},{13,1},{2,14},{6,10},... | collective-permute-start | bytes 393224 | tf_op jit(solution)/shard_map/ppermute | solution.py:37
  23.2 17.5 %collective-permute-start.1 = (bf16[64,1024]{1,0:T(8,128)(2,1)}, bf16[64,1024]{1,0:T(8,128)(2,1)S(1)}, u32[]{:S(2)}, u32[]{:S(2)}) collective-permute-start(bf16[64,1024]{1,0:T(8,128)(2,1)} %get-tuple-element.18.refs_0_.refs_4_), channel_id=1, source_target_pairs={{0,8},{8,0},{1,9},{9,1},{2,10},{10,2},{3,11},{11,3},{4,12},{12,4},... | collective-permute-start | bytes 393224 | tf_op jit(solution)/shard_map/ppermute | solution.py:37
  24.1 16.6 %collective-permute-start = (bf16[64,1024]{1,0:T(8,128)(2,1)}, bf16[64,1024]{1,0:T(8,128)(2,1)S(1)}, u32[]{:S(2)}, u32[]{:S(2)}) collective-permute-start(bf16[64,1024]{1,0:T(8,128)(2,1)} %get-tuple-element.18.refs_0_.refs_4_), channel_id=1, source_target_pairs={{0,4},{4,0},{1,5},{5,1},{2,6},{6,2},{3,7},{7,3},{8,12},{12,8},{9,1... | collective-permute-start | bytes 393224 | tf_op jit(solution)/shard_map/ppermute | solution.py:37
  26.3 12.4 %all-to-all-start = ((f32[16,3,8]{2,1,0:T(4,128)}), f32[16,3,8]{2,1,0:T(4,128)S(1)}, u32[]{:S(2)}, u32[]{:S(2)}) async-start(f32[16,3,8]{2,1,0:T(4,128)} %broadcast_in_dim.20), calls=%async_computation | async-start | bytes 65536 | tf_op jit(solution)/shard_map/all_to_all | solution.py:356
  40.7 0.7 copy-start.5
  40.7 0.7 copy-start.6
  40.7 0.7 copy-start.7
  55.8 1.4 copy-start
  57.2 6.7 %copy-start.10 = (bf16[2,2,128,512]{3,2,1,0:T(8,128)(2,1)S(1)}, bf16[2,2,128,512]{3,2,1,0:T(8,128)(2,1)}, u32[]{:S(2)}) copy-start(bf16[2,2,128,512]{3,2,1,0:T(8,128)(2,1)} %get-tuple-element.23) | copy-start | bytes 1572868
  57.2 38.9 %collective-permute-start.5 = (bf16[2,528,1024]{2,1,0:T(8,128)(2,1)}, bf16[2,528,1024]{2,1,0:T(8,128)(2,1)}, u32[]{:S(2)}, u32[]{:S(2)}) collective-permute-start(bf16[2,528,1024]{2,1,0:T(8,128)(2,1)} %tied.5.refs_15_.refs_2_), channel_id=1, source_target_pairs={{0,4},{4,0},{1,5},{5,1},{2,6},{6,2},{3,7},{7,3},{8,12},{12,8},{9,1... | collective-permute-start | bytes 6488072 | tf_op jit(solution)/shard_map/ppermute | solution.py:37
  57.2 8.4 %collective-permute-start.3 = (bf16[528,1024]{1,0:T(8,128)(2,1)}, bf16[528,1024]{1,0:T(8,128)(2,1)S(1)}, u32[]{:S(2)}, u32[]{:S(2)}) collective-permute-start(bf16[528,1024]{1,0:T(8,128)(2,1)} %get-tuple-element.22), channel_id=1, source_target_pairs={{0,4},{4,0},{1,5},{5,1},{2,6},{6,2},{3,7},{7,3},{8,12},{12,8},{9,1... | collective-permute-start | bytes 3244040 | tf_op jit(solution)/shard_map/ppermute | solution.py:37
  57.8 24.3 %all-to-all-start.1 = ((f32[16,16,512]{2,1,0:T(8,128)}), f32[16,16,512]{2,1,0:T(8,128)S(1)}, u32[]{:S(2)}, u32[]{:S(2)}) async-start(f32[16,16,512]{2,1,0:T(8,128)} %bitcast.19), calls=%async_computation.1 | async-start | bytes 1048576 | tf_op jit(solution)/shard_map/all_to_all | solution.py:356
  64.0 16.9 %collective-permute-start.7 = (bf16[512,512]{1,0:T(8,128)(2,1)S(1)}, bf16[512,512]{1,0:T(8,128)(2,1)S(1)}, u32[]{:S(2)}, u32[]{:S(2)}) collective-permute-start(bf16[512,512]{1,0:T(8,128)(2,1)S(1)} %bitcast.72), channel_id=1, source_target_pairs={{0,16},{16,0},{1,17},{17,1},{2,18},{18,2},{3,19},{19,3},{4,20},{20... | collective-permute-start | bytes 1572872 | tf_op jit(solution)/shard_map/ppermute | solution.py:37
  65.5 30.6 %collective-permute-start.6 = (bf16[512,512]{1,0:T(8,128)(2,1)S(1)}, bf16[512,512]{1,0:T(8,128)(2,1)S(1)}, u32[]{:S(2)}, u32[]{:S(2)}) collective-permute-start(bf16[512,512]{1,0:T(8,128)(2,1)S(1)} %bitcast.73), channel_id=1, source_target_pairs={{0,4},{4,0},{1,5},{5,1},{2,6},{6,2},{3,7},{7,3},{8,12},{12,8},{9,1... | collective-permute-start | bytes 1572872 | tf_op jit(solution)/shard_map/ppermute | solution.py:37
  65.7 1.0 copy-start.2
  80.9 0.8 copy-start.4
  81.7 14.4 %collective-permute-start.8 = (bf16[512,512]{1,0:T(8,128)(2,1)}, bf16[512,512]{1,0:T(8,128)(2,1)S(1)}, u32[]{:S(2)}, u32[]{:S(2)}) collective-permute-start(bf16[512,512]{1,0:T(8,128)(2,1)} %tied.6.refs_1_.refs_6_), channel_id=1, source_target_pairs={{0,4},{4,0},{1,5},{5,1},{2,6},{6,2},{3,7},{7,3},{8,12},{12,8},{9,1... | collective-permute-start | bytes 1572872 | tf_op jit(solution)/shard_map/ppermute | solution.py:37
  82.0 0.8 copy-start.9
  84.9 6.0 %copy-start.19 = (bf16[16,512]{1,0:T(8,128)(2,1)S(1)}, bf16[16,512]{1,0:T(8,128)(2,1)}, u32[]{:S(2)}) copy-start(bf16[16,512]{1,0:T(8,128)(2,1)} %row_grads.2) | copy-start | bytes 49156
  84.9 6.0 %collective-permute-start.9 = (bf16[16,512]{1,0:T(8,128)(2,1)}, bf16[16,512]{1,0:T(8,128)(2,1)S(1)}, u32[]{:S(2)}, u32[]{:S(2)}) collective-permute-start(bf16[16,512]{1,0:T(8,128)(2,1)} %row_grads.2), channel_id=1, source_target_pairs={{0,4},{4,0},{1,5},{5,1},{2,6},{6,2},{3,7},{7,3},{8,12},{12,8},{9,1... | collective-permute-start | bytes 49160 | tf_op jit(solution)/shard_map/ppermute | solution.py:37
  85.1 26.4 %all-to-all-start.2 = ((f32[16,16,512]{2,1,0:T(8,128)}), f32[16,16,512]{2,1,0:T(8,128)S(1)}, u32[]{:S(2)}, u32[]{:S(2)}) async-start(f32[16,16,512]{2,1,0:T(8,128)} %bitcast.65), calls=%async_computation.2 | async-start | bytes 1048576 | tf_op jit(solution)/shard_map/all_to_all | solution.py:356
  90.9 5.2 %copy-start.18 = (bf16[32,512]{1,0:T(8,128)(2,1)}, bf16[32,512]{1,0:T(8,128)(2,1)S(1)}, u32[]{:S(2)}) copy-start(bf16[32,512]{1,0:T(8,128)(2,1)S(1)} %pad_maximum_fusion.2.refs_8_) | copy-start | bytes 98308
  91.0 4.0 %collective-permute-start.10 = (bf16[32,512]{1,0:T(8,128)(2,1)S(1)}, bf16[32,512]{1,0:T(8,128)(2,1)S(1)}, u32[]{:S(2)}, u32[]{:S(2)}) collective-permute-start(bf16[32,512]{1,0:T(8,128)(2,1)S(1)} %pad_maximum_fusion.2.refs_8_), channel_id=1, source_target_pairs={{0,16},{16,0},{1,17},{17,1},{2,18},{18,2},{3,19},{19,3},{4,20},{20... | collective-permute-start | bytes 98312 | tf_op jit(solution)/shard_map/ppermute | solution.py:37
  94.9 0.6 copy-start.16
  95.5 15.4 %collective-permute-start.16 = (bf16[512,512]{1,0:T(8,128)(2,1)}, bf16[512,512]{1,0:T(8,128)(2,1)S(1)}, u32[]{:S(2)}, u32[]{:S(2)}) collective-permute-start(bf16[512,512]{1,0:T(8,128)(2,1)} %tied.8.refs_4_), channel_id=1, source_target_pairs={{0,16},{16,0},{1,17},{17,1},{2,18},{18,2},{3,19},{19,3},{4,20},{20... | collective-permute-start | bytes 1572872 | tf_op jit(solution)/shard_map/ppermute | solution.py:37
  96.1 0.8 copy-start.14
  96.1 1.0 copy-start.15
  97.1 13.9 %copy-start.1 = (bf16[512,512]{1,0:T(8,128)(2,1)S(1)}, bf16[512,512]{1,0:T(8,128)(2,1)}, u32[]{:S(2)}) copy-start(bf16[512,512]{1,0:T(8,128)(2,1)} %tied.8.refs_4_) | copy-start | bytes 1572868
  109.0 23.3 %collective-permute-start.11 = (f16[528,512]{1,0:T(8,128)(2,1)S(1)}, f16[528,512]{1,0:T(8,128)(2,1)}, u32[]{:S(2)}, u32[]{:S(2)}) collective-permute-start(f16[528,512]{1,0:T(8,128)(2,1)S(1)} %slice_convert_fusion.1), channel_id=1, source_target_pairs={{0,8},{8,0},{1,9},{9,1},{2,10},{10,2},{3,11},{11,3},{4,12},{12,4},... | collective-permute-start | bytes 1622024 | tf_op jit(solution)/shard_map/ppermute | solution.py:37
  111.0 7.0 %collective-permute-start.15 = (bf16[512,512]{1,0:T(8,128)(2,1)S(1)}, bf16[512,512]{1,0:T(8,128)(2,1)S(1)}, u32[]{:S(2)}, u32[]{:S(2)}) collective-permute-start(bf16[512,512]{1,0:T(8,128)(2,1)S(1)} %copy-done.1), channel_id=1, source_target_pairs={{0,4},{4,0},{1,5},{5,1},{2,6},{6,2},{3,7},{7,3},{8,12},{12,8},{9,1... | collective-permute-start | bytes 1572872 | tf_op jit(solution)/shard_map/ppermute | solution.py:37
  111.0 9.4 %copy-start.11 = (bf16[512,512]{1,0:T(8,128)(2,1)}, bf16[512,512]{1,0:T(8,128)(2,1)S(1)}, u32[]{:S(2)}) copy-start(bf16[512,512]{1,0:T(8,128)(2,1)S(1)} %collective-permute-done.16.refs_6_) | copy-start | bytes 1572868
  111.0 9.4 %collective-permute-start.17 = (bf16[512,512]{1,0:T(8,128)(2,1)S(1)}, bf16[512,512]{1,0:T(8,128)(2,1)S(1)}, u32[]{:S(2)}, u32[]{:S(2)}) collective-permute-start(bf16[512,512]{1,0:T(8,128)(2,1)S(1)} %collective-permute-done.16.refs_6_), channel_id=1, source_target_pairs={{0,4},{4,0},{1,5},{5,1},{2,6},{6,2},{3,7},{7,3},{8,12},{12,8},{9,1... | collective-permute-start | bytes 1572872 | tf_op jit(solution)/shard_map/ppermute | solution.py:37
  111.5 0.8 copy-start.8
  114.4 1.4 collective-permute-start.18
  116.5 3.9 %copy-start.17 = (bf16[32,512]{1,0:T(8,128)(2,1)}, bf16[32,512]{1,0:T(8,128)(2,1)S(1)}, u32[]{:S(2)}) copy-start(bf16[32,512]{1,0:T(8,128)(2,1)S(1)} %pad_maximum_fusion.3.refs_8_) | copy-start | bytes 98308
  116.5 3.9 %collective-permute-start.19 = (bf16[32,512]{1,0:T(8,128)(2,1)S(1)}, bf16[32,512]{1,0:T(8,128)(2,1)S(1)}, u32[]{:S(2)}, u32[]{:S(2)}) collective-permute-start(bf16[32,512]{1,0:T(8,128)(2,1)S(1)} %pad_maximum_fusion.3.refs_8_), channel_id=1, source_target_pairs={{0,16},{16,0},{1,17},{17,1},{2,18},{18,2},{3,19},{19,3},{4,20},{20... | collective-permute-start | bytes 98312 | tf_op jit(solution)/shard_map/ppermute | solution.py:37
  118.0 2.4 %copy-start.12 = (bf16[512,512]{1,0:T(8,128)(2,1)}, bf16[512,512]{1,0:T(8,128)(2,1)S(1)}, u32[]{:S(2)}) copy-start(bf16[512,512]{1,0:T(8,128)(2,1)S(1)} %collective-permute-done.15.refs_5_) | copy-start | bytes 1572868
  120.4 0.6 copy-start.20
  121.0 0.8 copy-start.13
  132.3 5.0 %copy-start.3 = (f32[528,1024]{1,0:T(8,128)S(1)}, f32[528,1024]{1,0:T(8,128)}, u32[]{:S(2)}) copy-start(f32[528,1024]{1,0:T(8,128)} %weight_shares.3) | copy-start | bytes 6488068
  135.7 6.1 %collective-permute-start.12 = (f16[528,128]{1,0:T(8,128)(2,1)S(1)}, f16[528,128]{1,0:T(8,128)(2,1)S(1)}, u32[]{:S(2)}, u32[]{:S(2)}) collective-permute-start(f16[528,128]{1,0:T(8,128)(2,1)S(1)} %get-tuple-element.48), channel_id=1, source_target_pairs={{0,1},{1,0},{2,3},{3,2},{4,5},{5,4},{6,7},{7,6},{8,9},{9,8},{10,11... | collective-permute-start | bytes 405512 | tf_op jit(solution)/shard_map/ppermute | solution.py:37
  137.4 13.4 %collective-permute-start.20 = (f16[528,512]{1,0:T(8,128)(2,1)S(1)}, f16[528,512]{1,0:T(8,128)(2,1)S(1)}, u32[]{:S(2)}, u32[]{:S(2)}) collective-permute-start(f16[528,512]{1,0:T(8,128)(2,1)S(1)} %slice_convert_fusion), channel_id=1, source_target_pairs={{0,8},{8,0},{1,9},{9,1},{2,10},{10,2},{3,11},{11,3},{4,12},{12,4},... | collective-permute-start | bytes 1622024 | tf_op jit(solution)/shard_map/ppermute | solution.py:37
  138.0 12.4 %collective-permute-start.13 = (f16[528,128]{1,0:T(8,128)(2,1)S(1)}, f16[528,128]{1,0:T(8,128)(2,1)S(1)}, u32[]{:S(2)}, u32[]{:S(2)}) collective-permute-start(f16[528,128]{1,0:T(8,128)(2,1)S(1)} %get-tuple-element.49), channel_id=1, source_target_pairs={{0,2},{1,3},{2,0},{3,1},{4,6},{5,7},{6,4},{7,5},{8,10},{9,11},{10,... | collective-permute-start | bytes 405512 | tf_op jit(solution)/shard_map/ppermute | solution.py:37
  140.4 10.1 %collective-permute-start.14 = (f16[528,128]{1,0:T(8,128)(2,1)S(1)}, f16[528,128]{1,0:T(8,128)(2,1)S(1)}, u32[]{:S(2)}, u32[]{:S(2)}) collective-permute-start(f16[528,128]{1,0:T(8,128)(2,1)S(1)} %get-tuple-element.50), channel_id=1, source_target_pairs={{0,3},{1,2},{2,1},{3,0},{4,7},{5,6},{6,5},{7,4},{8,11},{9,10},{10,... | collective-permute-start | bytes 405512 | tf_op jit(solution)/shard_map/ppermute | solution.py:37
  151.2 6.0 %collective-permute-start.21 = (f16[528,128]{1,0:T(8,128)(2,1)S(1)}, f16[528,128]{1,0:T(8,128)(2,1)S(1)}, u32[]{:S(2)}, u32[]{:S(2)}) collective-permute-start(f16[528,128]{1,0:T(8,128)(2,1)S(1)} %get-tuple-element.45), channel_id=1, source_target_pairs={{0,1},{1,0},{2,3},{3,2},{4,5},{5,4},{6,7},{7,6},{8,9},{9,8},{10,11... | collective-permute-start | bytes 405512 | tf_op jit(solution)/shard_map/ppermute | solution.py:37
  153.2 14.0 %collective-permute-start.24 = (f32[512,128]{1,0:T(8,128)S(1)}, f32[512,128]{1,0:T(8,128)S(1)}, u32[]{:S(2)}, u32[]{:S(2)}) collective-permute-start(f32[512,128]{1,0:T(8,128)S(1)} %fusion.11), channel_id=1, source_target_pairs={{0,16},{16,0},{1,17},{17,1},{2,18},{18,2},{3,19},{19,3},{4,20},{20... | collective-permute-start | bytes 786440 | tf_op jit(solution)/shard_map/ppermute | solution.py:37
  154.7 11.3 %collective-permute-start.22 = (f16[528,128]{1,0:T(8,128)(2,1)S(1)}, f16[528,128]{1,0:T(8,128)(2,1)S(1)}, u32[]{:S(2)}, u32[]{:S(2)}) collective-permute-start(f16[528,128]{1,0:T(8,128)(2,1)S(1)} %get-tuple-element.46), channel_id=1, source_target_pairs={{0,2},{1,3},{2,0},{3,1},{4,6},{5,7},{6,4},{7,5},{8,10},{9,11},{10,... | collective-permute-start | bytes 405512 | tf_op jit(solution)/shard_map/ppermute | solution.py:37
  155.8 10.2 %collective-permute-start.23 = (f16[528,128]{1,0:T(8,128)(2,1)S(1)}, f16[528,128]{1,0:T(8,128)(2,1)S(1)}, u32[]{:S(2)}, u32[]{:S(2)}) collective-permute-start(f16[528,128]{1,0:T(8,128)(2,1)S(1)} %get-tuple-element.47), channel_id=1, source_target_pairs={{0,3},{1,2},{2,1},{3,0},{4,7},{5,6},{6,5},{7,4},{8,11},{9,10},{10,... | collective-permute-start | bytes 405512 | tf_op jit(solution)/shard_map/ppermute | solution.py:37
  166.1 6.4 %collective-permute-start.25 = (f32[512,128]{1,0:T(8,128)S(1)}, f32[512,128]{1,0:T(8,128)S(1)}, u32[]{:S(2)}, u32[]{:S(2)}) collective-permute-start(f32[512,128]{1,0:T(8,128)S(1)} %fusion.8), channel_id=1, source_target_pairs={{0,16},{16,0},{1,17},{17,1},{2,18},{18,2},{3,19},{19,3},{4,20},{20... | collective-permute-start | bytes 786440 | tf_op jit(solution)/shard_map/ppermute | solution.py:37

commit v4 on v2

--- a/solution.py
+++ b/solution.py
@@ -46,11 +46,10 @@
     return jnp.cos(angle), jnp.sin(angle) * sign[None, :]
 
 
-def column_copies(groups, counts, place_ref, source_ref, first, sub_ref, targets, sems):
+def column_copies(groups, counts, place_ref, source_ref, rows, sub_ref, first, targets, sems):
     n_grp, n_chip, n_core, n_resp, block = counts
-    rows = source_ref.shape[0] - first
     sub = targets[0].shape[0] - rows
-    own = pl.ds(pl.multiple_of(place_ref[3] * sub, sub), sub)
+    own = pl.ds(pl.multiple_of(first + place_ref[3] * sub, sub), sub)
     copies = []
     for i, (e, c) in enumerate(groups):
         copies.append([])
@@ -63,7 +62,7 @@
                 j = d * n_resp + r
                 target = slice(j * block, (j + 1) * block)
                 pairs = (
-                    (source_ref.at[first:, source], targets[i].at[:rows, target]),
+                    (source_ref.at[:rows, source], targets[i].at[:rows, target]),
                     (sub_ref.at[own, source], targets[i].at[rows:, target]),
                 )
                 for m, (src, dst) in enumerate(pairs):
@@ -76,7 +75,7 @@
     beside, across, held, sems, out_sems = refs
     outs = [beside, across.at[0], across.at[1]]
     targets = [held.at[i] for i in range(len(groups))]
-    copies = column_copies(groups, counts, place_ref, states_ref, 0, prompt_ref, targets, sems)
+    copies = column_copies(groups, counts, place_ref, states_ref, states_ref.shape[0], prompt_ref, 0, targets, sems)
     leaving = []
     for i, arriving in enumerate(copies):
         for copy in arriving:
@@ -134,8 +133,8 @@
         part = slice(k * PROJECT_BLOCK, (k + 1) * PROJECT_BLOCK)
         pairs = (
             (wk_hbm.at[part, :], wk_ref.at[part, :]),
-            (p_hbm.at[:, part], x_ref.at[:shard, part]),
-            (r_hbm.at[:, part], x_ref.at[shard:, part]),
+            (p_hbm.at[:, part], x_ref.at[rows:, part]),
+            (r_hbm.at[:, part], x_ref.at[:rows, part]),
             (wv_hbm.at[part, :], wv_ref.at[part, :]),
         )
         copies.append([pltpu.make_async_copy(src, dst, sems.at[k, i]) for i, (src, dst) in enumerate(pairs)])
@@ -147,7 +146,7 @@
         for copy in copies[k]:
             copy.wait()
         if k == steps - 1 and selected:
-            leaving = column_copies(groups, counts, place_ref, x_ref, shard, x_ref, selected, out_sems)
+            leaving = column_copies(groups, counts, place_ref, x_ref, rows, x_ref, rows, selected, out_sems)
         for acc, w_ref in ((acc_k, wk_ref), (acc_v, wv_ref)):
             share = jnp.dot(x_ref[:, part], w_ref[part, :], preferred_element_type=F32)
             if k:
@@ -155,8 +154,8 @@
             else:
                 acc[...] = share
     for place, raw_ref, both_ref in (
-        (slice(0, shard), p_raw, p_both),
-        (slice(shard, shard + rows), r_raw, r_both),
+        (slice(rows, rows + shard), p_raw, p_both),
+        (slice(0, rows), r_raw, r_both),
     ):
         both_ref[:, width:] = acc_v[place, :].astype(BF16)
         raw_ref[...] = acc_k[place, :]
@@ -297,7 +296,7 @@
     g_ref[0, 1] = acc_v[prompt_len:, :].T.astype(BF16)
 
 
-def attend(first, per, offset, chunk_heads, coef, ints, query, grad_output, prompt_both, own_both, raw, cosine, sine, before, after):
+def attend(first, per, coef, ints, query, grad_output, prompt_both, own_both, raw, cosine, sine, before, after):
     rows, query_width = query.shape
     width = raw.shape[1]
     heads = width // HEAD_DIM
@@ -330,12 +329,12 @@
         in_specs=in_specs,
         out_specs=[
             wide,
-            pl.BlockSpec((prompt_len, 2 * HEAD_DIM), lambda h: (0, offset + h)),
+            pl.BlockSpec((prompt_len, 2 * HEAD_DIM), here),
             pl.BlockSpec((1, 2, HEAD_DIM, rows), lambda h: (h, 0, 0, 0)),
         ],
         out_shape=[
             jax.ShapeDtypeStruct((rows, query_width), BF16),
-            jax.ShapeDtypeStruct((prompt_len, 2 * chunk_heads * HEAD_DIM), F32),
+            jax.ShapeDtypeStruct((prompt_len, 2 * width), F32),
             jax.ShapeDtypeStruct((per, 2, HEAD_DIM, rows), BF16),
         ],
         scratch_shapes=[
@@ -356,13 +355,11 @@
     return lax.all_to_all(value, names, split_axis=0, concat_axis=0, tiled=True)
 
 
-def weight_kernel(parts, tokens_count, *refs):
+def weight_kernel(parts, *refs):
     states = refs[:parts]
     grads = refs[parts : 2 * parts]
-    tokens = refs[2 * parts : 2 * parts + tokens_count]
-    out_ref, scale_ref, side_ref = refs[-3:]
-    columns, rows = grads[0].shape
-    total_rows = parts * states[0].shape[-2]
+    out_ref, peak_ref, side_ref = refs[-3:]
+    rows = grads[0].shape[1]
 
     @pl.when(pl.program_id(0) == 0)
     def _():
@@ -371,31 +368,19 @@
             value = grad[...]
             side_ref[:, d * rows : (d + 1) * rows] = value
             highest = jnp.maximum(highest, jnp.max(jnp.abs(value), axis=0, keepdims=True).astype(F32))
-        peak = jnp.max(highest, axis=1, keepdims=True)
-        for token in tokens:
-            highest = jnp.max(jnp.abs(token[...].astype(F32)), axis=0, keepdims=True)
-            peak = jnp.maximum(peak, jnp.max(highest, axis=1, keepdims=True))
-        reach = jnp.maximum(peak * (STATE_BOUND * total_rows), 1e-30)
-        exponent = jnp.clip(jnp.ceil(jnp.log2(reach)), -90.0, 120.0)
-        scale_ref[...] = jnp.broadcast_to(exponent, scale_ref.shape)
-
-    exponent = scale_ref[:1, :1]
-    response = jnp.concatenate([part[:rows, :] for part in states], axis=0)
-    prompt = jnp.concatenate([part[rows:, :] for part in states], axis=0)
-    token = jnp.concatenate([token[...] for token in tokens], axis=0)
-    total = jnp.dot(side_ref[...], response, preferred_element_type=F32)
-    total = total + lax.dot_general(token, prompt, BY_ROWS, preferred_element_type=F32)
-    out_ref[:columns, :] = total * jnp.exp2(14.0 - exponent)
-    out_ref[columns:, :] = jnp.broadcast_to(exponent, (MARK, out_ref.shape[1]))
-
-
-def weight_shares(states, grads, tokens):
+        peak_ref[...] = jnp.broadcast_to(jnp.max(highest, axis=1, keepdims=True), peak_ref.shape)
+
+    response = jnp.concatenate([part[...] for part in states], axis=0)
+    out_ref[...] = jnp.dot(side_ref[...], response, preferred_element_type=F32)
+
+
+def weight_shares(states, grads, after):
     parts = len(states)
-    rows, depth = states[0][0].shape
-    columns = grads[0].shape[0]
+    depth = states[0][0].shape[1]
+    columns, rows = grads[0].shape
     step = 2 * HEAD_DIM
     return pl.pallas_call(
-        functools.partial(weight_kernel, parts, len(tokens)),
+        functools.partial(weight_kernel, parts),
         grid=(depth // step,),
         in_specs=[
             pl.BlockSpec((rows, step), lambda j: (0, j))
@@ -403,27 +388,29 @@
             else pl.BlockSpec((None, rows, step), lambda j, index=index: (index, 0, j))
             for _, index in states
         ]
-        + [pl.BlockSpec(x.shape, lambda j: (0, 0)) for x in (*grads, *tokens)],
-        out_specs=pl.BlockSpec((columns + MARK, step), lambda j: (0, j)),
-        out_shape=jax.ShapeDtypeStruct((columns + MARK, depth), F32),
-        scratch_shapes=[pltpu.VMEM((8, HEAD_DIM), F32), pltpu.VMEM((columns, parts * grads[0].shape[1]), BF16)],
+        + [pl.BlockSpec(grad.shape, lambda j: (0, 0)) for grad in grads]
+        + [pl.BlockSpec(memory_space=pl.ANY)] * len(after),
+        out_specs=[pl.BlockSpec((columns, step), lambda j: (0, j)), pl.BlockSpec((8, HEAD_DIM), lambda j: (0, 0))],
+        out_shape=[jax.ShapeDtypeStruct((columns, depth), F32), jax.ShapeDtypeStruct((8, HEAD_DIM), F32)],
+        scratch_shapes=[pltpu.VMEM((columns, parts * rows), BF16)],
         compiler_params=pltpu.CompilerParams(vmem_limit_bytes=VMEM),
         cost_estimate=FREE,
         name="weight_shares",
-    )(*[array for array, _ in states], *grads, *tokens)
-
-
-def rows_kernel(first, place_ref, sums_ref, raw_ref, cos_ref, sin_ref, *refs):
+    )(*[array for array, _ in states], *grads, *after)
+
+
+def rows_kernel(place_ref, sums_ref, raw_ref, cos_ref, sin_ref, *refs):
     out_ref = refs[-1]
     sub = sums_ref.shape[1]
     own = pl.ds(pl.multiple_of(place_ref[3] * sub, sub), sub)
-    cosine = cos_ref[own, :]
-    sine = sin_ref[own, :]
+    turn = pl.ds(pl.multiple_of(cos_ref.shape[0] - raw_ref.shape[0] + place_ref[3] * sub, sub), sub)
+    cosine = cos_ref[turn, :]
+    sine = sin_ref[turn, :]
     for head in range(out_ref.shape[1] // (2 * HEAD_DIM)):
         start = 2 * head * HEAD_DIM
         both = jnp.sum(sums_ref[:, :, start : start + 2 * HEAD_DIM], axis=0)
         grad = both[:, :HEAD_DIM]
-        raw = raw_ref[own, (first + head) * HEAD_DIM : (first + head + 1) * HEAD_DIM]
+        raw = raw_ref[own, head * HEAD_DIM : (head + 1) * HEAD_DIM]
         factor = lax.rsqrt(jnp.mean(raw * raw, axis=-1, keepdims=True) + EPS)
         normed = raw * factor
         unturned = grad * cosine - pltpu.roll(grad, HEAD_DIM // 2, 1) * sine
@@ -432,9 +419,9 @@
         out_ref[:, start + HEAD_DIM : start + 2 * HEAD_DIM] = both[:, HEAD_DIM:].astype(BF16)
 
 
-def row_grads(first, place, sums, raw, cosine, sine, after):
+def row_grads(place, sums, raw, cosine, sine, after):
     return pl.pallas_call(
-        functools.partial(rows_kernel, first),
+        rows_kernel,
         in_specs=[pl.BlockSpec(memory_space=pltpu.SMEM)]
         + [pl.BlockSpec(memory_space=pltpu.VMEM)] * 4
         + [pl.BlockSpec(memory_space=pl.ANY)] * len(after),
@@ -506,15 +493,15 @@
     coef = advantage / length.astype(F32)
     ints = jnp.stack([length[0], prompt.astype(jnp.int32)])
 
-    prompt_cos, prompt_sin = rotary_tables(prompt * shard + jnp.arange(shard, dtype=jnp.int32))
-    own_cos, own_sin = rotary_tables(prompt_len + jnp.arange(rows, dtype=jnp.int32))
+    line = jnp.arange(rows + shard, dtype=jnp.int32)
+    cosine, sine = rotary_tables(jnp.where(line < rows, prompt_len + line, prompt * shard + line - rows))
     (prompt_raw, mine, own_raw, own_both), parts = project(
         own_prompt,
         states,
         key_weight,
         value_weight,
-        jnp.concatenate([prompt_cos, own_cos]),
-        jnp.concatenate([prompt_sin, own_sin]),
+        cosine,
+        sine,
         place,
         groups[:1],
         counts,
@@ -524,12 +511,12 @@
     for d in range(1, n_prompt):
         prompt_both.append(exchange(mine, [("chip", d // n_core), ("core", d % n_core)]))
 
-    def run(first, per, chunk_first, chunk_heads, grads, sums, after):
+    def run(first, per, before, after):
         grads, sums, own_g = attend(
-            first, per, first - chunk_first, chunk_heads, coef, ints, queries[0, 0], grad_output[0, 0],
-            prompt_both, own_both, own_raw, own_cos, own_sin, [grads, sums], after,
+            first, per, coef, ints, queries[0, 0], grad_output[0, 0],
+            prompt_both, own_both, own_raw, cosine, sine, before, after,
         )
-        return grads, sums, own_g.reshape(-1, rows)
+        return [grads, sums], own_g.reshape(-1, rows)
 
     def across(own_g):
         return [exchange(own_g, [("grp", e)]) for e in range(1, n_grp)]
@@ -538,23 +525,27 @@
         held = [own_g] + hops
         return [exchange(held[e], [("core", c)]) if c else held[e] for e, c in groups]
 
-    def row_tokens(sums, chunk_first, after):
-        sums = everyone(sums.reshape(n_prompt * n_resp, sub, -1), ("chip", "core", "resp"))
-        own = row_grads(chunk_first, place, sums, prompt_raw, prompt_cos, prompt_sin, after)
-        held = jnp.concatenate([own] + [exchange(own, [("core", c)]) for c in range(1, n_core)])
-        return [held] + [exchange(held, [("grp", e)]) for e in range(1, n_grp)]
-
     wide = n_resp * block
 
-    def chip_terms(shares):
-        return [exchange(shares[:, d * wide : (d + 1) * wide].astype(jnp.float16), [("chip", d)]) for d in range(1, n_chip)]
-
-    def resp_terms(kept, sent):
-        exponents = [exponent_of(x) for x in [kept] + sent]
-        top = functools.reduce(jnp.maximum, exponents) + math.ceil(math.log2(n_chip))
-        total = values_of(kept, exponents[0] - top)
-        for payload, exponent in zip(sent, exponents[1:]):
-            total = total + values_of(payload, exponent - top)
+    def chip_terms(shares, peak, token):
+        peak = jnp.maximum(peak[0, 0], jnp.max(jnp.abs(token.astype(F32))))
+        reach = jnp.maximum(peak * (STATE_BOUND * len(groups) * (rows + sub)), 1e-30)
+        exponent = jnp.clip(jnp.ceil(jnp.log2(reach)), -90.0, 120.0)
+        total = shares + lax.dot_general(token, prompt_part, BY_ROWS, preferred_element_type=F32)
+        total = total * jnp.exp2(14.0 - exponent)
+        tail = jnp.full((MARK, wide), exponent, F32)
+        sent = []
+        for d in range(1, n_chip):
+            payload = jnp.concatenate([total[:, d * wide : (d + 1) * wide], tail], axis=0).astype(jnp.float16)
+            sent.append(exchange(payload, [("chip", d)]))
+        return total[:, :wide], exponent, sent
+
+    def resp_terms(kept, exponent, sent):
+        exponents = [exponent_of(x) for x in sent]
+        top = functools.reduce(jnp.maximum, exponents, exponent) + math.ceil(math.log2(n_chip))
+        total = kept * jnp.exp2(exponent - top)
+        for payload, other in zip(sent, exponents):
+            total = total + values_of(payload, other - top)
         payload = jnp.concatenate([total, jnp.broadcast_to(top, (MARK, wide))], axis=0).astype(jnp.float16)
         half = lax.dynamic_slice_in_dim(total * jnp.exp2(top - 14.0), resp * block, block, 1)
         pieces = []
@@ -569,25 +560,31 @@
         return half, exchange(half, [("grp", 1)])
 
     early, late = CALLS
-    grads, sums_early, g_early = run(0, early, 0, early, None, None, [])
+    before, g_early = run(0, early, [None, None], [])
     hops_early = across(g_early)
     across_grp = tied(across_grp, g_early)
-    grads, sums_late, g_late = run(early, late, early, late, grads, None, [beside, across_grp])
+    (grads, sums), g_late = run(early, late, before, [beside, across_grp])
     parts = [(parts[0], None), (beside, None), (across_grp, 0), (exchange(across_grp, [("core", 1)]), 1)]
+    prompt_part = jnp.concatenate([x[rows:] if i is None else x[i, rows:] for x, i in parts], axis=0)
     hops_early = [tied(x, g_late) for x in hops_early]
     g_late = tied(g_late, *hops_early)
-    sums_late = tied(sums_late, *hops_early)
+    sums = tied(sums, *hops_early)
     hops_late = across(g_late)
-    tokens = row_tokens(sums_early, 0, [g_late])
-    shares_early = weight_shares(parts, everywhere(g_early, hops_early), tokens)
-    tokens = row_tokens(sums_late, early, [])
-    shares_late = weight_shares(parts, everywhere(g_late, hops_late), tokens)
-    sent_early = chip_terms(shares_early)
-    sent_late = chip_terms(shares_late)
-    half_early, pieces_early = resp_terms(shares_early[:, :wide], sent_early)
+
+    sums = everyone(sums.reshape(n_prompt * n_resp, sub, 2 * width), ("chip", "core", "resp"))
+    shares_early, peak_early = weight_shares(parts, everywhere(g_early, hops_early), [])
+    own = row_grads(place, sums, prompt_raw, cosine, sine, [peak_early])
+    held = jnp.concatenate([own] + [exchange(own, [("core", c)]) for c in range(1, n_core)])
+    tokens = jnp.concatenate([held] + across(held))
+    cut = 2 * early * HEAD_DIM
+    kept_early, exponent_early, sent_early = chip_terms(shares_early, peak_early, tokens[:, :cut])
+    hops_late = [tied(x, peak_early) for x in hops_late]
+    shares_late, peak_late = weight_shares(parts, everywhere(g_late, hops_late), [kept_early])
+    kept_late, exponent_late, sent_late = chip_terms(shares_late, peak_late, tokens[:, cut:])
+    half_early, pieces_early = resp_terms(kept_early, exponent_early, sent_early)
     done_early = finish(half_early, pieces_early)
     sent_late = [lax.optimization_barrier((x, done_early[0]))[0] for x in sent_late]
-    half_late, pieces_late = resp_terms(shares_late[:, :wide], sent_late)
+    half_late, pieces_late = resp_terms(kept_late, exponent_late, sent_late)
     finished = [done_early, finish(half_late, pieces_late)]
 
     mine = jnp.concatenate([pair[0] for pair in finished], axis=0)

time: 175 us -> 203 us (1.16)
  waiting for transfers between devices: 44.7 us -> 65.3 us
  starting transfers between devices: 41.2 us -> 32.9 us
  local copies, waits for them, and re-layouts: 10.3 us -> 17.1 us
  other arithmetic: 11 us -> 16.3 us
  between operations: 4.36 us -> 6.96 us
  matrix products: 0 us -> 2.28 us
    all_to_all x3 -> x2, waiting for transfers between devices: 5.21 us -> 20.1 us  [everyone(): return lax.all_to_all(value, names, split_axis=0, concat_axis=0, tiled=True)]
    all_to_all x3 -> x2, starting transfers between devices: 18.6 us -> 12.7 us  [everyone(): return lax.all_to_all(value, names, split_axis=0, concat_axis=0, tiled=True)]
    ppermute x26 -> x24, waiting for transfers between devices: 39.5 us -> 45.2 us  [exchange(): return lax.ppermute(value, names, [(j, j ^ mask) for j in range(total)])]
    mul x0 -> x2, other arithmetic: none -> 4.05 us  [chip_terms(): total = total * jnp.exp2(14.0 - exponent)]
    slice x0 -> x4, local copies, waits for them, and re-layouts: none -> 3.96 us  [the longest x2 2.44 us: chip_terms(): peak = jnp.maximum(peak[0, 0], jnp.max(jnp.abs(token.astype(F32))))]
    ppermute x26 -> x24, starting transfers between devices: 22.7 us -> 20.2 us  [exchange(): return lax.ppermute(value, names, [(j, j ^ mask) for j in range(total)])]
    dot_general x0 -> x2, matrix products: none -> 2.28 us  [chip_terms(): lax.dot_general(token, prompt_part, BY_ROWS, preferred_element_type=F32)]
    pallas_call x4 -> x3, Pallas kernels: 18.5 us -> 16.3 us  [the longest x2 14.1 us: weight_shares(): pl.pallas_call(functools.partial(weight_kernel, parts), grid=(depth // st...]
  transfers between devices with their start and end apart: 29 -> 26, of which waited for: 12 -> 13; matrix products, arithmetic and copies ran while one was open for 4% -> 11% of each run, Pallas kernels for 33% -> 23%
where the time goes in v4:
time: 203 us; the launch traced here: 202 us
  waiting for transfers between devices  65.3 us (32%)
  Pallas kernels  60.8 us (30%)
  starting transfers between devices  32.9 us (16%)
  local copies, waits for them, and re-layouts  17.1 us (8%)
  other arithmetic  16.3 us (8%)
  between operations  6.96 us (3%)
  matrix products  2.28 us (1%)
    ppermute x24, waiting for transfers between devices, exchange(): return lax.ppermute(value, names, [(j, j ^ mask) for j in range(total)])  45.2 us
    pallas_call x2, Pallas kernels, attend(): pl.pallas_call(functools.partial(attend_kernel, parts, fold), grid=(per,)...  28.3 us
    ppermute x24, starting transfers between devices, exchange(): return lax.ppermute(value, names, [(j, j ^ mask) for j in range(total)])  20.2 us
    all_to_all x2, waiting for transfers between devices, everyone(): return lax.all_to_all(value, names, split_axis=0, concat_axis=0, tiled=True)  20.1 us
    pallas_call x2, Pallas kernels, weight_shares(): pl.pallas_call(functools.partial(weight_kernel, parts), grid=(depth // st...  14.1 us
    all_to_all x2, starting transfers between devices, everyone(): return lax.all_to_all(value, names, split_axis=0, concat_axis=0, tiled=True)  12.7 us
    pallas_call x1, Pallas kernels, project(): pl.pallas_call(functools.partial(project_kernel, groups, counts), in_spec...  11.8 us
    unnamed x25, local copies, waits for them, and re-layouts  7.78 us
  transfers between devices with their start and end apart: 26, of which 13 were waited for; matrix products, arithmetic and copies ran while one was open for 11% of the time, Pallas kernels for 23%

profile of v4, /device:TPU:0, one launch (start us, length us, event | category | flops | bytes accessed | tf_op | source)
XLA Modules:
  0.0 201.5 jit_solution(17407722300742170307)
XLA Ops:
  0.6 0.7 pad_add_fusion.1.place_ref
  1.3 4.3 %select_columns.1 = (bf16[528,1024]{1,0:T(8,128)(2,1)}, bf16[2,528,1024]{2,1,0:T(8,128)(2,1)}) custom-call(s32[4]{0:T(128)} %pad_add_fusion.1.place_ref, bf16[512,4096]{1,0:T(8,128)(2,1)} %bitcast.59, bf16[64,4096]{1,0:T(8,128)(2,1)} %bitcast.68), custom_call_target="tpu_custom_call" | custom-call | flops 1 | bytes 1 | tf_op jit(solution)/shard_map/select_columns/pallas_call | solution.py:104
  5.6 3.0 %collective-permute-start.4 = (bf16[2,528,1024]{2,1,0:T(8,128)(2,1)}, bf16[2,528,1024]{2,1,0:T(8,128)(2,1)S(1)}, u32[]{:S(2)}, u32[]{:S(2)}) collective-permute-start(bf16[2,528,1024]{2,1,0:T(8,128)(2,1)} %get-tuple-element.21.after_ref), channel_id=1, source_target_pairs={{0,16},{16,0},{1,17},{17,1},{2,18},{18,2},{3,19},{19,3},{4,20},{20... | collective-permute-start | bytes 6488072 | tf_op jit(solution)/shard_map/ppermute | solution.py:36
  8.6 2.0 fusion.4
  10.6 11.8 %project.1 = (f32[64,512]{1,0:T(8,128)}, bf16[64,1024]{1,0:T(8,128)(2,1)}, f32[512,512]{1,0:T(8,128)}, bf16[512,1024]{1,0:T(8,128)(2,1)}, bf16[528,1024]{1,0:T(8,128)(2,1)}) custom-call(s32[4]{0:T(128)} %pad_add_fusion.1.place_ref, bf16[64,4096]{1,0:T(8,128)(2,1)} %bitcast.69, bf16[512,4096]{1,0:T(8,128)(2,1)} %bitcast.60, bf16[4096,512]{1,0:T(8,128)(2,1)} %wk_hbm.1, ...), custom_call_target="tpu_custom_call" | custom-call | flops 1 | bytes 1 | tf_op jit(solution)/shard_map/project/pallas_call | solution.py:184
  22.5 1.6 collective-permute-start.1
  26.0 0.6 broadcast_in_dim.20
  26.7 5.9 %all-to-all-start = ((f32[16,3,8]{2,1,0:T(4,128)}), f32[16,3,8]{2,1,0:T(4,128)S(1)}, u32[]{:S(2)}, u32[]{:S(2)}) async-start(f32[16,3,8]{2,1,0:T(4,128)} %broadcast_in_dim.20), calls=%async_computation | async-start | bytes 65536 | tf_op jit(solution)/shard_map/all_to_all | solution.py:355
  33.3 0.6 pad_add_fusion.ints_ref
  33.9 5.2 %all-to-all-done = f32[16,3,8]{2,1,0:T(4,128)S(1)} async-done(((f32[16,3,8]{2,1,0:T(4,128)}), f32[16,3,8]{2,1,0:T(4,128)S(1)}, u32[]{:S(2)}, u32[]{:S(2)}) %all-to-all-start) | async-done | bytes 1568 | tf_op jit(solution)/shard_map/all_to_all | solution.py:355
  39.1 0.6 select_reduce_fusion
  41.1 0.6 copy-done.6
  41.7 14.1 %attend.2 = (bf16[512,2048]{1,0:T(8,128)(2,1)}, f32[256,1024]{1,0:T(8,128)}, bf16[2,2,128,512]{3,2,1,0:T(8,128)(2,1)}) custom-call(f32[1]{0:T(128)S(6)} %div.21.coef_ref, s32[2]{0:T(128)} %pad_add_fusion.ints_ref, bf16[512,2048]{1,0:T(8,128)(2,1)} %bitcast.62, bf16[512,2048]{1,0:T(8,128)(2,1)} %bitcast.64, ...), custom_call_target="tpu_custom_call" | custom-call | flops 1 | bytes 1 | tf_op jit(solution)/shard_map/attend/pallas_call | solution.py:326
  55.9 0.6 collective-permute-start.7
  56.5 1.3 copy-done
  57.8 1.0 copy-done.1
  58.8 14.2 %attend.3 = (bf16[512,2048]{1,0:T(8,128)(2,1)}, f32[256,1024]{1,0:T(8,128)}, bf16[2,2,128,512]{3,2,1,0:T(8,128)(2,1)}) custom-call(f32[1]{0:T(128)S(6)} %div.21.coef_ref, s32[2]{0:T(128)} %pad_add_fusion.ints_ref, bf16[512,2048]{1,0:T(8,128)(2,1)} %bitcast.63, bf16[512,2048]{1,0:T(8,128)(2,1)} %bitcast.65, ...), custom_call_target="tpu_custom_call", output_to_operand_aliasing={{0}: (17, {}), {1}: (18, {})} | custom-call | flops 1 | bytes 1 | tf_op jit(solution)/shard_map/attend/pallas_call | solution.py:326
  73.0 6.7 %all-to-all-start.1 = ((f32[16,16,1024]{2,1,0:T(8,128)}), f32[16,16,1024]{2,1,0:T(8,128)S(1)}, u32[]{:S(2)}, u32[]{:S(2)}) async-start(f32[16,16,1024]{2,1,0:T(8,128)} %bitcast.61), calls=%async_computation.1 | async-start | bytes 2097152 | tf_op jit(solution)/shard_map/all_to_all | solution.py:355
  80.3 0.8 slice.105
  81.1 0.8 slice.135
  81.9 0.7 collective-permute-done.8.refs_7_
  82.7 0.8 copy-done.11
  83.5 1.4 copy-done.2
  84.9 6.9 %weight_shares.2 = (f32[512,1024]{1,0:T(8,128)}, f32[8,128]{1,0:T(8,128)}) custom-call(bf16[528,1024]{1,0:T(8,128)(2,1)} %get-tuple-element.30.refs_0_, bf16[528,1024]{1,0:T(8,128)(2,1)} %copy-done.1, bf16[2,528,1024]{2,1,0:T(8,128)(2,1)} %tied.5.refs_16_.refs_2_, bf16[2,528,1024]{2,1,0:T(8,128)(2,1)} %copy-done.2, bf16[512,512]{1,0:T(8,128)(2,1)} %bitcast.73, ...), custom_call_target="tpu_custom_call" | custom-call | flops 1 | bytes 1 | tf_op jit(solution)/shard_map/weight_shares/pallas_call | solution.py:382
  91.8 14.9 %all-to-all-done.1.sums_ref = f32[16,16,1024]{2,1,0:T(8,128)S(1)} async-done(((f32[16,16,1024]{2,1,0:T(8,128)}), f32[16,16,1024]{2,1,0:T(8,128)S(1)}, u32[]{:S(2)}, u32[]{:S(2)}) %all-to-all-start.1) | async-done | bytes 1048608 | tf_op jit(solution)/shard_map/all_to_all | solution.py:355
  106.7 1.0 copy-done.5
  107.7 2.3 %row_grads.1 = bf16[16,1024]{1,0:T(8,128)(2,1)} custom-call(s32[4]{0:T(128)} %pad_add_fusion.1.place_ref, f32[16,16,1024]{2,1,0:T(8,128)} %copy-done.5, f32[64,512]{1,0:T(8,128)} %get-tuple-element.34.raw_ref, f32[576,128]{1,0:T(8,128)} %get-tuple-element.65.cos_ref.refs_11_, f32[576,128]{1,0:T(8,128)} %get-tuple-element.64.sin_ref.refs_12_, ...), custom_call_target="tpu_custom_call" | custom-call | flops 1 | bytes 1 | tf_op jit(solution)/shard_map/row_grads/pallas_call | solution.py:423
  109.9 0.8 slice_bitcast_fusion.1
  110.7 0.6 collective-permute-start.16
  111.3 0.8 pad_maximum_fusion.4
  112.1 1.4 collective-permute-start.10
  113.5 0.8 slice_bitcast_fusion
  114.2 1.2 slice.109
  115.5 11.1 %collective-permute-done.10 = bf16[32,1024]{1,0:T(8,128)(2,1)S(1)} collective-permute-done((bf16[32,1024]{1,0:T(8,128)(2,1)S(1)}, bf16[32,1024]{1,0:T(8,128)(2,1)S(1)}, u32[]{:S(2)}, u32[]{:S(2)}) %collective-permute-start.10) | collective-permute-done | bytes 65568 | tf_op jit(solution)/shard_map/ppermute | solution.py:36
  126.6 0.8 pad_maximum_fusion.2
  127.4 0.6 abs_reduce_fusion
  129.9 2.0 %add_multiply_fusion.1 = f32[512,1024]{1,0:T(8,128)S(1)} fusion(f32[512,1024]{1,0:T(8,128)} %get-tuple-element.32, f32[512,1024]{1,0:T(8,128)S(1)} %fusion.19, f32[]{:T(128)S(6)} %exp2.85), kind=kLoop, calls=%fused_computation.1 | loop fusion | flops 1048576 | bytes 6291460 | tf_op jit(solution)/shard_map/mul | solution.py:535
  132.1 0.9 concatenate.37
  133.5 0.8 copy-done.8
  134.8 1.8 fusion.17
  136.7 10.5 %collective-permute-done.11 = f16[528,512]{1,0:T(8,128)(2,1)} collective-permute-done((f16[528,512]{1,0:T(8,128)(2,1)}, f16[528,512]{1,0:T(8,128)(2,1)}, u32[]{:S(2)}, u32[]{:S(2)}) %collective-permute-start.11) | collective-permute-done | bytes 540704 | tf_op jit(solution)/shard_map/ppermute | solution.py:36
  147.2 0.7 multiply_exponential_fusion.3
  147.9 2.7 %fusion.57 = (f16[512,512]{1,0:T(8,128)(2,1)S(1)}, f32[512,512]{1,0:T(8,128)}, f32[512,512]{1,0:T(8,128)}) fusion(f32[512]{0:T(512)S(1)} %bitcast.81, f16[528,512]{1,0:T(8,128)(2,1)} %collective-permute-done.11, f32[512]{0:T(512)S(1)} %bitcast.82, f32[512,1024]{1,0:T(8,128)S(1)} %add_multiply_fusion.1), kind=kLoop, calls=%fused_computation.120 | loop fusion | flops 1310720 | bytes 4198400 | tf_op jit(solution)/shard_map/convert.5
  150.6 0.8 copy-done.9
  151.4 7.2 %weight_shares.3 = (f32[512,1024]{1,0:T(8,128)}, f32[8,128]{1,0:T(8,128)}) custom-call(bf16[528,1024]{1,0:T(8,128)(2,1)} %get-tuple-element.30.refs_0_, bf16[528,1024]{1,0:T(8,128)(2,1)} %copy-done.1, bf16[2,528,1024]{2,1,0:T(8,128)(2,1)} %tied.5.refs_16_.refs_2_, bf16[2,528,1024]{2,1,0:T(8,128)(2,1)} %copy-done.2, bf16[512,512]{1,0:T(8,128)(2,1)} %tied.8.refs_4_, ...), custom_call_target="tpu_custom_call" | custom-call | flops 1 | bytes 1 | tf_op jit(solution)/shard_map/weight_shares/pallas_call | solution.py:382
  158.6 1.2 slice.121
  161.1 0.7 convert_reduce_fusion.1
  161.9 0.8 collective-permute-start.14
  162.8 3.6 %collective-permute-start.12 = (f16[528,128]{1,0:T(8,128)(2,1)S(1)}, f16[528,128]{1,0:T(8,128)(2,1)S(1)}, u32[]{:S(2)}, u32[]{:S(2)}) collective-permute-start(f16[528,128]{1,0:T(8,128)(2,1)S(1)} %get-tuple-element.61), channel_id=1, source_target_pairs={{0,1},{1,0},{2,3},{3,2},{4,5},{5,4},{6,7},{7,6},{8,9},{9,8},{10,11... | collective-permute-start | bytes 405512 | tf_op jit(solution)/shard_map/ppermute | solution.py:36
  166.5 2.0 %add_multiply_fusion = f32[512,1024]{1,0:T(8,128)S(1)} fusion(f32[512,1024]{1,0:T(8,128)} %get-tuple-element.36, f32[512,1024]{1,0:T(8,128)S(1)} %copy-done.3, f32[]{:T(128)S(6)} %exp2.99), kind=kLoop, calls=%fused_computation | loop fusion | flops 1048576 | bytes 6291460 | tf_op jit(solution)/shard_map/mul | solution.py:535
  169.1 1.2 collective-permute-done.14
  170.3 4.0 %collective-permute-done.13 = f16[528,128]{1,0:T(8,128)(2,1)S(1)} collective-permute-done((f16[528,128]{1,0:T(8,128)(2,1)S(1)}, f16[528,128]{1,0:T(8,128)(2,1)S(1)}, u32[]{:S(2)}, u32[]{:S(2)}) %collective-permute-start.13) | collective-permute-done | bytes 135200 | tf_op jit(solution)/shard_map/ppermute | solution.py:36
  174.4 1.1 fusion.10
  175.5 5.5 %collective-permute-done.18 = f16[528,512]{1,0:T(8,128)(2,1)S(1)} collective-permute-done((f16[528,512]{1,0:T(8,128)(2,1)S(1)}, f16[528,512]{1,0:T(8,128)(2,1)S(1)}, u32[]{:S(2)}, u32[]{:S(2)}) %collective-permute-start.18) | collective-permute-done | bytes 540704 | tf_op jit(solution)/shard_map/ppermute | solution.py:36
  181.4 0.8 collective-permute-start.21
  182.1 0.6 collective-permute-start.22
  182.7 1.0 collective-permute-start.20
  183.7 2.6 %collective-permute-start.19 = (f16[528,128]{1,0:T(8,128)(2,1)S(1)}, f16[528,128]{1,0:T(8,128)(2,1)S(1)}, u32[]{:S(2)}, u32[]{:S(2)}) collective-permute-start(f16[528,128]{1,0:T(8,128)(2,1)S(1)} %get-tuple-element.55), channel_id=1, source_target_pairs={{0,1},{1,0},{2,3},{3,2},{4,5},{5,4},{6,7},{7,6},{8,9},{9,8},{10,11... | collective-permute-start | bytes 405512 | tf_op jit(solution)/shard_map/ppermute | solution.py:36
  186.5 2.4 %collective-permute-done.21 = f16[528,128]{1,0:T(8,128)(2,1)S(1)} collective-permute-done((f16[528,128]{1,0:T(8,128)(2,1)S(1)}, f16[528,128]{1,0:T(8,128)(2,1)S(1)}, u32[]{:S(2)}, u32[]{:S(2)}) %collective-permute-start.21) | collective-permute-done | bytes 135200 | tf_op jit(solution)/shard_map/ppermute | solution.py:36
  188.9 3.9 %collective-permute-done.20 = f16[528,128]{1,0:T(8,128)(2,1)S(1)} collective-permute-done((f16[528,128]{1,0:T(8,128)(2,1)S(1)}, f16[528,128]{1,0:T(8,128)(2,1)S(1)}, u32[]{:S(2)}, u32[]{:S(2)}) %collective-permute-start.20) | collective-permute-done | bytes 135200 | tf_op jit(solution)/shard_map/ppermute | solution.py:36
  192.9 0.9 collective-permute-start.23
  193.8 5.5 %collective-permute-done.23 = f32[512,128]{1,0:T(8,128)S(1)} collective-permute-done((f32[512,128]{1,0:T(8,128)S(1)}, f32[512,128]{1,0:T(8,128)S(1)}, u32[]{:S(2)}, u32[]{:S(2)}) %collective-permute-start.23) | collective-permute-done | bytes 262176 | tf_op jit(solution)/shard_map/ppermute | solution.py:36
  199.5 1.0 copy.26
  200.5 1.0 copy.27
  (78 shorter events, 4.9 us)
Async XLA Ops:
  5.6 50.9 %collective-permute-start.4 = (bf16[2,528,1024]{2,1,0:T(8,128)(2,1)}, bf16[2,528,1024]{2,1,0:T(8,128)(2,1)S(1)}, u32[]{:S(2)}, u32[]{:S(2)}) collective-permute-start(bf16[2,528,1024]{2,1,0:T(8,128)(2,1)} %get-tuple-element.21.after_ref), channel_id=1, source_target_pairs={{0,16},{16,0},{1,17},{17,1},{2,18},{18,2},{3,19},{19,3},{4,20},{20... | collective-permute-start | bytes 6488072 | tf_op jit(solution)/shard_map/ppermute | solution.py:36
  22.4 18.6 %collective-permute-start = (bf16[64,1024]{1,0:T(8,128)(2,1)}, bf16[64,1024]{1,0:T(8,128)(2,1)S(1)}, u32[]{:S(2)}, u32[]{:S(2)}) collective-permute-start(bf16[64,1024]{1,0:T(8,128)(2,1)} %get-tuple-element.22.refs_0_.refs_4_), channel_id=1, source_target_pairs={{0,4},{4,0},{1,5},{5,1},{2,6},{6,2},{3,7},{7,3},{8,12},{12,8},{9,1... | collective-permute-start | bytes 393224 | tf_op jit(solution)/shard_map/ppermute | solution.py:36
  22.5 18.5 %collective-permute-start.1 = (bf16[64,1024]{1,0:T(8,128)(2,1)}, bf16[64,1024]{1,0:T(8,128)(2,1)S(1)}, u32[]{:S(2)}, u32[]{:S(2)}) collective-permute-start(bf16[64,1024]{1,0:T(8,128)(2,1)} %get-tuple-element.22.refs_0_.refs_4_), channel_id=1, source_target_pairs={{0,8},{8,0},{1,9},{9,1},{2,10},{10,2},{3,11},{11,3},{4,12},{12,4},... | collective-permute-start | bytes 393224 | tf_op jit(solution)/shard_map/ppermute | solution.py:36
  24.1 17.0 %collective-permute-start.2 = (bf16[64,1024]{1,0:T(8,128)(2,1)}, bf16[64,1024]{1,0:T(8,128)(2,1)}, u32[]{:S(2)}, u32[]{:S(2)}) collective-permute-start(bf16[64,1024]{1,0:T(8,128)(2,1)} %get-tuple-element.22.refs_0_.refs_4_), channel_id=1, source_target_pairs={{0,12},{4,8},{8,4},{12,0},{1,13},{5,9},{9,5},{13,1},{2,14},{6,10},... | collective-permute-start | bytes 393224 | tf_op jit(solution)/shard_map/ppermute | solution.py:36
  24.4 33.5 %collective-permute-start.3 = (bf16[528,1024]{1,0:T(8,128)(2,1)}, bf16[528,1024]{1,0:T(8,128)(2,1)S(1)}, u32[]{:S(2)}, u32[]{:S(2)}) collective-permute-start(bf16[528,1024]{1,0:T(8,128)(2,1)} %get-tuple-element.27), channel_id=1, source_target_pairs={{0,4},{4,0},{1,5},{5,1},{2,6},{6,2},{3,7},{7,3},{8,12},{12,8},{9,1... | collective-permute-start | bytes 3244040 | tf_op jit(solution)/shard_map/ppermute | solution.py:36
  26.7 12.4 %all-to-all-start = ((f32[16,3,8]{2,1,0:T(4,128)}), f32[16,3,8]{2,1,0:T(4,128)S(1)}, u32[]{:S(2)}, u32[]{:S(2)}) async-start(f32[16,3,8]{2,1,0:T(4,128)} %broadcast_in_dim.20), calls=%async_computation | async-start | bytes 65536 | tf_op jit(solution)/shard_map/all_to_all | solution.py:355
  41.0 0.7 copy-start.6
  41.0 0.7 copy-start.7
  55.9 17.1 %collective-permute-start.7 = (bf16[512,512]{1,0:T(8,128)(2,1)}, bf16[512,512]{1,0:T(8,128)(2,1)}, u32[]{:S(2)}, u32[]{:S(2)}) collective-permute-start(bf16[512,512]{1,0:T(8,128)(2,1)} %bitcast.70), channel_id=1, source_target_pairs={{0,16},{16,0},{1,17},{17,1},{2,18},{18,2},{3,19},{19,3},{4,20},{20... | collective-permute-start | bytes 1572872 | tf_op jit(solution)/shard_map/ppermute | solution.py:36
  56.5 1.3 copy-start
  57.8 24.9 %collective-permute-start.5 = (bf16[2,528,1024]{2,1,0:T(8,128)(2,1)}, bf16[2,528,1024]{2,1,0:T(8,128)(2,1)S(1)}, u32[]{:S(2)}, u32[]{:S(2)}) collective-permute-start(bf16[2,528,1024]{2,1,0:T(8,128)(2,1)} %tied.5.refs_16_.refs_2_), channel_id=1, source_target_pairs={{0,4},{4,0},{1,5},{5,1},{2,6},{6,2},{3,7},{7,3},{8,12},{12,8},{9,1... | collective-permute-start | bytes 6488072 | tf_op jit(solution)/shard_map/ppermute | solution.py:36
  57.8 1.0 copy-start.1
  73.0 33.7 %all-to-all-start.1 = ((f32[16,16,1024]{2,1,0:T(8,128)}), f32[16,16,1024]{2,1,0:T(8,128)S(1)}, u32[]{:S(2)}, u32[]{:S(2)}) async-start(f32[16,16,1024]{2,1,0:T(8,128)} %bitcast.61), calls=%async_computation.1 | async-start | bytes 2097152 | tf_op jit(solution)/shard_map/all_to_all | solution.py:355
  79.7 2.2 %collective-permute-start.6 = (bf16[512,512]{1,0:T(8,128)(2,1)}, bf16[512,512]{1,0:T(8,128)(2,1)S(1)}, u32[]{:S(2)}, u32[]{:S(2)}) collective-permute-start(bf16[512,512]{1,0:T(8,128)(2,1)} %bitcast.72), channel_id=1, source_target_pairs={{0,4},{4,0},{1,5},{5,1},{2,6},{6,2},{3,7},{7,3},{8,12},{12,8},{9,1... | collective-permute-start | bytes 1572872 | tf_op jit(solution)/shard_map/ppermute | solution.py:36
  80.2 2.5 %collective-permute-start.8 = (bf16[512,512]{1,0:T(8,128)(2,1)}, bf16[512,512]{1,0:T(8,128)(2,1)S(1)}, u32[]{:S(2)}, u32[]{:S(2)}) collective-permute-start(bf16[512,512]{1,0:T(8,128)(2,1)} %tied.6.refs_6_.refs_1_), channel_id=1, source_target_pairs={{0,4},{4,0},{1,5},{5,1},{2,6},{6,2},{3,7},{7,3},{8,12},{12,8},{9,1... | collective-permute-start | bytes 1572872 | tf_op jit(solution)/shard_map/ppermute | solution.py:36
  81.9 0.8 copy-start.10
  82.7 0.8 copy-start.11
  83.5 1.4 copy-start.2
  106.7 1.0 copy-start.5
  109.9 1.4 collective-permute-start.9
  110.7 22.9 %collective-permute-start.16 = (bf16[512,512]{1,0:T(8,128)(2,1)}, bf16[512,512]{1,0:T(8,128)(2,1)S(1)}, u32[]{:S(2)}, u32[]{:S(2)}) collective-permute-start(bf16[512,512]{1,0:T(8,128)(2,1)} %tied.8.refs_4_), channel_id=1, source_target_pairs={{0,16},{16,0},{1,17},{17,1},{2,18},{18,2},{3,19},{19,3},{4,20},{20... | collective-permute-start | bytes 1572872 | tf_op jit(solution)/shard_map/ppermute | solution.py:36
  112.1 14.5 %collective-permute-start.10 = (bf16[32,1024]{1,0:T(8,128)(2,1)S(1)}, bf16[32,1024]{1,0:T(8,128)(2,1)S(1)}, u32[]{:S(2)}, u32[]{:S(2)}) collective-permute-start(bf16[32,1024]{1,0:T(8,128)(2,1)S(1)} %pad_maximum_fusion.4), channel_id=1, source_target_pairs={{0,16},{16,0},{1,17},{17,1},{2,18},{18,2},{3,19},{19,3},{4,20},{20... | collective-permute-start | bytes 196616 | tf_op jit(solution)/shard_map/ppermute | solution.py:36
  131.9 1.6 copy-start.4
  133.0 14.2 %collective-permute-start.11 = (f16[528,512]{1,0:T(8,128)(2,1)}, f16[528,512]{1,0:T(8,128)(2,1)}, u32[]{:S(2)}, u32[]{:S(2)}) collective-permute-start(f16[528,512]{1,0:T(8,128)(2,1)} %concatenate.37), channel_id=1, source_target_pairs={{0,8},{8,0},{1,9},{9,1},{2,10},{10,2},{3,11},{11,3},{4,12},{12,4},... | collective-permute-start | bytes 1622024 | tf_op jit(solution)/shard_map/ppermute | solution.py:36
  133.5 17.1 %collective-permute-start.15 = (bf16[512,512]{1,0:T(8,128)(2,1)S(1)}, bf16[512,512]{1,0:T(8,128)(2,1)}, u32[]{:S(2)}, u32[]{:S(2)}) collective-permute-start(bf16[512,512]{1,0:T(8,128)(2,1)S(1)} %copy-done.4), channel_id=1, source_target_pairs={{0,4},{4,0},{1,5},{5,1},{2,6},{6,2},{3,7},{7,3},{8,12},{12,8},{9,1... | collective-permute-start | bytes 1572872 | tf_op jit(solution)/shard_map/ppermute | solution.py:36
  133.5 0.8 copy-start.8
  134.3 16.3 %collective-permute-start.17 = (bf16[512,512]{1,0:T(8,128)(2,1)}, bf16[512,512]{1,0:T(8,128)(2,1)S(1)}, u32[]{:S(2)}, u32[]{:S(2)}) collective-permute-start(bf16[512,512]{1,0:T(8,128)(2,1)} %tied.9.refs_6_), channel_id=1, source_target_pairs={{0,4},{4,0},{1,5},{5,1},{2,6},{6,2},{3,7},{7,3},{8,12},{12,8},{9,1... | collective-permute-start | bytes 1572872 | tf_op jit(solution)/shard_map/ppermute | solution.py:36
  150.6 0.8 copy-start.9
  151.4 15.0 %copy-start.3 = (f32[512,1024]{1,0:T(8,128)S(1)}, f32[512,1024]{1,0:T(8,128)}, u32[]{:S(2)}) copy-start(f32[512,1024]{1,0:T(8,128)} %fusion.17) | copy-start | bytes 6291460
  161.9 8.4 %collective-permute-start.14 = (f16[528,128]{1,0:T(8,128)(2,1)S(1)}, f16[528,128]{1,0:T(8,128)(2,1)S(1)}, u32[]{:S(2)}, u32[]{:S(2)}) collective-permute-start(f16[528,128]{1,0:T(8,128)(2,1)S(1)} %get-tuple-element.63), channel_id=1, source_target_pairs={{0,3},{1,2},{2,1},{3,0},{4,7},{5,6},{6,5},{7,4},{8,11},{9,10},{10,... | collective-permute-start | bytes 405512 | tf_op jit(solution)/shard_map/ppermute | solution.py:36
  162.8 11.6 %collective-permute-start.13 = (f16[528,128]{1,0:T(8,128)(2,1)S(1)}, f16[528,128]{1,0:T(8,128)(2,1)S(1)}, u32[]{:S(2)}, u32[]{:S(2)}) collective-permute-start(f16[528,128]{1,0:T(8,128)(2,1)S(1)} %get-tuple-element.62), channel_id=1, source_target_pairs={{0,2},{1,3},{2,0},{3,1},{4,6},{5,7},{6,4},{7,5},{8,10},{9,11},{10,... | collective-permute-start | bytes 405512 | tf_op jit(solution)/shard_map/ppermute | solution.py:36
  162.8 11.6 %collective-permute-start.12 = (f16[528,128]{1,0:T(8,128)(2,1)S(1)}, f16[528,128]{1,0:T(8,128)(2,1)S(1)}, u32[]{:S(2)}, u32[]{:S(2)}) collective-permute-start(f16[528,128]{1,0:T(8,128)(2,1)S(1)} %get-tuple-element.61), channel_id=1, source_target_pairs={{0,1},{1,0},{2,3},{3,2},{4,5},{5,4},{6,7},{7,6},{8,9},{9,8},{10,11... | collective-permute-start | bytes 405512 | tf_op jit(solution)/shard_map/ppermute | solution.py:36
  168.7 12.2 %collective-permute-start.18 = (f16[528,512]{1,0:T(8,128)(2,1)S(1)}, f16[528,512]{1,0:T(8,128)(2,1)S(1)}, u32[]{:S(2)}, u32[]{:S(2)}) collective-permute-start(f16[528,512]{1,0:T(8,128)(2,1)S(1)} %concatenate.39), channel_id=1, source_target_pairs={{0,8},{8,0},{1,9},{9,1},{2,10},{10,2},{3,11},{11,3},{4,12},{12,4},... | collective-permute-start | bytes 1622024 | tf_op jit(solution)/shard_map/ppermute | solution.py:36
  181.4 7.6 %collective-permute-start.21 = (f16[528,128]{1,0:T(8,128)(2,1)S(1)}, f16[528,128]{1,0:T(8,128)(2,1)S(1)}, u32[]{:S(2)}, u32[]{:S(2)}) collective-permute-start(f16[528,128]{1,0:T(8,128)(2,1)S(1)} %get-tuple-element.57), channel_id=1, source_target_pairs={{0,3},{1,2},{2,1},{3,0},{4,7},{5,6},{6,5},{7,4},{8,11},{9,10},{10,... | collective-permute-start | bytes 405512 | tf_op jit(solution)/shard_map/ppermute | solution.py:36
  182.1 11.7 %collective-permute-start.22 = (f32[512,128]{1,0:T(8,128)S(1)}, f32[512,128]{1,0:T(8,128)S(1)}, u32[]{:S(2)}, u32[]{:S(2)}) collective-permute-start(f32[512,128]{1,0:T(8,128)S(1)} %fusion.10), channel_id=1, source_target_pairs={{0,16},{16,0},{1,17},{17,1},{2,18},{18,2},{3,19},{19,3},{4,20},{20... | collective-permute-start | bytes 786440 | tf_op jit(solution)/shard_map/ppermute | solution.py:36
  182.7 10.1 %collective-permute-start.20 = (f16[528,128]{1,0:T(8,128)(2,1)S(1)}, f16[528,128]{1,0:T(8,128)(2,1)S(1)}, u32[]{:S(2)}, u32[]{:S(2)}) collective-permute-start(f16[528,128]{1,0:T(8,128)(2,1)S(1)} %get-tuple-element.56), channel_id=1, source_target_pairs={{0,2},{1,3},{2,0},{3,1},{4,6},{5,7},{6,4},{7,5},{8,10},{9,11},{10,... | collective-permute-start | bytes 405512 | tf_op jit(solution)/shard_map/ppermute | solution.py:36
  183.7 9.0 %collective-permute-start.19 = (f16[528,128]{1,0:T(8,128)(2,1)S(1)}, f16[528,128]{1,0:T(8,128)(2,1)S(1)}, u32[]{:S(2)}, u32[]{:S(2)}) collective-permute-start(f16[528,128]{1,0:T(8,128)(2,1)S(1)} %get-tuple-element.55), channel_id=1, source_target_pairs={{0,1},{1,0},{2,3},{3,2},{4,5},{5,4},{6,7},{7,6},{8,9},{9,8},{10,11... | collective-permute-start | bytes 405512 | tf_op jit(solution)/shard_map/ppermute | solution.py:36
  192.9 6.4 %collective-permute-start.23 = (f32[512,128]{1,0:T(8,128)S(1)}, f32[512,128]{1,0:T(8,128)S(1)}, u32[]{:S(2)}, u32[]{:S(2)}) collective-permute-start(f32[512,128]{1,0:T(8,128)S(1)} %fusion.7), channel_id=1, source_target_pairs={{0,16},{16,0},{1,17},{17,1},{2,18},{18,2},{3,19},{19,3},{4,20},{20... | collective-permute-start | bytes 786440 | tf_op jit(solution)/shard_map/ppermute | solution.py:36

commit v5 on v2

--- a/solution.py
+++ b/solution.py
@@ -46,11 +46,10 @@
     return jnp.cos(angle), jnp.sin(angle) * sign[None, :]
 
 
-def column_copies(groups, counts, place_ref, source_ref, first, sub_ref, targets, sems):
+def column_copies(groups, counts, place_ref, source_ref, rows, sub_ref, first, targets, sems):
     n_grp, n_chip, n_core, n_resp, block = counts
-    rows = source_ref.shape[0] - first
     sub = targets[0].shape[0] - rows
-    own = pl.ds(pl.multiple_of(place_ref[3] * sub, sub), sub)
+    own = pl.ds(pl.multiple_of(first + place_ref[3] * sub, sub), sub)
     copies = []
     for i, (e, c) in enumerate(groups):
         copies.append([])
@@ -63,7 +62,7 @@
                 j = d * n_resp + r
                 target = slice(j * block, (j + 1) * block)
                 pairs = (
-                    (source_ref.at[first:, source], targets[i].at[:rows, target]),
+                    (source_ref.at[:rows, source], targets[i].at[:rows, target]),
                     (sub_ref.at[own, source], targets[i].at[rows:, target]),
                 )
                 for m, (src, dst) in enumerate(pairs):
@@ -76,7 +75,7 @@
     beside, across, held, sems, out_sems = refs
     outs = [beside, across.at[0], across.at[1]]
     targets = [held.at[i] for i in range(len(groups))]
-    copies = column_copies(groups, counts, place_ref, states_ref, 0, prompt_ref, targets, sems)
+    copies = column_copies(groups, counts, place_ref, states_ref, states_ref.shape[0], prompt_ref, 0, targets, sems)
     leaving = []
     for i, arriving in enumerate(copies):
         for copy in arriving:
@@ -134,8 +133,8 @@
         part = slice(k * PROJECT_BLOCK, (k + 1) * PROJECT_BLOCK)
         pairs = (
             (wk_hbm.at[part, :], wk_ref.at[part, :]),
-            (p_hbm.at[:, part], x_ref.at[:shard, part]),
-            (r_hbm.at[:, part], x_ref.at[shard:, part]),
+            (p_hbm.at[:, part], x_ref.at[rows:, part]),
+            (r_hbm.at[:, part], x_ref.at[:rows, part]),
             (wv_hbm.at[part, :], wv_ref.at[part, :]),
         )
         copies.append([pltpu.make_async_copy(src, dst, sems.at[k, i]) for i, (src, dst) in enumerate(pairs)])
@@ -147,7 +146,7 @@
         for copy in copies[k]:
             copy.wait()
         if k == steps - 1 and selected:
-            leaving = column_copies(groups, counts, place_ref, x_ref, shard, x_ref, selected, out_sems)
+            leaving = column_copies(groups, counts, place_ref, x_ref, rows, x_ref, rows, selected, out_sems)
         for acc, w_ref in ((acc_k, wk_ref), (acc_v, wv_ref)):
             share = jnp.dot(x_ref[:, part], w_ref[part, :], preferred_element_type=F32)
             if k:
@@ -155,8 +154,8 @@
             else:
                 acc[...] = share
     for place, raw_ref, both_ref in (
-        (slice(0, shard), p_raw, p_both),
-        (slice(shard, shard + rows), r_raw, r_both),
+        (slice(rows, rows + shard), p_raw, p_both),
+        (slice(0, rows), r_raw, r_both),
     ):
         both_ref[:, width:] = acc_v[place, :].astype(BF16)
         raw_ref[...] = acc_k[place, :]
@@ -389,7 +388,7 @@
     out_ref[columns:, :] = jnp.broadcast_to(exponent, (MARK, out_ref.shape[1]))
 
 
-def weight_shares(states, grads, tokens):
+def weight_shares(states, grads, tokens, after):
     parts = len(states)
     rows, depth = states[0][0].shape
     columns = grads[0].shape[0]
@@ -403,22 +402,24 @@
             else pl.BlockSpec((None, rows, step), lambda j, index=index: (index, 0, j))
             for _, index in states
         ]
-        + [pl.BlockSpec(x.shape, lambda j: (0, 0)) for x in (*grads, *tokens)],
+        + [pl.BlockSpec(x.shape, lambda j: (0, 0)) for x in (*grads, *tokens)]
+        + [pl.BlockSpec(memory_space=pl.ANY)] * len(after),
         out_specs=pl.BlockSpec((columns + MARK, step), lambda j: (0, j)),
         out_shape=jax.ShapeDtypeStruct((columns + MARK, depth), F32),
         scratch_shapes=[pltpu.VMEM((8, HEAD_DIM), F32), pltpu.VMEM((columns, parts * grads[0].shape[1]), BF16)],
         compiler_params=pltpu.CompilerParams(vmem_limit_bytes=VMEM),
         cost_estimate=FREE,
         name="weight_shares",
-    )(*[array for array, _ in states], *grads, *tokens)
+    )(*[array for array, _ in states], *grads, *tokens, *after)
 
 
 def rows_kernel(first, place_ref, sums_ref, raw_ref, cos_ref, sin_ref, *refs):
     out_ref = refs[-1]
     sub = sums_ref.shape[1]
     own = pl.ds(pl.multiple_of(place_ref[3] * sub, sub), sub)
-    cosine = cos_ref[own, :]
-    sine = sin_ref[own, :]
+    turn = pl.ds(pl.multiple_of(cos_ref.shape[0] - raw_ref.shape[0] + place_ref[3] * sub, sub), sub)
+    cosine = cos_ref[turn, :]
+    sine = sin_ref[turn, :]
     for head in range(out_ref.shape[1] // (2 * HEAD_DIM)):
         start = 2 * head * HEAD_DIM
         both = jnp.sum(sums_ref[:, :, start : start + 2 * HEAD_DIM], axis=0)
@@ -506,15 +507,15 @@
     coef = advantage / length.astype(F32)
     ints = jnp.stack([length[0], prompt.astype(jnp.int32)])
 
-    prompt_cos, prompt_sin = rotary_tables(prompt * shard + jnp.arange(shard, dtype=jnp.int32))
-    own_cos, own_sin = rotary_tables(prompt_len + jnp.arange(rows, dtype=jnp.int32))
+    line = jnp.arange(rows + shard, dtype=jnp.int32)
+    cosine, sine = rotary_tables(jnp.where(line < rows, prompt_len + line, prompt * shard + line - rows))
     (prompt_raw, mine, own_raw, own_both), parts = project(
         own_prompt,
         states,
         key_weight,
         value_weight,
-        jnp.concatenate([prompt_cos, own_cos]),
-        jnp.concatenate([prompt_sin, own_sin]),
+        cosine,
+        sine,
         place,
         groups[:1],
         counts,
@@ -527,7 +528,7 @@
     def run(first, per, chunk_first, chunk_heads, grads, sums, after):
         grads, sums, own_g = attend(
             first, per, first - chunk_first, chunk_heads, coef, ints, queries[0, 0], grad_output[0, 0],
-            prompt_both, own_both, own_raw, own_cos, own_sin, [grads, sums], after,
+            prompt_both, own_both, own_raw, cosine, sine, [grads, sums], after,
         )
         return grads, sums, own_g.reshape(-1, rows)
 
@@ -540,9 +541,9 @@
 
     def row_tokens(sums, chunk_first, after):
         sums = everyone(sums.reshape(n_prompt * n_resp, sub, -1), ("chip", "core", "resp"))
-        own = row_grads(chunk_first, place, sums, prompt_raw, prompt_cos, prompt_sin, after)
+        own = row_grads(chunk_first, place, sums, prompt_raw, cosine, sine, after)
         held = jnp.concatenate([own] + [exchange(own, [("core", c)]) for c in range(1, n_core)])
-        return [held] + [exchange(held, [("grp", e)]) for e in range(1, n_grp)]
+        return [held] + across(held), own
 
     wide = n_resp * block
 
@@ -577,11 +578,13 @@
     hops_early = [tied(x, g_late) for x in hops_early]
     g_late = tied(g_late, *hops_early)
     sums_late = tied(sums_late, *hops_early)
+    tokens_early, _ = row_tokens(sums_early, 0, [g_late])
+    g_late = tied(g_late, *tokens_early[1:])
     hops_late = across(g_late)
-    tokens = row_tokens(sums_early, 0, [g_late])
-    shares_early = weight_shares(parts, everywhere(g_early, hops_early), tokens)
-    tokens = row_tokens(sums_late, early, [])
-    shares_late = weight_shares(parts, everywhere(g_late, hops_late), tokens)
+    tokens_late, own_late = row_tokens(sums_late, early, [])
+    shares_early = weight_shares(parts, everywhere(g_early, hops_early), tokens_early, [own_late])
+    hops_late = [tied(x, shares_early) for x in hops_late]
+    shares_late = weight_shares(parts, everywhere(g_late, hops_late), tokens_late, [])
     sent_early = chip_terms(shares_early)
     sent_late = chip_terms(shares_late)
     half_early, pieces_early = resp_terms(shares_early[:, :wide], sent_early)

time: 175 us -> 174 us (level)
  Pallas kernels: 62.7 us -> 51 us
  waiting for transfers between devices: 44.7 us -> 54.1 us
    pallas_call x2, Pallas kernels: 28.3 us -> 16 us  [attend(): pl.pallas_call(functools.partial(attend_kernel, parts, fold), grid=(per,)...]
    all_to_all x3, waiting for transfers between devices: 5.21 us -> 11.6 us  [everyone(): return lax.all_to_all(value, names, split_axis=0, concat_axis=0, tiled=True)]
    ppermute x26, waiting for transfers between devices: 39.5 us -> 42.5 us  [exchange(): return lax.ppermute(value, names, [(j, j ^ mask) for j in range(total)])]
    unnamed x41 -> x43, local copies, waits for them, and re-layouts: 7.53 us -> 8.35 us
  transfers between devices with their start and end apart: 29 -> 29, of which waited for: 12 -> 15; matrix products, arithmetic and copies ran while one was open for 4% -> 4% of each run, Pallas kernels for 33% -> 27%
where the time goes in v5:
time: 174 us; the launch traced here: 173 us
  waiting for transfers between devices  54.1 us (31%)
  Pallas kernels  51 us (29%)
  starting transfers between devices  42.4 us (24%)
  local copies, waits for them, and re-layouts  11.1 us (6%)
  other arithmetic  10.1 us (6%)
  between operations  4.19 us (2%)
    ppermute x26, waiting for transfers between devices, exchange(): return lax.ppermute(value, names, [(j, j ^ mask) for j in range(total)])  42.5 us
    ppermute x26, starting transfers between devices, exchange(): return lax.ppermute(value, names, [(j, j ^ mask) for j in range(total)])  22.3 us
    all_to_all x3, starting transfers between devices, everyone(): return lax.all_to_all(value, names, split_axis=0, concat_axis=0, tiled=True)  20.1 us
    pallas_call x2, Pallas kernels, attend(): pl.pallas_call(functools.partial(attend_kernel, parts, fold), grid=(per,)...  16 us
    pallas_call x2, Pallas kernels, weight_shares(): pl.pallas_call(functools.partial(weight_kernel, parts, len(tokens)), grid...  14.7 us
    pallas_call x1, Pallas kernels, project(): pl.pallas_call(functools.partial(project_kernel, groups, counts), in_spec...  11.9 us
    all_to_all x3, waiting for transfers between devices, everyone(): return lax.all_to_all(value, names, split_axis=0, concat_axis=0, tiled=True)  11.6 us
    unnamed x43, local copies, waits for them, and re-layouts  8.35 us
  transfers between devices with their start and end apart: 29, of which 15 were waited for; matrix products, arithmetic and copies ran while one was open for 4% of the time, Pallas kernels for 27%

profile of v5, /device:TPU:0, one launch (start us, length us, event | category | flops | bytes accessed | tf_op | source)
XLA Modules:
  0.0 172.9 jit_solution(5467426411327513161)
XLA Ops:
  0.6 0.7 pad_add_fusion.1.place_ref
  1.3 4.3 %select_columns.1 = (bf16[528,1024]{1,0:T(8,128)(2,1)}, bf16[2,528,1024]{2,1,0:T(8,128)(2,1)}) custom-call(s32[4]{0:T(128)} %pad_add_fusion.1.place_ref, bf16[512,4096]{1,0:T(8,128)(2,1)} %bitcast.54, bf16[64,4096]{1,0:T(8,128)(2,1)} %bitcast.63), custom_call_target="tpu_custom_call" | custom-call | flops 1 | bytes 1 | tf_op jit(solution)/shard_map/select_columns/pallas_call | solution.py:104
  5.6 3.0 %collective-permute-start.4 = (bf16[2,528,1024]{2,1,0:T(8,128)(2,1)}, bf16[2,528,1024]{2,1,0:T(8,128)(2,1)S(1)}, u32[]{:S(2)}, u32[]{:S(2)}) collective-permute-start(bf16[2,528,1024]{2,1,0:T(8,128)(2,1)} %get-tuple-element.17.after_ref), channel_id=1, source_target_pairs={{0,16},{16,0},{1,17},{17,1},{2,18},{18,2},{3,19},{19,3},{4,20},{20... | collective-permute-start | bytes 6488072 | tf_op jit(solution)/shard_map/ppermute | solution.py:36
  8.6 2.0 %fusion.5 = (f32[576,128]{1,0:T(8,128)}, f32[576,128]{1,0:T(8,128)}) fusion(f32[128]{0:T(128)S(1)} %get-tuple-element.59, f32[128]{0:T(128)S(1)} %get-tuple-element.60, f32[576]{0:T(1024)S(1)} %select_convert_fusion), kind=kLoop, calls=%fused_computation.27 | loop fusion | flops 147456 | bytes 593152 | tf_op jit(solution)/shard_map/mul | solution.py:46
  10.6 11.9 %project.1 = (f32[64,512]{1,0:T(8,128)}, bf16[64,1024]{1,0:T(8,128)(2,1)}, f32[512,512]{1,0:T(8,128)}, bf16[512,1024]{1,0:T(8,128)(2,1)}, bf16[528,1024]{1,0:T(8,128)(2,1)}) custom-call(s32[4]{0:T(128)} %pad_add_fusion.1.place_ref, bf16[64,4096]{1,0:T(8,128)(2,1)} %bitcast.64, bf16[512,4096]{1,0:T(8,128)(2,1)} %bitcast.55, bf16[4096,512]{1,0:T(8,128)(2,1)} %wk_hbm.1, ...), custom_call_target="tpu_custom_call" | custom-call | flops 1 | bytes 1 | tf_op jit(solution)/shard_map/project/pallas_call | solution.py:184
  22.5 1.6 collective-permute-start.1
  25.8 0.6 broadcast_in_dim.20
  26.4 5.9 %all-to-all-start = ((f32[16,3,8]{2,1,0:T(4,128)}), f32[16,3,8]{2,1,0:T(4,128)S(1)}, u32[]{:S(2)}, u32[]{:S(2)}) async-start(f32[16,3,8]{2,1,0:T(4,128)} %broadcast_in_dim.20), calls=%async_computation | async-start | bytes 65536 | tf_op jit(solution)/shard_map/all_to_all | solution.py:355
  33.0 0.6 pad_add_fusion.ints_ref
  33.6 5.2 %all-to-all-done = f32[16,3,8]{2,1,0:T(4,128)S(1)} async-done(((f32[16,3,8]{2,1,0:T(4,128)}), f32[16,3,8]{2,1,0:T(4,128)S(1)}, u32[]{:S(2)}, u32[]{:S(2)}) %all-to-all-start) | async-done | bytes 1568 | tf_op jit(solution)/shard_map/all_to_all | solution.py:355
  38.9 0.6 select_reduce_fusion
  40.8 0.6 copy-done.6
  41.5 8.0 %attend.2 = (bf16[512,2048]{1,0:T(8,128)(2,1)}, f32[256,512]{1,0:T(8,128)}, bf16[2,2,128,512]{3,2,1,0:T(8,128)(2,1)}) custom-call(f32[1]{0:T(128)S(6)} %div.21.coef_ref, s32[2]{0:T(128)} %pad_add_fusion.ints_ref, bf16[512,2048]{1,0:T(8,128)(2,1)} %bitcast.58, bf16[512,2048]{1,0:T(8,128)(2,1)} %bitcast.60, ...), custom_call_target="tpu_custom_call" | custom-call | flops 1 | bytes 1 | tf_op jit(solution)/shard_map/attend/pallas_call | solution.py:326
  49.5 6.3 %collective-permute-done.4.refs_0_ = bf16[2,528,1024]{2,1,0:T(8,128)(2,1)S(1)} collective-permute-done((bf16[2,528,1024]{2,1,0:T(8,128)(2,1)}, bf16[2,528,1024]{2,1,0:T(8,128)(2,1)S(1)}, u32[]{:S(2)}, u32[]{:S(2)}) %collective-permute-start.4) | collective-permute-done | bytes 2162720 | tf_op jit(solution)/shard_map/ppermute | solution.py:36
  55.8 1.4 copy-done
  57.3 0.5 collective-permute-start.3
  57.8 6.2 %all-to-all-start.1 = ((f32[16,16,512]{2,1,0:T(8,128)}), f32[16,16,512]{2,1,0:T(8,128)S(1)}, u32[]{:S(2)}, u32[]{:S(2)}) async-start(f32[16,16,512]{2,1,0:T(8,128)} %bitcast.19), calls=%async_computation.1 | async-start | bytes 1048576 | tf_op jit(solution)/shard_map/all_to_all | solution.py:355
  64.0 1.6 collective-permute-start.7
  65.5 1.0 copy-done.2
  66.6 8.0 %attend.3 = (bf16[512,2048]{1,0:T(8,128)(2,1)}, f32[256,512]{1,0:T(8,128)}, bf16[2,2,128,512]{3,2,1,0:T(8,128)(2,1)}) custom-call(f32[1]{0:T(128)S(6)} %div.21.coef_ref, s32[2]{0:T(128)} %pad_add_fusion.ints_ref, bf16[512,2048]{1,0:T(8,128)(2,1)} %bitcast.59, bf16[512,2048]{1,0:T(8,128)(2,1)} %bitcast.61, ...), custom_call_target="tpu_custom_call", output_to_operand_aliasing={{0}: (17, {})} | custom-call | flops 1 | bytes 1 | tf_op jit(solution)/shard_map/attend/pallas_call | solution.py:326
  74.6 3.7 %collective-permute-done.7.refs_0_ = bf16[512,512]{1,0:T(8,128)(2,1)S(1)} collective-permute-done((bf16[512,512]{1,0:T(8,128)(2,1)S(1)}, bf16[512,512]{1,0:T(8,128)(2,1)S(1)}, u32[]{:S(2)}, u32[]{:S(2)}) %collective-permute-start.7) | collective-permute-done | bytes 524320 | tf_op jit(solution)/shard_map/ppermute | solution.py:36
  78.3 0.8 copy-done.4
  79.1 0.5 all-to-all-done.1.sums_ref
  79.7 8.0 %all-to-all-start.2 = ((f32[16,16,512]{2,1,0:T(8,128)}), f32[16,16,512]{2,1,0:T(8,128)S(1)}, u32[]{:S(2)}, u32[]{:S(2)}) async-start(f32[16,16,512]{2,1,0:T(8,128)} %bitcast.65), calls=%async_computation.2 | async-start | bytes 1048576 | tf_op jit(solution)/shard_map/all_to_all | solution.py:355
  88.3 2.1 %row_grads.2 = bf16[16,512]{1,0:T(8,128)(2,1)} custom-call(s32[4]{0:T(128)} %pad_add_fusion.1.place_ref, f32[16,16,512]{2,1,0:T(8,128)} %copy-done.10, f32[64,512]{1,0:T(8,128)} %get-tuple-element.28.raw_ref, f32[576,128]{1,0:T(8,128)} %get-tuple-element.52.cos_ref.refs_11_, f32[576,128]{1,0:T(8,128)} %get-tuple-element.51.sin_ref.refs_12_, ...), custom_call_target="tpu_custom_call" | custom-call | flops 1 | bytes 1 | tf_op jit(solution)/shard_map/row_grads/pallas_call | solution.py:437
  90.7 1.0 collective-permute-done.9
  91.7 0.7 pad_maximum_fusion.2.refs_8_
  92.4 0.5 collective-permute-start.10
  93.0 3.4 %collective-permute-done.10.refs_9_.refs_1_ = bf16[32,512]{1,0:T(8,128)(2,1)S(1)} collective-permute-done((bf16[32,512]{1,0:T(8,128)(2,1)S(1)}, bf16[32,512]{1,0:T(8,128)(2,1)S(1)}, u32[]{:S(2)}, u32[]{:S(2)}) %collective-permute-start.10) | collective-permute-done | bytes 32800 | tf_op jit(solution)/shard_map/ppermute | solution.py:36
  96.4 0.6 copy-done.17
  97.0 0.5 collective-permute-start.16
  97.5 5.8 %all-to-all-done.2.sums_ref = f32[16,16,512]{2,1,0:T(8,128)S(1)} async-done(((f32[16,16,512]{2,1,0:T(8,128)}), f32[16,16,512]{2,1,0:T(8,128)S(1)}, u32[]{:S(2)}, u32[]{:S(2)}) %all-to-all-start.2) | async-done | bytes 524320 | tf_op jit(solution)/shard_map/all_to_all | solution.py:355
  103.4 0.8 copy-done.9
  104.2 2.1 %row_grads.3.refs_10_ = bf16[16,512]{1,0:T(8,128)(2,1)} custom-call(s32[4]{0:T(128)} %pad_add_fusion.1.place_ref, f32[16,16,512]{2,1,0:T(8,128)} %copy-done.9, f32[64,512]{1,0:T(8,128)} %get-tuple-element.28.raw_ref, f32[576,128]{1,0:T(8,128)} %get-tuple-element.52.cos_ref.refs_11_, f32[576,128]{1,0:T(8,128)} %get-tuple-element.51.sin_ref.refs_12_), custom_call_target="tpu_custom_call" | custom-call | flops 1 | bytes 1 | tf_op jit(solution)/shard_map/row_grads/pallas_call | solution.py:437
  106.3 0.8 copy-done.15
  107.0 7.4 %weight_shares.2.refs_1_ = f32[528,1024]{1,0:T(8,128)} custom-call(bf16[528,1024]{1,0:T(8,128)(2,1)} %get-tuple-element.25.refs_0_, bf16[528,1024]{1,0:T(8,128)(2,1)} %copy-done.2, bf16[2,528,1024]{2,1,0:T(8,128)(2,1)} %tied.6.refs_15_.refs_2_, bf16[2,528,1024]{2,1,0:T(8,128)(2,1)} %collective-permute-done.5.refs_3_, bf16[512,512]{1,0:T(8,128)(2,1)} %bitcast.71, ...), custom_call_target="tpu_custom_call" | custom-call | flops 1 | bytes 1 | tf_op jit(solution)/shard_map/weight_shares/pallas_call | solution.py:396
  114.4 1.4 slice_convert_fusion.1
  115.8 0.6 collective-permute-start.11
  116.4 0.8 copy-done.12
  117.2 0.5 collective-permute-start.17
  117.7 1.4 collective-permute-done.18
  119.2 0.5 collective-permute-start.19
  119.7 3.4 %collective-permute-done.19.refs_9_ = bf16[32,512]{1,0:T(8,128)(2,1)S(1)} collective-permute-done((bf16[32,512]{1,0:T(8,128)(2,1)S(1)}, bf16[32,512]{1,0:T(8,128)(2,1)S(1)}, u32[]{:S(2)}, u32[]{:S(2)}) %collective-permute-start.19) | collective-permute-done | bytes 32800 | tf_op jit(solution)/shard_map/ppermute | solution.py:36
  123.1 0.6 copy-done.20
  123.7 0.8 copy-done.14
  124.5 7.3 %weight_shares.3 = f32[528,1024]{1,0:T(8,128)} custom-call(bf16[528,1024]{1,0:T(8,128)(2,1)} %get-tuple-element.25.refs_0_, bf16[528,1024]{1,0:T(8,128)(2,1)} %copy-done.2, bf16[2,528,1024]{2,1,0:T(8,128)(2,1)} %tied.6.refs_15_.refs_2_, bf16[2,528,1024]{2,1,0:T(8,128)(2,1)} %collective-permute-done.5.refs_3_, bf16[512,512]{1,0:T(8,128)(2,1)} %tied.10.refs_4_, ...), custom_call_target="tpu_custom_call" | custom-call | flops 1 | bytes 1 | tf_op jit(solution)/shard_map/weight_shares/pallas_call | solution.py:396
  131.8 0.9 multiply_exponential_fusion.3
  132.7 0.7 multiply_exponential_fusion.5
  133.4 1.4 fusion.52
  135.0 2.0 %collective-permute-start.14 = (f16[528,128]{1,0:T(8,128)(2,1)S(1)}, f16[528,128]{1,0:T(8,128)(2,1)S(1)}, u32[]{:S(2)}, u32[]{:S(2)}) collective-permute-start(f16[528,128]{1,0:T(8,128)(2,1)S(1)} %get-tuple-element.50), channel_id=1, source_target_pairs={{0,3},{1,2},{2,1},{3,0},{4,7},{5,6},{6,5},{7,4},{8,11},{9,10},{10,... | collective-permute-start | bytes 405512 | tf_op jit(solution)/shard_map/ppermute | solution.py:36
  137.2 0.4 collective-permute-start.20
  138.0 3.1 %collective-permute-start.12 = (f16[528,128]{1,0:T(8,128)(2,1)S(1)}, f16[528,128]{1,0:T(8,128)(2,1)S(1)}, u32[]{:S(2)}, u32[]{:S(2)}) collective-permute-start(f16[528,128]{1,0:T(8,128)(2,1)S(1)} %get-tuple-element.48), channel_id=1, source_target_pairs={{0,1},{1,0},{2,3},{3,2},{4,5},{5,4},{6,7},{7,6},{8,9},{9,8},{10,11... | collective-permute-start | bytes 405512 | tf_op jit(solution)/shard_map/ppermute | solution.py:36
  141.2 2.3 %collective-permute-done.14 = f16[528,128]{1,0:T(8,128)(2,1)S(1)} collective-permute-done((f16[528,128]{1,0:T(8,128)(2,1)S(1)}, f16[528,128]{1,0:T(8,128)(2,1)S(1)}, u32[]{:S(2)}, u32[]{:S(2)}) %collective-permute-start.14) | collective-permute-done | bytes 135200 | tf_op jit(solution)/shard_map/ppermute | solution.py:36
  143.4 5.4 %collective-permute-done.13 = f16[528,128]{1,0:T(8,128)(2,1)S(1)} collective-permute-done((f16[528,128]{1,0:T(8,128)(2,1)S(1)}, f16[528,128]{1,0:T(8,128)(2,1)S(1)}, u32[]{:S(2)}, u32[]{:S(2)}) %collective-permute-start.13) | collective-permute-done | bytes 135200 | tf_op jit(solution)/shard_map/ppermute | solution.py:36
  149.0 1.4 collective-permute-done.20
  150.9 1.9 %collective-permute-start.23 = (f16[528,128]{1,0:T(8,128)(2,1)S(1)}, f16[528,128]{1,0:T(8,128)(2,1)S(1)}, u32[]{:S(2)}, u32[]{:S(2)}) collective-permute-start(f16[528,128]{1,0:T(8,128)(2,1)S(1)} %get-tuple-element.47), channel_id=1, source_target_pairs={{0,3},{1,2},{2,1},{3,0},{4,7},{5,6},{6,5},{7,4},{8,11},{9,10},{10,... | collective-permute-start | bytes 405512 | tf_op jit(solution)/shard_map/ppermute | solution.py:36
  152.8 0.5 collective-permute-start.24
  153.3 2.5 %collective-permute-start.21 = (f16[528,128]{1,0:T(8,128)(2,1)S(1)}, f16[528,128]{1,0:T(8,128)(2,1)S(1)}, u32[]{:S(2)}, u32[]{:S(2)}) collective-permute-start(f16[528,128]{1,0:T(8,128)(2,1)S(1)} %get-tuple-element.45), channel_id=1, source_target_pairs={{0,1},{1,0},{2,3},{3,2},{4,5},{5,4},{6,7},{7,6},{8,9},{9,8},{10,11... | collective-permute-start | bytes 405512 | tf_op jit(solution)/shard_map/ppermute | solution.py:36
  155.9 3.3 %collective-permute-done.23 = f16[528,128]{1,0:T(8,128)(2,1)S(1)} collective-permute-done((f16[528,128]{1,0:T(8,128)(2,1)S(1)}, f16[528,128]{1,0:T(8,128)(2,1)S(1)}, u32[]{:S(2)}, u32[]{:S(2)}) %collective-permute-start.23) | collective-permute-done | bytes 135200 | tf_op jit(solution)/shard_map/ppermute | solution.py:36
  159.2 3.8 %collective-permute-done.22 = f16[528,128]{1,0:T(8,128)(2,1)S(1)} collective-permute-done((f16[528,128]{1,0:T(8,128)(2,1)S(1)}, f16[528,128]{1,0:T(8,128)(2,1)S(1)}, u32[]{:S(2)}, u32[]{:S(2)}) %collective-permute-start.22) | collective-permute-done | bytes 135200 | tf_op jit(solution)/shard_map/ppermute | solution.py:36
  163.2 0.6 collective-permute-start.25
  163.8 6.9 %collective-permute-done.25 = f32[512,128]{1,0:T(8,128)S(1)} collective-permute-done((f32[512,128]{1,0:T(8,128)S(1)}, f32[512,128]{1,0:T(8,128)S(1)}, u32[]{:S(2)}, u32[]{:S(2)}) %collective-permute-start.25) | collective-permute-done | bytes 262176 | tf_op jit(solution)/shard_map/ppermute | solution.py:36
  170.9 1.0 copy.26
  171.9 1.0 copy.27
  (93 shorter events, 3.2 us)
Async XLA Ops:
  5.6 50.2 %collective-permute-start.4 = (bf16[2,528,1024]{2,1,0:T(8,128)(2,1)}, bf16[2,528,1024]{2,1,0:T(8,128)(2,1)S(1)}, u32[]{:S(2)}, u32[]{:S(2)}) collective-permute-start(bf16[2,528,1024]{2,1,0:T(8,128)(2,1)} %get-tuple-element.17.after_ref), channel_id=1, source_target_pairs={{0,16},{16,0},{1,17},{17,1},{2,18},{18,2},{3,19},{19,3},{4,20},{20... | collective-permute-start | bytes 6488072 | tf_op jit(solution)/shard_map/ppermute | solution.py:36
  22.5 18.3 %collective-permute-start = (bf16[64,1024]{1,0:T(8,128)(2,1)}, bf16[64,1024]{1,0:T(8,128)(2,1)S(1)}, u32[]{:S(2)}, u32[]{:S(2)}) collective-permute-start(bf16[64,1024]{1,0:T(8,128)(2,1)} %get-tuple-element.18.refs_0_.refs_4_), channel_id=1, source_target_pairs={{0,4},{4,0},{1,5},{5,1},{2,6},{6,2},{3,7},{7,3},{8,12},{12,8},{9,1... | collective-permute-start | bytes 393224 | tf_op jit(solution)/shard_map/ppermute | solution.py:36
  22.5 18.2 %collective-permute-start.1 = (bf16[64,1024]{1,0:T(8,128)(2,1)}, bf16[64,1024]{1,0:T(8,128)(2,1)S(1)}, u32[]{:S(2)}, u32[]{:S(2)}) collective-permute-start(bf16[64,1024]{1,0:T(8,128)(2,1)} %get-tuple-element.18.refs_0_.refs_4_), channel_id=1, source_target_pairs={{0,8},{8,0},{1,9},{9,1},{2,10},{10,2},{3,11},{11,3},{4,12},{12,4},... | collective-permute-start | bytes 393224 | tf_op jit(solution)/shard_map/ppermute | solution.py:36
  24.1 16.7 %collective-permute-start.2 = (bf16[64,1024]{1,0:T(8,128)(2,1)}, bf16[64,1024]{1,0:T(8,128)(2,1)S(1)}, u32[]{:S(2)}, u32[]{:S(2)}) collective-permute-start(bf16[64,1024]{1,0:T(8,128)(2,1)} %get-tuple-element.18.refs_0_.refs_4_), channel_id=1, source_target_pairs={{0,12},{4,8},{8,4},{12,0},{1,13},{5,9},{9,5},{13,1},{2,14},{6,10},... | collective-permute-start | bytes 393224 | tf_op jit(solution)/shard_map/ppermute | solution.py:36
  26.4 12.4 %all-to-all-start = ((f32[16,3,8]{2,1,0:T(4,128)}), f32[16,3,8]{2,1,0:T(4,128)S(1)}, u32[]{:S(2)}, u32[]{:S(2)}) async-start(f32[16,3,8]{2,1,0:T(4,128)} %broadcast_in_dim.20), calls=%async_computation | async-start | bytes 65536 | tf_op jit(solution)/shard_map/all_to_all | solution.py:355
  40.8 0.7 copy-start.6
  40.8 0.7 copy-start.7
  40.8 0.7 copy-start.8
  55.8 1.4 copy-start
  57.3 6.7 %copy-start.11 = (bf16[2,2,128,512]{3,2,1,0:T(8,128)(2,1)S(1)}, bf16[2,2,128,512]{3,2,1,0:T(8,128)(2,1)}, u32[]{:S(2)}) copy-start(bf16[2,2,128,512]{3,2,1,0:T(8,128)(2,1)} %get-tuple-element.23) | copy-start | bytes 1572868
  57.3 49.0 %collective-permute-start.5 = (bf16[2,528,1024]{2,1,0:T(8,128)(2,1)}, bf16[2,528,1024]{2,1,0:T(8,128)(2,1)}, u32[]{:S(2)}, u32[]{:S(2)}) collective-permute-start(bf16[2,528,1024]{2,1,0:T(8,128)(2,1)} %tied.6.refs_15_.refs_2_), channel_id=1, source_target_pairs={{0,4},{4,0},{1,5},{5,1},{2,6},{6,2},{3,7},{7,3},{8,12},{12,8},{9,1... | collective-permute-start | bytes 6488072 | tf_op jit(solution)/shard_map/ppermute | solution.py:36
  57.3 8.3 %collective-permute-start.3 = (bf16[528,1024]{1,0:T(8,128)(2,1)}, bf16[528,1024]{1,0:T(8,128)(2,1)S(1)}, u32[]{:S(2)}, u32[]{:S(2)}) collective-permute-start(bf16[528,1024]{1,0:T(8,128)(2,1)} %get-tuple-element.22), channel_id=1, source_target_pairs={{0,4},{4,0},{1,5},{5,1},{2,6},{6,2},{3,7},{7,3},{8,12},{12,8},{9,1... | collective-permute-start | bytes 3244040 | tf_op jit(solution)/shard_map/ppermute | solution.py:36
  57.8 21.9 %all-to-all-start.1 = ((f32[16,16,512]{2,1,0:T(8,128)}), f32[16,16,512]{2,1,0:T(8,128)S(1)}, u32[]{:S(2)}, u32[]{:S(2)}) async-start(f32[16,16,512]{2,1,0:T(8,128)} %bitcast.19), calls=%async_computation.1 | async-start | bytes 1048576 | tf_op jit(solution)/shard_map/all_to_all | solution.py:355
  64.0 14.3 %collective-permute-start.7 = (bf16[512,512]{1,0:T(8,128)(2,1)S(1)}, bf16[512,512]{1,0:T(8,128)(2,1)S(1)}, u32[]{:S(2)}, u32[]{:S(2)}) collective-permute-start(bf16[512,512]{1,0:T(8,128)(2,1)S(1)} %bitcast.72), channel_id=1, source_target_pairs={{0,16},{16,0},{1,17},{17,1},{2,18},{18,2},{3,19},{19,3},{4,20},{20... | collective-permute-start | bytes 1572872 | tf_op jit(solution)/shard_map/ppermute | solution.py:36
  65.5 1.0 copy-start.2
  78.3 0.8 copy-start.4
  79.1 9.0 %copy-start.5 = (bf16[512,512]{1,0:T(8,128)(2,1)S(1)}, bf16[512,512]{1,0:T(8,128)(2,1)}, u32[]{:S(2)}) copy-start(bf16[512,512]{1,0:T(8,128)(2,1)} %tied.7.refs_1_.refs_6_) | copy-start | bytes 1572868
  79.7 8.6 %copy-start.10 = (f32[16,16,512]{2,1,0:T(8,128)}, f32[16,16,512]{2,1,0:T(8,128)S(1)}, u32[]{:S(2)}) copy-start(f32[16,16,512]{2,1,0:T(8,128)S(1)} %all-to-all-done.1.sums_ref) | copy-start | bytes 1572868
  79.7 23.7 %all-to-all-start.2 = ((f32[16,16,512]{2,1,0:T(8,128)}), f32[16,16,512]{2,1,0:T(8,128)S(1)}, u32[]{:S(2)}, u32[]{:S(2)}) async-start(f32[16,16,512]{2,1,0:T(8,128)} %bitcast.65), calls=%async_computation.2 | async-start | bytes 1048576 | tf_op jit(solution)/shard_map/all_to_all | solution.py:355
  87.7 18.5 %collective-permute-start.6 = (bf16[512,512]{1,0:T(8,128)(2,1)S(1)}, bf16[512,512]{1,0:T(8,128)(2,1)S(1)}, u32[]{:S(2)}, u32[]{:S(2)}) collective-permute-start(bf16[512,512]{1,0:T(8,128)(2,1)S(1)} %bitcast.73), channel_id=1, source_target_pairs={{0,4},{4,0},{1,5},{5,1},{2,6},{6,2},{3,7},{7,3},{8,12},{12,8},{9,1... | collective-permute-start | bytes 1572872 | tf_op jit(solution)/shard_map/ppermute | solution.py:36
  88.1 18.1 %collective-permute-start.8 = (bf16[512,512]{1,0:T(8,128)(2,1)S(1)}, bf16[512,512]{1,0:T(8,128)(2,1)}, u32[]{:S(2)}, u32[]{:S(2)}) collective-permute-start(bf16[512,512]{1,0:T(8,128)(2,1)S(1)} %copy-done.5), channel_id=1, source_target_pairs={{0,4},{4,0},{1,5},{5,1},{2,6},{6,2},{3,7},{7,3},{8,12},{12,8},{9,1... | collective-permute-start | bytes 1572872 | tf_op jit(solution)/shard_map/ppermute | solution.py:36
  90.3 1.4 collective-permute-start.9
  92.4 13.8 %copy-start.19 = (bf16[32,512]{1,0:T(8,128)(2,1)}, bf16[32,512]{1,0:T(8,128)(2,1)S(1)}, u32[]{:S(2)}) copy-start(bf16[32,512]{1,0:T(8,128)(2,1)S(1)} %pad_maximum_fusion.2.refs_8_) | copy-start | bytes 98308
  92.4 3.9 %collective-permute-start.10 = (bf16[32,512]{1,0:T(8,128)(2,1)S(1)}, bf16[32,512]{1,0:T(8,128)(2,1)S(1)}, u32[]{:S(2)}, u32[]{:S(2)}) collective-permute-start(bf16[32,512]{1,0:T(8,128)(2,1)S(1)} %pad_maximum_fusion.2.refs_8_), channel_id=1, source_target_pairs={{0,16},{16,0},{1,17},{17,1},{2,18},{18,2},{3,19},{19,3},{4,20},{20... | collective-permute-start | bytes 98312 | tf_op jit(solution)/shard_map/ppermute | solution.py:36
  96.4 0.6 copy-start.17
  97.0 19.4 %collective-permute-start.16 = (bf16[512,512]{1,0:T(8,128)(2,1)}, bf16[512,512]{1,0:T(8,128)(2,1)S(1)}, u32[]{:S(2)}, u32[]{:S(2)}) collective-permute-start(bf16[512,512]{1,0:T(8,128)(2,1)} %tied.10.refs_4_), channel_id=1, source_target_pairs={{0,16},{16,0},{1,17},{17,1},{2,18},{18,2},{3,19},{19,3},{4,20},{20... | collective-permute-start | bytes 1572872 | tf_op jit(solution)/shard_map/ppermute | solution.py:36
  103.4 0.8 copy-start.9
  106.2 0.8 copy-start.15
  107.0 9.4 %copy-start.1 = (bf16[512,512]{1,0:T(8,128)(2,1)S(1)}, bf16[512,512]{1,0:T(8,128)(2,1)}, u32[]{:S(2)}) copy-start(bf16[512,512]{1,0:T(8,128)(2,1)} %tied.10.refs_4_) | copy-start | bytes 1572868
  114.4 3.3 %copy-start.16 = (bf16[16,512]{1,0:T(8,128)(2,1)S(1)}, bf16[16,512]{1,0:T(8,128)(2,1)}, u32[]{:S(2)}) copy-start(bf16[16,512]{1,0:T(8,128)(2,1)} %row_grads.3.refs_10_) | copy-start | bytes 49156
  115.8 16.0 %collective-permute-start.11 = (f16[528,512]{1,0:T(8,128)(2,1)S(1)}, f16[528,512]{1,0:T(8,128)(2,1)S(1)}, u32[]{:S(2)}, u32[]{:S(2)}) collective-permute-start(f16[528,512]{1,0:T(8,128)(2,1)S(1)} %slice_convert_fusion.1), channel_id=1, source_target_pairs={{0,8},{8,0},{1,9},{9,1},{2,10},{10,2},{3,11},{11,3},{4,12},{12,4},... | collective-permute-start | bytes 1622024 | tf_op jit(solution)/shard_map/ppermute | solution.py:36
  116.4 3.3 %collective-permute-start.15 = (bf16[512,512]{1,0:T(8,128)(2,1)S(1)}, bf16[512,512]{1,0:T(8,128)(2,1)S(1)}, u32[]{:S(2)}, u32[]{:S(2)}) collective-permute-start(bf16[512,512]{1,0:T(8,128)(2,1)S(1)} %copy-done.1), channel_id=1, source_target_pairs={{0,4},{4,0},{1,5},{5,1},{2,6},{6,2},{3,7},{7,3},{8,12},{12,8},{9,1... | collective-permute-start | bytes 1572872 | tf_op jit(solution)/shard_map/ppermute | solution.py:36
  116.4 0.8 copy-start.12
  117.2 5.9 %collective-permute-start.17 = (bf16[512,512]{1,0:T(8,128)(2,1)}, bf16[512,512]{1,0:T(8,128)(2,1)S(1)}, u32[]{:S(2)}, u32[]{:S(2)}) collective-permute-start(bf16[512,512]{1,0:T(8,128)(2,1)} %tied.11.refs_6_), channel_id=1, source_target_pairs={{0,4},{4,0},{1,5},{5,1},{2,6},{6,2},{3,7},{7,3},{8,12},{12,8},{9,1... | collective-permute-start | bytes 1572872 | tf_op jit(solution)/shard_map/ppermute | solution.py:36
  117.7 1.4 collective-permute-start.18
  119.2 3.9 %copy-start.18 = (bf16[32,512]{1,0:T(8,128)(2,1)}, bf16[32,512]{1,0:T(8,128)(2,1)S(1)}, u32[]{:S(2)}) copy-start(bf16[32,512]{1,0:T(8,128)(2,1)S(1)} %pad_maximum_fusion.3.refs_8_) | copy-start | bytes 98308
  119.2 3.9 %collective-permute-start.19 = (bf16[32,512]{1,0:T(8,128)(2,1)S(1)}, bf16[32,512]{1,0:T(8,128)(2,1)S(1)}, u32[]{:S(2)}, u32[]{:S(2)}) collective-permute-start(bf16[32,512]{1,0:T(8,128)(2,1)S(1)} %pad_maximum_fusion.3.refs_8_), channel_id=1, source_target_pairs={{0,16},{16,0},{1,17},{17,1},{2,18},{18,2},{3,19},{19,3},{4,20},{20... | collective-permute-start | bytes 98312 | tf_op jit(solution)/shard_map/ppermute | solution.py:36
  119.7 3.4 %copy-start.13 = (bf16[512,512]{1,0:T(8,128)(2,1)}, bf16[512,512]{1,0:T(8,128)(2,1)S(1)}, u32[]{:S(2)}) copy-start(bf16[512,512]{1,0:T(8,128)(2,1)S(1)} %collective-permute-done.15.refs_5_) | copy-start | bytes 1572868
  123.1 0.6 copy-start.20
  123.7 0.8 copy-start.14
  131.8 5.3 %copy-start.3 = (f32[528,1024]{1,0:T(8,128)S(1)}, f32[528,1024]{1,0:T(8,128)}, u32[]{:S(2)}) copy-start(f32[528,1024]{1,0:T(8,128)} %weight_shares.3) | copy-start | bytes 6488068
  135.0 8.4 %collective-permute-start.14 = (f16[528,128]{1,0:T(8,128)(2,1)S(1)}, f16[528,128]{1,0:T(8,128)(2,1)S(1)}, u32[]{:S(2)}, u32[]{:S(2)}) collective-permute-start(f16[528,128]{1,0:T(8,128)(2,1)S(1)} %get-tuple-element.50), channel_id=1, source_target_pairs={{0,3},{1,2},{2,1},{3,0},{4,7},{5,6},{6,5},{7,4},{8,11},{9,10},{10,... | collective-permute-start | bytes 405512 | tf_op jit(solution)/shard_map/ppermute | solution.py:36
  137.2 13.2 %collective-permute-start.20 = (f16[528,512]{1,0:T(8,128)(2,1)S(1)}, f16[528,512]{1,0:T(8,128)(2,1)S(1)}, u32[]{:S(2)}, u32[]{:S(2)}) collective-permute-start(f16[528,512]{1,0:T(8,128)(2,1)S(1)} %slice_convert_fusion), channel_id=1, source_target_pairs={{0,8},{8,0},{1,9},{9,1},{2,10},{10,2},{3,11},{11,3},{4,12},{12,4},... | collective-permute-start | bytes 1622024 | tf_op jit(solution)/shard_map/ppermute | solution.py:36
  137.6 11.3 %collective-permute-start.13 = (f16[528,128]{1,0:T(8,128)(2,1)S(1)}, f16[528,128]{1,0:T(8,128)(2,1)S(1)}, u32[]{:S(2)}, u32[]{:S(2)}) collective-permute-start(f16[528,128]{1,0:T(8,128)(2,1)S(1)} %get-tuple-element.49), channel_id=1, source_target_pairs={{0,2},{1,3},{2,0},{3,1},{4,6},{5,7},{6,4},{7,5},{8,10},{9,11},{10,... | collective-permute-start | bytes 405512 | tf_op jit(solution)/shard_map/ppermute | solution.py:36
  138.0 10.9 %collective-permute-start.12 = (f16[528,128]{1,0:T(8,128)(2,1)S(1)}, f16[528,128]{1,0:T(8,128)(2,1)S(1)}, u32[]{:S(2)}, u32[]{:S(2)}) collective-permute-start(f16[528,128]{1,0:T(8,128)(2,1)S(1)} %get-tuple-element.48), channel_id=1, source_target_pairs={{0,1},{1,0},{2,3},{3,2},{4,5},{5,4},{6,7},{7,6},{8,9},{9,8},{10,11... | collective-permute-start | bytes 405512 | tf_op jit(solution)/shard_map/ppermute | solution.py:36
  150.9 8.4 %collective-permute-start.23 = (f16[528,128]{1,0:T(8,128)(2,1)S(1)}, f16[528,128]{1,0:T(8,128)(2,1)S(1)}, u32[]{:S(2)}, u32[]{:S(2)}) collective-permute-start(f16[528,128]{1,0:T(8,128)(2,1)S(1)} %get-tuple-element.47), channel_id=1, source_target_pairs={{0,3},{1,2},{2,1},{3,0},{4,7},{5,6},{6,5},{7,4},{8,11},{9,10},{10,... | collective-permute-start | bytes 405512 | tf_op jit(solution)/shard_map/ppermute | solution.py:36
  152.8 11.0 %collective-permute-start.24 = (f32[512,128]{1,0:T(8,128)S(1)}, f32[512,128]{1,0:T(8,128)S(1)}, u32[]{:S(2)}, u32[]{:S(2)}) collective-permute-start(f32[512,128]{1,0:T(8,128)S(1)} %fusion.11), channel_id=1, source_target_pairs={{0,16},{16,0},{1,17},{17,1},{2,18},{18,2},{3,19},{19,3},{4,20},{20... | collective-permute-start | bytes 786440 | tf_op jit(solution)/shard_map/ppermute | solution.py:36
  153.3 9.8 %collective-permute-start.22 = (f16[528,128]{1,0:T(8,128)(2,1)S(1)}, f16[528,128]{1,0:T(8,128)(2,1)S(1)}, u32[]{:S(2)}, u32[]{:S(2)}) collective-permute-start(f16[528,128]{1,0:T(8,128)(2,1)S(1)} %get-tuple-element.46), channel_id=1, source_target_pairs={{0,2},{1,3},{2,0},{3,1},{4,6},{5,7},{6,4},{7,5},{8,10},{9,11},{10,... | collective-permute-start | bytes 405512 | tf_op jit(solution)/shard_map/ppermute | solution.py:36
  153.3 9.8 %collective-permute-start.21 = (f16[528,128]{1,0:T(8,128)(2,1)S(1)}, f16[528,128]{1,0:T(8,128)(2,1)S(1)}, u32[]{:S(2)}, u32[]{:S(2)}) collective-permute-start(f16[528,128]{1,0:T(8,128)(2,1)S(1)} %get-tuple-element.45), channel_id=1, source_target_pairs={{0,1},{1,0},{2,3},{3,2},{4,5},{5,4},{6,7},{7,6},{8,9},{9,8},{10,11... | collective-permute-start | bytes 405512 | tf_op jit(solution)/shard_map/ppermute | solution.py:36
  163.2 7.6 %collective-permute-start.25 = (f32[512,128]{1,0:T(8,128)S(1)}, f32[512,128]{1,0:T(8,128)S(1)}, u32[]{:S(2)}, u32[]{:S(2)}) collective-permute-start(f32[512,128]{1,0:T(8,128)S(1)} %fusion.8), channel_id=1, source_target_pairs={{0,16},{16,0},{1,17},{17,1},{2,18},{18,2},{3,19},{19,3},{4,20},{20... | collective-permute-start | bytes 786440 | tf_op jit(solution)/shard_map/ppermute | solution.py:36

commit v6 on v5

--- a/solution.py
+++ b/solution.py
@@ -388,7 +388,7 @@
     out_ref[columns:, :] = jnp.broadcast_to(exponent, (MARK, out_ref.shape[1]))
 
 
-def weight_shares(states, grads, tokens, after):
+def weight_shares(states, grads, tokens):
     parts = len(states)
     rows, depth = states[0][0].shape
     columns = grads[0].shape[0]
@@ -402,15 +402,14 @@
             else pl.BlockSpec((None, rows, step), lambda j, index=index: (index, 0, j))
             for _, index in states
         ]
-        + [pl.BlockSpec(x.shape, lambda j: (0, 0)) for x in (*grads, *tokens)]
-        + [pl.BlockSpec(memory_space=pl.ANY)] * len(after),
+        + [pl.BlockSpec(x.shape, lambda j: (0, 0)) for x in (*grads, *tokens)],
         out_specs=pl.BlockSpec((columns + MARK, step), lambda j: (0, j)),
         out_shape=jax.ShapeDtypeStruct((columns + MARK, depth), F32),
         scratch_shapes=[pltpu.VMEM((8, HEAD_DIM), F32), pltpu.VMEM((columns, parts * grads[0].shape[1]), BF16)],
         compiler_params=pltpu.CompilerParams(vmem_limit_bytes=VMEM),
         cost_estimate=FREE,
         name="weight_shares",
-    )(*[array for array, _ in states], *grads, *tokens, *after)
+    )(*[array for array, _ in states], *grads, *tokens)
 
 
 def rows_kernel(first, place_ref, sums_ref, raw_ref, cos_ref, sin_ref, *refs):
@@ -542,8 +541,7 @@
     def row_tokens(sums, chunk_first, after):
         sums = everyone(sums.reshape(n_prompt * n_resp, sub, -1), ("chip", "core", "resp"))
         own = row_grads(chunk_first, place, sums, prompt_raw, cosine, sine, after)
-        held = jnp.concatenate([own] + [exchange(own, [("core", c)]) for c in range(1, n_core)])
-        return [held] + across(held), own
+        return [exchange(own, [("grp", e), ("core", c)]) if e or c else own for e, c in groups]
 
     wide = n_resp * block
 
@@ -578,13 +576,13 @@
     hops_early = [tied(x, g_late) for x in hops_early]
     g_late = tied(g_late, *hops_early)
     sums_late = tied(sums_late, *hops_early)
-    tokens_early, _ = row_tokens(sums_early, 0, [g_late])
-    g_late = tied(g_late, *tokens_early[1:])
+    tokens_early = row_tokens(sums_early, 0, [g_late])
+    g_late = tied(g_late, *[token for token, (e, c) in zip(tokens_early, groups) if e])
     hops_late = across(g_late)
-    tokens_late, own_late = row_tokens(sums_late, early, [])
-    shares_early = weight_shares(parts, everywhere(g_early, hops_early), tokens_early, [own_late])
+    shares_early = weight_shares(parts, everywhere(g_early, hops_early), tokens_early)
     hops_late = [tied(x, shares_early) for x in hops_late]
-    shares_late = weight_shares(parts, everywhere(g_late, hops_late), tokens_late, [])
+    tokens_late = row_tokens(sums_late, early, [shares_early])
+    shares_late = weight_shares(parts, everywhere(g_late, hops_late), tokens_late)
     sent_early = chip_terms(shares_early)
     sent_late = chip_terms(shares_late)
     half_early, pieces_early = resp_terms(shares_early[:, :wide], sent_early)

time: 174 us -> 172 us (0.989)
  waiting for transfers between devices: 54.1 us -> 37.5 us
  Pallas kernels: 51 us -> 63.2 us
  starting transfers between devices: 42.4 us -> 44.7 us
    ppermute x26 -> x28, waiting for transfers between devices: 42.5 us -> 29.9 us  [exchange(): return lax.ppermute(value, names, [(j, j ^ mask) for j in range(total)])]
    pallas_call x2, Pallas kernels: 16 us -> 28.3 us  [attend(): pl.pallas_call(functools.partial(attend_kernel, parts, fold), grid=(per,)...]
    all_to_all x3, waiting for transfers between devices: 11.6 us -> 7.64 us  [everyone(): return lax.all_to_all(value, names, split_axis=0, concat_axis=0, tiled=True)]
    ppermute x26 -> x28, starting transfers between devices: 22.3 us -> 26.1 us  [exchange(): return lax.ppermute(value, names, [(j, j ^ mask) for j in range(total)])]
    unnamed x43 -> x45, local copies, waits for them, and re-layouts: 8.35 us -> 9.11 us
  transfers between devices with their start and end apart: 29 -> 31, of which waited for: 15 -> 14; matrix products, arithmetic and copies ran while one was open for 4% -> 3% of each run, Pallas kernels for 27% -> 34%
where the time goes in v6:
time: 172 us; the launch traced here: 171 us
  Pallas kernels  63.2 us (37%)
  starting transfers between devices  44.7 us (26%)
  waiting for transfers between devices  37.5 us (22%)
  local copies, waits for them, and re-layouts  11.9 us (7%)
  other arithmetic  9.31 us (5%)
  between operations  4.28 us (2%)
    ppermute x28, waiting for transfers between devices, exchange(): return lax.ppermute(value, names, [(j, j ^ mask) for j in range(total)])  29.9 us
    pallas_call x2, Pallas kernels, attend(): pl.pallas_call(functools.partial(attend_kernel, parts, fold), grid=(per,)...  28.3 us
    ppermute x28, starting transfers between devices, exchange(): return lax.ppermute(value, names, [(j, j ^ mask) for j in range(total)])  26.1 us
    all_to_all x3, starting transfers between devices, everyone(): return lax.all_to_all(value, names, split_axis=0, concat_axis=0, tiled=True)  18.6 us
    pallas_call x2, Pallas kernels, weight_shares(): pl.pallas_call(functools.partial(weight_kernel, parts, len(tokens)), grid...  14.7 us
    pallas_call x1, Pallas kernels, project(): pl.pallas_call(functools.partial(project_kernel, groups, counts), in_spec...  11.8 us
    unnamed x45, local copies, waits for them, and re-layouts  9.11 us
    all_to_all x3, waiting for transfers between devices, everyone(): return lax.all_to_all(value, names, split_axis=0, concat_axis=0, tiled=True)  7.64 us
  transfers between devices with their start and end apart: 31, of which 14 were waited for; matrix products, arithmetic and copies ran while one was open for 3% of the time, Pallas kernels for 34%

profile of v6, /device:TPU:0, one launch (start us, length us, event | category | flops | bytes accessed | tf_op | source)
XLA Modules:
  0.0 170.9 jit_solution(3459514962654830133)
XLA Ops:
  0.6 0.6 pad_add_fusion.1.place_ref
  1.3 4.3 %select_columns.1 = (bf16[528,1024]{1,0:T(8,128)(2,1)}, bf16[2,528,1024]{2,1,0:T(8,128)(2,1)}) custom-call(s32[4]{0:T(128)} %pad_add_fusion.1.place_ref, bf16[512,4096]{1,0:T(8,128)(2,1)} %bitcast.54, bf16[64,4096]{1,0:T(8,128)(2,1)} %bitcast.63), custom_call_target="tpu_custom_call" | custom-call | flops 1 | bytes 1 | tf_op jit(solution)/shard_map/select_columns/pallas_call | solution.py:104
  5.6 3.0 %collective-permute-start.4 = (bf16[2,528,1024]{2,1,0:T(8,128)(2,1)}, bf16[2,528,1024]{2,1,0:T(8,128)(2,1)S(1)}, u32[]{:S(2)}, u32[]{:S(2)}) collective-permute-start(bf16[2,528,1024]{2,1,0:T(8,128)(2,1)} %get-tuple-element.17.after_ref), channel_id=1, source_target_pairs={{0,16},{16,0},{1,17},{17,1},{2,18},{18,2},{3,19},{19,3},{4,20},{20... | collective-permute-start | bytes 6488072 | tf_op jit(solution)/shard_map/ppermute | solution.py:36
  8.6 2.0 %fusion.5 = (f32[576,128]{1,0:T(8,128)}, f32[576,128]{1,0:T(8,128)}) fusion(f32[128]{0:T(128)S(1)} %get-tuple-element.59, f32[128]{0:T(128)S(1)} %get-tuple-element.60, f32[576]{0:T(1024)S(1)} %select_convert_fusion), kind=kLoop, calls=%fused_computation.27 | loop fusion | flops 147456 | bytes 593152 | tf_op jit(solution)/shard_map/mul | solution.py:46
  10.5 11.8 %project.1 = (f32[64,512]{1,0:T(8,128)}, bf16[64,1024]{1,0:T(8,128)(2,1)}, f32[512,512]{1,0:T(8,128)}, bf16[512,1024]{1,0:T(8,128)(2,1)}, bf16[528,1024]{1,0:T(8,128)(2,1)}) custom-call(s32[4]{0:T(128)} %pad_add_fusion.1.place_ref, bf16[64,4096]{1,0:T(8,128)(2,1)} %bitcast.64, bf16[512,4096]{1,0:T(8,128)(2,1)} %bitcast.55, bf16[4096,512]{1,0:T(8,128)(2,1)} %wk_hbm.1, ...), custom_call_target="tpu_custom_call" | custom-call | flops 1 | bytes 1 | tf_op jit(solution)/shard_map/project/pallas_call | solution.py:184
  22.5 1.6 collective-permute-start.1
  25.7 0.6 broadcast_in_dim.20
  26.3 5.9 %all-to-all-start = ((f32[16,3,8]{2,1,0:T(4,128)}), f32[16,3,8]{2,1,0:T(4,128)S(1)}, u32[]{:S(2)}, u32[]{:S(2)}) async-start(f32[16,3,8]{2,1,0:T(4,128)} %broadcast_in_dim.20), calls=%async_computation | async-start | bytes 65536 | tf_op jit(solution)/shard_map/all_to_all | solution.py:355
  32.9 0.6 pad_add_fusion.ints_ref
  33.5 5.3 %all-to-all-done = f32[16,3,8]{2,1,0:T(4,128)S(1)} async-done(((f32[16,3,8]{2,1,0:T(4,128)}), f32[16,3,8]{2,1,0:T(4,128)S(1)}, u32[]{:S(2)}, u32[]{:S(2)}) %all-to-all-start) | async-done | bytes 1568 | tf_op jit(solution)/shard_map/all_to_all | solution.py:355
  38.8 0.6 select_reduce_fusion
  40.8 0.6 copy-done.5
  41.5 14.1 %attend.2 = (bf16[512,2048]{1,0:T(8,128)(2,1)}, f32[256,512]{1,0:T(8,128)}, bf16[2,2,128,512]{3,2,1,0:T(8,128)(2,1)}) custom-call(f32[1]{0:T(128)S(6)} %div.21.coef_ref, s32[2]{0:T(128)} %pad_add_fusion.ints_ref, bf16[512,2048]{1,0:T(8,128)(2,1)} %bitcast.58, bf16[512,2048]{1,0:T(8,128)(2,1)} %bitcast.60, ...), custom_call_target="tpu_custom_call" | custom-call | flops 1 | bytes 1 | tf_op jit(solution)/shard_map/attend/pallas_call | solution.py:326
  55.8 1.4 copy-done
  57.2 0.5 collective-permute-start.3
  57.7 6.2 %all-to-all-start.1 = ((f32[16,16,512]{2,1,0:T(8,128)}), f32[16,16,512]{2,1,0:T(8,128)S(1)}, u32[]{:S(2)}, u32[]{:S(2)}) async-start(f32[16,16,512]{2,1,0:T(8,128)} %bitcast.19), calls=%async_computation.1 | async-start | bytes 1048576 | tf_op jit(solution)/shard_map/all_to_all | solution.py:355
  64.0 1.6 collective-permute-start.7
  65.7 1.0 copy-done.2
  66.7 14.2 %attend.3 = (bf16[512,2048]{1,0:T(8,128)(2,1)}, f32[256,512]{1,0:T(8,128)}, bf16[2,2,128,512]{3,2,1,0:T(8,128)(2,1)}) custom-call(f32[1]{0:T(128)S(6)} %div.21.coef_ref, s32[2]{0:T(128)} %pad_add_fusion.ints_ref, bf16[512,2048]{1,0:T(8,128)(2,1)} %bitcast.59, bf16[512,2048]{1,0:T(8,128)(2,1)} %bitcast.61, ...), custom_call_target="tpu_custom_call", output_to_operand_aliasing={{0}: (17, {})} | custom-call | flops 1 | bytes 1 | tf_op jit(solution)/shard_map/attend/pallas_call | solution.py:326
  80.9 0.8 copy-done.4
  81.7 0.8 copy-done.9
  82.5 2.1 %row_grads.2.refs_8_ = bf16[16,512]{1,0:T(8,128)(2,1)} custom-call(s32[4]{0:T(128)} %pad_add_fusion.1.place_ref, f32[16,16,512]{2,1,0:T(8,128)} %copy-done.9, f32[64,512]{1,0:T(8,128)} %get-tuple-element.28.raw_ref, f32[576,128]{1,0:T(8,128)} %get-tuple-element.52.cos_ref.refs_11_, f32[576,128]{1,0:T(8,128)} %get-tuple-element.51.sin_ref.refs_12_, ...), custom_call_target="tpu_custom_call" | custom-call | flops 1 | bytes 1 | tf_op jit(solution)/shard_map/row_grads/pallas_call | solution.py:436
  84.5 0.9 collective-permute-start.10
  85.4 1.0 collective-permute-start.11
  86.4 2.1 %collective-permute-done.10.refs_10_.refs_1_ = bf16[16,512]{1,0:T(8,128)(2,1)S(1)} collective-permute-done((bf16[16,512]{1,0:T(8,128)(2,1)}, bf16[16,512]{1,0:T(8,128)(2,1)S(1)}, u32[]{:S(2)}, u32[]{:S(2)}) %collective-permute-start.10) | collective-permute-done | bytes 16416 | tf_op jit(solution)/shard_map/ppermute | solution.py:36
  88.5 0.4 collective-permute-done.11.refs_11_.refs_2_
  89.1 0.6 copy-done.17
  89.7 0.9 collective-permute-start.17
  90.6 6.4 %all-to-all-start.2 = ((f32[16,16,512]{2,1,0:T(8,128)}), f32[16,16,512]{2,1,0:T(8,128)S(1)}, u32[]{:S(2)}, u32[]{:S(2)}) async-start(f32[16,16,512]{2,1,0:T(8,128)} %bitcast.65), calls=%async_computation.2 | async-start | bytes 1048576 | tf_op jit(solution)/shard_map/all_to_all | solution.py:355
  97.0 0.5 collective-permute-start.9
  97.6 0.7 collective-permute-done.9.refs_9_
  98.3 0.6 copy-done.21
  98.9 7.3 %weight_shares.2.refs_1_.refs_0_ = f32[528,1024]{1,0:T(8,128)} custom-call(bf16[528,1024]{1,0:T(8,128)(2,1)} %get-tuple-element.25.refs_0_, bf16[528,1024]{1,0:T(8,128)(2,1)} %copy-done.2, bf16[2,528,1024]{2,1,0:T(8,128)(2,1)} %tied.6.refs_15_.refs_2_, bf16[2,528,1024]{2,1,0:T(8,128)(2,1)} %collective-permute-done.5.refs_3_, bf16[512,512]{1,0:T(8,128)(2,1)} %bitcast.71, ...), custom_call_target="tpu_custom_call" | custom-call | flops 1 | bytes 1 | tf_op jit(solution)/shard_map/weight_shares/pallas_call | solution.py:396
  106.2 1.3 slice_convert_fusion.1
  107.6 1.9 %collective-permute-start.12 = (f16[528,512]{1,0:T(8,128)(2,1)S(1)}, f16[528,512]{1,0:T(8,128)(2,1)S(1)}, u32[]{:S(2)}, u32[]{:S(2)}) collective-permute-start(f16[528,512]{1,0:T(8,128)(2,1)S(1)} %slice_convert_fusion.1), channel_id=1, source_target_pairs={{0,8},{8,0},{1,9},{9,1},{2,10},{10,2},{3,11},{11,3},{4,12},{12,4},... | collective-permute-start | bytes 1622024 | tf_op jit(solution)/shard_map/ppermute | solution.py:36
  109.5 0.8 copy-done.11
  110.3 2.4 %all-to-all-done.2.sums_ref = f32[16,16,512]{2,1,0:T(8,128)S(1)} async-done(((f32[16,16,512]{2,1,0:T(8,128)}), f32[16,16,512]{2,1,0:T(8,128)S(1)}, u32[]{:S(2)}, u32[]{:S(2)}) %all-to-all-start.2) | async-done | bytes 524320 | tf_op jit(solution)/shard_map/all_to_all | solution.py:355
  112.7 0.8 copy-done.8
  113.5 2.1 %row_grads.3.refs_8_ = bf16[16,512]{1,0:T(8,128)(2,1)} custom-call(s32[4]{0:T(128)} %pad_add_fusion.1.place_ref, f32[16,16,512]{2,1,0:T(8,128)} %copy-done.8, f32[64,512]{1,0:T(8,128)} %get-tuple-element.28.raw_ref, f32[576,128]{1,0:T(8,128)} %get-tuple-element.52.cos_ref.refs_11_, f32[576,128]{1,0:T(8,128)} %get-tuple-element.51.sin_ref.refs_12_, ...), custom_call_target="tpu_custom_call" | custom-call | flops 1 | bytes 1 | tf_op jit(solution)/shard_map/row_grads/pallas_call | solution.py:436
  115.5 1.1 collective-permute-start.20
  116.6 0.8 collective-permute-start.21
  117.4 2.1 %collective-permute-done.20.refs_10_ = bf16[16,512]{1,0:T(8,128)(2,1)S(1)} collective-permute-done((bf16[16,512]{1,0:T(8,128)(2,1)}, bf16[16,512]{1,0:T(8,128)(2,1)S(1)}, u32[]{:S(2)}, u32[]{:S(2)}) %collective-permute-start.20) | collective-permute-done | bytes 16416 | tf_op jit(solution)/shard_map/ppermute | solution.py:36
  119.5 0.5 collective-permute-done.21.refs_11_
  120.1 0.5 copy-done.20
  120.6 0.8 copy-done.14
  121.4 7.4 %weight_shares.3 = f32[528,1024]{1,0:T(8,128)} custom-call(bf16[528,1024]{1,0:T(8,128)(2,1)} %get-tuple-element.25.refs_0_, bf16[528,1024]{1,0:T(8,128)(2,1)} %copy-done.2, bf16[2,528,1024]{2,1,0:T(8,128)(2,1)} %tied.6.refs_15_.refs_2_, bf16[2,528,1024]{2,1,0:T(8,128)(2,1)} %collective-permute-done.5.refs_3_, bf16[512,512]{1,0:T(8,128)(2,1)} %tied.9.refs_4_, ...), custom_call_target="tpu_custom_call" | custom-call | flops 1 | bytes 1 | tf_op jit(solution)/shard_map/weight_shares/pallas_call | solution.py:396
  128.8 0.9 multiply_exponential_fusion.3
  129.7 0.7 multiply_exponential_fusion.5
  130.4 1.4 fusion.52
  132.0 1.5 collective-permute-start.15
  133.6 1.2 collective-permute-start.22
  134.9 2.6 %collective-permute-start.13 = (f16[528,128]{1,0:T(8,128)(2,1)S(1)}, f16[528,128]{1,0:T(8,128)(2,1)S(1)}, u32[]{:S(2)}, u32[]{:S(2)}) collective-permute-start(f16[528,128]{1,0:T(8,128)(2,1)S(1)} %get-tuple-element.48), channel_id=1, source_target_pairs={{0,1},{1,0},{2,3},{3,2},{4,5},{5,4},{6,7},{7,6},{8,9},{9,8},{10,11... | collective-permute-start | bytes 405512 | tf_op jit(solution)/shard_map/ppermute | solution.py:36
  137.6 2.8 %collective-permute-done.15 = f16[528,128]{1,0:T(8,128)(2,1)S(1)} collective-permute-done((f16[528,128]{1,0:T(8,128)(2,1)S(1)}, f16[528,128]{1,0:T(8,128)(2,1)S(1)}, u32[]{:S(2)}, u32[]{:S(2)}) %collective-permute-start.15) | collective-permute-done | bytes 135200 | tf_op jit(solution)/shard_map/ppermute | solution.py:36
  140.4 5.6 %collective-permute-done.14 = f16[528,128]{1,0:T(8,128)(2,1)S(1)} collective-permute-done((f16[528,128]{1,0:T(8,128)(2,1)S(1)}, f16[528,128]{1,0:T(8,128)(2,1)S(1)}, u32[]{:S(2)}, u32[]{:S(2)}) %collective-permute-start.14) | collective-permute-done | bytes 135200 | tf_op jit(solution)/shard_map/ppermute | solution.py:36
  146.1 1.5 collective-permute-done.22
  148.1 2.9 %collective-permute-start.25 = (f16[528,128]{1,0:T(8,128)(2,1)S(1)}, f16[528,128]{1,0:T(8,128)(2,1)S(1)}, u32[]{:S(2)}, u32[]{:S(2)}) collective-permute-start(f16[528,128]{1,0:T(8,128)(2,1)S(1)} %get-tuple-element.47), channel_id=1, source_target_pairs={{0,3},{1,2},{2,1},{3,0},{4,7},{5,6},{6,5},{7,4},{8,11},{9,10},{10,... | collective-permute-start | bytes 405512 | tf_op jit(solution)/shard_map/ppermute | solution.py:36
  151.0 0.9 collective-permute-start.26
  151.9 1.5 collective-permute-start.23
  153.5 2.5 %collective-permute-done.25 = f16[528,128]{1,0:T(8,128)(2,1)S(1)} collective-permute-done((f16[528,128]{1,0:T(8,128)(2,1)S(1)}, f16[528,128]{1,0:T(8,128)(2,1)S(1)}, u32[]{:S(2)}, u32[]{:S(2)}) %collective-permute-start.25) | collective-permute-done | bytes 135200 | tf_op jit(solution)/shard_map/ppermute | solution.py:36
  156.0 4.9 %collective-permute-done.24 = f16[528,128]{1,0:T(8,128)(2,1)S(1)} collective-permute-done((f16[528,128]{1,0:T(8,128)(2,1)S(1)}, f16[528,128]{1,0:T(8,128)(2,1)S(1)}, u32[]{:S(2)}, u32[]{:S(2)}) %collective-permute-start.24) | collective-permute-done | bytes 135200 | tf_op jit(solution)/shard_map/ppermute | solution.py:36
  161.1 1.0 collective-permute-start.27
  162.1 6.7 %collective-permute-done.27 = f32[512,128]{1,0:T(8,128)S(1)} collective-permute-done((f32[512,128]{1,0:T(8,128)S(1)}, f32[512,128]{1,0:T(8,128)S(1)}, u32[]{:S(2)}, u32[]{:S(2)}) %collective-permute-start.27) | collective-permute-done | bytes 262176 | tf_op jit(solution)/shard_map/ppermute | solution.py:36
  168.9 1.0 copy.26
  169.9 1.0 copy.27
  (97 shorter events, 2.7 us)
Async XLA Ops:
  5.6 50.2 %collective-permute-start.4 = (bf16[2,528,1024]{2,1,0:T(8,128)(2,1)}, bf16[2,528,1024]{2,1,0:T(8,128)(2,1)S(1)}, u32[]{:S(2)}, u32[]{:S(2)}) collective-permute-start(bf16[2,528,1024]{2,1,0:T(8,128)(2,1)} %get-tuple-element.17.after_ref), channel_id=1, source_target_pairs={{0,16},{16,0},{1,17},{17,1},{2,18},{18,2},{3,19},{19,3},{4,20},{20... | collective-permute-start | bytes 6488072 | tf_op jit(solution)/shard_map/ppermute | solution.py:36
  22.4 18.4 %collective-permute-start = (bf16[64,1024]{1,0:T(8,128)(2,1)}, bf16[64,1024]{1,0:T(8,128)(2,1)S(1)}, u32[]{:S(2)}, u32[]{:S(2)}) collective-permute-start(bf16[64,1024]{1,0:T(8,128)(2,1)} %get-tuple-element.18.refs_0_.refs_4_), channel_id=1, source_target_pairs={{0,4},{4,0},{1,5},{5,1},{2,6},{6,2},{3,7},{7,3},{8,12},{12,8},{9,1... | collective-permute-start | bytes 393224 | tf_op jit(solution)/shard_map/ppermute | solution.py:36
  22.5 18.3 %collective-permute-start.1 = (bf16[64,1024]{1,0:T(8,128)(2,1)}, bf16[64,1024]{1,0:T(8,128)(2,1)S(1)}, u32[]{:S(2)}, u32[]{:S(2)}) collective-permute-start(bf16[64,1024]{1,0:T(8,128)(2,1)} %get-tuple-element.18.refs_0_.refs_4_), channel_id=1, source_target_pairs={{0,8},{8,0},{1,9},{9,1},{2,10},{10,2},{3,11},{11,3},{4,12},{12,4},... | collective-permute-start | bytes 393224 | tf_op jit(solution)/shard_map/ppermute | solution.py:36
  24.1 16.7 %collective-permute-start.2 = (bf16[64,1024]{1,0:T(8,128)(2,1)}, bf16[64,1024]{1,0:T(8,128)(2,1)S(1)}, u32[]{:S(2)}, u32[]{:S(2)}) collective-permute-start(bf16[64,1024]{1,0:T(8,128)(2,1)} %get-tuple-element.18.refs_0_.refs_4_), channel_id=1, source_target_pairs={{0,12},{4,8},{8,4},{12,0},{1,13},{5,9},{9,5},{13,1},{2,14},{6,10},... | collective-permute-start | bytes 393224 | tf_op jit(solution)/shard_map/ppermute | solution.py:36
  26.3 12.4 %all-to-all-start = ((f32[16,3,8]{2,1,0:T(4,128)}), f32[16,3,8]{2,1,0:T(4,128)S(1)}, u32[]{:S(2)}, u32[]{:S(2)}) async-start(f32[16,3,8]{2,1,0:T(4,128)} %broadcast_in_dim.20), calls=%async_computation | async-start | bytes 65536 | tf_op jit(solution)/shard_map/all_to_all | solution.py:355
  40.8 0.7 copy-start.5
  40.8 0.7 copy-start.6
  40.8 0.7 copy-start.7
  55.8 1.4 copy-start
  57.2 6.7 %copy-start.10 = (bf16[2,2,128,512]{3,2,1,0:T(8,128)(2,1)S(1)}, bf16[2,2,128,512]{3,2,1,0:T(8,128)(2,1)}, u32[]{:S(2)}) copy-start(bf16[2,2,128,512]{3,2,1,0:T(8,128)(2,1)} %get-tuple-element.23) | copy-start | bytes 1572868
  57.2 41.1 %collective-permute-start.5 = (bf16[2,528,1024]{2,1,0:T(8,128)(2,1)}, bf16[2,528,1024]{2,1,0:T(8,128)(2,1)}, u32[]{:S(2)}, u32[]{:S(2)}) collective-permute-start(bf16[2,528,1024]{2,1,0:T(8,128)(2,1)} %tied.6.refs_15_.refs_2_), channel_id=1, source_target_pairs={{0,4},{4,0},{1,5},{5,1},{2,6},{6,2},{3,7},{7,3},{8,12},{12,8},{9,1... | collective-permute-start | bytes 6488072 | tf_op jit(solution)/shard_map/ppermute | solution.py:36
  57.2 8.4 %collective-permute-start.3 = (bf16[528,1024]{1,0:T(8,128)(2,1)}, bf16[528,1024]{1,0:T(8,128)(2,1)S(1)}, u32[]{:S(2)}, u32[]{:S(2)}) collective-permute-start(bf16[528,1024]{1,0:T(8,128)(2,1)} %get-tuple-element.22), channel_id=1, source_target_pairs={{0,4},{4,0},{1,5},{5,1},{2,6},{6,2},{3,7},{7,3},{8,12},{12,8},{9,1... | collective-permute-start | bytes 3244040 | tf_op jit(solution)/shard_map/ppermute | solution.py:36
  57.7 23.9 %all-to-all-start.1 = ((f32[16,16,512]{2,1,0:T(8,128)}), f32[16,16,512]{2,1,0:T(8,128)S(1)}, u32[]{:S(2)}, u32[]{:S(2)}) async-start(f32[16,16,512]{2,1,0:T(8,128)} %bitcast.19), calls=%async_computation.1 | async-start | bytes 1048576 | tf_op jit(solution)/shard_map/all_to_all | solution.py:355
  64.0 16.9 %collective-permute-start.7 = (bf16[512,512]{1,0:T(8,128)(2,1)S(1)}, bf16[512,512]{1,0:T(8,128)(2,1)S(1)}, u32[]{:S(2)}, u32[]{:S(2)}) collective-permute-start(bf16[512,512]{1,0:T(8,128)(2,1)S(1)} %bitcast.72), channel_id=1, source_target_pairs={{0,16},{16,0},{1,17},{17,1},{2,18},{18,2},{3,19},{19,3},{4,20},{20... | collective-permute-start | bytes 1572872 | tf_op jit(solution)/shard_map/ppermute | solution.py:36
  65.5 32.0 %collective-permute-start.6 = (bf16[512,512]{1,0:T(8,128)(2,1)S(1)}, bf16[512,512]{1,0:T(8,128)(2,1)S(1)}, u32[]{:S(2)}, u32[]{:S(2)}) collective-permute-start(bf16[512,512]{1,0:T(8,128)(2,1)S(1)} %bitcast.73), channel_id=1, source_target_pairs={{0,4},{4,0},{1,5},{5,1},{2,6},{6,2},{3,7},{7,3},{8,12},{12,8},{9,1... | collective-permute-start | bytes 1572872 | tf_op jit(solution)/shard_map/ppermute | solution.py:36
  65.7 1.0 copy-start.2
  80.9 0.8 copy-start.4
  81.7 16.6 %collective-permute-start.8 = (bf16[512,512]{1,0:T(8,128)(2,1)}, bf16[512,512]{1,0:T(8,128)(2,1)}, u32[]{:S(2)}, u32[]{:S(2)}) collective-permute-start(bf16[512,512]{1,0:T(8,128)(2,1)} %tied.7.refs_1_.refs_6_), channel_id=1, source_target_pairs={{0,4},{4,0},{1,5},{5,1},{2,6},{6,2},{3,7},{7,3},{8,12},{12,8},{9,1... | collective-permute-start | bytes 1572872 | tf_op jit(solution)/shard_map/ppermute | solution.py:36
  81.7 0.8 copy-start.9
  84.5 12.5 %copy-start.15 = (bf16[16,512]{1,0:T(8,128)(2,1)S(1)}, bf16[16,512]{1,0:T(8,128)(2,1)}, u32[]{:S(2)}) copy-start(bf16[16,512]{1,0:T(8,128)(2,1)} %row_grads.2.refs_8_) | copy-start | bytes 49156
  84.5 3.9 %collective-permute-start.10 = (bf16[16,512]{1,0:T(8,128)(2,1)}, bf16[16,512]{1,0:T(8,128)(2,1)S(1)}, u32[]{:S(2)}, u32[]{:S(2)}) collective-permute-start(bf16[16,512]{1,0:T(8,128)(2,1)} %row_grads.2.refs_8_), channel_id=1, source_target_pairs={{0,16},{16,0},{1,17},{17,1},{2,18},{18,2},{3,19},{19,3},{4,20},{20... | collective-permute-start | bytes 49160 | tf_op jit(solution)/shard_map/ppermute | solution.py:36
  85.4 3.5 %collective-permute-start.11 = (bf16[16,512]{1,0:T(8,128)(2,1)}, bf16[16,512]{1,0:T(8,128)(2,1)S(1)}, u32[]{:S(2)}, u32[]{:S(2)}) collective-permute-start(bf16[16,512]{1,0:T(8,128)(2,1)} %row_grads.2.refs_8_), channel_id=1, source_target_pairs={{0,20},{4,16},{16,4},{20,0},{1,21},{5,17},{17,5},{21,1},{2,22},{6,... | collective-permute-start | bytes 49160 | tf_op jit(solution)/shard_map/ppermute | solution.py:36
  88.5 0.6 copy-start.16
  89.1 0.6 copy-start.17
  89.7 7.8 %copy-start.1 = (bf16[512,512]{1,0:T(8,128)(2,1)S(1)}, bf16[512,512]{1,0:T(8,128)(2,1)}, u32[]{:S(2)}) copy-start(bf16[512,512]{1,0:T(8,128)(2,1)} %tied.9.refs_4_) | copy-start | bytes 1572868
  89.7 19.8 %collective-permute-start.17 = (bf16[512,512]{1,0:T(8,128)(2,1)}, bf16[512,512]{1,0:T(8,128)(2,1)S(1)}, u32[]{:S(2)}, u32[]{:S(2)}) collective-permute-start(bf16[512,512]{1,0:T(8,128)(2,1)} %tied.9.refs_4_), channel_id=1, source_target_pairs={{0,16},{16,0},{1,17},{17,1},{2,18},{18,2},{3,19},{19,3},{4,20},{20... | collective-permute-start | bytes 1572872 | tf_op jit(solution)/shard_map/ppermute | solution.py:36
  90.6 22.1 %all-to-all-start.2 = ((f32[16,16,512]{2,1,0:T(8,128)}), f32[16,16,512]{2,1,0:T(8,128)S(1)}, u32[]{:S(2)}, u32[]{:S(2)}) async-start(f32[16,16,512]{2,1,0:T(8,128)} %bitcast.65), calls=%async_computation.2 | async-start | bytes 1048576 | tf_op jit(solution)/shard_map/all_to_all | solution.py:355
  97.0 1.3 collective-permute-start.9
  97.5 0.8 copy-start.13
  97.5 19.1 %collective-permute-start.16 = (bf16[512,512]{1,0:T(8,128)(2,1)S(1)}, bf16[512,512]{1,0:T(8,128)(2,1)S(1)}, u32[]{:S(2)}, u32[]{:S(2)}) collective-permute-start(bf16[512,512]{1,0:T(8,128)(2,1)S(1)} %copy-done.1), channel_id=1, source_target_pairs={{0,4},{4,0},{1,5},{5,1},{2,6},{6,2},{3,7},{7,3},{8,12},{12,8},{9,1... | collective-permute-start | bytes 1572872 | tf_op jit(solution)/shard_map/ppermute | solution.py:36
  98.3 0.6 copy-start.21
  107.6 21.2 %collective-permute-start.12 = (f16[528,512]{1,0:T(8,128)(2,1)S(1)}, f16[528,512]{1,0:T(8,128)(2,1)S(1)}, u32[]{:S(2)}, u32[]{:S(2)}) collective-permute-start(f16[528,512]{1,0:T(8,128)(2,1)S(1)} %slice_convert_fusion.1), channel_id=1, source_target_pairs={{0,8},{8,0},{1,9},{9,1},{2,10},{10,2},{3,11},{11,3},{4,12},{12,4},... | collective-permute-start | bytes 1622024 | tf_op jit(solution)/shard_map/ppermute | solution.py:36
  109.5 0.8 copy-start.11
  110.3 9.7 %collective-permute-start.18 = (bf16[512,512]{1,0:T(8,128)(2,1)}, bf16[512,512]{1,0:T(8,128)(2,1)S(1)}, u32[]{:S(2)}, u32[]{:S(2)}) collective-permute-start(bf16[512,512]{1,0:T(8,128)(2,1)} %tied.10.refs_6_), channel_id=1, source_target_pairs={{0,4},{4,0},{1,5},{5,1},{2,6},{6,2},{3,7},{7,3},{8,12},{12,8},{9,1... | collective-permute-start | bytes 1572872 | tf_op jit(solution)/shard_map/ppermute | solution.py:36
  112.7 0.8 copy-start.8
  115.5 1.9 %collective-permute-start.19 = (bf16[16,512]{1,0:T(8,128)(2,1)}, bf16[16,512]{1,0:T(8,128)(2,1)S(1)}, u32[]{:S(2)}, u32[]{:S(2)}) collective-permute-start(bf16[16,512]{1,0:T(8,128)(2,1)} %row_grads.3.refs_8_), channel_id=1, source_target_pairs={{0,4},{4,0},{1,5},{5,1},{2,6},{6,2},{3,7},{7,3},{8,12},{12,8},{9,1... | collective-permute-start | bytes 49160 | tf_op jit(solution)/shard_map/ppermute | solution.py:36
  115.5 3.9 %collective-permute-start.20 = (bf16[16,512]{1,0:T(8,128)(2,1)}, bf16[16,512]{1,0:T(8,128)(2,1)S(1)}, u32[]{:S(2)}, u32[]{:S(2)}) collective-permute-start(bf16[16,512]{1,0:T(8,128)(2,1)} %row_grads.3.refs_8_), channel_id=1, source_target_pairs={{0,16},{16,0},{1,17},{17,1},{2,18},{18,2},{3,19},{19,3},{4,20},{20... | collective-permute-start | bytes 49160 | tf_op jit(solution)/shard_map/ppermute | solution.py:36
  116.6 3.4 %copy-start.12 = (bf16[512,512]{1,0:T(8,128)(2,1)}, bf16[512,512]{1,0:T(8,128)(2,1)S(1)}, u32[]{:S(2)}) copy-start(bf16[512,512]{1,0:T(8,128)(2,1)S(1)} %collective-permute-done.16.refs_5_) | copy-start | bytes 1572868
  116.6 3.4 %collective-permute-start.21 = (bf16[16,512]{1,0:T(8,128)(2,1)}, bf16[16,512]{1,0:T(8,128)(2,1)S(1)}, u32[]{:S(2)}, u32[]{:S(2)}) collective-permute-start(bf16[16,512]{1,0:T(8,128)(2,1)} %row_grads.3.refs_8_), channel_id=1, source_target_pairs={{0,20},{4,16},{16,4},{20,0},{1,21},{5,17},{17,5},{21,1},{2,22},{6,... | collective-permute-start | bytes 49160 | tf_op jit(solution)/shard_map/ppermute | solution.py:36
  117.4 2.6 %copy-start.18 = (bf16[16,512]{1,0:T(8,128)(2,1)}, bf16[16,512]{1,0:T(8,128)(2,1)S(1)}, u32[]{:S(2)}) copy-start(bf16[16,512]{1,0:T(8,128)(2,1)S(1)} %collective-permute-done.19.refs_9_) | copy-start | bytes 49156
  119.5 0.6 copy-start.19
  120.0 0.6 copy-start.20
  120.6 0.8 copy-start.14
  128.7 4.8 %copy-start.3 = (f32[528,1024]{1,0:T(8,128)S(1)}, f32[528,1024]{1,0:T(8,128)}, u32[]{:S(2)}) copy-start(f32[528,1024]{1,0:T(8,128)} %weight_shares.3) | copy-start | bytes 6488068
  132.0 8.4 %collective-permute-start.15 = (f16[528,128]{1,0:T(8,128)(2,1)S(1)}, f16[528,128]{1,0:T(8,128)(2,1)S(1)}, u32[]{:S(2)}, u32[]{:S(2)}) collective-permute-start(f16[528,128]{1,0:T(8,128)(2,1)S(1)} %get-tuple-element.50), channel_id=1, source_target_pairs={{0,3},{1,2},{2,1},{3,0},{4,7},{5,6},{6,5},{7,4},{8,11},{9,10},{10,... | collective-permute-start | bytes 405512 | tf_op jit(solution)/shard_map/ppermute | solution.py:36
  133.6 14.0 %collective-permute-start.22 = (f16[528,512]{1,0:T(8,128)(2,1)S(1)}, f16[528,512]{1,0:T(8,128)(2,1)S(1)}, u32[]{:S(2)}, u32[]{:S(2)}) collective-permute-start(f16[528,512]{1,0:T(8,128)(2,1)S(1)} %slice_convert_fusion), channel_id=1, source_target_pairs={{0,8},{8,0},{1,9},{9,1},{2,10},{10,2},{3,11},{11,3},{4,12},{12,4},... | collective-permute-start | bytes 1622024 | tf_op jit(solution)/shard_map/ppermute | solution.py:36
  134.8 11.1 %collective-permute-start.14 = (f16[528,128]{1,0:T(8,128)(2,1)S(1)}, f16[528,128]{1,0:T(8,128)(2,1)S(1)}, u32[]{:S(2)}, u32[]{:S(2)}) collective-permute-start(f16[528,128]{1,0:T(8,128)(2,1)S(1)} %get-tuple-element.49), channel_id=1, source_target_pairs={{0,2},{1,3},{2,0},{3,1},{4,6},{5,7},{6,4},{7,5},{8,10},{9,11},{10,... | collective-permute-start | bytes 405512 | tf_op jit(solution)/shard_map/ppermute | solution.py:36
  134.9 11.0 %collective-permute-start.13 = (f16[528,128]{1,0:T(8,128)(2,1)S(1)}, f16[528,128]{1,0:T(8,128)(2,1)S(1)}, u32[]{:S(2)}, u32[]{:S(2)}) collective-permute-start(f16[528,128]{1,0:T(8,128)(2,1)S(1)} %get-tuple-element.48), channel_id=1, source_target_pairs={{0,1},{1,0},{2,3},{3,2},{4,5},{5,4},{6,7},{7,6},{8,9},{9,8},{10,11... | collective-permute-start | bytes 405512 | tf_op jit(solution)/shard_map/ppermute | solution.py:36
  148.1 7.9 %collective-permute-start.25 = (f16[528,128]{1,0:T(8,128)(2,1)S(1)}, f16[528,128]{1,0:T(8,128)(2,1)S(1)}, u32[]{:S(2)}, u32[]{:S(2)}) collective-permute-start(f16[528,128]{1,0:T(8,128)(2,1)S(1)} %get-tuple-element.47), channel_id=1, source_target_pairs={{0,3},{1,2},{2,1},{3,0},{4,7},{5,6},{6,5},{7,4},{8,11},{9,10},{10,... | collective-permute-start | bytes 405512 | tf_op jit(solution)/shard_map/ppermute | solution.py:36
  151.0 11.1 %collective-permute-start.26 = (f32[512,128]{1,0:T(8,128)S(1)}, f32[512,128]{1,0:T(8,128)S(1)}, u32[]{:S(2)}, u32[]{:S(2)}) collective-permute-start(f32[512,128]{1,0:T(8,128)S(1)} %fusion.11), channel_id=1, source_target_pairs={{0,16},{16,0},{1,17},{17,1},{2,18},{18,2},{3,19},{19,3},{4,20},{20... | collective-permute-start | bytes 786440 | tf_op jit(solution)/shard_map/ppermute | solution.py:36
  151.9 9.0 %collective-permute-start.24 = (f16[528,128]{1,0:T(8,128)(2,1)S(1)}, f16[528,128]{1,0:T(8,128)(2,1)S(1)}, u32[]{:S(2)}, u32[]{:S(2)}) collective-permute-start(f16[528,128]{1,0:T(8,128)(2,1)S(1)} %get-tuple-element.46), channel_id=1, source_target_pairs={{0,2},{1,3},{2,0},{3,1},{4,6},{5,7},{6,4},{7,5},{8,10},{9,11},{10,... | collective-permute-start | bytes 405512 | tf_op jit(solution)/shard_map/ppermute | solution.py:36
  151.9 9.0 %collective-permute-start.23 = (f16[528,128]{1,0:T(8,128)(2,1)S(1)}, f16[528,128]{1,0:T(8,128)(2,1)S(1)}, u32[]{:S(2)}, u32[]{:S(2)}) collective-permute-start(f16[528,128]{1,0:T(8,128)(2,1)S(1)} %get-tuple-element.45), channel_id=1, source_target_pairs={{0,1},{1,0},{2,3},{3,2},{4,5},{5,4},{6,7},{7,6},{8,9},{9,8},{10,11... | collective-permute-start | bytes 405512 | tf_op jit(solution)/shard_map/ppermute | solution.py:36
  161.1 7.7 %collective-permute-start.27 = (f32[512,128]{1,0:T(8,128)S(1)}, f32[512,128]{1,0:T(8,128)S(1)}, u32[]{:S(2)}, u32[]{:S(2)}) collective-permute-start(f32[512,128]{1,0:T(8,128)S(1)} %fusion.8), channel_id=1, source_target_pairs={{0,16},{16,0},{1,17},{17,1},{2,18},{18,2},{3,19},{19,3},{4,20},{20... | collective-permute-start | bytes 786440 | tf_op jit(solution)/shard_map/ppermute | solution.py:36

commit v7 on v6

--- a/solution.py
+++ b/solution.py
@@ -240,9 +240,12 @@
     k_turned[...] = k_all[...].T
     acc_k[...] = jnp.zeros_like(acc_k)
     acc_v[...] = jnp.zeros_like(acc_v)
-    def one_block(first):
+    width = fold * QROWS
+    key = lax.broadcasted_iota(jnp.int32, (QROWS, width), 0)
+    row = lax.broadcasted_iota(jnp.int32, (QROWS, width), 1) % QROWS
+
+    def begin(first):
         seen = prompt_len + first + QROWS
-        width = fold * QROWS
         position = first + lax.broadcasted_iota(jnp.int32, (QROWS, HEAD_DIM), 0)
         factor = jnp.where(position < length, coef, 0.0)
         parts_q = []
@@ -254,17 +257,21 @@
         query = jnp.concatenate(parts_q, axis=0)
         dout = jnp.concatenate(parts_d, axis=0)
         scores = lax.dot_general(k_all[:seen, :], query, BY_COLS, preferred_element_type=F32)
-        key = lax.broadcasted_iota(jnp.int32, (QROWS, width), 0)
-        row = lax.broadcasted_iota(jnp.int32, (QROWS, width), 1) % QROWS
+        dprobs = lax.dot_general(v_all[:seen, :], dout, BY_COLS, preferred_element_type=F32)
+        return first, seen, query, dout, scores, dprobs
+
+    def middle(first, seen, query, dout, scores, dprobs):
         tail = jnp.where(key <= row, scores[seen - QROWS :, :], -jnp.inf)
         scores = jnp.concatenate([scores[: seen - QROWS, :], tail], axis=0)
         peak = jnp.max(scores, axis=0, keepdims=True)
         expo = jnp.exp2((scores - peak) * (scale * math.log2(math.e)))
         probs = expo * (1.0 / jnp.sum(expo, axis=0, keepdims=True))
         probs_b = probs.astype(BF16)
-        dprobs = lax.dot_general(v_all[:seen, :], dout, BY_COLS, preferred_element_type=F32)
         delta = jnp.sum(probs_b.astype(F32) * dprobs, axis=0, keepdims=True)
         dscores = (probs * (dprobs - delta)).astype(BF16)
+        return first, seen, query, dout, probs_b, dscores
+
+    def end(first, seen, query, dout, probs_b, dscores):
         grad_q = jnp.dot(k_turned[:, :seen], dscores, preferred_element_type=F32) * scale
         for f in range(fold):
             gq_ref[first : first + QROWS, f * HEAD_DIM : (f + 1) * HEAD_DIM] = (
@@ -273,16 +280,16 @@
         acc_k[:seen, :] += jnp.dot(dscores, query, preferred_element_type=F32)
         acc_v[:seen, :] += jnp.dot(probs_b, dout, preferred_element_type=F32)
 
-    for start in range(0, rows, 2 * QROWS):
-
-        @pl.when(start < length)
-        def _(start=start):
-            one_block(start)
-            one_block(start + QROWS)
-
-        @pl.when(start >= length)
-        def _(start=start):
-            gq_ref[start : start + 2 * QROWS, :] = jnp.zeros((2 * QROWS, gq_ref.shape[1]), BF16)
+    blocks = range(0, rows, QROWS)
+    ready = begin(0)
+    waiting = None
+    for first in blocks:
+        following = begin(first + QROWS) if first + QROWS < rows else None
+        if waiting is not None:
+            end(*waiting)
+        waiting = middle(*ready)
+        ready = following
+    end(*waiting)
 
     sum_ref[:, :HEAD_DIM] = acc_k[:prompt_len, :] * scale
     sum_ref[:, HEAD_DIM:] = acc_v[:prompt_len, :]
@@ -546,7 +553,7 @@
     wide = n_resp * block
 
     def chip_terms(shares):
-        return [exchange(shares[:, d * wide : (d + 1) * wide].astype(jnp.float16), [("chip", d)]) for d in range(1, n_chip)]
+        return [shares[:, d * wide : (d + 1) * wide].astype(jnp.float16) for d in range(1, n_chip)]
 
     def resp_terms(kept, sent):
         exponents = [exponent_of(x) for x in [kept] + sent]
@@ -583,8 +590,10 @@
     hops_late = [tied(x, shares_early) for x in hops_late]
     tokens_late = row_tokens(sums_late, early, [shares_early])
     shares_late = weight_shares(parts, everywhere(g_late, hops_late), tokens_late)
-    sent_early = chip_terms(shares_early)
-    sent_late = chip_terms(shares_late)
+    sent_early = [exchange(x, [("chip", d)]) for d, x in enumerate(chip_terms(shares_early), 1)]
+    payload_late = chip_terms(shares_late)
+    sent_early = [lax.optimization_barrier((x, payload_late[0]))[0] for x in sent_early]
+    sent_late = [exchange(x, [("chip", d)]) for d, x in enumerate(payload_late, 1)]
     half_early, pieces_early = resp_terms(shares_early[:, :wide], sent_early)
     done_early = finish(half_early, pieces_early)
     sent_late = [lax.optimization_barrier((x, done_early[0]))[0] for x in sent_late]

time: 172 us -> 174 us (1.012)
  other arithmetic: 9.31 us -> 12.6 us
  Pallas kernels: 63.2 us -> 60.3 us
  waiting for transfers between devices: 37.5 us -> 39.9 us
    ppermute x28, waiting for transfers between devices: 29.9 us -> 32.9 us  [exchange(): return lax.ppermute(value, names, [(j, j ^ mask) for j in range(total)])]
    pallas_call x2, Pallas kernels: 28.3 us -> 25.4 us  [attend(): pl.pallas_call(functools.partial(attend_kernel, parts, fold), grid=(per,)...]
    another operation x6, other arithmetic: 3.14 us -> 5.16 us
    unnamed x45 -> x43, local copies, waits for them, and re-layouts: 9.11 us -> 8.82 us
  transfers between devices with their start and end apart: 31 -> 31, of which waited for: 14 -> 14; matrix products, arithmetic and copies ran while one was open for 3% -> 4% of each run, Pallas kernels for 34% -> 32%
where the time goes in v7:
time: 174 us; the launch traced here: 173 us
  Pallas kernels  60.3 us (35%)
  starting transfers between devices  44.3 us (25%)
  waiting for transfers between devices  39.9 us (23%)
  other arithmetic  12.6 us (7%)
  local copies, waits for them, and re-layouts  11.6 us (7%)
  between operations  4.28 us (2%)
    ppermute x28, waiting for transfers between devices, exchange(): return lax.ppermute(value, names, [(j, j ^ mask) for j in range(total)])  32.9 us
    ppermute x28, starting transfers between devices, exchange(): return lax.ppermute(value, names, [(j, j ^ mask) for j in range(total)])  26.4 us
    pallas_call x2, Pallas kernels, attend(): pl.pallas_call(functools.partial(attend_kernel, parts, fold), grid=(per,)...  25.4 us
    all_to_all x3, starting transfers between devices, everyone(): return lax.all_to_all(value, names, split_axis=0, concat_axis=0, tiled=True)  17.9 us
    pallas_call x2, Pallas kernels, weight_shares(): pl.pallas_call(functools.partial(weight_kernel, parts, len(tokens)), grid...  14.7 us
    pallas_call x1, Pallas kernels, project(): pl.pallas_call(functools.partial(project_kernel, groups, counts), in_spec...  11.8 us
    unnamed x43, local copies, waits for them, and re-layouts  8.82 us
    all_to_all x3, waiting for transfers between devices, everyone(): return lax.all_to_all(value, names, split_axis=0, concat_axis=0, tiled=True)  7.02 us
  transfers between devices with their start and end apart: 31, of which 14 were waited for; matrix products, arithmetic and copies ran while one was open for 4% of the time, Pallas kernels for 32%

profile of v7, /device:TPU:0, one launch (start us, length us, event | category | flops | bytes accessed | tf_op | source)
XLA Modules:
  0.0 173.0 jit_solution(5876342954461167360)
XLA Ops:
  0.6 0.6 pad_add_fusion.1.place_ref
  1.3 4.3 %select_columns.1 = (bf16[528,1024]{1,0:T(8,128)(2,1)}, bf16[2,528,1024]{2,1,0:T(8,128)(2,1)}) custom-call(s32[4]{0:T(128)} %pad_add_fusion.1.place_ref, bf16[512,4096]{1,0:T(8,128)(2,1)} %bitcast.54, bf16[64,4096]{1,0:T(8,128)(2,1)} %bitcast.63), custom_call_target="tpu_custom_call" | custom-call | flops 1 | bytes 1 | tf_op jit(solution)/shard_map/select_columns/pallas_call | solution.py:104
  5.5 3.0 %collective-permute-start.4 = (bf16[2,528,1024]{2,1,0:T(8,128)(2,1)}, bf16[2,528,1024]{2,1,0:T(8,128)(2,1)S(1)}, u32[]{:S(2)}, u32[]{:S(2)}) collective-permute-start(bf16[2,528,1024]{2,1,0:T(8,128)(2,1)} %get-tuple-element.18.after_ref), channel_id=1, source_target_pairs={{0,16},{16,0},{1,17},{17,1},{2,18},{18,2},{3,19},{19,3},{4,20},{20... | collective-permute-start | bytes 6488072 | tf_op jit(solution)/shard_map/ppermute | solution.py:36
  8.6 2.0 %fusion.5 = (f32[576,128]{1,0:T(8,128)}, f32[576,128]{1,0:T(8,128)}) fusion(f32[128]{0:T(128)S(1)} %get-tuple-element.61, f32[128]{0:T(128)S(1)} %get-tuple-element.62, f32[576]{0:T(1024)S(1)} %select_convert_fusion), kind=kLoop, calls=%fused_computation.27 | loop fusion | flops 147456 | bytes 593152 | tf_op jit(solution)/shard_map/mul | solution.py:46
  10.5 11.8 %project.1 = (f32[64,512]{1,0:T(8,128)}, bf16[64,1024]{1,0:T(8,128)(2,1)}, f32[512,512]{1,0:T(8,128)}, bf16[512,1024]{1,0:T(8,128)(2,1)}, bf16[528,1024]{1,0:T(8,128)(2,1)}) custom-call(s32[4]{0:T(128)} %pad_add_fusion.1.place_ref, bf16[64,4096]{1,0:T(8,128)(2,1)} %bitcast.64, bf16[512,4096]{1,0:T(8,128)(2,1)} %bitcast.55, bf16[4096,512]{1,0:T(8,128)(2,1)} %wk_hbm.1, ...), custom_call_target="tpu_custom_call" | custom-call | flops 1 | bytes 1 | tf_op jit(solution)/shard_map/project/pallas_call | solution.py:184
  22.5 1.6 collective-permute-start.1
  25.7 0.6 broadcast_in_dim.20
  26.3 5.9 %all-to-all-start = ((f32[16,3,8]{2,1,0:T(4,128)}), f32[16,3,8]{2,1,0:T(4,128)S(1)}, u32[]{:S(2)}, u32[]{:S(2)}) async-start(f32[16,3,8]{2,1,0:T(4,128)} %broadcast_in_dim.20), calls=%async_computation | async-start | bytes 65536 | tf_op jit(solution)/shard_map/all_to_all | solution.py:362
  32.9 0.6 pad_add_fusion.ints_ref
  33.5 5.2 %all-to-all-done = f32[16,3,8]{2,1,0:T(4,128)S(1)} async-done(((f32[16,3,8]{2,1,0:T(4,128)}), f32[16,3,8]{2,1,0:T(4,128)S(1)}, u32[]{:S(2)}, u32[]{:S(2)}) %all-to-all-start) | async-done | bytes 1568 | tf_op jit(solution)/shard_map/all_to_all | solution.py:362
  38.8 0.7 select_reduce_fusion
  40.8 0.6 copy-done.6
  41.5 12.7 %attend.2 = (bf16[512,2048]{1,0:T(8,128)(2,1)}, f32[256,512]{1,0:T(8,128)}, bf16[2,2,128,512]{3,2,1,0:T(8,128)(2,1)}) custom-call(f32[1]{0:T(128)S(6)} %div.21.coef_ref, s32[2]{0:T(128)} %pad_add_fusion.ints_ref, bf16[512,2048]{1,0:T(8,128)(2,1)} %bitcast.58, bf16[512,2048]{1,0:T(8,128)(2,1)} %bitcast.60, ...), custom_call_target="tpu_custom_call" | custom-call | flops 1 | bytes 1 | tf_op jit(solution)/shard_map/attend/pallas_call | solution.py:333
  54.2 1.6 collective-permute-done.4.refs_0_
  55.8 1.4 copy-done
  57.7 6.2 %all-to-all-start.1 = ((f32[16,16,512]{2,1,0:T(8,128)}), f32[16,16,512]{2,1,0:T(8,128)S(1)}, u32[]{:S(2)}, u32[]{:S(2)}) async-start(f32[16,16,512]{2,1,0:T(8,128)} %bitcast.19), calls=%async_computation.1 | async-start | bytes 1048576 | tf_op jit(solution)/shard_map/all_to_all | solution.py:362
  64.0 1.6 collective-permute-start.7
  65.5 1.0 copy-done.3
  66.5 12.7 %attend.3 = (bf16[512,2048]{1,0:T(8,128)(2,1)}, f32[256,512]{1,0:T(8,128)}, bf16[2,2,128,512]{3,2,1,0:T(8,128)(2,1)}) custom-call(f32[1]{0:T(128)S(6)} %div.21.coef_ref, s32[2]{0:T(128)} %pad_add_fusion.ints_ref, bf16[512,2048]{1,0:T(8,128)(2,1)} %bitcast.59, bf16[512,2048]{1,0:T(8,128)(2,1)} %bitcast.61, ...), custom_call_target="tpu_custom_call", output_to_operand_aliasing={{0}: (17, {})} | custom-call | flops 1 | bytes 1 | tf_op jit(solution)/shard_map/attend/pallas_call | solution.py:333
  79.2 0.8 copy-done.4
  80.0 0.8 copy-done.10
  80.8 2.1 %row_grads.2.refs_8_ = bf16[16,512]{1,0:T(8,128)(2,1)} custom-call(s32[4]{0:T(128)} %pad_add_fusion.1.place_ref, f32[16,16,512]{2,1,0:T(8,128)} %copy-done.10, f32[64,512]{1,0:T(8,128)} %get-tuple-element.29.raw_ref, f32[576,128]{1,0:T(8,128)} %get-tuple-element.54.cos_ref.refs_11_, f32[576,128]{1,0:T(8,128)} %get-tuple-element.53.sin_ref.refs_12_, ...), custom_call_target="tpu_custom_call" | custom-call | flops 1 | bytes 1 | tf_op jit(solution)/shard_map/row_grads/pallas_call | solution.py:443
  82.9 1.1 collective-permute-start.10
  84.4 0.6 collective-permute-start.6
  85.0 1.8 %collective-permute-done.10.refs_10_.refs_1_ = bf16[16,512]{1,0:T(8,128)(2,1)S(1)} collective-permute-done((bf16[16,512]{1,0:T(8,128)(2,1)}, bf16[16,512]{1,0:T(8,128)(2,1)S(1)}, u32[]{:S(2)}, u32[]{:S(2)}) %collective-permute-start.10) | collective-permute-done | bytes 16416 | tf_op jit(solution)/shard_map/ppermute | solution.py:36
  87.4 0.6 copy-done.16
  88.0 1.1 collective-permute-start.14
  89.1 5.8 %all-to-all-start.2 = ((f32[16,16,512]{2,1,0:T(8,128)}), f32[16,16,512]{2,1,0:T(8,128)S(1)}, u32[]{:S(2)}, u32[]{:S(2)}) async-start(f32[16,16,512]{2,1,0:T(8,128)} %bitcast.65), calls=%async_computation.2 | async-start | bytes 1048576 | tf_op jit(solution)/shard_map/all_to_all | solution.py:362
  95.6 0.7 collective-permute-done.9.refs_9_
  96.3 0.6 copy-done.20
  97.1 7.4 %weight_shares.2.refs_1_.refs_0_ = f32[528,1024]{1,0:T(8,128)} custom-call(bf16[528,1024]{1,0:T(8,128)(2,1)} %get-tuple-element.26.refs_0_, bf16[528,1024]{1,0:T(8,128)(2,1)} %copy-done.3, bf16[2,528,1024]{2,1,0:T(8,128)(2,1)} %tied.6.refs_15_.refs_2_, bf16[2,528,1024]{2,1,0:T(8,128)(2,1)} %collective-permute-done.5.refs_3_, bf16[512,512]{1,0:T(8,128)(2,1)} %bitcast.71, ...), custom_call_target="tpu_custom_call" | custom-call | flops 1 | bytes 1 | tf_op jit(solution)/shard_map/weight_shares/pallas_call | solution.py:403
  104.9 1.2 copy-done.1
  106.0 0.9 slice_convert_fusion.1
  107.0 1.9 %collective-permute-start.12 = (f16[528,512]{1,0:T(8,128)(2,1)}, f16[528,512]{1,0:T(8,128)(2,1)S(1)}, u32[]{:S(2)}, u32[]{:S(2)}) collective-permute-start(f16[528,512]{1,0:T(8,128)(2,1)} %slice_convert_fusion.1), channel_id=1, source_target_pairs={{0,8},{8,0},{1,9},{9,1},{2,10},{10,2},{3,11},{11,3},{4,12},{12,4},... | collective-permute-start | bytes 1622024 | tf_op jit(solution)/shard_map/ppermute | solution.py:36
  108.8 1.8 %all-to-all-done.2.sums_ref = f32[16,16,512]{2,1,0:T(8,128)S(1)} async-done(((f32[16,16,512]{2,1,0:T(8,128)}), f32[16,16,512]{2,1,0:T(8,128)S(1)}, u32[]{:S(2)}, u32[]{:S(2)}) %all-to-all-start.2) | async-done | bytes 524320 | tf_op jit(solution)/shard_map/all_to_all | solution.py:362
  110.6 0.8 copy-done.9
  111.4 2.1 %row_grads.3.refs_8_ = bf16[16,512]{1,0:T(8,128)(2,1)} custom-call(s32[4]{0:T(128)} %pad_add_fusion.1.place_ref, f32[16,16,512]{2,1,0:T(8,128)} %copy-done.9, f32[64,512]{1,0:T(8,128)} %get-tuple-element.29.raw_ref, f32[576,128]{1,0:T(8,128)} %get-tuple-element.54.cos_ref.refs_11_, f32[576,128]{1,0:T(8,128)} %get-tuple-element.53.sin_ref.refs_12_, ...), custom_call_target="tpu_custom_call" | custom-call | flops 1 | bytes 1 | tf_op jit(solution)/shard_map/row_grads/pallas_call | solution.py:443
  113.5 1.3 collective-permute-start.17
  115.3 2.1 %collective-permute-done.17.refs_10_ = bf16[16,512]{1,0:T(8,128)(2,1)S(1)} collective-permute-done((bf16[16,512]{1,0:T(8,128)(2,1)}, bf16[16,512]{1,0:T(8,128)(2,1)S(1)}, u32[]{:S(2)}, u32[]{:S(2)}) %collective-permute-start.17) | collective-permute-done | bytes 16416 | tf_op jit(solution)/shard_map/ppermute | solution.py:36
  117.4 0.7 collective-permute-done.18.refs_11_
  118.2 0.6 copy-done.19
  118.8 7.3 %weight_shares.3 = f32[528,1024]{1,0:T(8,128)} custom-call(bf16[528,1024]{1,0:T(8,128)(2,1)} %get-tuple-element.26.refs_0_, bf16[528,1024]{1,0:T(8,128)(2,1)} %copy-done.3, bf16[2,528,1024]{2,1,0:T(8,128)(2,1)} %tied.6.refs_15_.refs_2_, bf16[2,528,1024]{2,1,0:T(8,128)(2,1)} %collective-permute-done.5.refs_3_, bf16[512,512]{1,0:T(8,128)(2,1)} %tied.9.refs_4_, ...), custom_call_target="tpu_custom_call" | custom-call | flops 1 | bytes 1 | tf_op jit(solution)/shard_map/weight_shares/pallas_call | solution.py:403
  126.1 1.3 slice_convert_fusion
  127.4 0.7 multiply_exponential_fusion.3
  128.2 0.7 multiply_exponential_fusion.5
  128.9 1.4 fusion.50
  130.5 1.6 collective-permute-start.21
  132.1 1.1 collective-permute-start.22
  133.3 2.6 %collective-permute-start.19 = (f16[528,128]{1,0:T(8,128)(2,1)S(1)}, f16[528,128]{1,0:T(8,128)(2,1)S(1)}, u32[]{:S(2)}, u32[]{:S(2)}) collective-permute-start(f16[528,128]{1,0:T(8,128)(2,1)S(1)} %get-tuple-element.50), channel_id=1, source_target_pairs={{0,1},{1,0},{2,3},{3,2},{4,5},{5,4},{6,7},{7,6},{8,9},{9,8},{10,11... | collective-permute-start | bytes 405512 | tf_op jit(solution)/shard_map/ppermute | solution.py:36
  136.0 2.9 %collective-permute-done.21 = f16[528,128]{1,0:T(8,128)(2,1)S(1)} collective-permute-done((f16[528,128]{1,0:T(8,128)(2,1)S(1)}, f16[528,128]{1,0:T(8,128)(2,1)S(1)}, u32[]{:S(2)}, u32[]{:S(2)}) %collective-permute-start.21) | collective-permute-done | bytes 135200 | tf_op jit(solution)/shard_map/ppermute | solution.py:36
  138.9 5.6 %collective-permute-done.20 = f16[528,128]{1,0:T(8,128)(2,1)S(1)} collective-permute-done((f16[528,128]{1,0:T(8,128)(2,1)S(1)}, f16[528,128]{1,0:T(8,128)(2,1)S(1)}, u32[]{:S(2)}, u32[]{:S(2)}) %collective-permute-start.20) | collective-permute-done | bytes 135200 | tf_op jit(solution)/shard_map/ppermute | solution.py:36
  144.6 1.9 %collective-permute-done.22 = f16[528,512]{1,0:T(8,128)(2,1)S(1)} collective-permute-done((f16[528,512]{1,0:T(8,128)(2,1)S(1)}, f16[528,512]{1,0:T(8,128)(2,1)S(1)}, u32[]{:S(2)}, u32[]{:S(2)}) %collective-permute-start.22) | collective-permute-done | bytes 540704 | tf_op jit(solution)/shard_map/ppermute | solution.py:36
  146.5 0.7 multiply_exponential_fusion
  147.2 0.7 multiply_exponential_fusion.2
  148.0 1.4 fusion.48
  149.5 2.4 %collective-permute-start.25 = (f16[528,128]{1,0:T(8,128)(2,1)S(1)}, f16[528,128]{1,0:T(8,128)(2,1)S(1)}, u32[]{:S(2)}, u32[]{:S(2)}) collective-permute-start(f16[528,128]{1,0:T(8,128)(2,1)S(1)} %get-tuple-element.49), channel_id=1, source_target_pairs={{0,3},{1,2},{2,1},{3,0},{4,7},{5,6},{6,5},{7,4},{8,11},{9,10},{10,... | collective-permute-start | bytes 405512 | tf_op jit(solution)/shard_map/ppermute | solution.py:36
  152.0 0.7 collective-permute-start.26
  152.7 2.0 %collective-permute-start.23 = (f16[528,128]{1,0:T(8,128)(2,1)S(1)}, f16[528,128]{1,0:T(8,128)(2,1)S(1)}, u32[]{:S(2)}, u32[]{:S(2)}) collective-permute-start(f16[528,128]{1,0:T(8,128)(2,1)S(1)} %get-tuple-element.47), channel_id=1, source_target_pairs={{0,1},{1,0},{2,3},{3,2},{4,5},{5,4},{6,7},{7,6},{8,9},{9,8},{10,11... | collective-permute-start | bytes 405512 | tf_op jit(solution)/shard_map/ppermute | solution.py:36
  154.8 3.1 %collective-permute-done.25 = f16[528,128]{1,0:T(8,128)(2,1)S(1)} collective-permute-done((f16[528,128]{1,0:T(8,128)(2,1)S(1)}, f16[528,128]{1,0:T(8,128)(2,1)S(1)}, u32[]{:S(2)}, u32[]{:S(2)}) %collective-permute-start.25) | collective-permute-done | bytes 135200 | tf_op jit(solution)/shard_map/ppermute | solution.py:36
  157.9 4.5 %collective-permute-done.24 = f16[528,128]{1,0:T(8,128)(2,1)S(1)} collective-permute-done((f16[528,128]{1,0:T(8,128)(2,1)S(1)}, f16[528,128]{1,0:T(8,128)(2,1)S(1)}, u32[]{:S(2)}, u32[]{:S(2)}) %collective-permute-start.24) | collective-permute-done | bytes 135200 | tf_op jit(solution)/shard_map/ppermute | solution.py:36
  162.5 0.8 collective-permute-start.27
  163.4 7.4 %collective-permute-done.27 = f32[512,128]{1,0:T(8,128)S(1)} collective-permute-done((f32[512,128]{1,0:T(8,128)S(1)}, f32[512,128]{1,0:T(8,128)S(1)}, u32[]{:S(2)}, u32[]{:S(2)}) %collective-permute-start.27) | collective-permute-done | bytes 262176 | tf_op jit(solution)/shard_map/ppermute | solution.py:36
  171.0 1.0 copy.26
  172.0 1.0 copy.27
  (95 shorter events, 5.0 us)
Async XLA Ops:
  5.5 50.2 %collective-permute-start.4 = (bf16[2,528,1024]{2,1,0:T(8,128)(2,1)}, bf16[2,528,1024]{2,1,0:T(8,128)(2,1)S(1)}, u32[]{:S(2)}, u32[]{:S(2)}) collective-permute-start(bf16[2,528,1024]{2,1,0:T(8,128)(2,1)} %get-tuple-element.18.after_ref), channel_id=1, source_target_pairs={{0,16},{16,0},{1,17},{17,1},{2,18},{18,2},{3,19},{19,3},{4,20},{20... | collective-permute-start | bytes 6488072 | tf_op jit(solution)/shard_map/ppermute | solution.py:36
  22.4 18.4 %collective-permute-start = (bf16[64,1024]{1,0:T(8,128)(2,1)}, bf16[64,1024]{1,0:T(8,128)(2,1)S(1)}, u32[]{:S(2)}, u32[]{:S(2)}) collective-permute-start(bf16[64,1024]{1,0:T(8,128)(2,1)} %get-tuple-element.19.refs_0_.refs_4_), channel_id=1, source_target_pairs={{0,4},{4,0},{1,5},{5,1},{2,6},{6,2},{3,7},{7,3},{8,12},{12,8},{9,1... | collective-permute-start | bytes 393224 | tf_op jit(solution)/shard_map/ppermute | solution.py:36
  22.5 18.3 %collective-permute-start.1 = (bf16[64,1024]{1,0:T(8,128)(2,1)}, bf16[64,1024]{1,0:T(8,128)(2,1)S(1)}, u32[]{:S(2)}, u32[]{:S(2)}) collective-permute-start(bf16[64,1024]{1,0:T(8,128)(2,1)} %get-tuple-element.19.refs_0_.refs_4_), channel_id=1, source_target_pairs={{0,8},{8,0},{1,9},{9,1},{2,10},{10,2},{3,11},{11,3},{4,12},{12,4},... | collective-permute-start | bytes 393224 | tf_op jit(solution)/shard_map/ppermute | solution.py:36
  24.1 16.7 %collective-permute-start.2 = (bf16[64,1024]{1,0:T(8,128)(2,1)}, bf16[64,1024]{1,0:T(8,128)(2,1)S(1)}, u32[]{:S(2)}, u32[]{:S(2)}) collective-permute-start(bf16[64,1024]{1,0:T(8,128)(2,1)} %get-tuple-element.19.refs_0_.refs_4_), channel_id=1, source_target_pairs={{0,12},{4,8},{8,4},{12,0},{1,13},{5,9},{9,5},{13,1},{2,14},{6,10},... | collective-permute-start | bytes 393224 | tf_op jit(solution)/shard_map/ppermute | solution.py:36
  26.3 12.4 %all-to-all-start = ((f32[16,3,8]{2,1,0:T(4,128)}), f32[16,3,8]{2,1,0:T(4,128)S(1)}, u32[]{:S(2)}, u32[]{:S(2)}) async-start(f32[16,3,8]{2,1,0:T(4,128)} %broadcast_in_dim.20), calls=%async_computation | async-start | bytes 65536 | tf_op jit(solution)/shard_map/all_to_all | solution.py:362
  40.8 0.7 copy-start.6
  40.8 0.7 copy-start.7
  40.8 0.7 copy-start.8
  55.8 1.4 copy-start
  57.2 6.7 %copy-start.11 = (bf16[2,2,128,512]{3,2,1,0:T(8,128)(2,1)S(1)}, bf16[2,2,128,512]{3,2,1,0:T(8,128)(2,1)}, u32[]{:S(2)}) copy-start(bf16[2,2,128,512]{3,2,1,0:T(8,128)(2,1)} %get-tuple-element.24) | copy-start | bytes 1572868
  57.2 39.0 %collective-permute-start.5 = (bf16[2,528,1024]{2,1,0:T(8,128)(2,1)}, bf16[2,528,1024]{2,1,0:T(8,128)(2,1)}, u32[]{:S(2)}, u32[]{:S(2)}) collective-permute-start(bf16[2,528,1024]{2,1,0:T(8,128)(2,1)} %tied.6.refs_15_.refs_2_), channel_id=1, source_target_pairs={{0,4},{4,0},{1,5},{5,1},{2,6},{6,2},{3,7},{7,3},{8,12},{12,8},{9,1... | collective-permute-start | bytes 6488072 | tf_op jit(solution)/shard_map/ppermute | solution.py:36
  57.2 8.3 %collective-permute-start.3 = (bf16[528,1024]{1,0:T(8,128)(2,1)}, bf16[528,1024]{1,0:T(8,128)(2,1)S(1)}, u32[]{:S(2)}, u32[]{:S(2)}) collective-permute-start(bf16[528,1024]{1,0:T(8,128)(2,1)} %get-tuple-element.23), channel_id=1, source_target_pairs={{0,4},{4,0},{1,5},{5,1},{2,6},{6,2},{3,7},{7,3},{8,12},{12,8},{9,1... | collective-permute-start | bytes 3244040 | tf_op jit(solution)/shard_map/ppermute | solution.py:36
  57.7 22.3 %all-to-all-start.1 = ((f32[16,16,512]{2,1,0:T(8,128)}), f32[16,16,512]{2,1,0:T(8,128)S(1)}, u32[]{:S(2)}, u32[]{:S(2)}) async-start(f32[16,16,512]{2,1,0:T(8,128)} %bitcast.19), calls=%async_computation.1 | async-start | bytes 1048576 | tf_op jit(solution)/shard_map/all_to_all | solution.py:362
  64.0 15.2 %collective-permute-start.7 = (bf16[512,512]{1,0:T(8,128)(2,1)S(1)}, bf16[512,512]{1,0:T(8,128)(2,1)S(1)}, u32[]{:S(2)}, u32[]{:S(2)}) collective-permute-start(bf16[512,512]{1,0:T(8,128)(2,1)S(1)} %bitcast.72), channel_id=1, source_target_pairs={{0,16},{16,0},{1,17},{17,1},{2,18},{18,2},{3,19},{19,3},{4,20},{20... | collective-permute-start | bytes 1572872 | tf_op jit(solution)/shard_map/ppermute | solution.py:36
  65.5 1.0 copy-start.3
  79.2 0.8 copy-start.4
  80.0 5.0 %copy-start.5 = (bf16[512,512]{1,0:T(8,128)(2,1)S(1)}, bf16[512,512]{1,0:T(8,128)(2,1)}, u32[]{:S(2)}) copy-start(bf16[512,512]{1,0:T(8,128)(2,1)} %tied.7.refs_1_.refs_6_) | copy-start | bytes 1572868
  80.0 0.8 copy-start.10
  82.9 12.0 %copy-start.14 = (bf16[16,512]{1,0:T(8,128)(2,1)S(1)}, bf16[16,512]{1,0:T(8,128)(2,1)}, u32[]{:S(2)}) copy-start(bf16[16,512]{1,0:T(8,128)(2,1)} %row_grads.2.refs_8_) | copy-start | bytes 49156
  82.9 3.9 %collective-permute-start.10 = (bf16[16,512]{1,0:T(8,128)(2,1)}, bf16[16,512]{1,0:T(8,128)(2,1)S(1)}, u32[]{:S(2)}, u32[]{:S(2)}) collective-permute-start(bf16[16,512]{1,0:T(8,128)(2,1)} %row_grads.2.refs_8_), channel_id=1, source_target_pairs={{0,16},{16,0},{1,17},{17,1},{2,18},{18,2},{3,19},{19,3},{4,20},{20... | collective-permute-start | bytes 49160 | tf_op jit(solution)/shard_map/ppermute | solution.py:36
  84.0 3.4 %collective-permute-start.11 = (bf16[16,512]{1,0:T(8,128)(2,1)}, bf16[16,512]{1,0:T(8,128)(2,1)S(1)}, u32[]{:S(2)}, u32[]{:S(2)}) collective-permute-start(bf16[16,512]{1,0:T(8,128)(2,1)} %row_grads.2.refs_8_), channel_id=1, source_target_pairs={{0,20},{4,16},{16,4},{20,0},{1,21},{5,17},{17,5},{21,1},{2,22},{6,... | collective-permute-start | bytes 49160 | tf_op jit(solution)/shard_map/ppermute | solution.py:36
  84.4 11.0 %collective-permute-start.6 = (bf16[512,512]{1,0:T(8,128)(2,1)S(1)}, bf16[512,512]{1,0:T(8,128)(2,1)S(1)}, u32[]{:S(2)}, u32[]{:S(2)}) collective-permute-start(bf16[512,512]{1,0:T(8,128)(2,1)S(1)} %bitcast.73), channel_id=1, source_target_pairs={{0,4},{4,0},{1,5},{5,1},{2,6},{6,2},{3,7},{7,3},{8,12},{12,8},{9,1... | collective-permute-start | bytes 1572872 | tf_op jit(solution)/shard_map/ppermute | solution.py:36
  85.0 11.2 %collective-permute-start.8 = (bf16[512,512]{1,0:T(8,128)(2,1)S(1)}, bf16[512,512]{1,0:T(8,128)(2,1)S(1)}, u32[]{:S(2)}, u32[]{:S(2)}) collective-permute-start(bf16[512,512]{1,0:T(8,128)(2,1)S(1)} %copy-done.5), channel_id=1, source_target_pairs={{0,4},{4,0},{1,5},{5,1},{2,6},{6,2},{3,7},{7,3},{8,12},{12,8},{9,1... | collective-permute-start | bytes 1572872 | tf_op jit(solution)/shard_map/ppermute | solution.py:36
  86.8 0.6 copy-start.15
  87.4 0.6 copy-start.16
  88.0 7.4 %copy-start.2 = (bf16[512,512]{1,0:T(8,128)(2,1)S(1)}, bf16[512,512]{1,0:T(8,128)(2,1)}, u32[]{:S(2)}) copy-start(bf16[512,512]{1,0:T(8,128)(2,1)} %tied.9.refs_4_) | copy-start | bytes 1572868
  88.0 16.4 %collective-permute-start.14 = (bf16[512,512]{1,0:T(8,128)(2,1)}, bf16[512,512]{1,0:T(8,128)(2,1)}, u32[]{:S(2)}, u32[]{:S(2)}) collective-permute-start(bf16[512,512]{1,0:T(8,128)(2,1)} %tied.9.refs_4_), channel_id=1, source_target_pairs={{0,16},{16,0},{1,17},{17,1},{2,18},{18,2},{3,19},{19,3},{4,20},{20... | collective-permute-start | bytes 1572872 | tf_op jit(solution)/shard_map/ppermute | solution.py:36
  89.1 21.5 %all-to-all-start.2 = ((f32[16,16,512]{2,1,0:T(8,128)}), f32[16,16,512]{2,1,0:T(8,128)S(1)}, u32[]{:S(2)}, u32[]{:S(2)}) async-start(f32[16,16,512]{2,1,0:T(8,128)} %bitcast.65), calls=%async_computation.2 | async-start | bytes 1048576 | tf_op jit(solution)/shard_map/all_to_all | solution.py:362
  94.9 1.3 collective-permute-start.9
  95.4 0.8 copy-start.12
  95.4 19.4 %collective-permute-start.13 = (bf16[512,512]{1,0:T(8,128)(2,1)S(1)}, bf16[512,512]{1,0:T(8,128)(2,1)}, u32[]{:S(2)}, u32[]{:S(2)}) collective-permute-start(bf16[512,512]{1,0:T(8,128)(2,1)S(1)} %copy-done.2), channel_id=1, source_target_pairs={{0,4},{4,0},{1,5},{5,1},{2,6},{6,2},{3,7},{7,3},{8,12},{12,8},{9,1... | collective-permute-start | bytes 1572872 | tf_op jit(solution)/shard_map/ppermute | solution.py:36
  96.2 0.6 copy-start.20
  96.2 0.8 copy-start.13
  104.4 1.6 copy-start.1
  104.5 13.7 %collective-permute-start.15 = (bf16[512,512]{1,0:T(8,128)(2,1)}, bf16[512,512]{1,0:T(8,128)(2,1)}, u32[]{:S(2)}, u32[]{:S(2)}) collective-permute-start(bf16[512,512]{1,0:T(8,128)(2,1)} %tied.10.refs_6_), channel_id=1, source_target_pairs={{0,4},{4,0},{1,5},{5,1},{2,6},{6,2},{3,7},{7,3},{8,12},{12,8},{9,1... | collective-permute-start | bytes 1572872 | tf_op jit(solution)/shard_map/ppermute | solution.py:36
  107.0 20.5 %collective-permute-start.12 = (f16[528,512]{1,0:T(8,128)(2,1)}, f16[528,512]{1,0:T(8,128)(2,1)S(1)}, u32[]{:S(2)}, u32[]{:S(2)}) collective-permute-start(f16[528,512]{1,0:T(8,128)(2,1)} %slice_convert_fusion.1), channel_id=1, source_target_pairs={{0,8},{8,0},{1,9},{9,1},{2,10},{10,2},{3,11},{11,3},{4,12},{12,4},... | collective-permute-start | bytes 1622024 | tf_op jit(solution)/shard_map/ppermute | solution.py:36
  110.6 0.8 copy-start.9
  113.5 1.9 %collective-permute-start.16 = (bf16[16,512]{1,0:T(8,128)(2,1)}, bf16[16,512]{1,0:T(8,128)(2,1)S(1)}, u32[]{:S(2)}, u32[]{:S(2)}) collective-permute-start(bf16[16,512]{1,0:T(8,128)(2,1)} %row_grads.3.refs_8_), channel_id=1, source_target_pairs={{0,4},{4,0},{1,5},{5,1},{2,6},{6,2},{3,7},{7,3},{8,12},{12,8},{9,1... | collective-permute-start | bytes 49160 | tf_op jit(solution)/shard_map/ppermute | solution.py:36
  113.5 3.9 %collective-permute-start.17 = (bf16[16,512]{1,0:T(8,128)(2,1)}, bf16[16,512]{1,0:T(8,128)(2,1)S(1)}, u32[]{:S(2)}, u32[]{:S(2)}) collective-permute-start(bf16[16,512]{1,0:T(8,128)(2,1)} %row_grads.3.refs_8_), channel_id=1, source_target_pairs={{0,16},{16,0},{1,17},{17,1},{2,18},{18,2},{3,19},{19,3},{4,20},{20... | collective-permute-start | bytes 49160 | tf_op jit(solution)/shard_map/ppermute | solution.py:36
  114.8 3.4 %collective-permute-start.18 = (bf16[16,512]{1,0:T(8,128)(2,1)}, bf16[16,512]{1,0:T(8,128)(2,1)S(1)}, u32[]{:S(2)}, u32[]{:S(2)}) collective-permute-start(bf16[16,512]{1,0:T(8,128)(2,1)} %row_grads.3.refs_8_), channel_id=1, source_target_pairs={{0,20},{4,16},{16,4},{20,0},{1,21},{5,17},{17,5},{21,1},{2,22},{6,... | collective-permute-start | bytes 49160 | tf_op jit(solution)/shard_map/ppermute | solution.py:36
  115.3 2.8 %copy-start.17 = (bf16[16,512]{1,0:T(8,128)(2,1)}, bf16[16,512]{1,0:T(8,128)(2,1)S(1)}, u32[]{:S(2)}) copy-start(bf16[16,512]{1,0:T(8,128)(2,1)S(1)} %collective-permute-done.16.refs_9_) | copy-start | bytes 49156
  117.4 0.7 copy-start.18
  118.2 0.6 copy-start.19
  130.5 8.4 %collective-permute-start.21 = (f16[528,128]{1,0:T(8,128)(2,1)S(1)}, f16[528,128]{1,0:T(8,128)(2,1)S(1)}, u32[]{:S(2)}, u32[]{:S(2)}) collective-permute-start(f16[528,128]{1,0:T(8,128)(2,1)S(1)} %get-tuple-element.52), channel_id=1, source_target_pairs={{0,3},{1,2},{2,1},{3,0},{4,7},{5,6},{6,5},{7,4},{8,11},{9,10},{10,... | collective-permute-start | bytes 405512 | tf_op jit(solution)/shard_map/ppermute | solution.py:36
  132.1 14.4 %collective-permute-start.22 = (f16[528,512]{1,0:T(8,128)(2,1)S(1)}, f16[528,512]{1,0:T(8,128)(2,1)S(1)}, u32[]{:S(2)}, u32[]{:S(2)}) collective-permute-start(f16[528,512]{1,0:T(8,128)(2,1)S(1)} %slice_convert_fusion), channel_id=1, source_target_pairs={{0,8},{8,0},{1,9},{9,1},{2,10},{10,2},{3,11},{11,3},{4,12},{12,4},... | collective-permute-start | bytes 1622024 | tf_op jit(solution)/shard_map/ppermute | solution.py:36
  133.2 11.3 %collective-permute-start.20 = (f16[528,128]{1,0:T(8,128)(2,1)S(1)}, f16[528,128]{1,0:T(8,128)(2,1)S(1)}, u32[]{:S(2)}, u32[]{:S(2)}) collective-permute-start(f16[528,128]{1,0:T(8,128)(2,1)S(1)} %get-tuple-element.51), channel_id=1, source_target_pairs={{0,2},{1,3},{2,0},{3,1},{4,6},{5,7},{6,4},{7,5},{8,10},{9,11},{10,... | collective-permute-start | bytes 405512 | tf_op jit(solution)/shard_map/ppermute | solution.py:36
  133.3 11.2 %collective-permute-start.19 = (f16[528,128]{1,0:T(8,128)(2,1)S(1)}, f16[528,128]{1,0:T(8,128)(2,1)S(1)}, u32[]{:S(2)}, u32[]{:S(2)}) collective-permute-start(f16[528,128]{1,0:T(8,128)(2,1)S(1)} %get-tuple-element.50), channel_id=1, source_target_pairs={{0,1},{1,0},{2,3},{3,2},{4,5},{5,4},{6,7},{7,6},{8,9},{9,8},{10,11... | collective-permute-start | bytes 405512 | tf_op jit(solution)/shard_map/ppermute | solution.py:36
  149.5 8.4 %collective-permute-start.25 = (f16[528,128]{1,0:T(8,128)(2,1)S(1)}, f16[528,128]{1,0:T(8,128)(2,1)S(1)}, u32[]{:S(2)}, u32[]{:S(2)}) collective-permute-start(f16[528,128]{1,0:T(8,128)(2,1)S(1)} %get-tuple-element.49), channel_id=1, source_target_pairs={{0,3},{1,2},{2,1},{3,0},{4,7},{5,6},{6,5},{7,4},{8,11},{9,10},{10,... | collective-permute-start | bytes 405512 | tf_op jit(solution)/shard_map/ppermute | solution.py:36
  152.0 11.4 %collective-permute-start.26 = (f32[512,128]{1,0:T(8,128)S(1)}, f32[512,128]{1,0:T(8,128)S(1)}, u32[]{:S(2)}, u32[]{:S(2)}) collective-permute-start(f32[512,128]{1,0:T(8,128)S(1)} %fusion.11), channel_id=1, source_target_pairs={{0,16},{16,0},{1,17},{17,1},{2,18},{18,2},{3,19},{19,3},{4,20},{20... | collective-permute-start | bytes 786440 | tf_op jit(solution)/shard_map/ppermute | solution.py:36
  152.7 9.7 %collective-permute-start.24 = (f16[528,128]{1,0:T(8,128)(2,1)S(1)}, f16[528,128]{1,0:T(8,128)(2,1)S(1)}, u32[]{:S(2)}, u32[]{:S(2)}) collective-permute-start(f16[528,128]{1,0:T(8,128)(2,1)S(1)} %get-tuple-element.48), channel_id=1, source_target_pairs={{0,2},{1,3},{2,0},{3,1},{4,6},{5,7},{6,4},{7,5},{8,10},{9,11},{10,... | collective-permute-start | bytes 405512 | tf_op jit(solution)/shard_map/ppermute | solution.py:36
  152.7 9.7 %collective-permute-start.23 = (f16[528,128]{1,0:T(8,128)(2,1)S(1)}, f16[528,128]{1,0:T(8,128)(2,1)S(1)}, u32[]{:S(2)}, u32[]{:S(2)}) collective-permute-start(f16[528,128]{1,0:T(8,128)(2,1)S(1)} %get-tuple-element.47), channel_id=1, source_target_pairs={{0,1},{1,0},{2,3},{3,2},{4,5},{5,4},{6,7},{7,6},{8,9},{9,8},{10,11... | collective-permute-start | bytes 405512 | tf_op jit(solution)/shard_map/ppermute | solution.py:36
  162.5 8.3 %collective-permute-start.27 = (f32[512,128]{1,0:T(8,128)S(1)}, f32[512,128]{1,0:T(8,128)S(1)}, u32[]{:S(2)}, u32[]{:S(2)}) collective-permute-start(f32[512,128]{1,0:T(8,128)S(1)} %fusion.8), channel_id=1, source_target_pairs={{0,16},{16,0},{1,17},{17,1},{2,18},{18,2},{3,19},{19,3},{4,20},{20... | collective-permute-start | bytes 786440 | tf_op jit(solution)/shard_map/ppermute | solution.py:36

commit v8 on v7

--- a/solution.py
+++ b/solution.py
@@ -553,7 +553,7 @@
     wide = n_resp * block
 
     def chip_terms(shares):
-        return [shares[:, d * wide : (d + 1) * wide].astype(jnp.float16) for d in range(1, n_chip)]
+        return [exchange(shares[:, d * wide : (d + 1) * wide].astype(jnp.float16), [("chip", d)]) for d in range(1, n_chip)]
 
     def resp_terms(kept, sent):
         exponents = [exponent_of(x) for x in [kept] + sent]
@@ -590,10 +590,8 @@
     hops_late = [tied(x, shares_early) for x in hops_late]
     tokens_late = row_tokens(sums_late, early, [shares_early])
     shares_late = weight_shares(parts, everywhere(g_late, hops_late), tokens_late)
-    sent_early = [exchange(x, [("chip", d)]) for d, x in enumerate(chip_terms(shares_early), 1)]
-    payload_late = chip_terms(shares_late)
-    sent_early = [lax.optimization_barrier((x, payload_late[0]))[0] for x in sent_early]
-    sent_late = [exchange(x, [("chip", d)]) for d, x in enumerate(payload_late, 1)]
+    sent_early = chip_terms(shares_early)
+    sent_late = chip_terms(shares_late)
     half_early, pieces_early = resp_terms(shares_early[:, :wide], sent_early)
     done_early = finish(half_early, pieces_early)
     sent_late = [lax.optimization_barrier((x, done_early[0]))[0] for x in sent_late]

time: 174 us -> 170 us (0.977)
  other arithmetic: 12.6 us -> 9.31 us
    another operation x6, other arithmetic: 5.16 us -> 3.14 us
    unnamed x43 -> x45, local copies, waits for them, and re-layouts: 8.82 us -> 9.51 us
  transfers between devices with their start and end apart: 31 -> 31, of which waited for: 14 -> 13; matrix products, arithmetic and copies ran while one was open for 4% -> 3% of each run, Pallas kernels for 32% -> 33%
where the time goes in v8:
time: 170 us
  Pallas kernels  60.3 us (35%)
  starting transfers between devices  44.1 us (26%)
  waiting for transfers between devices  39.3 us (23%)
  local copies, waits for them, and re-layouts  12.3 us (7%)
  other arithmetic  9.31 us (5%)
  between operations  4.28 us (3%)
    ppermute x28, waiting for transfers between devices, exchange(): return lax.ppermute(value, names, [(j, j ^ mask) for j in range(total)])  31.7 us
    ppermute x28, starting transfers between devices, exchange(): return lax.ppermute(value, names, [(j, j ^ mask) for j in range(total)])  26 us
    pallas_call x2, Pallas kernels, attend(): pl.pallas_call(functools.partial(attend_kernel, parts, fold), grid=(per,)...  25.4 us
    all_to_all x3, starting transfers between devices, everyone(): return lax.all_to_all(value, names, split_axis=0, concat_axis=0, tiled=True)  18.1 us
    pallas_call x2, Pallas kernels, weight_shares(): pl.pallas_call(functools.partial(weight_kernel, parts, len(tokens)), grid...  14.7 us
    pallas_call x1, Pallas kernels, project(): pl.pallas_call(functools.partial(project_kernel, groups, counts), in_spec...  11.8 us
    unnamed x45, local copies, waits for them, and re-layouts  9.51 us
    all_to_all x3, waiting for transfers between devices, everyone(): return lax.all_to_all(value, names, split_axis=0, concat_axis=0, tiled=True)  7.64 us
  transfers between devices with their start and end apart: 31, of which 13 were waited for; matrix products, arithmetic and copies ran while one was open for 3% of the time, Pallas kernels for 33%

profile of v8, /device:TPU:0, one launch (start us, length us, event | category | flops | bytes accessed | tf_op | source)
XLA Modules:
  0.0 169.6 jit_solution(3395948866761134559)
XLA Ops:
  0.6 0.6 pad_add_fusion.1.place_ref
  1.3 4.3 %select_columns.1 = (bf16[528,1024]{1,0:T(8,128)(2,1)}, bf16[2,528,1024]{2,1,0:T(8,128)(2,1)}) custom-call(s32[4]{0:T(128)} %pad_add_fusion.1.place_ref, bf16[512,4096]{1,0:T(8,128)(2,1)} %bitcast.54, bf16[64,4096]{1,0:T(8,128)(2,1)} %bitcast.63), custom_call_target="tpu_custom_call" | custom-call | flops 1 | bytes 1 | tf_op jit(solution)/shard_map/select_columns/pallas_call | solution.py:104
  5.6 3.0 %collective-permute-start.4 = (bf16[2,528,1024]{2,1,0:T(8,128)(2,1)}, bf16[2,528,1024]{2,1,0:T(8,128)(2,1)S(1)}, u32[]{:S(2)}, u32[]{:S(2)}) collective-permute-start(bf16[2,528,1024]{2,1,0:T(8,128)(2,1)} %get-tuple-element.17.after_ref), channel_id=1, source_target_pairs={{0,16},{16,0},{1,17},{17,1},{2,18},{18,2},{3,19},{19,3},{4,20},{20... | collective-permute-start | bytes 6488072 | tf_op jit(solution)/shard_map/ppermute | solution.py:36
  8.6 2.0 %fusion.5 = (f32[576,128]{1,0:T(8,128)}, f32[576,128]{1,0:T(8,128)}) fusion(f32[128]{0:T(128)S(1)} %get-tuple-element.59, f32[128]{0:T(128)S(1)} %get-tuple-element.60, f32[576]{0:T(1024)S(1)} %select_convert_fusion), kind=kLoop, calls=%fused_computation.27 | loop fusion | flops 147456 | bytes 593152 | tf_op jit(solution)/shard_map/mul | solution.py:46
  10.5 11.8 %project.1 = (f32[64,512]{1,0:T(8,128)}, bf16[64,1024]{1,0:T(8,128)(2,1)}, f32[512,512]{1,0:T(8,128)}, bf16[512,1024]{1,0:T(8,128)(2,1)}, bf16[528,1024]{1,0:T(8,128)(2,1)}) custom-call(s32[4]{0:T(128)} %pad_add_fusion.1.place_ref, bf16[64,4096]{1,0:T(8,128)(2,1)} %bitcast.64, bf16[512,4096]{1,0:T(8,128)(2,1)} %bitcast.55, bf16[4096,512]{1,0:T(8,128)(2,1)} %wk_hbm.1, ...), custom_call_target="tpu_custom_call" | custom-call | flops 1 | bytes 1 | tf_op jit(solution)/shard_map/project/pallas_call | solution.py:184
  22.5 1.6 collective-permute-start.1
  25.7 0.6 broadcast_in_dim.20
  26.3 5.9 %all-to-all-start = ((f32[16,3,8]{2,1,0:T(4,128)}), f32[16,3,8]{2,1,0:T(4,128)S(1)}, u32[]{:S(2)}, u32[]{:S(2)}) async-start(f32[16,3,8]{2,1,0:T(4,128)} %broadcast_in_dim.20), calls=%async_computation | async-start | bytes 65536 | tf_op jit(solution)/shard_map/all_to_all | solution.py:362
  32.9 0.6 pad_add_fusion.ints_ref
  33.5 5.3 %all-to-all-done = f32[16,3,8]{2,1,0:T(4,128)S(1)} async-done(((f32[16,3,8]{2,1,0:T(4,128)}), f32[16,3,8]{2,1,0:T(4,128)S(1)}, u32[]{:S(2)}, u32[]{:S(2)}) %all-to-all-start) | async-done | bytes 1568 | tf_op jit(solution)/shard_map/all_to_all | solution.py:362
  38.8 0.6 select_reduce_fusion
  40.8 0.6 copy-done.5
  41.5 12.7 %attend.2 = (bf16[512,2048]{1,0:T(8,128)(2,1)}, f32[256,512]{1,0:T(8,128)}, bf16[2,2,128,512]{3,2,1,0:T(8,128)(2,1)}) custom-call(f32[1]{0:T(128)S(6)} %div.21.coef_ref, s32[2]{0:T(128)} %pad_add_fusion.ints_ref, bf16[512,2048]{1,0:T(8,128)(2,1)} %bitcast.58, bf16[512,2048]{1,0:T(8,128)(2,1)} %bitcast.60, ...), custom_call_target="tpu_custom_call" | custom-call | flops 1 | bytes 1 | tf_op jit(solution)/shard_map/attend/pallas_call | solution.py:333
  54.2 1.6 collective-permute-done.4.refs_0_
  55.8 1.4 copy-done
  57.2 0.5 collective-permute-start.3
  57.7 6.2 %all-to-all-start.1 = ((f32[16,16,512]{2,1,0:T(8,128)}), f32[16,16,512]{2,1,0:T(8,128)S(1)}, u32[]{:S(2)}, u32[]{:S(2)}) async-start(f32[16,16,512]{2,1,0:T(8,128)} %bitcast.19), calls=%async_computation.1 | async-start | bytes 1048576 | tf_op jit(solution)/shard_map/all_to_all | solution.py:362
  64.0 1.6 collective-permute-start.7
  65.7 1.0 copy-done.2
  66.7 12.7 %attend.3 = (bf16[512,2048]{1,0:T(8,128)(2,1)}, f32[256,512]{1,0:T(8,128)}, bf16[2,2,128,512]{3,2,1,0:T(8,128)(2,1)}) custom-call(f32[1]{0:T(128)S(6)} %div.21.coef_ref, s32[2]{0:T(128)} %pad_add_fusion.ints_ref, bf16[512,2048]{1,0:T(8,128)(2,1)} %bitcast.59, bf16[512,2048]{1,0:T(8,128)(2,1)} %bitcast.61, ...), custom_call_target="tpu_custom_call", output_to_operand_aliasing={{0}: (17, {})} | custom-call | flops 1 | bytes 1 | tf_op jit(solution)/shard_map/attend/pallas_call | solution.py:333
  79.4 0.8 copy-done.4
  80.6 0.8 copy-done.9
  81.4 2.1 %row_grads.2.refs_8_ = bf16[16,512]{1,0:T(8,128)(2,1)} custom-call(s32[4]{0:T(128)} %pad_add_fusion.1.place_ref, f32[16,16,512]{2,1,0:T(8,128)} %copy-done.9, f32[64,512]{1,0:T(8,128)} %get-tuple-element.28.raw_ref, f32[576,128]{1,0:T(8,128)} %get-tuple-element.52.cos_ref.refs_11_, f32[576,128]{1,0:T(8,128)} %get-tuple-element.51.sin_ref.refs_12_, ...), custom_call_target="tpu_custom_call" | custom-call | flops 1 | bytes 1 | tf_op jit(solution)/shard_map/row_grads/pallas_call | solution.py:443
  83.4 0.6 collective-permute-start.10
  84.0 0.9 collective-permute-start.11
  84.9 2.6 %collective-permute-done.10.refs_10_.refs_1_ = bf16[16,512]{1,0:T(8,128)(2,1)S(1)} collective-permute-done((bf16[16,512]{1,0:T(8,128)(2,1)}, bf16[16,512]{1,0:T(8,128)(2,1)S(1)}, u32[]{:S(2)}, u32[]{:S(2)}) %collective-permute-start.10) | collective-permute-done | bytes 16416 | tf_op jit(solution)/shard_map/ppermute | solution.py:36
  87.5 0.6 copy-done.16
  88.1 0.6 copy-done.17
  88.7 0.8 collective-permute-start.17
  89.6 6.0 %all-to-all-start.2 = ((f32[16,16,512]{2,1,0:T(8,128)}), f32[16,16,512]{2,1,0:T(8,128)S(1)}, u32[]{:S(2)}, u32[]{:S(2)}) async-start(f32[16,16,512]{2,1,0:T(8,128)} %bitcast.65), calls=%async_computation.2 | async-start | bytes 1048576 | tf_op jit(solution)/shard_map/all_to_all | solution.py:362
  96.2 0.7 collective-permute-done.9.refs_9_
  96.9 0.6 copy-done.21
  97.4 7.3 %weight_shares.2.refs_1_.refs_0_ = f32[528,1024]{1,0:T(8,128)} custom-call(bf16[528,1024]{1,0:T(8,128)(2,1)} %get-tuple-element.25.refs_0_, bf16[528,1024]{1,0:T(8,128)(2,1)} %copy-done.2, bf16[2,528,1024]{2,1,0:T(8,128)(2,1)} %tied.6.refs_15_.refs_2_, bf16[2,528,1024]{2,1,0:T(8,128)(2,1)} %collective-permute-done.5.refs_3_, bf16[512,512]{1,0:T(8,128)(2,1)} %bitcast.71, ...), custom_call_target="tpu_custom_call" | custom-call | flops 1 | bytes 1 | tf_op jit(solution)/shard_map/weight_shares/pallas_call | solution.py:403
  104.8 1.3 slice_convert_fusion.1
  106.1 1.9 %collective-permute-start.12 = (f16[528,512]{1,0:T(8,128)(2,1)S(1)}, f16[528,512]{1,0:T(8,128)(2,1)S(1)}, u32[]{:S(2)}, u32[]{:S(2)}) collective-permute-start(f16[528,512]{1,0:T(8,128)(2,1)S(1)} %slice_convert_fusion.1), channel_id=1, source_target_pairs={{0,8},{8,0},{1,9},{9,1},{2,10},{10,2},{3,11},{11,3},{4,12},{12,4},... | collective-permute-start | bytes 1622024 | tf_op jit(solution)/shard_map/ppermute | solution.py:36
  108.0 0.8 copy-done.11
  108.8 2.4 %all-to-all-done.2.sums_ref = f32[16,16,512]{2,1,0:T(8,128)S(1)} async-done(((f32[16,16,512]{2,1,0:T(8,128)}), f32[16,16,512]{2,1,0:T(8,128)S(1)}, u32[]{:S(2)}, u32[]{:S(2)}) %all-to-all-start.2) | async-done | bytes 524320 | tf_op jit(solution)/shard_map/all_to_all | solution.py:362
  111.2 0.8 copy-done.8
  112.0 2.1 %row_grads.3.refs_8_ = bf16[16,512]{1,0:T(8,128)(2,1)} custom-call(s32[4]{0:T(128)} %pad_add_fusion.1.place_ref, f32[16,16,512]{2,1,0:T(8,128)} %copy-done.8, f32[64,512]{1,0:T(8,128)} %get-tuple-element.28.raw_ref, f32[576,128]{1,0:T(8,128)} %get-tuple-element.52.cos_ref.refs_11_, f32[576,128]{1,0:T(8,128)} %get-tuple-element.51.sin_ref.refs_12_, ...), custom_call_target="tpu_custom_call" | custom-call | flops 1 | bytes 1 | tf_op jit(solution)/shard_map/row_grads/pallas_call | solution.py:443
  114.1 1.2 collective-permute-start.20
  115.3 0.6 collective-permute-start.21
  115.9 2.1 %collective-permute-done.20.refs_10_ = bf16[16,512]{1,0:T(8,128)(2,1)S(1)} collective-permute-done((bf16[16,512]{1,0:T(8,128)(2,1)}, bf16[16,512]{1,0:T(8,128)(2,1)S(1)}, u32[]{:S(2)}, u32[]{:S(2)}) %collective-permute-start.20) | collective-permute-done | bytes 16416 | tf_op jit(solution)/shard_map/ppermute | solution.py:36
  118.0 0.7 collective-permute-done.21.refs_11_
  118.7 0.6 copy-done.20
  119.3 0.8 copy-done.14
  120.1 7.4 %weight_shares.3 = f32[528,1024]{1,0:T(8,128)} custom-call(bf16[528,1024]{1,0:T(8,128)(2,1)} %get-tuple-element.25.refs_0_, bf16[528,1024]{1,0:T(8,128)(2,1)} %copy-done.2, bf16[2,528,1024]{2,1,0:T(8,128)(2,1)} %tied.6.refs_15_.refs_2_, bf16[2,528,1024]{2,1,0:T(8,128)(2,1)} %collective-permute-done.5.refs_3_, bf16[512,512]{1,0:T(8,128)(2,1)} %tied.9.refs_4_, ...), custom_call_target="tpu_custom_call" | custom-call | flops 1 | bytes 1 | tf_op jit(solution)/shard_map/weight_shares/pallas_call | solution.py:403
  127.4 0.9 multiply_exponential_fusion.3
  128.3 0.7 multiply_exponential_fusion.5
  129.1 1.4 fusion.52
  130.7 1.5 collective-permute-start.15
  132.3 1.2 collective-permute-start.22
  133.6 2.6 %collective-permute-start.13 = (f16[528,128]{1,0:T(8,128)(2,1)S(1)}, f16[528,128]{1,0:T(8,128)(2,1)S(1)}, u32[]{:S(2)}, u32[]{:S(2)}) collective-permute-start(f16[528,128]{1,0:T(8,128)(2,1)S(1)} %get-tuple-element.48), channel_id=1, source_target_pairs={{0,1},{1,0},{2,3},{3,2},{4,5},{5,4},{6,7},{7,6},{8,9},{9,8},{10,11... | collective-permute-start | bytes 405512 | tf_op jit(solution)/shard_map/ppermute | solution.py:36
  136.3 2.8 %collective-permute-done.15 = f16[528,128]{1,0:T(8,128)(2,1)S(1)} collective-permute-done((f16[528,128]{1,0:T(8,128)(2,1)S(1)}, f16[528,128]{1,0:T(8,128)(2,1)S(1)}, u32[]{:S(2)}, u32[]{:S(2)}) %collective-permute-start.15) | collective-permute-done | bytes 135200 | tf_op jit(solution)/shard_map/ppermute | solution.py:36
  139.0 5.6 %collective-permute-done.14 = f16[528,128]{1,0:T(8,128)(2,1)S(1)} collective-permute-done((f16[528,128]{1,0:T(8,128)(2,1)S(1)}, f16[528,128]{1,0:T(8,128)(2,1)S(1)}, u32[]{:S(2)}, u32[]{:S(2)}) %collective-permute-start.14) | collective-permute-done | bytes 135200 | tf_op jit(solution)/shard_map/ppermute | solution.py:36
  144.8 1.5 collective-permute-done.22
  146.7 2.9 %collective-permute-start.25 = (f16[528,128]{1,0:T(8,128)(2,1)S(1)}, f16[528,128]{1,0:T(8,128)(2,1)S(1)}, u32[]{:S(2)}, u32[]{:S(2)}) collective-permute-start(f16[528,128]{1,0:T(8,128)(2,1)S(1)} %get-tuple-element.47), channel_id=1, source_target_pairs={{0,3},{1,2},{2,1},{3,0},{4,7},{5,6},{6,5},{7,4},{8,11},{9,10},{10,... | collective-permute-start | bytes 405512 | tf_op jit(solution)/shard_map/ppermute | solution.py:36
  149.7 0.8 collective-permute-start.26
  150.5 1.6 collective-permute-start.23
  152.1 2.7 %collective-permute-done.25 = f16[528,128]{1,0:T(8,128)(2,1)S(1)} collective-permute-done((f16[528,128]{1,0:T(8,128)(2,1)S(1)}, f16[528,128]{1,0:T(8,128)(2,1)S(1)}, u32[]{:S(2)}, u32[]{:S(2)}) %collective-permute-start.25) | collective-permute-done | bytes 135200 | tf_op jit(solution)/shard_map/ppermute | solution.py:36
  154.8 4.8 %collective-permute-done.24 = f16[528,128]{1,0:T(8,128)(2,1)S(1)} collective-permute-done((f16[528,128]{1,0:T(8,128)(2,1)S(1)}, f16[528,128]{1,0:T(8,128)(2,1)S(1)}, u32[]{:S(2)}, u32[]{:S(2)}) %collective-permute-start.24) | collective-permute-done | bytes 135200 | tf_op jit(solution)/shard_map/ppermute | solution.py:36
  159.7 0.9 collective-permute-start.27
  160.7 6.7 %collective-permute-done.27 = f32[512,128]{1,0:T(8,128)S(1)} collective-permute-done((f32[512,128]{1,0:T(8,128)S(1)}, f32[512,128]{1,0:T(8,128)S(1)}, u32[]{:S(2)}, u32[]{:S(2)}) %collective-permute-start.27) | collective-permute-done | bytes 262176 | tf_op jit(solution)/shard_map/ppermute | solution.py:36
  167.6 1.0 copy.26
  168.6 1.0 copy.27
  (97 shorter events, 3.1 us)
Async XLA Ops:
  5.6 50.2 %collective-permute-start.4 = (bf16[2,528,1024]{2,1,0:T(8,128)(2,1)}, bf16[2,528,1024]{2,1,0:T(8,128)(2,1)S(1)}, u32[]{:S(2)}, u32[]{:S(2)}) collective-permute-start(bf16[2,528,1024]{2,1,0:T(8,128)(2,1)} %get-tuple-element.17.after_ref), channel_id=1, source_target_pairs={{0,16},{16,0},{1,17},{17,1},{2,18},{18,2},{3,19},{19,3},{4,20},{20... | collective-permute-start | bytes 6488072 | tf_op jit(solution)/shard_map/ppermute | solution.py:36
  22.4 18.4 %collective-permute-start = (bf16[64,1024]{1,0:T(8,128)(2,1)}, bf16[64,1024]{1,0:T(8,128)(2,1)S(1)}, u32[]{:S(2)}, u32[]{:S(2)}) collective-permute-start(bf16[64,1024]{1,0:T(8,128)(2,1)} %get-tuple-element.18.refs_0_.refs_4_), channel_id=1, source_target_pairs={{0,4},{4,0},{1,5},{5,1},{2,6},{6,2},{3,7},{7,3},{8,12},{12,8},{9,1... | collective-permute-start | bytes 393224 | tf_op jit(solution)/shard_map/ppermute | solution.py:36
  22.5 18.3 %collective-permute-start.1 = (bf16[64,1024]{1,0:T(8,128)(2,1)}, bf16[64,1024]{1,0:T(8,128)(2,1)S(1)}, u32[]{:S(2)}, u32[]{:S(2)}) collective-permute-start(bf16[64,1024]{1,0:T(8,128)(2,1)} %get-tuple-element.18.refs_0_.refs_4_), channel_id=1, source_target_pairs={{0,8},{8,0},{1,9},{9,1},{2,10},{10,2},{3,11},{11,3},{4,12},{12,4},... | collective-permute-start | bytes 393224 | tf_op jit(solution)/shard_map/ppermute | solution.py:36
  24.1 16.7 %collective-permute-start.2 = (bf16[64,1024]{1,0:T(8,128)(2,1)}, bf16[64,1024]{1,0:T(8,128)(2,1)S(1)}, u32[]{:S(2)}, u32[]{:S(2)}) collective-permute-start(bf16[64,1024]{1,0:T(8,128)(2,1)} %get-tuple-element.18.refs_0_.refs_4_), channel_id=1, source_target_pairs={{0,12},{4,8},{8,4},{12,0},{1,13},{5,9},{9,5},{13,1},{2,14},{6,10},... | collective-permute-start | bytes 393224 | tf_op jit(solution)/shard_map/ppermute | solution.py:36
  26.3 12.4 %all-to-all-start = ((f32[16,3,8]{2,1,0:T(4,128)}), f32[16,3,8]{2,1,0:T(4,128)S(1)}, u32[]{:S(2)}, u32[]{:S(2)}) async-start(f32[16,3,8]{2,1,0:T(4,128)} %broadcast_in_dim.20), calls=%async_computation | async-start | bytes 65536 | tf_op jit(solution)/shard_map/all_to_all | solution.py:362
  40.8 0.7 copy-start.5
  40.8 0.7 copy-start.6
  40.8 0.7 copy-start.7
  55.8 1.4 copy-start
  57.2 6.7 %copy-start.10 = (bf16[2,2,128,512]{3,2,1,0:T(8,128)(2,1)S(1)}, bf16[2,2,128,512]{3,2,1,0:T(8,128)(2,1)}, u32[]{:S(2)}) copy-start(bf16[2,2,128,512]{3,2,1,0:T(8,128)(2,1)} %get-tuple-element.23) | copy-start | bytes 1572868
  57.2 39.6 %collective-permute-start.5 = (bf16[2,528,1024]{2,1,0:T(8,128)(2,1)}, bf16[2,528,1024]{2,1,0:T(8,128)(2,1)}, u32[]{:S(2)}, u32[]{:S(2)}) collective-permute-start(bf16[2,528,1024]{2,1,0:T(8,128)(2,1)} %tied.6.refs_15_.refs_2_), channel_id=1, source_target_pairs={{0,4},{4,0},{1,5},{5,1},{2,6},{6,2},{3,7},{7,3},{8,12},{12,8},{9,1... | collective-permute-start | bytes 6488072 | tf_op jit(solution)/shard_map/ppermute | solution.py:36
  57.2 8.4 %collective-permute-start.3 = (bf16[528,1024]{1,0:T(8,128)(2,1)}, bf16[528,1024]{1,0:T(8,128)(2,1)S(1)}, u32[]{:S(2)}, u32[]{:S(2)}) collective-permute-start(bf16[528,1024]{1,0:T(8,128)(2,1)} %get-tuple-element.22), channel_id=1, source_target_pairs={{0,4},{4,0},{1,5},{5,1},{2,6},{6,2},{3,7},{7,3},{8,12},{12,8},{9,1... | collective-permute-start | bytes 3244040 | tf_op jit(solution)/shard_map/ppermute | solution.py:36
  57.7 22.8 %all-to-all-start.1 = ((f32[16,16,512]{2,1,0:T(8,128)}), f32[16,16,512]{2,1,0:T(8,128)S(1)}, u32[]{:S(2)}, u32[]{:S(2)}) async-start(f32[16,16,512]{2,1,0:T(8,128)} %bitcast.19), calls=%async_computation.1 | async-start | bytes 1048576 | tf_op jit(solution)/shard_map/all_to_all | solution.py:362
  64.0 15.4 %collective-permute-start.7 = (bf16[512,512]{1,0:T(8,128)(2,1)S(1)}, bf16[512,512]{1,0:T(8,128)(2,1)S(1)}, u32[]{:S(2)}, u32[]{:S(2)}) collective-permute-start(bf16[512,512]{1,0:T(8,128)(2,1)S(1)} %bitcast.72), channel_id=1, source_target_pairs={{0,16},{16,0},{1,17},{17,1},{2,18},{18,2},{3,19},{19,3},{4,20},{20... | collective-permute-start | bytes 1572872 | tf_op jit(solution)/shard_map/ppermute | solution.py:36
  65.5 30.5 %collective-permute-start.6 = (bf16[512,512]{1,0:T(8,128)(2,1)S(1)}, bf16[512,512]{1,0:T(8,128)(2,1)S(1)}, u32[]{:S(2)}, u32[]{:S(2)}) collective-permute-start(bf16[512,512]{1,0:T(8,128)(2,1)S(1)} %bitcast.73), channel_id=1, source_target_pairs={{0,4},{4,0},{1,5},{5,1},{2,6},{6,2},{3,7},{7,3},{8,12},{12,8},{9,1... | collective-permute-start | bytes 1572872 | tf_op jit(solution)/shard_map/ppermute | solution.py:36
  65.7 1.0 copy-start.2
  79.4 0.8 copy-start.4
  80.2 16.7 %collective-permute-start.8 = (bf16[512,512]{1,0:T(8,128)(2,1)}, bf16[512,512]{1,0:T(8,128)(2,1)}, u32[]{:S(2)}, u32[]{:S(2)}) collective-permute-start(bf16[512,512]{1,0:T(8,128)(2,1)} %tied.7.refs_1_.refs_6_), channel_id=1, source_target_pairs={{0,4},{4,0},{1,5},{5,1},{2,6},{6,2},{3,7},{7,3},{8,12},{12,8},{9,1... | collective-permute-start | bytes 1572872 | tf_op jit(solution)/shard_map/ppermute | solution.py:36
  80.6 0.8 copy-start.9
  83.4 12.1 %copy-start.15 = (bf16[16,512]{1,0:T(8,128)(2,1)S(1)}, bf16[16,512]{1,0:T(8,128)(2,1)}, u32[]{:S(2)}) copy-start(bf16[16,512]{1,0:T(8,128)(2,1)} %row_grads.2.refs_8_) | copy-start | bytes 49156
  83.4 4.1 %collective-permute-start.10 = (bf16[16,512]{1,0:T(8,128)(2,1)}, bf16[16,512]{1,0:T(8,128)(2,1)S(1)}, u32[]{:S(2)}, u32[]{:S(2)}) collective-permute-start(bf16[16,512]{1,0:T(8,128)(2,1)} %row_grads.2.refs_8_), channel_id=1, source_target_pairs={{0,16},{16,0},{1,17},{17,1},{2,18},{18,2},{3,19},{19,3},{4,20},{20... | collective-permute-start | bytes 49160 | tf_op jit(solution)/shard_map/ppermute | solution.py:36
  84.0 3.6 %collective-permute-start.11 = (bf16[16,512]{1,0:T(8,128)(2,1)}, bf16[16,512]{1,0:T(8,128)(2,1)S(1)}, u32[]{:S(2)}, u32[]{:S(2)}) collective-permute-start(bf16[16,512]{1,0:T(8,128)(2,1)} %row_grads.2.refs_8_), channel_id=1, source_target_pairs={{0,20},{4,16},{16,4},{20,0},{1,21},{5,17},{17,5},{21,1},{2,22},{6,... | collective-permute-start | bytes 49160 | tf_op jit(solution)/shard_map/ppermute | solution.py:36
  87.5 0.6 copy-start.16
  88.1 0.6 copy-start.17
  88.7 7.3 %copy-start.1 = (bf16[512,512]{1,0:T(8,128)(2,1)S(1)}, bf16[512,512]{1,0:T(8,128)(2,1)}, u32[]{:S(2)}) copy-start(bf16[512,512]{1,0:T(8,128)(2,1)} %tied.9.refs_4_) | copy-start | bytes 1572868
  88.7 19.3 %collective-permute-start.17 = (bf16[512,512]{1,0:T(8,128)(2,1)}, bf16[512,512]{1,0:T(8,128)(2,1)S(1)}, u32[]{:S(2)}, u32[]{:S(2)}) collective-permute-start(bf16[512,512]{1,0:T(8,128)(2,1)} %tied.9.refs_4_), channel_id=1, source_target_pairs={{0,16},{16,0},{1,17},{17,1},{2,18},{18,2},{3,19},{19,3},{4,20},{20... | collective-permute-start | bytes 1572872 | tf_op jit(solution)/shard_map/ppermute | solution.py:36
  89.6 21.7 %all-to-all-start.2 = ((f32[16,16,512]{2,1,0:T(8,128)}), f32[16,16,512]{2,1,0:T(8,128)S(1)}, u32[]{:S(2)}, u32[]{:S(2)}) async-start(f32[16,16,512]{2,1,0:T(8,128)} %bitcast.65), calls=%async_computation.2 | async-start | bytes 1048576 | tf_op jit(solution)/shard_map/all_to_all | solution.py:362
  95.5 1.3 collective-permute-start.9
  96.0 0.8 copy-start.13
  96.0 19.3 %collective-permute-start.16 = (bf16[512,512]{1,0:T(8,128)(2,1)S(1)}, bf16[512,512]{1,0:T(8,128)(2,1)S(1)}, u32[]{:S(2)}, u32[]{:S(2)}) collective-permute-start(bf16[512,512]{1,0:T(8,128)(2,1)S(1)} %copy-done.1), channel_id=1, source_target_pairs={{0,4},{4,0},{1,5},{5,1},{2,6},{6,2},{3,7},{7,3},{8,12},{12,8},{9,1... | collective-permute-start | bytes 1572872 | tf_op jit(solution)/shard_map/ppermute | solution.py:36
  96.8 0.6 copy-start.21
  106.1 21.3 %collective-permute-start.12 = (f16[528,512]{1,0:T(8,128)(2,1)S(1)}, f16[528,512]{1,0:T(8,128)(2,1)S(1)}, u32[]{:S(2)}, u32[]{:S(2)}) collective-permute-start(f16[528,512]{1,0:T(8,128)(2,1)S(1)} %slice_convert_fusion.1), channel_id=1, source_target_pairs={{0,8},{8,0},{1,9},{9,1},{2,10},{10,2},{3,11},{11,3},{4,12},{12,4},... | collective-permute-start | bytes 1622024 | tf_op jit(solution)/shard_map/ppermute | solution.py:36
  108.0 0.8 copy-start.11
  108.8 9.8 %collective-permute-start.18 = (bf16[512,512]{1,0:T(8,128)(2,1)}, bf16[512,512]{1,0:T(8,128)(2,1)S(1)}, u32[]{:S(2)}, u32[]{:S(2)}) collective-permute-start(bf16[512,512]{1,0:T(8,128)(2,1)} %tied.10.refs_6_), channel_id=1, source_target_pairs={{0,4},{4,0},{1,5},{5,1},{2,6},{6,2},{3,7},{7,3},{8,12},{12,8},{9,1... | collective-permute-start | bytes 1572872 | tf_op jit(solution)/shard_map/ppermute | solution.py:36
  111.2 0.8 copy-start.8
  114.1 1.9 %collective-permute-start.19 = (bf16[16,512]{1,0:T(8,128)(2,1)}, bf16[16,512]{1,0:T(8,128)(2,1)S(1)}, u32[]{:S(2)}, u32[]{:S(2)}) collective-permute-start(bf16[16,512]{1,0:T(8,128)(2,1)} %row_grads.3.refs_8_), channel_id=1, source_target_pairs={{0,4},{4,0},{1,5},{5,1},{2,6},{6,2},{3,7},{7,3},{8,12},{12,8},{9,1... | collective-permute-start | bytes 49160 | tf_op jit(solution)/shard_map/ppermute | solution.py:36
  114.1 3.9 %collective-permute-start.20 = (bf16[16,512]{1,0:T(8,128)(2,1)}, bf16[16,512]{1,0:T(8,128)(2,1)S(1)}, u32[]{:S(2)}, u32[]{:S(2)}) collective-permute-start(bf16[16,512]{1,0:T(8,128)(2,1)} %row_grads.3.refs_8_), channel_id=1, source_target_pairs={{0,16},{16,0},{1,17},{17,1},{2,18},{18,2},{3,19},{19,3},{4,20},{20... | collective-permute-start | bytes 49160 | tf_op jit(solution)/shard_map/ppermute | solution.py:36
  115.3 3.4 %copy-start.12 = (bf16[512,512]{1,0:T(8,128)(2,1)}, bf16[512,512]{1,0:T(8,128)(2,1)S(1)}, u32[]{:S(2)}) copy-start(bf16[512,512]{1,0:T(8,128)(2,1)S(1)} %collective-permute-done.16.refs_5_) | copy-start | bytes 1572868
  115.3 3.4 %collective-permute-start.21 = (bf16[16,512]{1,0:T(8,128)(2,1)}, bf16[16,512]{1,0:T(8,128)(2,1)S(1)}, u32[]{:S(2)}, u32[]{:S(2)}) collective-permute-start(bf16[16,512]{1,0:T(8,128)(2,1)} %row_grads.3.refs_8_), channel_id=1, source_target_pairs={{0,20},{4,16},{16,4},{20,0},{1,21},{5,17},{17,5},{21,1},{2,22},{6,... | collective-permute-start | bytes 49160 | tf_op jit(solution)/shard_map/ppermute | solution.py:36
  115.9 2.8 %copy-start.18 = (bf16[16,512]{1,0:T(8,128)(2,1)}, bf16[16,512]{1,0:T(8,128)(2,1)S(1)}, u32[]{:S(2)}) copy-start(bf16[16,512]{1,0:T(8,128)(2,1)S(1)} %collective-permute-done.19.refs_9_) | copy-start | bytes 49156
  118.0 0.7 copy-start.19
  118.7 0.6 copy-start.20
  119.3 0.8 copy-start.14
  127.4 4.8 %copy-start.3 = (f32[528,1024]{1,0:T(8,128)S(1)}, f32[528,1024]{1,0:T(8,128)}, u32[]{:S(2)}) copy-start(f32[528,1024]{1,0:T(8,128)} %weight_shares.3) | copy-start | bytes 6488068
  130.7 8.4 %collective-permute-start.15 = (f16[528,128]{1,0:T(8,128)(2,1)S(1)}, f16[528,128]{1,0:T(8,128)(2,1)S(1)}, u32[]{:S(2)}, u32[]{:S(2)}) collective-permute-start(f16[528,128]{1,0:T(8,128)(2,1)S(1)} %get-tuple-element.50), channel_id=1, source_target_pairs={{0,3},{1,2},{2,1},{3,0},{4,7},{5,6},{6,5},{7,4},{8,11},{9,10},{10,... | collective-permute-start | bytes 405512 | tf_op jit(solution)/shard_map/ppermute | solution.py:36
  132.3 14.0 %collective-permute-start.22 = (f16[528,512]{1,0:T(8,128)(2,1)S(1)}, f16[528,512]{1,0:T(8,128)(2,1)S(1)}, u32[]{:S(2)}, u32[]{:S(2)}) collective-permute-start(f16[528,512]{1,0:T(8,128)(2,1)S(1)} %slice_convert_fusion), channel_id=1, source_target_pairs={{0,8},{8,0},{1,9},{9,1},{2,10},{10,2},{3,11},{11,3},{4,12},{12,4},... | collective-permute-start | bytes 1622024 | tf_op jit(solution)/shard_map/ppermute | solution.py:36
  133.5 11.1 %collective-permute-start.14 = (f16[528,128]{1,0:T(8,128)(2,1)S(1)}, f16[528,128]{1,0:T(8,128)(2,1)S(1)}, u32[]{:S(2)}, u32[]{:S(2)}) collective-permute-start(f16[528,128]{1,0:T(8,128)(2,1)S(1)} %get-tuple-element.49), channel_id=1, source_target_pairs={{0,2},{1,3},{2,0},{3,1},{4,6},{5,7},{6,4},{7,5},{8,10},{9,11},{10,... | collective-permute-start | bytes 405512 | tf_op jit(solution)/shard_map/ppermute | solution.py:36
  133.6 11.0 %collective-permute-start.13 = (f16[528,128]{1,0:T(8,128)(2,1)S(1)}, f16[528,128]{1,0:T(8,128)(2,1)S(1)}, u32[]{:S(2)}, u32[]{:S(2)}) collective-permute-start(f16[528,128]{1,0:T(8,128)(2,1)S(1)} %get-tuple-element.48), channel_id=1, source_target_pairs={{0,1},{1,0},{2,3},{3,2},{4,5},{5,4},{6,7},{7,6},{8,9},{9,8},{10,11... | collective-permute-start | bytes 405512 | tf_op jit(solution)/shard_map/ppermute | solution.py:36
  146.7 8.1 %collective-permute-start.25 = (f16[528,128]{1,0:T(8,128)(2,1)S(1)}, f16[528,128]{1,0:T(8,128)(2,1)S(1)}, u32[]{:S(2)}, u32[]{:S(2)}) collective-permute-start(f16[528,128]{1,0:T(8,128)(2,1)S(1)} %get-tuple-element.47), channel_id=1, source_target_pairs={{0,3},{1,2},{2,1},{3,0},{4,7},{5,6},{6,5},{7,4},{8,11},{9,10},{10,... | collective-permute-start | bytes 405512 | tf_op jit(solution)/shard_map/ppermute | solution.py:36
  149.7 11.0 %collective-permute-start.26 = (f32[512,128]{1,0:T(8,128)S(1)}, f32[512,128]{1,0:T(8,128)S(1)}, u32[]{:S(2)}, u32[]{:S(2)}) collective-permute-start(f32[512,128]{1,0:T(8,128)S(1)} %fusion.11), channel_id=1, source_target_pairs={{0,16},{16,0},{1,17},{17,1},{2,18},{18,2},{3,19},{19,3},{4,20},{20... | collective-permute-start | bytes 786440 | tf_op jit(solution)/shard_map/ppermute | solution.py:36
  150.5 9.2 %collective-permute-start.24 = (f16[528,128]{1,0:T(8,128)(2,1)S(1)}, f16[528,128]{1,0:T(8,128)(2,1)S(1)}, u32[]{:S(2)}, u32[]{:S(2)}) collective-permute-start(f16[528,128]{1,0:T(8,128)(2,1)S(1)} %get-tuple-element.46), channel_id=1, source_target_pairs={{0,2},{1,3},{2,0},{3,1},{4,6},{5,7},{6,4},{7,5},{8,10},{9,11},{10,... | collective-permute-start | bytes 405512 | tf_op jit(solution)/shard_map/ppermute | solution.py:36
  150.5 9.2 %collective-permute-start.23 = (f16[528,128]{1,0:T(8,128)(2,1)S(1)}, f16[528,128]{1,0:T(8,128)(2,1)S(1)}, u32[]{:S(2)}, u32[]{:S(2)}) collective-permute-start(f16[528,128]{1,0:T(8,128)(2,1)S(1)} %get-tuple-element.45), channel_id=1, source_target_pairs={{0,1},{1,0},{2,3},{3,2},{4,5},{5,4},{6,7},{7,6},{8,9},{9,8},{10,11... | collective-permute-start | bytes 405512 | tf_op jit(solution)/shard_map/ppermute | solution.py:36
  159.7 7.7 %collective-permute-start.27 = (f32[512,128]{1,0:T(8,128)S(1)}, f32[512,128]{1,0:T(8,128)S(1)}, u32[]{:S(2)}, u32[]{:S(2)}) collective-permute-start(f32[512,128]{1,0:T(8,128)S(1)} %fusion.8), channel_id=1, source_target_pairs={{0,16},{16,0},{1,17},{17,1},{2,18},{18,2},{3,19},{19,3},{4,20},{20... | collective-permute-start | bytes 786440 | tf_op jit(solution)/shard_map/ppermute | solution.py:36
